TPU v7x, 32 devices: a whole 2x2x4 slice. The times are simulated.
32 devices in a mesh: shots: 2 (over y), track: 8 (over z, x), depth: 2 (over core).
Axes of the slice: x: 2, y: 2, z: 4, core: 2. Of those that a mesh axis runs over, the one named last changes fastest.
Arguments:
- velocity: float32 [4, 512, 512], P('shots', 'track', 'depth'), parts along dimension 0, may hold values from -6 to 6
- stress: float32 [6, 512, 512], P('shots', 'track', 'depth'), parts along dimension 0, may hold values from -6 to 6
- adjoint_velocity: float32 [4, 512, 512], P('shots', 'track', 'depth'), parts along dimension 0, may hold values from -6 to 6
- adjoint_stress: float32 [6, 512, 512], P('shots', 'track', 'depth'), parts along dimension 0, may hold values from -6 to 6
- buoyancy: float32 [512, 512], P('track', 'depth'), may hold values from 0.3 to 0.8
- lame_lambda: float32 [512, 512], P('track', 'depth'), may hold values from 0.05 to 0.2
- shear_modulus: float32 [512, 512], P('track', 'depth'), may hold values from 0.05 to 0.2
- observed: float32 [8, 2048], P('shots', 'track'), parts along dimension 0, may hold values from -6 to 6
- owner_track: int32 [2048, 1], P('track'), may hold values from 0 to 7; in each aligned block of 256 rows (0 to 255, 256 to 511, ...) at most 64 rows name the same one
- fibre_cell: int32 [2048], P('track'), may hold values from 0 to 255
Outputs:
- gradient_lambda: float32 [1024, 512], P(('shots', 'track'), 'depth'), parts along dimension 0
- gradient_mu: float32 [1024, 512], P(('shots', 'track'), 'depth'), parts along dimension 0
- velocity_end: float32 [4, 512, 512], P('shots', 'track', 'depth'), parts along dimension 0
- residual_traces: float32 [8, 2048], P(('shots', 'depth'), 'track'), parts along dimension 0
There are 2 independent parts, one for each index of `shots`. A program takes and returns all parts, laid end to end along the dimension named above; an argument that names none is the same for every part. Nothing has to cross between parts.
Inputs may be any that keep to these rules, and one draw needn't show every extreme that they name: `owner_track`: among the channels of one index of track, no slab is named by more than 64 of them, a bound that some block reaches.
All inputs are finite; a program needn't handle non-finite values.
Results may differ from a plain program's by a relative error of at most 0.00002.
Values sent between devices are 32-bit elements; how exact they have to be, the bound alone decides.
No kernel may reach another device: no remote copies, remote signals or barrier semaphores. Data moves between devices by JAX's collectives and lax.ppermute only.
A program may use at most 64 MiB of HBM per device.

v0:
```python
import jax
import jax.numpy as jnp
from jax import lax
from jax.sharding import PartitionSpec as P

FIBRE_ROWS = 4


NEAR_WEIGHT = 9.0 / 8.0
FAR_WEIGHT = -1.0 / 24.0


def extended(cells, sides, width):
    for axis, dim in sides:
        count = lax.axis_size(axis)
        ends = count - 1
        head = lax.slice_in_dim(cells, 0, width, axis=dim)
        tail = lax.slice_in_dim(cells, cells.shape[dim] - width, cells.shape[dim], axis=dim)
        cells = jnp.concatenate(
            [
                lax.ppermute(tail, axis, [(i, (i + 1) % count) for i in range(ends)]),
                cells,
                lax.ppermute(head, axis, [((i + 1) % count, i) for i in range(ends)]),
            ],
            axis=dim,
        )
    return cells


def spread(block, axis, owner):
    block = jnp.where(lax.axis_index(axis) == owner, block, jnp.zeros_like(block))
    return lax.psum(block, axis)


def window_of(field, start_at, cut_count, dim_index):
    return lax.slice_in_dim(field, start_at, start_at + cut_count, axis=dim_index)


def ahead_diff(field, dim_index):
    cut_count = field.shape[dim_index] - 4
    return NEAR_WEIGHT * (
        window_of(field, 3, cut_count, dim_index) - window_of(field, 2, cut_count, dim_index)
    ) + FAR_WEIGHT * (
        window_of(field, 4, cut_count, dim_index) - window_of(field, 1, cut_count, dim_index)
    )


def behind_diff(field, dim_index):
    cut_count = field.shape[dim_index] - 4
    return NEAR_WEIGHT * (
        window_of(field, 2, cut_count, dim_index) - window_of(field, 1, cut_count, dim_index)
    ) + FAR_WEIGHT * (
        window_of(field, 3, cut_count, dim_index) - window_of(field, 0, cut_count, dim_index)
    )


def velocity_update(speed_along, speed_down, press_along, press_down, press_shear, buoy_part):
    new_along = speed_along + buoy_part * (
        behind_diff(press_along, 0)[:, 2:-2] + behind_diff(press_shear, 1)[2:-2, :]
    )
    new_down = speed_down + buoy_part * (
        ahead_diff(press_shear, 0)[:, 2:-2] + ahead_diff(press_down, 1)[2:-2, :]
    )
    return (new_along, new_down)


def stress_update(
    wide_along, wide_down, speed_along, speed_down, old_stress, lame_lambda, shear_modulus, modulus
):
    strain_along = ahead_diff(wide_along, 0)[:, 2:-2]
    strain_down = behind_diff(wide_down, 1)[2:-2, :]
    shear_rate = ahead_diff(wide_along, 1)[2:-2, :] + behind_diff(wide_down, 0)[:, 2:-2]
    new_xx = old_stress[0] + modulus * strain_along + lame_lambda * strain_down
    new_zz = old_stress[1] + lame_lambda * strain_along + modulus * strain_down
    new_xz = old_stress[2] + shear_modulus * shear_rate
    fields = jnp.stack([speed_along, speed_down, new_xx, new_zz, new_xz])
    return (fields, (strain_along, strain_down, shear_rate))


def advance(fields, wide_buoy, lame_lambda, shear_modulus, modulus):
    all_fields = extended(fields, (("track", 1), ("depth", 2)), 4)
    wide_along, wide_down = velocity_update(
        all_fields[0, 2:-2, 2:-2],
        all_fields[1, 2:-2, 2:-2],
        all_fields[2],
        all_fields[3],
        all_fields[4],
        wide_buoy,
    )
    return stress_update(
        wide_along,
        wide_down,
        wide_along[2:-2, 2:-2],
        wide_down[2:-2, 2:-2],
        fields[2:5],
        lame_lambda,
        shear_modulus,
        modulus,
    )


def per_device(
    velocity,
    stress,
    adjoint_velocity,
    adjoint_stress,
    buoyancy,
    lame_lambda,
    shear_modulus,
    observed,
    owner_track,
    fibre_cell,
):
    tracks = lax.axis_size("track")
    surface = lax.axis_index("depth") == 0
    row_count, depth_cells = buoyancy.shape
    moments = observed.shape[0]
    channels = fibre_cell.shape[0]
    modulus = lame_lambda + 2.0 * shear_modulus
    wide_buoy = extended(buoyancy, (("track", 0), ("depth", 1)), 2)
    capacity = 2 * channels // tracks
    owners = owner_track[:, 0]
    one_hot = (owners[:, None] == jnp.arange(tracks, dtype=jnp.int32)[None, :]).astype(jnp.int32)
    slot_rank = jnp.sum((jnp.cumsum(one_hot, axis=0) - 1) * one_hot, axis=1)
    placed = owners * capacity + slot_rank
    slot_count = tracks * capacity
    sent_obs = jnp.zeros((moments, slot_count), jnp.float32).at[:, placed].set(observed)
    sent_cell = jnp.full((1, slot_count), -1, jnp.int32).at[0, placed].set(fibre_cell)
    got_obs, got_cell = (
        lax.all_to_all(sent_obs, "track", split_axis=1, concat_axis=1, tiled=True),
        lax.all_to_all(sent_cell, "track", split_axis=1, concat_axis=1, tiled=True),
    )
    targets = got_cell[0]
    live_slot = targets >= 0
    safe_cell = jnp.where(live_slot, targets, 0)
    flat_cell = (safe_cell // FIBRE_ROWS * depth_cells + safe_cell % FIBRE_ROWS).astype(jnp.int32)
    inject = live_slot & surface
    fields = jnp.concatenate([velocity, stress], axis=0)
    saved = []
    records = []
    for step_index in range(moments):
        fields, strains = advance(fields, wide_buoy, lame_lambda, shear_modulus, modulus)
        saved.append(strains)
        records.append(jnp.where(inject, strains[0].reshape(-1)[flat_cell], 0.0))
    recorded = spread(jnp.stack(records), "depth", 0)
    residual = jnp.where(live_slot[None, :], recorded - got_obs, 0.0)
    adjoint = jnp.concatenate([adjoint_velocity, adjoint_stress], axis=0)
    gradient_lambda = jnp.zeros((row_count, depth_cells), jnp.float32)
    gradient_mu = jnp.zeros((row_count, depth_cells), jnp.float32)
    for back_index in range(moments):
        moment = moments - 1 - back_index
        press = adjoint[2].reshape(-1).at[flat_cell].add(jnp.where(inject, residual[moment], 0.0))
        adjoint = adjoint.at[2].set(press.reshape(row_count, depth_cells))
        adjoint, adjoint_strains = advance(adjoint, wide_buoy, lame_lambda, shear_modulus, modulus)
        fwd_along, fwd_down, fwd_shear = saved[moment]
        adj_along, adj_down, adj_shear = adjoint_strains
        gradient_lambda = gradient_lambda + (fwd_along + fwd_down) * (adj_along + adj_down)
        gradient_mu = (
            gradient_mu
            + 2.0 * (fwd_along * adj_along + fwd_down * adj_down)
            + fwd_shear * adj_shear
        )
    returned = lax.all_to_all(residual, "track", split_axis=1, concat_axis=1, tiled=True)
    whole_traces = returned[:, placed]
    own_moments = moments // lax.axis_size("depth")
    first_moment = lax.axis_index("depth") * own_moments
    residual_traces = lax.dynamic_slice_in_dim(whole_traces, first_moment, own_moments, 0)
    return (gradient_lambda, gradient_mu, fields[0:2], residual_traces)


def solution(mesh):
    return jax.shard_map(
        per_device,
        mesh=mesh,
        in_specs=(
            P("shots", "track", "depth"),
            P("shots", "track", "depth"),
            P("shots", "track", "depth"),
            P("shots", "track", "depth"),
            P("track", "depth"),
            P("track", "depth"),
            P("track", "depth"),
            P("shots", "track"),
            P("track", None),
            P("track"),
        ),
        out_specs=(
            P(("shots", "track"), "depth"),
            P(("shots", "track"), "depth"),
            P("shots", "track", "depth"),
            P(("shots", "depth"), "track"),
        ),
        check_vma=False,
    )
```

profile of v0, /device:TPU:0, one launch (start us, length us, event | category | flops | bytes accessed | tf_op | source)
XLA Modules:
  0.0 201.7 jit_solution(9178994262317502294)
XLA Ops:
  0.6 1.0 constant_dynamic-update-slice_fusion.1
  1.7 4.8 %collective-permute-start = (f32[5,4,256]{2,1,0:T(4,128)S(1)}, f32[5,4,256]{2,1,0:T(4,128)S(1)}, u32[]{:S(2)}, u32[]{:S(2)}) collective-permute-start(f32[5,4,256]{2,1,0:T(4,128)S(1)} %get-tuple-element.194), channel_id=1, source_target_pairs={{0,2},{2,4},{4,6},{6,8},{8,10},{10,12},{12,14},{1,3},{3,5},{5,7},{... | collective-permute-start | bytes 61448 | tf_op jit(solution)/shard_map/ppermute | solution.py:21
  6.5 1.3 collective-permute-start.1
  7.8 4.5 %collective-permute-start.4 = (f32[2,256]{1,0:T(2,128)S(1)}, f32[2,256]{1,0:T(2,128)S(1)}, u32[]{:S(2)}, u32[]{:S(2)}) collective-permute-start(f32[2,256]{1,0:T(2,128)S(1)} %get-tuple-element.390), channel_id=1, source_target_pairs={{0,2},{2,4},{4,6},{6,8},{8,10},{10,12},{12,14},{1,3},{3,5},{5,7},{... | collective-permute-start | bytes 6152 | tf_op jit(solution)/shard_map/ppermute | solution.py:21
  12.4 1.3 collective-permute-start.5
  14.7 3.6 %collective-permute-done.5 = f32[2,256]{1,0:T(2,128)S(1)} collective-permute-done((f32[2,256]{1,0:T(2,128)S(1)}, f32[2,256]{1,0:T(2,128)S(1)}, u32[]{:S(2)}, u32[]{:S(2)}) %collective-permute-start.5) | collective-permute-done | bytes 2080 | tf_op jit(solution)/shard_map/ppermute | solution.py:23
  18.5 1.3 collective-permute-start.2
  19.8 1.3 collective-permute-start.3
  21.2 3.0 %collective-permute-start.6 = (f32[68,2]{1,0:T(8,128)S(1)}, f32[68,2]{1,0:T(8,128)S(1)}, u32[]{:S(2)}, u32[]{:S(2)}) collective-permute-start(f32[68,2]{1,0:T(8,128)S(1)} %get-tuple-element.388), channel_id=1, source_target_pairs={{0,1},{2,3},{4,5},{6,7},{8,9},{10,11},{12,13},{14,15},{16,17},{18,... | collective-permute-start | bytes 1640 | tf_op jit(solution)/shard_map/ppermute | solution.py:21
  24.2 1.3 collective-permute-start.7
  26.3 1.1 collective-permute-done.7
  29.3 4.8 %collective-permute-start.8 = (f32[5,4,256]{2,1,0:T(4,128)S(1)}, f32[5,4,256]{2,1,0:T(4,128)S(1)}, u32[]{:S(2)}, u32[]{:S(2)}) collective-permute-start(f32[5,4,256]{2,1,0:T(4,128)S(1)} %get-tuple-element.192), channel_id=1, source_target_pairs={{0,2},{2,4},{4,6},{6,8},{8,10},{10,12},{12,14},{1,3},{3,5},{5,7},{... | collective-permute-start | bytes 61448 | tf_op jit(solution)/shard_map/ppermute | solution.py:21
  34.2 1.3 collective-permute-start.9
  35.5 1.6 scatter_custom_fusion
  37.7 5.9 %all-to-all-start = ((s32[1,8,64]{2,0,1:T(1,128)}), s32[1,8,64]{2,0,1:T(1,128)S(1)}, u32[]{:S(2)}, u32[]{:S(2)}) async-start(s32[1,8,64]{2,0,1:T(1,128)} %all_to_all.22), calls=%async_computation | async-start | bytes 8192 | tf_op jit(solution)/shard_map/all_to_all | solution.py:131
  43.9 1.3 collective-permute-start.10
  45.2 1.3 collective-permute-start.11
  46.5 2.0 collective-permute-done.11
  50.4 3.9 %collective-permute-start.12 = (f32[5,4,256]{2,1,0:T(4,128)S(1)}, f32[5,4,256]{2,1,0:T(4,128)S(1)}, u32[]{:S(2)}, u32[]{:S(2)}) collective-permute-start(f32[5,4,256]{2,1,0:T(4,128)S(1)} %get-tuple-element.190), channel_id=1, source_target_pairs={{0,2},{2,4},{4,6},{6,8},{8,10},{10,12},{12,14},{1,3},{3,5},{5,7},{... | collective-permute-start | bytes 61448 | tf_op jit(solution)/shard_map/ppermute | solution.py:21
  54.3 1.3 collective-permute-start.13
  56.5 1.2 scatter_custom_fusion.1
  58.6 6.6 %all-to-all-start.1 = ((f32[8,1,256]{2,1,0:T(1,128)}), f32[8,1,256]{2,1,0:T(1,128)S(1)}, u32[]{:S(2)}, u32[]{:S(2)}) async-start(f32[8,1,256]{2,1,0:T(1,128)} %reshape.617), calls=%async_computation.1 | async-start | bytes 16384 | tf_op jit(solution)/shard_map/all_to_all | solution.py:130
  66.6 1.3 collective-permute-start.14
  67.9 1.3 collective-permute-start.15
  69.3 2.0 collective-permute-done.15
  73.7 3.9 %collective-permute-start.16 = (f32[5,4,256]{2,1,0:T(4,128)S(1)}, f32[5,4,256]{2,1,0:T(4,128)S(1)}, u32[]{:S(2)}, u32[]{:S(2)}) collective-permute-start(f32[5,4,256]{2,1,0:T(4,128)S(1)} %get-tuple-element.188), channel_id=1, source_target_pairs={{0,2},{2,4},{4,6},{6,8},{8,10},{10,12},{12,14},{1,3},{3,5},{5,7},{... | collective-permute-start | bytes 61448 | tf_op jit(solution)/shard_map/ppermute | solution.py:21
  77.7 1.3 collective-permute-start.17
  79.1 4.2 %collective-permute-done.17 = f32[5,4,256]{2,1,0:T(4,128)S(1)} collective-permute-done((f32[5,4,256]{2,1,0:T(4,128)S(1)}, f32[5,4,256]{2,1,0:T(4,128)S(1)}, u32[]{:S(2)}, u32[]{:S(2)}) %collective-permute-start.17) | collective-permute-done | bytes 20512 | tf_op jit(solution)/shard_map/ppermute | solution.py:23
  83.5 1.3 collective-permute-start.18
  84.8 1.3 collective-permute-start.19
  87.7 3.1 %gather_fusion = f32[512]{0:T(512)S(1)} fusion(f32[16384]{0:T(1024)S(1)} %bitcast.353, s32[1024]{0:T(1024)S(1)} %pad_clamp_fusion.1), kind=kCustom, calls=%fused_computation | custom fusion | bytes 6144 | tf_op jit(solution)/shard_map/gather | solution.py:144
  90.9 3.1 %gather_fusion.1 = f32[512]{0:T(512)S(1)} fusion(f32[16384]{0:T(1024)S(1)} %bitcast.354, s32[1024]{0:T(1024)S(1)} %pad_clamp_fusion.1), kind=kCustom, calls=%fused_computation.1 | custom fusion | bytes 6144 | tf_op jit(solution)/shard_map/gather | solution.py:144
  94.1 3.1 %gather_fusion.2 = f32[512]{0:T(512)S(1)} fusion(f32[16384]{0:T(1024)S(1)} %bitcast.355, s32[1024]{0:T(1024)S(1)} %pad_clamp_fusion.1), kind=kCustom, calls=%fused_computation.2 | custom fusion | bytes 6144 | tf_op jit(solution)/shard_map/gather | solution.py:144
  98.5 3.1 %gather_fusion.3 = f32[512]{0:T(512)S(1)} fusion(f32[16384]{0:T(1024)S(1)} %bitcast.352, s32[1024]{0:T(1024)S(1)} %pad_clamp_fusion.1), kind=kCustom, calls=%fused_computation.3 | custom fusion | bytes 6144 | tf_op jit(solution)/shard_map/gather | solution.py:144
  101.7 3.3 %psum.7 = f32[4,512]{1,0:T(4,128)S(1)} all-reduce(f32[4,512]{1,0:T(4,128)S(1)} %maximum_select_fusion), channel_id=1, replica_groups=mesh['shots'=2,'track'=8,'depth'=2] {'depth'}, use_global_device_ids=true, to_apply=%region_4.5 | all-reduce | flops 2048 | bytes 16384 | tf_op jit(solution)/shard_map/psum | solution.py:32
  105.0 3.6 %scatter_fusion = f32[16384]{0:T(1024)S(1)} fusion(f32[16384]{0:T(1024)S(1)} %bitcast.348, s32[512]{0:T(512)S(1)} %bitcast.366, f32[512]{0:T(512)S(1)} %get-tuple-element.402), kind=kCustom, calls=%fused_computation.7 | custom fusion | flops 512 | bytes 8192 | tf_op jit(solution)/shard_map/scatter-add | solution.py:152
  108.7 4.7 %collective-permute-start.20 = (f32[5,4,256]{2,1,0:T(4,128)S(1)}, f32[5,4,256]{2,1,0:T(4,128)S(1)}, u32[]{:S(2)}, u32[]{:S(2)}) collective-permute-start(f32[5,4,256]{2,1,0:T(4,128)S(1)} %get-tuple-element.186), channel_id=1, source_target_pairs={{0,2},{2,4},{4,6},{6,8},{8,10},{10,12},{12,14},{1,3},{3,5},{5,7},{... | collective-permute-start | bytes 61448 | tf_op jit(solution)/shard_map/ppermute | solution.py:21
  113.5 1.3 collective-permute-start.21
  114.9 4.2 %collective-permute-done.21 = f32[5,4,256]{2,1,0:T(4,128)S(1)} collective-permute-done((f32[5,4,256]{2,1,0:T(4,128)S(1)}, f32[5,4,256]{2,1,0:T(4,128)S(1)}, u32[]{:S(2)}, u32[]{:S(2)}) %collective-permute-start.21) | collective-permute-done | bytes 20512 | tf_op jit(solution)/shard_map/ppermute | solution.py:23
  119.3 1.3 collective-permute-start.22
  120.6 1.3 collective-permute-start.23
  122.0 1.9 collective-permute-done.23
  125.6 3.4 %scatter_fusion.1 = f32[16384]{0:T(1024)S(1)} fusion(f32[16384]{0:T(1024)S(1)} %bitcast.350, s32[512]{0:T(512)S(1)} %bitcast.367, f32[512]{0:T(512)S(1)} %get-tuple-element.401), kind=kCustom, calls=%fused_computation.8 | custom fusion | flops 512 | bytes 8192 | tf_op jit(solution)/shard_map/scatter-add | solution.py:152
  129.9 3.3 %collective-permute-start.24 = (f32[5,4,256]{2,1,0:T(4,128)S(1)}, f32[5,4,256]{2,1,0:T(4,128)S(1)}, u32[]{:S(2)}, u32[]{:S(2)}) collective-permute-start(f32[5,4,256]{2,1,0:T(4,128)S(1)} %get-tuple-element.184), channel_id=1, source_target_pairs={{0,2},{2,4},{4,6},{6,8},{8,10},{10,12},{12,14},{1,3},{3,5},{5,7},{... | collective-permute-start | bytes 61448 | tf_op jit(solution)/shard_map/ppermute | solution.py:21
  133.2 1.3 collective-permute-start.25
  134.7 4.2 %collective-permute-done.25 = f32[5,4,256]{2,1,0:T(4,128)S(1)} collective-permute-done((f32[5,4,256]{2,1,0:T(4,128)S(1)}, f32[5,4,256]{2,1,0:T(4,128)S(1)}, u32[]{:S(2)}, u32[]{:S(2)}) %collective-permute-start.25) | collective-permute-done | bytes 20512 | tf_op jit(solution)/shard_map/ppermute | solution.py:23
  139.8 1.3 collective-permute-start.26
  141.1 1.3 collective-permute-start.27
  143.2 1.2 collective-permute-done.27
  147.5 3.4 %scatter_fusion.2 = f32[16384]{0:T(1024)S(1)} fusion(f32[16384]{0:T(1024)S(1)} %bitcast.349, s32[512]{0:T(512)S(1)} %bitcast.368, f32[512]{0:T(512)S(1)} %get-tuple-element.400), kind=kCustom, calls=%fused_computation.9 | custom fusion | flops 512 | bytes 8192 | tf_op jit(solution)/shard_map/scatter-add | solution.py:152
  153.4 4.6 %collective-permute-start.28 = (f32[5,4,256]{2,1,0:T(4,128)S(1)}, f32[5,4,256]{2,1,0:T(4,128)S(1)}, u32[]{:S(2)}, u32[]{:S(2)}) collective-permute-start(f32[5,4,256]{2,1,0:T(4,128)S(1)} %get-tuple-element.182), channel_id=1, source_target_pairs={{0,2},{2,4},{4,6},{6,8},{8,10},{10,12},{12,14},{1,3},{3,5},{5,7},{... | collective-permute-start | bytes 61448 | tf_op jit(solution)/shard_map/ppermute | solution.py:21
  158.0 1.3 collective-permute-start.29
  160.0 3.7 %collective-permute-done.29 = f32[5,4,256]{2,1,0:T(4,128)S(1)} collective-permute-done((f32[5,4,256]{2,1,0:T(4,128)S(1)}, f32[5,4,256]{2,1,0:T(4,128)S(1)}, u32[]{:S(2)}, u32[]{:S(2)}) %collective-permute-start.29) | collective-permute-done | bytes 20512 | tf_op jit(solution)/shard_map/ppermute | solution.py:23
  164.5 1.3 collective-permute-start.30
  165.8 1.3 collective-permute-start.31
  168.6 3.8 %all-to-all-start.2 = ((f32[8,1,256]{2,1,0:T(1,128)}), f32[8,1,256]{2,1,0:T(1,128)S(1)}, u32[]{:S(2)}, u32[]{:S(2)}) async-start(f32[8,1,256]{2,1,0:T(1,128)} %reshape.619), calls=%async_computation.2 | async-start | bytes 16384 | tf_op jit(solution)/shard_map/all_to_all | solution.py:163
  176.2 3.4 %scatter_fusion.3 = f32[16384]{0:T(1024)S(1)} fusion(f32[16384]{0:T(1024)S(1)} %bitcast.351, s32[512]{0:T(512)S(1)} %bitcast.369, f32[512]{0:T(512)S(1)} %get-tuple-element.78), kind=kCustom, calls=%fused_computation.10 | custom fusion | flops 512 | bytes 8192 | tf_op jit(solution)/shard_map/scatter-add | solution.py:152
  182.0 4.5 %collective-permute-start.32 = (f32[5,4,256]{2,1,0:T(4,128)S(1)}, f32[5,4,256]{2,1,0:T(4,128)S(1)}, u32[]{:S(2)}, u32[]{:S(2)}) collective-permute-start(f32[5,4,256]{2,1,0:T(4,128)S(1)} %get-tuple-element.180), channel_id=1, source_target_pairs={{0,2},{2,4},{4,6},{6,8},{8,10},{10,12},{12,14},{1,3},{3,5},{5,7},{... | collective-permute-start | bytes 61448 | tf_op jit(solution)/shard_map/ppermute | solution.py:21
  186.6 1.3 collective-permute-start.33
  190.2 2.0 %collective-permute-done.33 = f32[5,4,256]{2,1,0:T(4,128)S(1)} collective-permute-done((f32[5,4,256]{2,1,0:T(4,128)S(1)}, f32[5,4,256]{2,1,0:T(4,128)S(1)}, u32[]{:S(2)}, u32[]{:S(2)}) %collective-permute-start.33) | collective-permute-done | bytes 20512 | tf_op jit(solution)/shard_map/ppermute | solution.py:23
  193.1 1.3 collective-permute-start.34
  194.4 1.3 collective-permute-start.35
  196.5 1.5 collective-permute-done.35
  200.0 1.0 fusion.166
  (275 shorter events, 40.9 us)
Async XLA Ops:
  0.6 1.0 copy-start.2
  1.6 6.2 %copy-start.4 = (f32[64,256]{1,0:T(8,128)S(1)}, f32[64,256]{1,0:T(8,128)}, u32[]{:S(2)}) copy-start(f32[64,256]{1,0:T(8,128)} %param.22) | copy-start | bytes 196612
  1.7 16.7 %collective-permute-start = (f32[5,4,256]{2,1,0:T(4,128)S(1)}, f32[5,4,256]{2,1,0:T(4,128)S(1)}, u32[]{:S(2)}, u32[]{:S(2)}) collective-permute-start(f32[5,4,256]{2,1,0:T(4,128)S(1)} %get-tuple-element.194), channel_id=1, source_target_pairs={{0,2},{2,4},{4,6},{6,8},{8,10},{10,12},{12,14},{1,3},{3,5},{5,7},{... | collective-permute-start | bytes 61448 | tf_op jit(solution)/shard_map/ppermute | solution.py:21
  6.5 11.8 %collective-permute-start.1 = (f32[5,4,256]{2,1,0:T(4,128)S(1)}, f32[5,4,256]{2,1,0:T(4,128)S(1)}, u32[]{:S(2)}, u32[]{:S(2)}) collective-permute-start(f32[5,4,256]{2,1,0:T(4,128)S(1)} %get-tuple-element.195), channel_id=1, source_target_pairs={{2,0},{4,2},{6,4},{8,6},{10,8},{12,10},{14,12},{3,1},{5,3},{7,5},{... | collective-permute-start | bytes 61448 | tf_op jit(solution)/shard_map/ppermute | solution.py:23
  7.8 6.8 %collective-permute-start.4 = (f32[2,256]{1,0:T(2,128)S(1)}, f32[2,256]{1,0:T(2,128)S(1)}, u32[]{:S(2)}, u32[]{:S(2)}) collective-permute-start(f32[2,256]{1,0:T(2,128)S(1)} %get-tuple-element.390), channel_id=1, source_target_pairs={{0,2},{2,4},{4,6},{6,8},{8,10},{10,12},{12,14},{1,3},{3,5},{5,7},{... | collective-permute-start | bytes 6152 | tf_op jit(solution)/shard_map/ppermute | solution.py:21
  12.4 1.3 copy-start.20
  12.4 5.9 %collective-permute-start.5 = (f32[2,256]{1,0:T(2,128)S(1)}, f32[2,256]{1,0:T(2,128)S(1)}, u32[]{:S(2)}, u32[]{:S(2)}) collective-permute-start(f32[2,256]{1,0:T(2,128)S(1)} %get-tuple-element.391), channel_id=1, source_target_pairs={{2,0},{4,2},{6,4},{8,6},{10,8},{12,10},{14,12},{3,1},{5,3},{7,5},{... | collective-permute-start | bytes 6152 | tf_op jit(solution)/shard_map/ppermute | solution.py:23
  18.5 7.0 %collective-permute-start.2 = (f32[5,72,4]{2,1,0:T(8,128)S(1)}, f32[5,72,4]{2,1,0:T(8,128)S(1)}, u32[]{:S(2)}, u32[]{:S(2)}) collective-permute-start(f32[5,72,4]{2,1,0:T(8,128)S(1)} %get-tuple-element.178), channel_id=1, source_target_pairs={{0,1},{2,3},{4,5},{6,7},{8,9},{10,11},{12,13},{14,15},{16,17},{18,... | collective-permute-start | bytes 17288 | tf_op jit(solution)/shard_map/ppermute | solution.py:21
  19.8 5.7 %collective-permute-start.3 = (f32[5,72,4]{2,1,0:T(8,128)S(1)}, f32[5,72,4]{2,1,0:T(8,128)S(1)}, u32[]{:S(2)}, u32[]{:S(2)}) collective-permute-start(f32[5,72,4]{2,1,0:T(8,128)S(1)} %get-tuple-element.179), channel_id=1, source_target_pairs={{1,0},{3,2},{5,4},{7,6},{9,8},{11,10},{13,12},{15,14},{17,16},{19,... | collective-permute-start | bytes 17288 | tf_op jit(solution)/shard_map/ppermute | solution.py:23
  21.2 5.1 %collective-permute-start.6 = (f32[68,2]{1,0:T(8,128)S(1)}, f32[68,2]{1,0:T(8,128)S(1)}, u32[]{:S(2)}, u32[]{:S(2)}) collective-permute-start(f32[68,2]{1,0:T(8,128)S(1)} %get-tuple-element.388), channel_id=1, source_target_pairs={{0,1},{2,3},{4,5},{6,7},{8,9},{10,11},{12,13},{14,15},{16,17},{18,... | collective-permute-start | bytes 1640 | tf_op jit(solution)/shard_map/ppermute | solution.py:21
  24.2 3.1 %collective-permute-start.7 = (f32[68,2]{1,0:T(8,128)S(1)}, f32[68,2]{1,0:T(8,128)S(1)}, u32[]{:S(2)}, u32[]{:S(2)}) collective-permute-start(f32[68,2]{1,0:T(8,128)S(1)} %get-tuple-element.389), channel_id=1, source_target_pairs={{1,0},{3,2},{5,4},{7,6},{9,8},{11,10},{13,12},{15,14},{17,16},{19,... | collective-permute-start | bytes 1640 | tf_op jit(solution)/shard_map/ppermute | solution.py:23
  28.1 0.8 copy-start
  28.1 0.9 copy-start.1
  29.3 14.3 %collective-permute-start.8 = (f32[5,4,256]{2,1,0:T(4,128)S(1)}, f32[5,4,256]{2,1,0:T(4,128)S(1)}, u32[]{:S(2)}, u32[]{:S(2)}) collective-permute-start(f32[5,4,256]{2,1,0:T(4,128)S(1)} %get-tuple-element.192), channel_id=1, source_target_pairs={{0,2},{2,4},{4,6},{6,8},{8,10},{10,12},{12,14},{1,3},{3,5},{5,7},{... | collective-permute-start | bytes 61448 | tf_op jit(solution)/shard_map/ppermute | solution.py:21
  34.2 9.5 %collective-permute-start.9 = (f32[5,4,256]{2,1,0:T(4,128)S(1)}, f32[5,4,256]{2,1,0:T(4,128)S(1)}, u32[]{:S(2)}, u32[]{:S(2)}) collective-permute-start(f32[5,4,256]{2,1,0:T(4,128)S(1)} %get-tuple-element.193), channel_id=1, source_target_pairs={{2,0},{4,2},{6,4},{8,6},{10,8},{12,10},{14,12},{3,1},{5,3},{7,5},{... | collective-permute-start | bytes 61448 | tf_op jit(solution)/shard_map/ppermute | solution.py:23
  37.7 20.8 %all-to-all-start = ((s32[1,8,64]{2,0,1:T(1,128)}), s32[1,8,64]{2,0,1:T(1,128)S(1)}, u32[]{:S(2)}, u32[]{:S(2)}) async-start(s32[1,8,64]{2,0,1:T(1,128)} %all_to_all.22), calls=%async_computation | async-start | bytes 8192 | tf_op jit(solution)/shard_map/all_to_all | solution.py:131
  43.7 2.7 %copy-start.3 = (f32[3,64,256]{2,1,0:T(8,128)S(1)}, f32[3,64,256]{2,1,0:T(8,128)}, u32[]{:S(2)}) copy-start(f32[3,64,256]{2,1,0:T(8,128)} %param.21) | copy-start | bytes 589828
  43.9 2.6 %collective-permute-start.10 = (f32[5,72,4]{2,1,0:T(8,128)S(1)}, f32[5,72,4]{2,1,0:T(8,128)S(1)}, u32[]{:S(2)}, u32[]{:S(2)}) collective-permute-start(f32[5,72,4]{2,1,0:T(8,128)S(1)} %get-tuple-element.176), channel_id=1, source_target_pairs={{0,1},{2,3},{4,5},{6,7},{8,9},{10,11},{12,13},{14,15},{16,17},{18,... | collective-permute-start | bytes 17288 | tf_op jit(solution)/shard_map/ppermute | solution.py:21
  45.2 3.3 %collective-permute-start.11 = (f32[5,72,4]{2,1,0:T(8,128)S(1)}, f32[5,72,4]{2,1,0:T(8,128)S(1)}, u32[]{:S(2)}, u32[]{:S(2)}) collective-permute-start(f32[5,72,4]{2,1,0:T(8,128)S(1)} %get-tuple-element.177), channel_id=1, source_target_pairs={{1,0},{3,2},{5,4},{7,6},{9,8},{11,10},{13,12},{15,14},{17,16},{19,... | collective-permute-start | bytes 17288 | tf_op jit(solution)/shard_map/ppermute | solution.py:23
  50.2 5.4 %copy-start.19 = (f32[2,64,256]{2,1,0:T(8,128)S(1)}, f32[2,64,256]{2,1,0:T(8,128)}, u32[]{:S(2)}) copy-start(f32[2,64,256]{2,1,0:T(8,128)} %param.20) | copy-start | bytes 393220
  50.4 16.1 %collective-permute-start.12 = (f32[5,4,256]{2,1,0:T(4,128)S(1)}, f32[5,4,256]{2,1,0:T(4,128)S(1)}, u32[]{:S(2)}, u32[]{:S(2)}) collective-permute-start(f32[5,4,256]{2,1,0:T(4,128)S(1)} %get-tuple-element.190), channel_id=1, source_target_pairs={{0,2},{2,4},{4,6},{6,8},{8,10},{10,12},{12,14},{1,3},{3,5},{5,7},{... | collective-permute-start | bytes 61448 | tf_op jit(solution)/shard_map/ppermute | solution.py:21
  54.3 12.2 %collective-permute-start.13 = (f32[5,4,256]{2,1,0:T(4,128)S(1)}, f32[5,4,256]{2,1,0:T(4,128)S(1)}, u32[]{:S(2)}, u32[]{:S(2)}) collective-permute-start(f32[5,4,256]{2,1,0:T(4,128)S(1)} %get-tuple-element.191), channel_id=1, source_target_pairs={{2,0},{4,2},{6,4},{8,6},{10,8},{12,10},{14,12},{3,1},{5,3},{7,5},{... | collective-permute-start | bytes 61448 | tf_op jit(solution)/shard_map/ppermute | solution.py:23
  55.6 0.7 copy-start.21
  58.6 27.7 %all-to-all-start.1 = ((f32[8,1,256]{2,1,0:T(1,128)}), f32[8,1,256]{2,1,0:T(1,128)S(1)}, u32[]{:S(2)}, u32[]{:S(2)}) async-start(f32[8,1,256]{2,1,0:T(1,128)} %reshape.617), calls=%async_computation.1 | async-start | bytes 16384 | tf_op jit(solution)/shard_map/all_to_all | solution.py:130
  66.6 2.6 %collective-permute-start.14 = (f32[5,72,4]{2,1,0:T(8,128)S(1)}, f32[5,72,4]{2,1,0:T(8,128)S(1)}, u32[]{:S(2)}, u32[]{:S(2)}) collective-permute-start(f32[5,72,4]{2,1,0:T(8,128)S(1)} %get-tuple-element.174), channel_id=1, source_target_pairs={{0,1},{2,3},{4,5},{6,7},{8,9},{10,11},{12,13},{14,15},{16,17},{18,... | collective-permute-start | bytes 17288 | tf_op jit(solution)/shard_map/ppermute | solution.py:21
  67.9 3.3 %collective-permute-start.15 = (f32[5,72,4]{2,1,0:T(8,128)S(1)}, f32[5,72,4]{2,1,0:T(8,128)S(1)}, u32[]{:S(2)}, u32[]{:S(2)}) collective-permute-start(f32[5,72,4]{2,1,0:T(8,128)S(1)} %get-tuple-element.175), channel_id=1, source_target_pairs={{1,0},{3,2},{5,4},{7,6},{9,8},{11,10},{13,12},{15,14},{17,16},{19,... | collective-permute-start | bytes 17288 | tf_op jit(solution)/shard_map/ppermute | solution.py:23
  73.7 5.4 %collective-permute-start.16 = (f32[5,4,256]{2,1,0:T(4,128)S(1)}, f32[5,4,256]{2,1,0:T(4,128)S(1)}, u32[]{:S(2)}, u32[]{:S(2)}) collective-permute-start(f32[5,4,256]{2,1,0:T(4,128)S(1)} %get-tuple-element.188), channel_id=1, source_target_pairs={{0,2},{2,4},{4,6},{6,8},{8,10},{10,12},{12,14},{1,3},{3,5},{5,7},{... | collective-permute-start | bytes 61448 | tf_op jit(solution)/shard_map/ppermute | solution.py:21
  77.7 5.7 %collective-permute-start.17 = (f32[5,4,256]{2,1,0:T(4,128)S(1)}, f32[5,4,256]{2,1,0:T(4,128)S(1)}, u32[]{:S(2)}, u32[]{:S(2)}) collective-permute-start(f32[5,4,256]{2,1,0:T(4,128)S(1)} %get-tuple-element.189), channel_id=1, source_target_pairs={{2,0},{4,2},{6,4},{8,6},{10,8},{12,10},{14,12},{3,1},{5,3},{7,5},{... | collective-permute-start | bytes 61448 | tf_op jit(solution)/shard_map/ppermute | solution.py:23
  83.5 13.7 %collective-permute-start.18 = (f32[5,72,4]{2,1,0:T(8,128)S(1)}, f32[5,72,4]{2,1,0:T(8,128)S(1)}, u32[]{:S(2)}, u32[]{:S(2)}) collective-permute-start(f32[5,72,4]{2,1,0:T(8,128)S(1)} %get-tuple-element.172), channel_id=1, source_target_pairs={{0,1},{2,3},{4,5},{6,7},{8,9},{10,11},{12,13},{14,15},{16,17},{18,... | collective-permute-start | bytes 17288 | tf_op jit(solution)/shard_map/ppermute | solution.py:21
  84.8 12.4 %collective-permute-start.19 = (f32[5,72,4]{2,1,0:T(8,128)S(1)}, f32[5,72,4]{2,1,0:T(8,128)S(1)}, u32[]{:S(2)}, u32[]{:S(2)}) collective-permute-start(f32[5,72,4]{2,1,0:T(8,128)S(1)} %get-tuple-element.173), channel_id=1, source_target_pairs={{1,0},{3,2},{5,4},{7,6},{9,8},{11,10},{13,12},{15,14},{17,16},{19,... | collective-permute-start | bytes 17288 | tf_op jit(solution)/shard_map/ppermute | solution.py:23
  108.7 6.2 %collective-permute-start.20 = (f32[5,4,256]{2,1,0:T(4,128)S(1)}, f32[5,4,256]{2,1,0:T(4,128)S(1)}, u32[]{:S(2)}, u32[]{:S(2)}) collective-permute-start(f32[5,4,256]{2,1,0:T(4,128)S(1)} %get-tuple-element.186), channel_id=1, source_target_pairs={{0,2},{2,4},{4,6},{6,8},{8,10},{10,12},{12,14},{1,3},{3,5},{5,7},{... | collective-permute-start | bytes 61448 | tf_op jit(solution)/shard_map/ppermute | solution.py:21
  113.5 5.7 %collective-permute-start.21 = (f32[5,4,256]{2,1,0:T(4,128)S(1)}, f32[5,4,256]{2,1,0:T(4,128)S(1)}, u32[]{:S(2)}, u32[]{:S(2)}) collective-permute-start(f32[5,4,256]{2,1,0:T(4,128)S(1)} %get-tuple-element.187), channel_id=1, source_target_pairs={{2,0},{4,2},{6,4},{8,6},{10,8},{12,10},{14,12},{3,1},{5,3},{7,5},{... | collective-permute-start | bytes 61448 | tf_op jit(solution)/shard_map/ppermute | solution.py:23
  119.3 2.7 %collective-permute-start.22 = (f32[5,72,4]{2,1,0:T(8,128)S(1)}, f32[5,72,4]{2,1,0:T(8,128)S(1)}, u32[]{:S(2)}, u32[]{:S(2)}) collective-permute-start(f32[5,72,4]{2,1,0:T(8,128)S(1)} %get-tuple-element.170), channel_id=1, source_target_pairs={{0,1},{2,3},{4,5},{6,7},{8,9},{10,11},{12,13},{14,15},{16,17},{18,... | collective-permute-start | bytes 17288 | tf_op jit(solution)/shard_map/ppermute | solution.py:21
  120.6 3.3 %collective-permute-start.23 = (f32[5,72,4]{2,1,0:T(8,128)S(1)}, f32[5,72,4]{2,1,0:T(8,128)S(1)}, u32[]{:S(2)}, u32[]{:S(2)}) collective-permute-start(f32[5,72,4]{2,1,0:T(8,128)S(1)} %get-tuple-element.171), channel_id=1, source_target_pairs={{1,0},{3,2},{5,4},{7,6},{9,8},{11,10},{13,12},{15,14},{17,16},{19,... | collective-permute-start | bytes 17288 | tf_op jit(solution)/shard_map/ppermute | solution.py:23
  129.9 4.8 %collective-permute-start.24 = (f32[5,4,256]{2,1,0:T(4,128)S(1)}, f32[5,4,256]{2,1,0:T(4,128)S(1)}, u32[]{:S(2)}, u32[]{:S(2)}) collective-permute-start(f32[5,4,256]{2,1,0:T(4,128)S(1)} %get-tuple-element.184), channel_id=1, source_target_pairs={{0,2},{2,4},{4,6},{6,8},{8,10},{10,12},{12,14},{1,3},{3,5},{5,7},{... | collective-permute-start | bytes 61448 | tf_op jit(solution)/shard_map/ppermute | solution.py:21
  133.2 5.7 %collective-permute-start.25 = (f32[5,4,256]{2,1,0:T(4,128)S(1)}, f32[5,4,256]{2,1,0:T(4,128)S(1)}, u32[]{:S(2)}, u32[]{:S(2)}) collective-permute-start(f32[5,4,256]{2,1,0:T(4,128)S(1)} %get-tuple-element.185), channel_id=1, source_target_pairs={{2,0},{4,2},{6,4},{8,6},{10,8},{12,10},{14,12},{3,1},{5,3},{7,5},{... | collective-permute-start | bytes 61448 | tf_op jit(solution)/shard_map/ppermute | solution.py:23
  139.8 3.4 %collective-permute-start.26 = (f32[5,72,4]{2,1,0:T(8,128)}, f32[5,72,4]{2,1,0:T(8,128)S(1)}, u32[]{:S(2)}, u32[]{:S(2)}) collective-permute-start(f32[5,72,4]{2,1,0:T(8,128)} %get-tuple-element.168), channel_id=1, source_target_pairs={{0,1},{2,3},{4,5},{6,7},{8,9},{10,11},{12,13},{14,15},{16,17},{18,... | collective-permute-start | bytes 17288 | tf_op jit(solution)/shard_map/ppermute | solution.py:21
  141.1 3.3 %collective-permute-start.27 = (f32[5,72,4]{2,1,0:T(8,128)S(1)}, f32[5,72,4]{2,1,0:T(8,128)S(1)}, u32[]{:S(2)}, u32[]{:S(2)}) collective-permute-start(f32[5,72,4]{2,1,0:T(8,128)S(1)} %get-tuple-element.169), channel_id=1, source_target_pairs={{1,0},{3,2},{5,4},{7,6},{9,8},{11,10},{13,12},{15,14},{17,16},{19,... | collective-permute-start | bytes 17288 | tf_op jit(solution)/shard_map/ppermute | solution.py:23
  146.4 0.8 copy-start.17
  151.6 0.9 copy-start.7
  151.6 0.9 copy-start.8
  151.6 1.0 copy-start.9
  152.5 0.8 copy-start.14
  153.4 6.6 %collective-permute-start.28 = (f32[5,4,256]{2,1,0:T(4,128)S(1)}, f32[5,4,256]{2,1,0:T(4,128)S(1)}, u32[]{:S(2)}, u32[]{:S(2)}) collective-permute-start(f32[5,4,256]{2,1,0:T(4,128)S(1)} %get-tuple-element.182), channel_id=1, source_target_pairs={{0,2},{2,4},{4,6},{6,8},{8,10},{10,12},{12,14},{1,3},{3,5},{5,7},{... | collective-permute-start | bytes 61448 | tf_op jit(solution)/shard_map/ppermute | solution.py:21
  158.0 5.7 %collective-permute-start.29 = (f32[5,4,256]{2,1,0:T(4,128)S(1)}, f32[5,4,256]{2,1,0:T(4,128)S(1)}, u32[]{:S(2)}, u32[]{:S(2)}) collective-permute-start(f32[5,4,256]{2,1,0:T(4,128)S(1)} %get-tuple-element.183), channel_id=1, source_target_pairs={{2,0},{4,2},{6,4},{8,6},{10,8},{12,10},{14,12},{3,1},{5,3},{7,5},{... | collective-permute-start | bytes 61448 | tf_op jit(solution)/shard_map/ppermute | solution.py:23
  164.5 8.6 %collective-permute-start.30 = (f32[5,72,4]{2,1,0:T(8,128)}, f32[5,72,4]{2,1,0:T(8,128)S(1)}, u32[]{:S(2)}, u32[]{:S(2)}) collective-permute-start(f32[5,72,4]{2,1,0:T(8,128)} %get-tuple-element.166), channel_id=1, source_target_pairs={{0,1},{2,3},{4,5},{6,7},{8,9},{10,11},{12,13},{14,15},{16,17},{18,... | collective-permute-start | bytes 17288 | tf_op jit(solution)/shard_map/ppermute | solution.py:21
  165.8 7.3 %collective-permute-start.31 = (f32[5,72,4]{2,1,0:T(8,128)}, f32[5,72,4]{2,1,0:T(8,128)S(1)}, u32[]{:S(2)}, u32[]{:S(2)}) collective-permute-start(f32[5,72,4]{2,1,0:T(8,128)} %get-tuple-element.167), channel_id=1, source_target_pairs={{1,0},{3,2},{5,4},{7,6},{9,8},{11,10},{13,12},{15,14},{17,16},{19,... | collective-permute-start | bytes 17288 | tf_op jit(solution)/shard_map/ppermute | solution.py:23
  168.6 20.0 %all-to-all-start.2 = ((f32[8,1,256]{2,1,0:T(1,128)}), f32[8,1,256]{2,1,0:T(1,128)S(1)}, u32[]{:S(2)}, u32[]{:S(2)}) async-start(f32[8,1,256]{2,1,0:T(1,128)} %reshape.619), calls=%async_computation.2 | async-start | bytes 16384 | tf_op jit(solution)/shard_map/all_to_all | solution.py:163
  175.1 0.8 copy-start.18
  180.3 0.9 copy-start.5
  180.3 0.9 copy-start.6
  181.2 0.8 copy-start.13
  181.2 6.7 %copy-start.16 = (f32[1,64,256]{2,1,0:T(8,128)S(1)}, f32[1,64,256]{2,1,0:T(8,128)}, u32[]{:S(2)}) copy-start(f32[1,64,256]{2,1,0:T(8,128)} %slice_bitcast_fusion.33) | copy-start | bytes 196612
  182.0 5.9 %copy-start.15 = (f32[1,64,256]{2,1,0:T(8,128)S(1)}, f32[1,64,256]{2,1,0:T(8,128)}, u32[]{:S(2)}) copy-start(f32[1,64,256]{2,1,0:T(8,128)} %slice_bitcast_fusion.32) | copy-start | bytes 196612
  182.0 8.2 %collective-permute-start.32 = (f32[5,4,256]{2,1,0:T(4,128)S(1)}, f32[5,4,256]{2,1,0:T(4,128)S(1)}, u32[]{:S(2)}, u32[]{:S(2)}) collective-permute-start(f32[5,4,256]{2,1,0:T(4,128)S(1)} %get-tuple-element.180), channel_id=1, source_target_pairs={{0,2},{2,4},{4,6},{6,8},{8,10},{10,12},{12,14},{1,3},{3,5},{5,7},{... | collective-permute-start | bytes 61448 | tf_op jit(solution)/shard_map/ppermute | solution.py:21
  186.6 5.7 %collective-permute-start.33 = (f32[5,4,256]{2,1,0:T(4,128)S(1)}, f32[5,4,256]{2,1,0:T(4,128)S(1)}, u32[]{:S(2)}, u32[]{:S(2)}) collective-permute-start(f32[5,4,256]{2,1,0:T(4,128)S(1)} %get-tuple-element.181), channel_id=1, source_target_pairs={{2,0},{4,2},{6,4},{8,6},{10,8},{12,10},{14,12},{3,1},{5,3},{7,5},{... | collective-permute-start | bytes 61448 | tf_op jit(solution)/shard_map/ppermute | solution.py:23
  193.1 3.4 %collective-permute-start.34 = (f32[5,72,4]{2,1,0:T(8,128)}, f32[5,72,4]{2,1,0:T(8,128)S(1)}, u32[]{:S(2)}, u32[]{:S(2)}) collective-permute-start(f32[5,72,4]{2,1,0:T(8,128)} %get-tuple-element.164), channel_id=1, source_target_pairs={{0,1},{2,3},{4,5},{6,7},{8,9},{10,11},{12,13},{14,15},{16,17},{18,... | collective-permute-start | bytes 17288 | tf_op jit(solution)/shard_map/ppermute | solution.py:21
  194.4 3.5 %collective-permute-start.35 = (f32[5,72,4]{2,1,0:T(8,128)}, f32[5,72,4]{2,1,0:T(8,128)S(1)}, u32[]{:S(2)}, u32[]{:S(2)}) collective-permute-start(f32[5,72,4]{2,1,0:T(8,128)} %get-tuple-element.165), channel_id=1, source_target_pairs={{1,0},{3,2},{5,4},{7,6},{9,8},{11,10},{13,12},{15,14},{17,16},{19,... | collective-permute-start | bytes 17288 | tf_op jit(solution)/shard_map/ppermute | solution.py:23
  199.1 0.8 copy-start.10
  199.1 0.9 copy-start.11
  199.1 0.9 copy-start.12
where the time goes:
time: 203 us; the launch traced here: 202 us
  starting transfers between devices  92.3 us (45%)
  local copies, waits for them, and re-layouts  43.3 us (21%)
  waiting for transfers between devices  32 us (16%)
  other arithmetic  28.5 us (14%)
  blocking collectives  3.3 us (2%)
  between operations  2.32 us (1%)
    ppermute x18, starting transfers between devices, extended(): lax.ppermute(tail, axis, [(i, (i + 1) % count) for i in range(ends)])  52.6 us
    ppermute x18, waiting for transfers between devices, extended(): lax.ppermute(head, axis, [((i + 1) % count, i) for i in range(ends)])  31.6 us
    ppermute x18, starting transfers between devices, extended(): lax.ppermute(head, axis, [((i + 1) % count, i) for i in range(ends)])  23.3 us
    scatter-add x4, other arithmetic, per_device(): adjoint[2].reshape(-1).at[flat_cell]  14 us
    gather x4, local copies, waits for them, and re-layouts, per_device(): records.append(jnp.where(inject, strains[0].reshape(-1)[flat_cell], 0.0))  12.6 us
    unnamed x72, local copies, waits for them, and re-layouts  10.9 us
    all_to_all x1, starting transfers between devices, per_device(): lax.all_to_all(sent_obs, 'track', split_axis=1, concat_axis=1, tiled=True)  6.63 us
    slice x47, local copies, waits for them, and re-layouts, window_of(): lax.slice_in_dim(field, start_at, start_at + cut_count, axis=dim_index)  6.27 us
  transfers between devices with their start and end apart: 39, of which 14 were waited for; matrix products, arithmetic and copies ran while one was open for 18% of the time, Pallas kernels for 0%

commit v1 on v0

v1 whole, which is shorter than its diff:
```python
import jax
import jax.numpy as jnp
from jax import lax
from jax.experimental import pallas as pl
from jax.experimental.pallas import tpu as pltpu
from jax.sharding import PartitionSpec as P

FIBRE_ROWS = 4
NEAR = 9.0 / 8.0
RATIO = -1.0 / 27.0
HALO = 12
EDGE = 16
LANES = 128
PAD = 8
FIELDS = 13
STRIP = 16
OWN = LANES - 2 * HALO
VMEM = pltpu.VMEM


def lane_ids(rows):
    return lax.broadcasted_iota(jnp.int32, (rows, LANES), 1)


def params():
    return pltpu.CompilerParams(vmem_limit_bytes=40 * 1024 * 1024)


def field_refs(velocity, stress, adj_velocity, adj_stress, buoyancy, lame, shear):
    return (
        [velocity.at[i] for i in range(2)]
        + [stress.at[i] for i in range(3)]
        + [adj_velocity.at[i] for i in range(2)]
        + [adj_stress.at[i] for i in range(3)]
        + [buoyancy, lame, shear]
    )


def pack_kernel(*refs):
    fields = field_refs(*refs[:7])
    obs, along, row, depth_out, even_out, odd_out, strip_out = refs[7:]
    depth = lax.axis_index("depth")
    even = lax.rem(lax.axis_index("track"), 2) == 0
    rows = fields[0].shape[0]
    lane = lane_ids(rows)
    packed = [jnp.zeros((rows, LANES), jnp.float32) for _ in range(2)]
    strip = jnp.zeros((rows, LANES), jnp.float32)
    for f, ref in enumerate(fields):
        first, last = ref[:, :LANES], ref[:, LANES:]
        spot = EDGE * (f % 8)
        here = (lane >= spot) & (lane < spot + EDGE)
        edge = jnp.where(depth == 0, last, first)
        shift = lax.rem(spot + EDGE * (1 - depth), LANES)
        packed[f // 8] = jnp.where(here, pltpu.roll(edge, shift, 1), packed[f // 8])
        if f < 5 or f >= 10:
            k = f if f < 5 else f - 5
            mine = (lane >= STRIP * k) & (lane < STRIP * (k + 1))
            strip = jnp.where(mine, pltpu.roll(first, STRIP * k, 1), strip)
        low, high = ref[:HALO, :], ref[rows - HALO :, :]
        at = EDGE + HALO * f
        even_out[at : at + HALO, :] = jnp.where(even, high, low)
        odd_out[at : at + HALO, :] = jnp.where(even, low, high)
    tail = EDGE + HALO * FIELDS
    for out in (even_out, odd_out):
        out[:EDGE, :] = jnp.zeros((EDGE, 2 * LANES), jnp.float32)
        out[tail:, :] = jnp.zeros((out.shape[0] - tail, 2 * LANES), jnp.float32)
    depth_out[:, :LANES] = packed[0]
    depth_out[:, LANES:] = packed[1]
    turned = strip.T
    half = LANES // 2
    strip_out[:half, :] = jnp.concatenate([turned[:half], turned[half:]], axis=1)
    strip_out[half : half + 4, :] = obs[:, :LANES]
    strip_out[half + 4 : half + 8, :] = obs[:, LANES:]
    strip_out[half + 8 : half + 9, :] = along[:, :LANES].astype(jnp.float32)
    strip_out[half + 9 : half + 10, :] = along[:, LANES:].astype(jnp.float32)
    strip_out[half + 10 : half + 11, :] = row[:, :LANES].astype(jnp.float32)
    strip_out[half + 11 : half + 12, :] = row[:, LANES:].astype(jnp.float32)
    strip_out[half + 12 :, :] = jnp.zeros((4, LANES), jnp.float32)


def corner_kernel(got, even_in, odd_in, even_out, odd_out, sems):
    rows = got.shape[0]
    is_odd = lax.rem(lax.axis_index("track"), 2)
    high, low = (rows - EDGE) * (1 - is_odd), (rows - EDGE) * is_odd
    one = pltpu.make_async_copy(
        got.at[pl.ds(pl.multiple_of(high, EDGE), EDGE), :], even_out.at[pl.ds(0, EDGE), :], sems.at[0]
    )
    two = pltpu.make_async_copy(
        got.at[pl.ds(pl.multiple_of(low, EDGE), EDGE), :], odd_out.at[pl.ds(0, EDGE), :], sems.at[1]
    )
    one.start()
    two.start()
    one.wait()
    two.wait()


def turn(value, by):
    return pltpu.roll(value, by % LANES, 1)


def surface_kernel(tracks, columns, got, obs, along, row, inject_out, residual_out, state, media, rate):
    depth = lax.axis_index("depth")
    start = lax.axis_index("track") * columns - EDGE
    channels = obs.shape[1]
    grid_end = tracks * columns
    windows = -(-grid_end // OWN)
    lane = lane_ids(STRIP)
    state[...] = jnp.zeros(state.shape, jnp.float32)
    media[...] = jnp.zeros(media.shape, jnp.float32)
    own_along = along[...]

    def window(number, total):
        begin = number * OWN - HALO
        base = (begin + columns) // columns - 1
        offset = begin - base * columns
        part = lax.div(offset + lane, columns)
        where_x = begin + lane
        inside = (where_x >= 0) & (where_x < grid_end)
        half = LANES // 2
        for k in range(8):
            value = jnp.zeros((STRIP, LANES), jnp.float32)
            top = STRIP * (k % 4)
            for step in range(3):
                who = jnp.clip(base + step, 0, tracks - 1)
                block = got[2 * who, top : top + STRIP, :]
                shift = lax.rem(4 * LANES - offset + columns * step - half * (k // 4), LANES)
                value = jnp.where(part == step, pltpu.roll(block, shift, 1), value)
            value = jnp.where(inside, value, 0.0)
            if k < 5:
                state[k, PAD : PAD + STRIP, :] = value
            elif k == 5:
                media[0, :STRIP, :] = NEAR * value
            elif k == 6:
                lame = value
            else:
                media[1, :STRIP, :] = NEAR * (lame + 2.0 * value)
                media[2, :STRIP, :] = NEAR * lame
                media[3, :STRIP, :] = NEAR * value

        def at(f, r, by=0):
            return state[f, PAD + r + by : PAD + r + by + 8, :]

        strains = []
        for moment in range(4):
            for r in (0, 8) if moment < 2 else (0,):
                xx, xz, zz = at(2, r), at(4, r), at(3, r)
                near = (xx - turn(xx, 1)) + (xz - at(4, r, -1))
                far = (turn(xx, -1) - turn(xx, 2)) + (at(4, r, 1) - at(4, r, -2))
                b = media[0, r : r + 8, :]
                state[0, PAD + r : PAD + r + 8, :] = at(0, r) + b * (near + RATIO * far)
                if moment < 3:
                    near = (turn(xz, -1) - xz) + (at(3, r, 1) - zz)
                    far = (turn(xz, -2) - turn(xz, 1)) + (at(3, r, 2) - at(3, r, -1))
                    state[1, PAD + r : PAD + r + 8, :] = at(1, r) + b * (near + RATIO * far)
            for r in (0, 8) if moment < 1 else (0,):
                vx, vz = at(0, r), at(1, r)
                exx = (turn(vx, -1) - vx) + RATIO * (turn(vx, -2) - turn(vx, 1))
                if r == 0:
                    strains.append(NEAR * exx)
                if moment < 3:
                    ezz = (vz - at(1, r, -1)) + RATIO * (at(1, r, 1) - at(1, r, -2))
                    near = (at(0, r, 1) - vx) + (vz - turn(vz, 1))
                    far = (at(0, r, 2) - at(0, r, -1)) + (turn(vz, -1) - turn(vz, 2))
                    shear = near + RATIO * far
                    whole, lam, mu = (media[i, r : r + 8, :] for i in (1, 2, 3))
                    state[2, PAD + r : PAD + r + 8, :] = at(2, r) + (whole * exx + lam * ezz)
                    state[3, PAD + r : PAD + r + 8, :] = at(3, r) + (lam * exx + whole * ezz)
                    state[4, PAD + r : PAD + r + 8, :] = at(4, r) + mu * shear
        lane32 = lane_ids(32)
        mine = (lane32 >= HALO) & (lane32 < HALO + OWN)
        image = jnp.where(mine, jnp.concatenate(strains, axis=0), 0.0)
        spot = begin + lax.broadcasted_iota(jnp.int32, (LANES, channels), 0)
        hot = (spot == own_along).astype(jnp.float32)
        spot = begin + lax.broadcasted_iota(jnp.int32, (LANES, LANES), 0)
        pick = (spot == start + lax.broadcasted_iota(jnp.int32, (LANES, LANES), 1)).astype(jnp.float32)
        both = jnp.concatenate([hot, pick], axis=1)
        rate[...] += jnp.dot(
            image, both, precision=lax.Precision.HIGHEST, preferred_element_type=jnp.float32
        )
        return total

    rate[...] = jnp.zeros(rate.shape, jnp.float32)
    if windows <= 8:
        for number in range(windows):
            window(number, 0)
    else:
        lax.fori_loop(0, windows, window, 0)

    half = LANES // 2
    group = 8

    def images(number, total):
        weights, hots = [], []
        for k in range(group):
            who = 2 * (number * group + k)
            for h in range(2):
                chan_along = got[who, half + 8 + h : half + 9 + h, :]
                chan_row = got[who, half + 10 + h : half + 11 + h, :]
                mask = lax.broadcasted_iota(jnp.int32, (8, LANES), 0).astype(jnp.float32) == chan_row
                pieces = [
                    jnp.where(mask, got[who, half + 4 * h + t : half + 4 * h + t + 1, :], 0.0) for t in range(4)
                ]
                weights.append(jnp.concatenate(pieces + [mask.astype(jnp.float32)], axis=0))
                spot = (start + lax.broadcasted_iota(jnp.int32, (LANES, LANES), 0)).astype(jnp.float32)
                hots.append((spot == chan_along).astype(jnp.float32))
        return total + lax.dot_general(
            jnp.concatenate(weights, axis=1),
            jnp.concatenate(hots, axis=1),
            (((1,), (1,)), ((), ())),
            precision=lax.Precision.HIGHEST,
            preferred_element_type=jnp.float32,
        )

    total = jnp.zeros((40, LANES), jnp.float32)
    if tracks <= group:
        total = images(0, total)
    else:
        total = lax.fori_loop(0, tracks // group, images, total)
    count = total[32:40]
    rows = [
        count * rate[8 * t : 8 * t + 8, channels:] - total[8 * t : 8 * t + 8] for t in range(4)
    ]
    turned = jnp.concatenate(rows + [jnp.zeros((LANES - 32, LANES), jnp.float32)], axis=0).T
    window_rows = inject_out.shape[1]
    lane_w = lane_ids(window_rows)
    keep = (lane_w >= EDGE) & (lane_w < EDGE + 8) & (depth == 0)
    for t in range(4):
        inject_out[t] = jnp.where(keep, turn(turned[:window_rows], EDGE - 8 * t), 0.0)
    mask = lax.broadcasted_iota(jnp.int32, (8, channels), 0) == row[...]
    traces = [
        jnp.sum(jnp.where(mask, rate[8 * t : 8 * t + 8, :channels], 0.0), axis=0, keepdims=True)
        - obs[t : t + 1, :]
        for t in range(4)
    ]
    residual_out[...] = jnp.where(
        depth == 0, jnp.concatenate(traces[:2], axis=0), jnp.concatenate(traces[2:], axis=0)
    )


def main_kernel(*refs):
    fields = field_refs(*refs[:7])
    got_depth, got_even, got_odd, inject = refs[7:11]
    lambda_out, mu_out, end_out = refs[11:14]
    state, media, saved, sums = refs[14:]
    rows = fields[0].shape[0]
    depth = lax.axis_index("depth")
    even = lax.rem(lax.axis_index("track"), 2) == 0
    extent = rows + 2 * EDGE
    tiles = extent // 8
    edge_tiles = EDGE // 8

    zero_pad = jnp.zeros((PAD, LANES), jnp.float32)
    for f in range(10):
        for p in range(3):
            state[f, p, :PAD, :] = zero_pad
            state[f, p, PAD + extent :, :] = zero_pad

    def place(f, at, first, last, halo):
        count = first.shape[0]
        lane = lane_ids(count)
        spot = EDGE * (f % 8)
        shift = lax.rem(LANES - spot + (LANES - EDGE) * (1 - depth), LANES)
        beside = pltpu.roll(halo, shift, 1)
        return [
            jnp.where(lane >= EDGE, turn(first, EDGE), jnp.where(depth == 1, beside, 0.0)),
            jnp.where(lane < LANES // 2, turn(first, LANES // 2), turn(last, LANES // 2)),
            jnp.where(lane < LANES - EDGE, turn(last, -EDGE), jnp.where(depth == 0, beside, 0.0)),
        ]

    def put(f, at, planes):
        count = planes[0].shape[0]
        for p in range(3):
            if f < 10:
                state[f, p, PAD + at : PAD + at + count, :] = planes[p]
            elif f == 10:
                media[0, p, at : at + count, :] = NEAR * planes[p]
            elif f == 11:
                media[2, p, at : at + count, :] = NEAR * planes[p]
            else:
                mu = NEAR * planes[p]
                media[3, p, at : at + count, :] = mu
                media[1, p, at : at + count, :] = media[2, p, at : at + count, :] + 2.0 * mu

    for f, ref in enumerate(fields):
        col = LANES * (f // 8)
        low = EDGE + HALO * f - (EDGE - HALO)
        high = EDGE + HALO * f
        left = jnp.where(even, got_odd[low : low + EDGE, :], got_even[low : low + EDGE, :])
        left_halo = jnp.where(even, got_odd[:EDGE, col : col + LANES], got_even[:EDGE, col : col + LANES])
        right = jnp.where(even, got_even[high : high + EDGE, :], got_odd[high : high + EDGE, :])
        right_halo = jnp.where(even, got_even[:EDGE, col : col + LANES], got_odd[:EDGE, col : col + LANES])
        put(f, 0, place(f, 0, left[:, :LANES], left[:, LANES:], left_halo))
        put(
            f,
            EDGE,
            place(f, EDGE, ref[:, :LANES], ref[:, LANES:], got_depth[:, col : col + LANES]),
        )
        put(f, EDGE + rows, place(f, EDGE + rows, right[:, :LANES], right[:, LANES:], right_halo))

    def velocities(g, lo, hi):
        def body(i, carry):
            r = pl.multiple_of(i * 8, 8)
            for p in range(3):

                def at(f, by=0):
                    return state[g + f, p, pl.ds(r + PAD + by, 8), :]

                xx, xz, zz = at(2), at(4), at(3)
                b = media[0, p, pl.ds(r, 8), :]
                near = (xx - at(2, -1)) + (xz - turn(xz, 1))
                far = (at(2, 1) - at(2, -2)) + (turn(xz, -1) - turn(xz, 2))
                state[g, p, pl.ds(r + PAD, 8), :] = at(0) + b * (near + RATIO * far)
                near = (at(4, 1) - xz) + (turn(zz, -1) - zz)
                far = (at(4, 2) - at(4, -1)) + (turn(zz, -2) - turn(zz, 1))
                state[g + 1, p, pl.ds(r + PAD, 8), :] = at(1) + b * (near + RATIO * far)
            return carry

        lax.fori_loop(lo, hi, body, 0)

    def stresses(g, lo, hi, update, keep):
        def body(i, carry):
            r = pl.multiple_of(i * 8, 8)
            for p in range(3):

                def at(f, by=0):
                    return state[g + f, p, pl.ds(r + PAD + by, 8), :]

                vx, vz = at(0), at(1)
                exx = (at(0, 1) - vx) + RATIO * (at(0, 2) - at(0, -1))
                ezz = (vz - turn(vz, 1)) + RATIO * (turn(vz, -1) - turn(vz, 2))
                near = (turn(vx, -1) - vx) + (vz - at(1, -1))
                far = (turn(vx, -2) - turn(vx, 1)) + (at(1, 1) - at(1, -2))
                shear = near + RATIO * far
                keep(p, r, exx, ezz, shear)
                if update:
                    whole, lam, mu = (media[k, p, pl.ds(r, 8), :] for k in (1, 2, 3))
                    state[g + 2, p, pl.ds(r + PAD, 8), :] = at(2) + (whole * exx + lam * ezz)
                    state[g + 3, p, pl.ds(r + PAD, 8), :] = at(3) + (lam * exx + whole * ezz)
                    state[g + 4, p, pl.ds(r + PAD, 8), :] = at(4) + mu * shear
            return carry

        lax.fori_loop(lo, hi, body, 0)

    def spans(step):
        if step == 0:
            return (0, tiles), (0, tiles)
        if step < 3:
            return (1, tiles - 1), (1, tiles - 1)
        return (1, tiles - 1), (edge_tiles, tiles - edge_tiles)

    for step in range(4):
        fast, slow = spans(step)
        velocities(0, *fast)

        def save(p, r, exx, ezz, shear, step=step):
            saved[step, 0, p, pl.ds(r, 8), :] = exx
            saved[step, 1, p, pl.ds(r, 8), :] = ezz
            saved[step, 2, p, pl.ds(r, 8), :] = shear

        stresses(0, *slow, step < 3, save)

    def joined(planes):
        lane = lane_ids(planes[0].shape[0])
        middle = turn(planes[1], LANES // 2)
        return (
            jnp.where(lane < 88, turn(planes[0], -EDGE), middle),
            jnp.where(lane < 40, middle, turn(planes[2], EDGE)),
        )

    top = PAD + EDGE
    for f in range(2):
        first, last = joined([state[f, p, top : top + rows, :] for p in range(3)])
        end_out[f, :, :LANES] = first
        end_out[f, :, LANES:] = last

    sums[...] = jnp.zeros(sums.shape, jnp.float32)
    for step in range(4):
        fast, slow = spans(step)
        moment = 3 - step
        state[7, 0, PAD : PAD + extent, :] += inject[moment]
        velocities(5, *fast)

        def gather(p, r, exx, ezz, shear, moment=moment):
            fxx, fzz, fxz = (saved[moment, k, p, pl.ds(r, 8), :] for k in range(3))
            sums[0, p, pl.ds(r, 8), :] += (fxx + fzz) * (exx + ezz)
            sums[1, p, pl.ds(r, 8), :] += 2.0 * (fxx * exx + fzz * ezz) + fxz * shear

        stresses(5, *slow, step < 3, gather)

    for k, out in enumerate((lambda_out, mu_out)):
        first, last = joined([sums[k, p, EDGE : EDGE + rows, :] for p in range(3)])
        out[:, :LANES] = (NEAR * NEAR) * first
        out[:, LANES:] = (NEAR * NEAR) * last


def per_device(
    velocity,
    stress,
    adjoint_velocity,
    adjoint_stress,
    buoyancy,
    lame_lambda,
    shear_modulus,
    observed,
    owner_track,
    fibre_cell,
):
    tracks = lax.axis_size("track")
    rows, depth_cells = buoyancy.shape
    moments, channels = observed.shape
    f32 = jnp.float32
    cell = fibre_cell.reshape(1, channels)
    along = owner_track.reshape(1, channels) * rows + cell // FIBRE_ROWS
    fibre_row = cell % FIBRE_ROWS
    arrays = (velocity, stress, adjoint_velocity, adjoint_stress, buoyancy, lame_lambda, shear_modulus)
    length = EDGE + HALO * FIELDS
    length = length + (-length) % 8
    edges = jax.ShapeDtypeStruct((length, depth_cells), f32)
    inside = pl.BlockSpec(memory_space=VMEM)
    anywhere = pl.BlockSpec(memory_space=pl.ANY)

    to_depth, to_even, to_odd, strip = pl.pallas_call(
        pack_kernel,
        out_shape=(
            jax.ShapeDtypeStruct((rows, depth_cells), f32),
            edges,
            edges,
            jax.ShapeDtypeStruct((LANES // 2 + 16, LANES), f32),
        ),
        in_specs=[inside] * 10,
        out_specs=(inside,) * 4,
        compiler_params=params(),
        name="pack",
    )(*arrays, observed, along, fibre_row)

    strips = lax.all_gather(strip, ("track", "depth"), axis=0, tiled=False)
    got_depth = lax.ppermute(to_depth, "depth", [(0, 1), (1, 0)])
    to_even, to_odd = pl.pallas_call(
        corner_kernel,
        out_shape=(edges, edges),
        in_specs=[anywhere] * 3,
        out_specs=(anywhere,) * 2,
        input_output_aliases={1: 0, 2: 1},
        scratch_shapes=[pltpu.SemaphoreType.DMA((2,))],
        compiler_params=params(),
        name="corners",
    )(got_depth, to_even, to_odd)
    swap = lambda k: [pair for i in range(k, tracks - 1, 2) for pair in ((i, i + 1), (i + 1, i))]
    got_odd = lax.ppermute(to_odd, "track", swap(1))
    got_even = lax.ppermute(to_even, "track", swap(0))

    extent = rows + 2 * EDGE
    inject, residual = pl.pallas_call(
        lambda *refs: surface_kernel(tracks, rows, *refs),
        out_shape=(
            jax.ShapeDtypeStruct((moments, extent, LANES), f32),
            jax.ShapeDtypeStruct((moments // 2, channels), f32),
        ),
        in_specs=[inside] * 4,
        out_specs=(inside,) * 2,
        scratch_shapes=[
            VMEM((5, 2 * PAD + STRIP, LANES), f32),
            VMEM((4, STRIP, LANES), f32),
            VMEM((32, channels + LANES), f32),
        ],
        compiler_params=params(),
        name="surface",
    )(strips, observed, along, fibre_row)

    block = jax.ShapeDtypeStruct((rows, depth_cells), f32)
    gradient_lambda, gradient_mu, velocity_end = pl.pallas_call(
        main_kernel,
        out_shape=(block, block, jax.ShapeDtypeStruct(velocity.shape, f32)),
        in_specs=[inside] * 11,
        out_specs=(inside,) * 3,
        scratch_shapes=[
            VMEM((10, 3, extent + 2 * PAD, LANES), f32),
            VMEM((4, 3, extent, LANES), f32),
            VMEM((4, 3, 3, extent, LANES), f32),
            VMEM((2, 3, extent, LANES), f32),
        ],
        compiler_params=params(),
        name="window",
    )(*arrays, got_depth, got_even, got_odd, inject)
    return gradient_lambda, gradient_mu, velocity_end, residual


def solution(mesh):
    return jax.shard_map(
        per_device,
        mesh=mesh,
        in_specs=(
            P("shots", "track", "depth"),
            P("shots", "track", "depth"),
            P("shots", "track", "depth"),
            P("shots", "track", "depth"),
            P("track", "depth"),
            P("track", "depth"),
            P("track", "depth"),
            P("shots", "track"),
            P("track", None),
            P("track"),
        ),
        out_specs=(
            P(("shots", "track"), "depth"),
            P(("shots", "track"), "depth"),
            P("shots", "track", "depth"),
            P(("shots", "depth"), "track"),
        ),
        check_vma=False,
    )
```

time: 203 us -> 59.8 us (0.29)
  starting transfers between devices: 92.3 us -> 4.08 us
  local copies, waits for them, and re-layouts: 43.3 us -> 7.57 us
  waiting for transfers between devices: 32 us -> 0.91 us
  other arithmetic: 28.5 us -> 0.69 us
  Pallas kernels: 0 us -> 21.3 us
  blocking collectives: 3.3 us -> 23.9 us
    ppermute x36 -> x3, starting transfers between devices: 75.9 us -> 4.08 us  [the longest x1 2.91 us: per_device(): got_even = lax.ppermute(to_even, 'track', swap(0))]
    ppermute x36 -> x3, waiting for transfers between devices: 32 us -> 0.91 us  [the longest x1 0.9 us: per_device(): got_depth = lax.ppermute(to_depth, 'depth', [(0, 1), (1, 0)])]
    all_gather x0 -> x1, blocking collectives: none -> 23.9 us  [per_device(): strips = lax.all_gather(strip, ('track', 'depth'), axis=0, tiled=False)]
    pallas_call x0 -> x4, Pallas kernels: none -> 21.3 us  [the longest x1 16.9 us: per_device(): pl.pallas_call(main_kernel, out_shape=(block, block, jax.ShapeDtypeStruct...]
    all_to_all x3 -> x0, starting transfers between devices: 16.4 us -> none  [the longest x1 6.63 us: per_device(): lax.all_to_all(sent_obs, 'track', split_axis=1, concat_axis=1, tiled=True)]
    scatter-add x4 -> x0, other arithmetic: 14 us -> none  [per_device(): adjoint[2].reshape(-1).at[flat_cell]]
    gather x5 -> x0, local copies, waits for them, and re-layouts: 13.3 us -> none  [the longest x4 12.6 us: per_device(): records.append(jnp.where(inject, strains[0].reshape(-1)[flat_cell], 0.0))]
    slice x69 -> x0, local copies, waits for them, and re-layouts: 10.1 us -> none  [the longest x47 6.27 us: window_of(): lax.slice_in_dim(field, start_at, start_at + cut_count, axis=dim_index)]
  transfers between devices with their start and end apart: 39 -> 3, of which waited for: 14 -> 1; matrix products, arithmetic and copies ran while one was open for 18% -> 0% of each run, Pallas kernels for 0% -> 7%
where the time goes in v1:
time: 59.8 us; the launch traced here: 59.3 us
  blocking collectives  23.9 us (40%)
  Pallas kernels  21.3 us (36%)
  local copies, waits for them, and re-layouts  7.57 us (13%)
  starting transfers between devices  4.08 us (7%)
  waiting for transfers between devices  0.91 us (2%)
  between operations  0.78 us (1%)
  other arithmetic  0.69 us (1%)
    all_gather x1, blocking collectives, per_device(): strips = lax.all_gather(strip, ('track', 'depth'), axis=0, tiled=False)  23.9 us
    pallas_call x1, Pallas kernels, per_device(): pl.pallas_call(main_kernel, out_shape=(block, block, jax.ShapeDtypeStruct...  16.9 us
    unnamed x32, local copies, waits for them, and re-layouts  7.57 us
    pallas_call x1, Pallas kernels, per_device(): pl.pallas_call(lambda *refs: surface_kernel(tracks, rows, *refs), out_sha...  4.08 us
    ppermute x1, starting transfers between devices, per_device(): got_even = lax.ppermute(to_even, 'track', swap(0))  2.91 us
  transfers between devices with their start and end apart: 3, of which 1 were waited for; matrix products, arithmetic and copies ran while one was open for 0% of the time, Pallas kernels for 7%

profile of v1, /device:TPU:0, one launch (start us, length us, event | category | flops | bytes accessed | tf_op | source)
XLA Modules:
  0.0 59.3 jit_solution(5292262250862887174)
XLA Ops:
  0.6 0.7 %broadcast_multiply_fusion = s32[256,1]{0,1:T(1,128)S(1)} fusion(s32[256,1]{0,1:T(1,128)} %param.18), kind=kLoop, calls=%fused_computation.8 | loop fusion | flops 256 | bytes 2048 | tf_op jit(solution)/shard_map/mul | solution.py:413
  1.3 0.0 copy-start.15
  1.3 0.7 %copy-done.15 = s32[256]{0:T(256)S(1)} copy-done((s32[256]{0:T(256)S(1)}, s32[256]{0:T(256)}, u32[]{:S(2)}) %copy-start.15) | copy-done | bytes 1048
  2.0 0.0 copy-start.14
  2.0 0.7 %copy-done.14 = f32[4,256]{1,0:T(4,128)S(1)} copy-done((f32[4,256]{1,0:T(4,128)S(1)}, f32[4,256]{1,0:T(4,128)}, u32[]{:S(2)}) %copy-start.14) | copy-done | bytes 4120
  2.7 0.0 copy-start
  2.7 0.9 %copy-done = f32[3,64,256]{2,1,0:T(8,128)S(1)} copy-done((f32[3,64,256]{2,1,0:T(8,128)S(1)}, f32[3,64,256]{2,1,0:T(8,128)}, u32[]{:S(2)}) %copy-start) | copy-done | bytes 196632
  3.6 0.0 copy-start.2
  3.6 0.9 %copy-done.2 = f32[3,64,256]{2,1,0:T(8,128)S(1)} copy-done((f32[3,64,256]{2,1,0:T(8,128)S(1)}, f32[3,64,256]{2,1,0:T(8,128)}, u32[]{:S(2)}) %copy-start.2) | copy-done | bytes 196632
  4.5 0.0 copy-start.4
  4.6 0.9 %copy-done.4 = f32[2,64,256]{2,1,0:T(8,128)S(1)} copy-done((f32[2,64,256]{2,1,0:T(8,128)S(1)}, f32[2,64,256]{2,1,0:T(8,128)}, u32[]{:S(2)}) %copy-start.4) | copy-done | bytes 131096
  5.5 0.0 copy-start.6
  5.5 0.9 %copy-done.6 = f32[2,64,256]{2,1,0:T(8,128)S(1)} copy-done((f32[2,64,256]{2,1,0:T(8,128)S(1)}, f32[2,64,256]{2,1,0:T(8,128)}, u32[]{:S(2)}) %copy-start.6) | copy-done | bytes 131096
  6.4 0.0 copy-start.8
  6.4 0.8 %copy-done.8 = f32[64,256]{1,0:T(8,128)S(1)} copy-done((f32[64,256]{1,0:T(8,128)S(1)}, f32[64,256]{1,0:T(8,128)}, u32[]{:S(2)}) %copy-start.8) | copy-done | bytes 65560
  7.2 0.0 copy-start.10
  7.2 0.8 %copy-done.10 = f32[64,256]{1,0:T(8,128)S(1)} copy-done((f32[64,256]{1,0:T(8,128)S(1)}, f32[64,256]{1,0:T(8,128)}, u32[]{:S(2)}) %copy-start.10) | copy-done | bytes 65560
  8.0 0.0 copy-start.12
  8.0 0.8 %copy-done.12 = f32[64,256]{1,0:T(8,128)S(1)} copy-done((f32[64,256]{1,0:T(8,128)S(1)}, f32[64,256]{1,0:T(8,128)}, u32[]{:S(2)}) %copy-start.12) | copy-done | bytes 65560
  8.9 0.4 pack.1
  9.2 0.5 collective-permute-start
  9.8 0.9 %collective-permute-done.got.refs_7_ = f32[64,256]{1,0:T(8,128)S(1)} collective-permute-done((f32[64,256]{1,0:T(8,128)S(1)}, f32[64,256]{1,0:T(8,128)S(1)}, u32[]{:S(2)}, u32[]{:S(2)}) %collective-permute-start) | collective-permute-done | bytes 65568 | tf_op jit(solution)/shard_map/ppermute | solution.py:437
  10.7 2.9 %collective-permute-start.1 = (f32[176,256]{1,0:T(8,128)S(1)}, f32[176,256]{1,0:T(8,128)S(1)}, u32[]{:S(2)}, u32[]{:S(2)}) collective-permute-start(f32[176,256]{1,0:T(8,128)S(1)} %get-tuple-element.18), channel_id=1, source_target_pairs={{0,2},{2,0},{4,6},{6,4},{8,10},{10,8},{12,14},{14,12},{1,3},{3,1},... | collective-permute-start | bytes 540680 | tf_op jit(solution)/shard_map/ppermute | solution.py:450
  13.6 0.7 %collective-permute-start.2 = (f32[176,256]{1,0:T(8,128)S(1)}, f32[176,256]{1,0:T(8,128)S(1)}, u32[]{:S(2)}, u32[]{:S(2)}) collective-permute-start(f32[176,256]{1,0:T(8,128)S(1)} %get-tuple-element.19), channel_id=1, source_target_pairs={{2,4},{4,2},{6,8},{8,6},{10,12},{12,10},{3,5},{5,3},{7,9},{9,7},{1... | collective-permute-start | bytes 540680 | tf_op jit(solution)/shard_map/ppermute | solution.py:449
  14.3 0.0 copy-start.9
  14.3 0.0 copy-start.11
  14.3 0.0 copy-start.13
  14.3 23.9 %all-gather = f32[1280,128]{1,0:T(8,128)S(1)} all-gather(f32[80,128]{1,0:T(8,128)S(1)} %get-tuple-element.20), channel_id=2, replica_groups=mesh['shots'=2,'track'=8,'depth'=2] {'track','depth'}, dimensions={0}, use_global_device_ids=true | all-gather | bytes 696320 | tf_op jit(solution)/shard_map/all_gather | solution.py:436
  38.2 0.0 copy-start.1
  38.2 0.0 copy-start.3
  38.2 0.0 copy-start.5
  38.3 0.0 copy-start.7
  38.3 4.1 %surface.1 = (f32[4,96,128]{2,1,0:T(8,128)S(1)}, f32[2,256]{1,0:T(2,128)}) custom-call(f32[16,80,128]{2,1,0:T(8,128)S(1)} %bitcast.4, f32[4,256]{1,0:T(4,128)S(1)} %copy-done.14, s32[1,256]{1,0:T(1,128)S(1)} %bitcast.8, s32[1,256]{1,0:T(1,128)S(1)} %bitcast.6), custom_call_target="tpu_custom_call" | custom-call | tf_op jit(solution)/shard_map/surface/pallas_call | solution.py:453
  42.3 0.0 collective-permute-done.1.refs_8_
  42.4 0.0 collective-permute-done.2.refs_9_
  42.4 0.0 copy-done.9
  42.4 0.0 copy-done.11
  42.4 0.0 copy-done.13
  42.4 0.0 copy-done.1
  42.4 0.0 copy-done.3
  42.4 0.0 copy-done.5
  42.4 0.0 copy-done.7
  42.4 16.9 %window.1 = (f32[64,256]{1,0:T(8,128)}, f32[64,256]{1,0:T(8,128)}, f32[2,64,256]{2,1,0:T(8,128)}) custom-call(f32[2,64,256]{2,1,0:T(8,128)S(1)} %copy-done.5, f32[3,64,256]{2,1,0:T(8,128)S(1)} %copy-done.1, f32[2,64,256]{2,1,0:T(8,128)S(1)} %copy-done.7, f32[3,64,256]{2,1,0:T(8,128)S(1)} %copy-done.3, f32[64,256]{1,0:T(8,128)S(1)} %copy-done.9, ...), custom_call_target="tpu_custom_call" | custom-call | tf_op jit(solution)/shard_map/window/pallas_call | solution.py:471
  (2 shorter events, 0.0 us)
Async XLA Ops:
  1.3 0.7 %copy-start.15 = (s32[256]{0:T(256)S(1)}, s32[256]{0:T(256)}, u32[]{:S(2)}) copy-start(s32[256]{0:T(256)} %param.19) | copy-start | bytes 3076
  2.0 0.7 %copy-start.14 = (f32[4,256]{1,0:T(4,128)S(1)}, f32[4,256]{1,0:T(4,128)}, u32[]{:S(2)}) copy-start(f32[4,256]{1,0:T(4,128)} %refs_1_.4) | copy-start | bytes 12292
  2.7 0.9 %copy-start = (f32[3,64,256]{2,1,0:T(8,128)S(1)}, f32[3,64,256]{2,1,0:T(8,128)}, u32[]{:S(2)}) copy-start(f32[3,64,256]{2,1,0:T(8,128)} %refs_1_.5) | copy-start | bytes 589828
  3.6 0.9 %copy-start.2 = (f32[3,64,256]{2,1,0:T(8,128)S(1)}, f32[3,64,256]{2,1,0:T(8,128)}, u32[]{:S(2)}) copy-start(f32[3,64,256]{2,1,0:T(8,128)} %refs_3_.3) | copy-start | bytes 589828
  4.5 0.9 %copy-start.4 = (f32[2,64,256]{2,1,0:T(8,128)S(1)}, f32[2,64,256]{2,1,0:T(8,128)}, u32[]{:S(2)}) copy-start(f32[2,64,256]{2,1,0:T(8,128)} %refs_0_.3) | copy-start | bytes 393220
  5.5 0.9 %copy-start.6 = (f32[2,64,256]{2,1,0:T(8,128)S(1)}, f32[2,64,256]{2,1,0:T(8,128)}, u32[]{:S(2)}) copy-start(f32[2,64,256]{2,1,0:T(8,128)} %refs_2_.3) | copy-start | bytes 393220
  6.4 0.8 %copy-start.8 = (f32[64,256]{1,0:T(8,128)S(1)}, f32[64,256]{1,0:T(8,128)}, u32[]{:S(2)}) copy-start(f32[64,256]{1,0:T(8,128)} %refs_4_.3) | copy-start | bytes 196612
  7.2 0.8 %copy-start.10 = (f32[64,256]{1,0:T(8,128)S(1)}, f32[64,256]{1,0:T(8,128)}, u32[]{:S(2)}) copy-start(f32[64,256]{1,0:T(8,128)} %refs_5_.3) | copy-start | bytes 196612
  8.0 0.8 %copy-start.12 = (f32[64,256]{1,0:T(8,128)S(1)}, f32[64,256]{1,0:T(8,128)}, u32[]{:S(2)}) copy-start(f32[64,256]{1,0:T(8,128)} %refs_6_.3) | copy-start | bytes 196612
  9.2 1.4 %collective-permute-start = (f32[64,256]{1,0:T(8,128)S(1)}, f32[64,256]{1,0:T(8,128)S(1)}, u32[]{:S(2)}, u32[]{:S(2)}) collective-permute-start(f32[64,256]{1,0:T(8,128)S(1)} %get-tuple-element.15), channel_id=1, source_target_pairs={{0,1},{1,0},{2,3},{3,2},{4,5},{5,4},{6,7},{7,6},{8,9},{9,8},{10,11... | collective-permute-start | bytes 196616 | tf_op jit(solution)/shard_map/ppermute | solution.py:437
  10.7 31.6 %collective-permute-start.1 = (f32[176,256]{1,0:T(8,128)S(1)}, f32[176,256]{1,0:T(8,128)S(1)}, u32[]{:S(2)}, u32[]{:S(2)}) collective-permute-start(f32[176,256]{1,0:T(8,128)S(1)} %get-tuple-element.18), channel_id=1, source_target_pairs={{0,2},{2,0},{4,6},{6,4},{8,10},{10,8},{12,14},{14,12},{1,3},{3,1},... | collective-permute-start | bytes 540680 | tf_op jit(solution)/shard_map/ppermute | solution.py:450
  13.6 28.8 %collective-permute-start.2 = (f32[176,256]{1,0:T(8,128)S(1)}, f32[176,256]{1,0:T(8,128)S(1)}, u32[]{:S(2)}, u32[]{:S(2)}) collective-permute-start(f32[176,256]{1,0:T(8,128)S(1)} %get-tuple-element.19), channel_id=1, source_target_pairs={{2,4},{4,2},{6,8},{8,6},{10,12},{12,10},{3,5},{5,3},{7,9},{9,7},{1... | collective-permute-start | bytes 540680 | tf_op jit(solution)/shard_map/ppermute | solution.py:449
  14.3 28.1 %copy-start.9 = (f32[64,256]{1,0:T(8,128)S(1)}, f32[64,256]{1,0:T(8,128)}, u32[]{:S(2)}) copy-start(f32[64,256]{1,0:T(8,128)} %refs_4_.3) | copy-start | bytes 196612
  14.3 28.1 %copy-start.11 = (f32[64,256]{1,0:T(8,128)S(1)}, f32[64,256]{1,0:T(8,128)}, u32[]{:S(2)}) copy-start(f32[64,256]{1,0:T(8,128)} %refs_5_.3) | copy-start | bytes 196612
  14.3 28.1 %copy-start.13 = (f32[64,256]{1,0:T(8,128)S(1)}, f32[64,256]{1,0:T(8,128)}, u32[]{:S(2)}) copy-start(f32[64,256]{1,0:T(8,128)} %refs_6_.3) | copy-start | bytes 196612
  38.2 4.2 %copy-start.1 = (f32[3,64,256]{2,1,0:T(8,128)S(1)}, f32[3,64,256]{2,1,0:T(8,128)}, u32[]{:S(2)}) copy-start(f32[3,64,256]{2,1,0:T(8,128)} %refs_1_.5) | copy-start | bytes 589828
  38.2 4.2 %copy-start.3 = (f32[3,64,256]{2,1,0:T(8,128)S(1)}, f32[3,64,256]{2,1,0:T(8,128)}, u32[]{:S(2)}) copy-start(f32[3,64,256]{2,1,0:T(8,128)} %refs_3_.3) | copy-start | bytes 589828
  38.2 4.2 %copy-start.5 = (f32[2,64,256]{2,1,0:T(8,128)S(1)}, f32[2,64,256]{2,1,0:T(8,128)}, u32[]{:S(2)}) copy-start(f32[2,64,256]{2,1,0:T(8,128)} %refs_0_.3) | copy-start | bytes 393220
  38.3 4.2 %copy-start.7 = (f32[2,64,256]{2,1,0:T(8,128)S(1)}, f32[2,64,256]{2,1,0:T(8,128)}, u32[]{:S(2)}) copy-start(f32[2,64,256]{2,1,0:T(8,128)} %refs_2_.3) | copy-start | bytes 393220

commit v2 on v0

v2 whole, which is shorter than its diff:
```python
import jax
import jax.numpy as jnp
from jax import lax
from jax.experimental import pallas as pl
from jax.experimental.pallas import tpu as pltpu
from jax.sharding import PartitionSpec as P

FIBRE_ROWS = 4
NEAR = 9.0 / 8.0
RATIO = -1.0 / 27.0
HALO = 12
EDGE = 16
LANES = 128
PAD = 8
FIELDS = 13
MOMENTS = 4
IMAGE = MOMENTS * FIBRE_ROWS
NOTE = 24
VMEM = pltpu.VMEM
F32 = jnp.float32
BF16 = jnp.bfloat16


def lane_ids(rows):
    return lax.broadcasted_iota(jnp.int32, (rows, LANES), 1)


def row_ids(rows, columns):
    return lax.broadcasted_iota(jnp.int32, (rows, columns), 0)


def params():
    return pltpu.CompilerParams(vmem_limit_bytes=40 * 1024 * 1024)


def turn(value, by):
    return pltpu.roll(value, by % LANES, 1)


def is_even():
    return lax.rem(lax.axis_index("track"), 2) == 0


def fetch(sources, targets, sems):
    copies = [pltpu.make_async_copy(s, t, sems.at[i]) for i, (s, t) in enumerate(zip(sources, targets))]
    for copy in copies:
        copy.start()
    return copies


def field_refs(velocity, stress, adj_velocity, adj_stress, buoyancy, lame, shear):
    return (
        [velocity.at[i] for i in range(2)]
        + [stress.at[i] for i in range(3)]
        + [adj_velocity.at[i] for i in range(2)]
        + [adj_stress.at[i] for i in range(3)]
        + [buoyancy, lame, shear]
    )


def pack_kernel(*refs):
    sources, (depth_out, even_out, odd_out), held, sems = refs[:7], refs[7:10], refs[10:17], refs[17]
    copies = fetch(sources, held, sems)
    depth = lax.axis_index("depth")
    even = is_even()
    fields = field_refs(*held)
    rows = fields[0].shape[0]
    lane = lane_ids(rows)
    tail = EDGE + HALO * FIELDS
    for out in (even_out, odd_out):
        out[:EDGE, :] = jnp.zeros((EDGE, 2 * LANES), F32)
        out[tail:, :] = jnp.zeros((out.shape[0] - tail, 2 * LANES), F32)
    for copy in copies:
        copy.wait()
    packed = [jnp.zeros((rows, LANES), F32) for _ in range(2)]
    for f, ref in enumerate(fields):
        first, last = ref[:, :LANES], ref[:, LANES:]
        spot = EDGE * (f % 8)
        here = (lane >= spot) & (lane < spot + EDGE)
        edge = jnp.where(depth == 0, last, first)
        shift = lax.rem(spot + EDGE * (1 - depth), LANES)
        packed[f // 8] = jnp.where(here, pltpu.roll(edge, shift, 1), packed[f // 8])
        low, high = ref[:HALO, :], ref[rows - HALO :, :]
        at = EDGE + HALO * f
        even_out[at : at + HALO, :] = jnp.where(even, high, low)
        odd_out[at : at + HALO, :] = jnp.where(even, low, high)
    depth_out[:, :LANES] = packed[0]
    depth_out[:, LANES:] = packed[1]


def corner_kernel(got, even_in, odd_in, even_out, odd_out, sems):
    rows = got.shape[0]
    is_odd = lax.rem(lax.axis_index("track"), 2)
    high, low = (rows - EDGE) * (1 - is_odd), (rows - EDGE) * is_odd
    one = pltpu.make_async_copy(
        got.at[pl.ds(pl.multiple_of(high, EDGE), EDGE), :], even_out.at[pl.ds(0, EDGE), :], sems.at[0]
    )
    two = pltpu.make_async_copy(
        got.at[pl.ds(pl.multiple_of(low, EDGE), EDGE), :], odd_out.at[pl.ds(0, EDGE), :], sems.at[1]
    )
    one.start()
    two.start()
    one.wait()
    two.wait()


def windows(f, first, last, halo):
    depth = lax.axis_index("depth")
    lane = lane_ids(first.shape[0])
    shift = lax.rem(LANES - EDGE * (f % 8) + (LANES - EDGE) * (1 - depth), LANES)
    beside = pltpu.roll(halo, shift, 1)
    return [
        jnp.where(lane >= EDGE, turn(first, EDGE), jnp.where(depth == 1, beside, 0.0)),
        jnp.where(lane < LANES // 2, turn(first, LANES // 2), turn(last, LANES // 2)),
        jnp.where(lane < LANES - EDGE, turn(last, -EDGE), jnp.where(depth == 0, beside, 0.0)),
    ]


def joined(planes):
    lane = lane_ids(planes[0].shape[0])
    middle = turn(planes[1], LANES // 2)
    return (
        jnp.where(lane < 88, turn(planes[0], -EDGE), middle),
        jnp.where(lane < 40, middle, turn(planes[2], EDGE)),
    )


def own_kernel(*refs):
    sources, got_depth, planes_out, held, sems = refs[:7], refs[7], refs[8], refs[9:16], refs[16]
    for copy in fetch(sources, held, sems):
        copy.wait()
    for f, ref in enumerate(field_refs(*held)):
        col = LANES * (f // 8)
        planes = windows(f, ref[:, :LANES], ref[:, LANES:], got_depth[:, col : col + LANES])
        for p in range(3):
            planes_out[f, p] = planes[p]


def halo_windows(f, got_even, got_odd):
    even = is_even()
    col = LANES * (f // 8)
    high = EDGE + HALO * f
    low = high - (EDGE - HALO)
    corner_even, corner_odd = got_even[:EDGE, col : col + LANES], got_odd[:EDGE, col : col + LANES]
    left = jnp.where(even, got_odd[low : low + EDGE, :], got_even[low : low + EDGE, :])
    right = jnp.where(even, got_even[high : high + EDGE, :], got_odd[high : high + EDGE, :])
    left_halo = jnp.where(even, corner_odd, corner_even)
    right_halo = jnp.where(even, corner_even, corner_odd)
    return (
        windows(f, left[:, :LANES], left[:, LANES:], left_halo),
        windows(f, right[:, :LANES], right[:, LANES:], right_halo),
    )


def load_state(state, own, got_even, got_odd, base):
    rows = own.shape[2]
    extent = rows + 2 * EDGE
    for f in range(5):
        below, above = halo_windows(base + f, got_even, got_odd)
        for p in range(3):
            state[f, p, :PAD, :] = jnp.zeros((PAD, LANES), F32)
            state[f, p, PAD : PAD + EDGE, :] = below[p]
            state[f, p, PAD + EDGE : PAD + EDGE + rows, :] = own[base + f, p]
            state[f, p, PAD + EDGE + rows : PAD + extent, :] = above[p]
            state[f, p, PAD + extent :, :] = jnp.zeros((PAD, LANES), F32)


def velocities(state, media, span):
    for r in range(8 * span[0], 8 * span[1], 8):
        for p in range(3):

            def at(f, by=0):
                return state[f, p, r + PAD + by : r + PAD + by + 8, :]

            xx, xz, zz = at(2), at(4), at(3)
            b = media[0, p, r : r + 8, :]
            near = (xx - at(2, -1)) + (xz - turn(xz, 1))
            far = (at(2, 1) - at(2, -2)) + (turn(xz, -1) - turn(xz, 2))
            state[0, p, r + PAD : r + PAD + 8, :] = at(0) + b * (near + RATIO * far)
            near = (at(4, 1) - xz) + (turn(zz, -1) - zz)
            far = (at(4, 2) - at(4, -1)) + (turn(zz, -2) - turn(zz, 1))
            state[1, p, r + PAD : r + PAD + 8, :] = at(1) + b * (near + RATIO * far)


def stresses(state, media, span, update, keep):
    for r in range(8 * span[0], 8 * span[1], 8):
        for p in range(3):

            def at(f, by=0):
                return state[f, p, r + PAD + by : r + PAD + by + 8, :]

            vx, vz = at(0), at(1)
            exx = (at(0, 1) - vx) + RATIO * (at(0, 2) - at(0, -1))
            ezz = (vz - turn(vz, 1)) + RATIO * (turn(vz, -1) - turn(vz, 2))
            near = (turn(vx, -1) - vx) + (vz - at(1, -1))
            far = (turn(vx, -2) - turn(vx, 1)) + (at(1, 1) - at(1, -2))
            shear = near + RATIO * far
            keep(p, r - EDGE, exx, ezz, shear)
            if update:
                whole, lam, mu = (media[k, p, r : r + 8, :] for k in (1, 2, 3))
                state[2, p, r + PAD : r + PAD + 8, :] = at(2) + (whole * exx + lam * ezz)
                state[3, p, r + PAD : r + PAD + 8, :] = at(3) + (lam * exx + whole * ezz)
                state[4, p, r + PAD : r + PAD + 8, :] = at(4) + mu * shear


def spans(step, rows):
    tiles = (rows + 2 * EDGE) // 8
    if step == 0:
        return (0, tiles), (0, tiles)
    inner = (1, tiles - 1)
    return inner, inner if step < MOMENTS - 1 else (EDGE // 8, tiles - EDGE // 8)


def forward_kernel(
    own, got_even, got_odd, obs, owner, cell, media, saved, end_out, note_out, state, small, numbers, sems
):
    copies = fetch((obs, owner, cell), (small, numbers.at[0], numbers.at[1]), sems)
    rows = own.shape[2]
    extent = rows + 2 * EDGE
    parts = []
    for f in (10, 11, 12):
        below, above = halo_windows(f, got_even, got_odd)
        parts.append([(below[p], own[f, p], above[p]) for p in range(3)])
    for p in range(3):
        for k, at in enumerate((0, EDGE, EDGE + rows)):
            b, lam, mu = (NEAR * parts[i][p][k] for i in range(3))
            span = slice(at, at + b.shape[0])
            media[0, p, span, :] = b
            media[1, p, span, :] = lam + 2.0 * mu
            media[2, p, span, :] = lam
            media[3, p, span, :] = mu
    load_state(state, own, got_even, got_odd, 0)
    for step in range(MOMENTS):
        fast, slow = spans(step, rows)
        velocities(state, media, fast)

        def save(p, r, exx, ezz, shear):
            if 0 <= r < rows:
                saved[step, 0, p, r : r + 8, :] = exx
                saved[step, 1, p, r : r + 8, :] = ezz
                saved[step, 2, p, r : r + 8, :] = shear

        stresses(state, media, slow, step < MOMENTS - 1, save)

    top = PAD + EDGE
    for f in range(2):
        first, last = joined([state[f, p, top : top + rows, :] for p in range(3)])
        end_out[f, :, :LANES] = first
        end_out[f, :, LANES:] = last

    lane = lane_ids(rows)
    image = jnp.zeros((rows, LANES), F32)
    for step in range(MOMENTS):
        spot = FIBRE_ROWS * step
        here = (lane >= spot) & (lane < spot + FIBRE_ROWS)
        image = jnp.where(here, NEAR * turn(saved[step, 0, 0], spot - EDGE), image)
    turned = image.T
    for copy in copies:
        copy.wait()
    along = numbers[0] * rows + lax.shift_right_logical(numbers[1], 2)
    row = numbers[1] & 3
    half = IMAGE // 2
    block = jnp.concatenate(
        [
            jnp.concatenate([turned[:half], turned[half:IMAGE]], axis=1),
            jnp.concatenate([small[:, :LANES], small[:, LANES:]], axis=0),
            along[:, :LANES].astype(F32),
            along[:, LANES:].astype(F32),
            row[:, :LANES].astype(F32),
            row[:, LANES:].astype(F32),
            jnp.zeros((4, LANES), F32),
        ],
        axis=0,
    )
    note_out[...] = jnp.broadcast_to(block[None], note_out.shape)


def three(value):
    high = value.astype(BF16)
    rest = value - high.astype(F32)
    middle = rest.astype(BF16)
    low = (rest - middle.astype(F32)).astype(BF16)
    return [high, middle, low]


def add_up(value):
    return (value[2 * IMAGE : 3 * IMAGE] + value[IMAGE : 2 * IMAGE]) + value[:IMAGE]


def channel_sums(tracks, rows, notes, own_along):
    start = lax.axis_index("track") * rows - EDGE
    group = min(8, tracks)
    channels = own_along.shape[1]
    lane = lane_ids(8)
    half = LANES // 2
    wanted = jnp.concatenate([own_along, start + lax.broadcasted_iota(jnp.int32, (1, LANES), 1)], axis=1)
    row16 = row_ids(IMAGE, LANES)

    def body(number, carry):
        rate, image = carry
        base = number * group
        firsts, lasts = [], []
        for k in range(0, group, 2):
            a, b = notes[2 * (base + k), :8, :], notes[2 * (base + k + 1), :8, :]
            firsts.append(jnp.where(lane < half, a, turn(b, half)))
            lasts.append(jnp.where(lane < half, turn(a, half), b))
        strains = jnp.concatenate([jnp.concatenate(firsts, axis=1), jnp.concatenate(lasts, axis=1)], axis=0)
        spot = base * rows + row_ids(group * rows, channels + LANES)
        hot = (spot == wanted).astype(F32).astype(BF16)
        rate = rate + jnp.dot(jnp.concatenate(three(strains), axis=0), hot, preferred_element_type=F32)
        weights, hots = [], []
        for k in range(group):
            who = 2 * (base + k)
            for h in range(2):
                along = notes[who, 16 + h : 17 + h, :]
                mask = (row16 & 3).astype(F32) == notes[who, 18 + h : 19 + h, :]
                seen = [notes[who, 8 + 4 * h + t : 9 + 4 * h + t, :] for t in range(MOMENTS)]
                value = jnp.where(
                    row16 < 8,
                    jnp.where(row16 < 4, seen[0], seen[1]),
                    jnp.where(row16 < 12, seen[2], seen[3]),
                )
                pieces = three(jnp.where(mask, value, 0.0)) + [mask.astype(F32).astype(BF16)]
                weights.append(jnp.concatenate(pieces, axis=0))
                spot = (start + row_ids(LANES, LANES)).astype(F32)
                hots.append((spot == along).astype(F32).astype(BF16))
        image = image + lax.dot_general(
            jnp.concatenate(weights, axis=1),
            jnp.concatenate(hots, axis=1),
            (((1,), (1,)), ((), ())),
            preferred_element_type=F32,
        )
        return rate, image

    carry = jnp.zeros((3 * IMAGE, channels + LANES), F32), jnp.zeros((4 * IMAGE, LANES), F32)
    if tracks == group:
        carry = body(0, carry)
    else:
        carry = lax.fori_loop(0, tracks // group, body, carry)
    rate, image = carry
    return add_up(rate), add_up(image), image[3 * IMAGE :]


def adjoint_kernel(
    tracks, own, got_even, got_odd, media, saved, notes, obs, owner, cell,
    lambda_out, mu_out, residual_out, state, sums, small, numbers, sems,
):
    copies = fetch((obs, owner, cell), (small, numbers.at[0], numbers.at[1]), sems)
    rows = own.shape[2]
    extent = rows + 2 * EDGE
    depth = lax.axis_index("depth")
    load_state(state, own, got_even, got_odd, 5)
    sums[...] = jnp.zeros(sums.shape, F32)
    for copy in copies:
        copy.wait()
    along = numbers[0] * rows + lax.shift_right_logical(numbers[1], 2)
    row = numbers[1] & 3
    rate, seen, count = channel_sums(tracks, rows, notes, along)
    channels = along.shape[1]
    at_own = jnp.where((row_ids(IMAGE, channels) & 3) == row, rate[:, :channels], 0.0)
    traces = [
        jnp.sum(at_own[4 * t : 4 * t + 4], axis=0, keepdims=True) - small[t : t + 1, :] for t in range(MOMENTS)
    ]
    residual_out[...] = jnp.where(
        depth == 0, jnp.concatenate(traces[:2], axis=0), jnp.concatenate(traces[2:], axis=0)
    )
    sources = count * rate[:, channels:] - seen
    turned = jnp.concatenate([sources, jnp.zeros((LANES - IMAGE, LANES), F32)], axis=0).T[:extent]
    lane = lane_ids(extent)
    here = (lane >= EDGE) & (lane < EDGE + FIBRE_ROWS) & (depth == 0)

    for step in range(MOMENTS):
        fast, slow = spans(step, rows)
        moment = MOMENTS - 1 - step
        added = jnp.where(here, turn(turned, EDGE - FIBRE_ROWS * moment), 0.0)
        state[2, 0, PAD : PAD + extent, :] += added
        velocities(state, media, fast)

        def gather(p, r, exx, ezz, shear):
            if 0 <= r < rows:
                fxx, fzz, fxz = (saved[moment, k, p, r : r + 8, :] for k in range(3))
                sums[0, p, r : r + 8, :] += (fxx + fzz) * (exx + ezz)
                sums[1, p, r : r + 8, :] += 2.0 * (fxx * exx + fzz * ezz) + fxz * shear

        stresses(state, media, slow, step < MOMENTS - 1, gather)

    for k, out in enumerate((lambda_out, mu_out)):
        first, last = joined([sums[k, p] for p in range(3)])
        out[:, :LANES] = (NEAR * NEAR) * first
        out[:, LANES:] = (NEAR * NEAR) * last


def per_device(
    velocity,
    stress,
    adjoint_velocity,
    adjoint_stress,
    buoyancy,
    lame_lambda,
    shear_modulus,
    observed,
    owner_track,
    fibre_cell,
):
    tracks = lax.axis_size("track")
    rows, depth_cells = buoyancy.shape
    moments, channels = observed.shape
    owner = owner_track.reshape(1, channels)
    cell = fibre_cell.reshape(1, channels)
    arrays = (velocity, stress, adjoint_velocity, adjoint_stress, buoyancy, lame_lambda, shear_modulus)
    length = EDGE + HALO * FIELDS
    length = length + (-length) % 8
    extent = rows + 2 * EDGE
    block = jax.ShapeDtypeStruct((rows, depth_cells), F32)
    edges = jax.ShapeDtypeStruct((length, depth_cells), F32)
    inside = pl.BlockSpec(memory_space=VMEM)
    outside = pl.BlockSpec(memory_space=pltpu.HBM)
    anywhere = pl.BlockSpec(memory_space=pl.ANY)
    held = [VMEM(a.shape, F32) for a in arrays]
    channel_scratch = [
        VMEM((moments, channels), F32),
        VMEM((2, 1, channels), jnp.int32),
        pltpu.SemaphoreType.DMA((3,)),
    ]

    to_depth, to_even, to_odd = pl.pallas_call(
        pack_kernel,
        out_shape=(block, edges, edges),
        in_specs=[outside] * 7,
        out_specs=(inside,) * 3,
        scratch_shapes=held + [pltpu.SemaphoreType.DMA((7,))],
        compiler_params=params(),
        name="pack",
    )(*arrays)

    got_depth = lax.ppermute(to_depth, "depth", [(0, 1), (1, 0)])
    to_even, to_odd = pl.pallas_call(
        corner_kernel,
        out_shape=(edges, edges),
        in_specs=[anywhere] * 3,
        out_specs=(anywhere,) * 2,
        input_output_aliases={1: 0, 2: 1},
        scratch_shapes=[pltpu.SemaphoreType.DMA((2,))],
        compiler_params=params(),
        name="corners",
    )(got_depth, to_even, to_odd)
    swap = lambda k: [pair for i in range(k, tracks - 1, 2) for pair in ((i, i + 1), (i + 1, i))]
    got_odd = lax.ppermute(to_odd, "track", swap(1))
    got_even = lax.ppermute(to_even, "track", swap(0))

    own = pl.pallas_call(
        own_kernel,
        out_shape=jax.ShapeDtypeStruct((FIELDS, 3, rows, LANES), F32),
        in_specs=[outside] * 7 + [inside],
        out_specs=inside,
        scratch_shapes=held + [pltpu.SemaphoreType.DMA((7,))],
        compiler_params=params(),
        name="own_planes",
    )(*arrays, got_depth)

    devices = tracks * lax.axis_size("depth")
    media, saved, velocity_end, note = pl.pallas_call(
        forward_kernel,
        out_shape=(
            jax.ShapeDtypeStruct((4, 3, extent, LANES), F32),
            jax.ShapeDtypeStruct((moments, 3, 3, rows, LANES), F32),
            jax.ShapeDtypeStruct(velocity.shape, F32),
            jax.ShapeDtypeStruct((devices, NOTE, LANES), F32),
        ),
        in_specs=[inside] * 3 + [outside] * 3,
        out_specs=(inside,) * 4,
        scratch_shapes=[VMEM((5, 3, extent + 2 * PAD, LANES), F32)] + channel_scratch,
        compiler_params=params(),
        name="forward",
    )(own, got_even, got_odd, observed, owner, cell)

    notes = lax.all_to_all(note, ("track", "depth"), split_axis=0, concat_axis=0, tiled=True)

    gradient_lambda, gradient_mu, residual = pl.pallas_call(
        lambda *refs: adjoint_kernel(tracks, *refs),
        out_shape=(block, block, jax.ShapeDtypeStruct((moments // 2, channels), F32)),
        in_specs=[inside] * 6 + [outside] * 3,
        out_specs=(inside,) * 3,
        scratch_shapes=[
            VMEM((5, 3, extent + 2 * PAD, LANES), F32),
            VMEM((2, 3, rows, LANES), F32),
        ]
        + channel_scratch,
        compiler_params=params(),
        name="adjoint",
    )(own, got_even, got_odd, media, saved, notes, observed, owner, cell)
    return gradient_lambda, gradient_mu, velocity_end, residual


def solution(mesh):
    return jax.shard_map(
        per_device,
        mesh=mesh,
        in_specs=(
            P("shots", "track", "depth"),
            P("shots", "track", "depth"),
            P("shots", "track", "depth"),
            P("shots", "track", "depth"),
            P("track", "depth"),
            P("track", "depth"),
            P("track", "depth"),
            P("shots", "track"),
            P("track", None),
            P("track"),
        ),
        out_specs=(
            P(("shots", "track"), "depth"),
            P(("shots", "track"), "depth"),
            P("shots", "track", "depth"),
            P(("shots", "depth"), "track"),
        ),
        check_vma=False,
    )
```

time: 203 us -> 41.8 us (0.21)
  starting transfers between devices: 92.3 us -> 4.09 us
  local copies, waits for them, and re-layouts: 43.3 us -> 6.19 us
  other arithmetic: 28.5 us -> 0 us
  waiting for transfers between devices: 32 us -> 6.4 us
  blocking collectives: 3.3 us -> 14.9 us
  Pallas kernels: 0 us -> 9.12 us
    ppermute x36 -> x3, starting transfers between devices: 75.9 us -> 4.09 us  [the longest x1 2.91 us: per_device(): got_even = lax.ppermute(to_even, 'track', swap(0))]
    ppermute x36 -> x3, waiting for transfers between devices: 32 us -> 6.4 us  [the longest x1 5.5 us: per_device(): got_even = lax.ppermute(to_even, 'track', swap(0))]
    all_to_all x3 -> x0, starting transfers between devices: 16.4 us -> none  [the longest x1 6.63 us: per_device(): lax.all_to_all(sent_obs, 'track', split_axis=1, concat_axis=1, tiled=True)]
    all_to_all x0 -> x1, blocking collectives: none -> 14.9 us  [per_device(): lax.all_to_all(note, ('track', 'depth'), split_axis=0, concat_axis=0, til...]
    scatter-add x4 -> x0, other arithmetic: 14 us -> none  [per_device(): adjoint[2].reshape(-1).at[flat_cell]]
    gather x5 -> x0, local copies, waits for them, and re-layouts: 13.3 us -> none  [the longest x4 12.6 us: per_device(): records.append(jnp.where(inject, strains[0].reshape(-1)[flat_cell], 0.0))]
    slice x69 -> x0, local copies, waits for them, and re-layouts: 10.1 us -> none  [the longest x47 6.27 us: window_of(): lax.slice_in_dim(field, start_at, start_at + cut_count, axis=dim_index)]
    pallas_call x0 -> x5, Pallas kernels: none -> 9.12 us  [the longest x1 2.99 us: per_device(): pl.pallas_call(lambda *refs: adjoint_kernel(tracks, *refs), out_shape=(bl...]
  transfers between devices with their start and end apart: 39 -> 3, of which waited for: 14 -> 2; matrix products, arithmetic and copies ran while one was open for 18% -> 0% of each run, Pallas kernels for 0% -> 4%
where the time goes in v2:
time: 41.8 us; the launch traced here: 41.4 us
  blocking collectives  14.9 us (36%)
  Pallas kernels  9.12 us (22%)
  waiting for transfers between devices  6.4 us (15%)
  local copies, waits for them, and re-layouts  6.19 us (15%)
  starting transfers between devices  4.09 us (10%)
  between operations  0.72 us (2%)
    all_to_all x1, blocking collectives, per_device(): lax.all_to_all(note, ('track', 'depth'), split_axis=0, concat_axis=0, til...  14.9 us
    unnamed x26, local copies, waits for them, and re-layouts  6.19 us
    ppermute x1, waiting for transfers between devices, per_device(): got_even = lax.ppermute(to_even, 'track', swap(0))  5.5 us
    pallas_call x1, Pallas kernels, per_device(): pl.pallas_call(lambda *refs: adjoint_kernel(tracks, *refs), out_shape=(bl...  2.99 us
    pallas_call x1, Pallas kernels, per_device(): pl.pallas_call(forward_kernel, out_shape=(jax.ShapeDtypeStruct((4, 3, ext...  2.94 us
    ppermute x1, starting transfers between devices, per_device(): got_even = lax.ppermute(to_even, 'track', swap(0))  2.91 us
    pallas_call x1, Pallas kernels, per_device(): pl.pallas_call(own_kernel, out_shape=jax.ShapeDtypeStruct((FIELDS, 3, row...  1.78 us
    pallas_call x1, Pallas kernels, per_device(): pl.pallas_call(pack_kernel, out_shape=(block, edges, edges), in_specs=[ou...  1.35 us
  transfers between devices with their start and end apart: 3, of which 2 were waited for; matrix products, arithmetic and copies ran while one was open for 0% of the time, Pallas kernels for 4%

profile of v2, /device:TPU:0, one launch (start us, length us, event | category | flops | bytes accessed | tf_op | source)
XLA Modules:
  0.0 41.4 jit_solution(7619874761818013056)
XLA Ops:
  0.6 0.0 copy-start
  0.6 0.9 %copy-done = f32[3,64,256]{2,1,0:T(8,128)S(1)} copy-done((f32[3,64,256]{2,1,0:T(8,128)S(1)}, f32[3,64,256]{2,1,0:T(8,128)}, u32[]{:S(2)}) %copy-start) | copy-done | bytes 196632
  1.6 0.0 copy-start.2
  1.6 0.9 %copy-done.2 = f32[3,64,256]{2,1,0:T(8,128)S(1)} copy-done((f32[3,64,256]{2,1,0:T(8,128)S(1)}, f32[3,64,256]{2,1,0:T(8,128)}, u32[]{:S(2)}) %copy-start.2) | copy-done | bytes 196632
  2.5 0.0 copy-start.3
  2.5 0.9 %copy-done.3 = f32[2,64,256]{2,1,0:T(8,128)S(1)} copy-done((f32[2,64,256]{2,1,0:T(8,128)S(1)}, f32[2,64,256]{2,1,0:T(8,128)}, u32[]{:S(2)}) %copy-start.3) | copy-done | bytes 131096
  3.4 0.0 copy-start.5
  3.4 0.9 %copy-done.5 = f32[2,64,256]{2,1,0:T(8,128)S(1)} copy-done((f32[2,64,256]{2,1,0:T(8,128)S(1)}, f32[2,64,256]{2,1,0:T(8,128)}, u32[]{:S(2)}) %copy-start.5) | copy-done | bytes 131096
  4.3 0.0 copy-start.7
  4.3 0.8 %copy-done.7 = f32[64,256]{1,0:T(8,128)S(1)} copy-done((f32[64,256]{1,0:T(8,128)S(1)}, f32[64,256]{1,0:T(8,128)}, u32[]{:S(2)}) %copy-start.7) | copy-done | bytes 65560
  5.1 0.0 copy-start.8
  5.1 0.8 %copy-done.8 = f32[64,256]{1,0:T(8,128)S(1)} copy-done((f32[64,256]{1,0:T(8,128)S(1)}, f32[64,256]{1,0:T(8,128)}, u32[]{:S(2)}) %copy-start.8) | copy-done | bytes 65560
  6.0 0.0 copy-start.9
  6.0 0.8 %copy-done.9 = f32[64,256]{1,0:T(8,128)S(1)} copy-done((f32[64,256]{1,0:T(8,128)S(1)}, f32[64,256]{1,0:T(8,128)}, u32[]{:S(2)}) %copy-start.9) | copy-done | bytes 65560
  6.8 0.0 copy-start.1
  6.8 0.0 copy-start.4
  6.8 0.0 copy-start.6
  6.8 1.3 %pack.1 = (f32[64,256]{1,0:T(8,128)S(1)}, f32[176,256]{1,0:T(8,128)S(1)}, f32[176,256]{1,0:T(8,128)S(1)}) custom-call(f32[2,64,256]{2,1,0:T(8,128)S(1)} %copy-done.3, f32[3,64,256]{2,1,0:T(8,128)S(1)} %copy-done, f32[2,64,256]{2,1,0:T(8,128)S(1)} %copy-done.5, f32[3,64,256]{2,1,0:T(8,128)S(1)} %copy-done.2, f32[64,256]{1,0:T(8,128)S(1)} %copy-done.7, ...), custom_call_target="tpu_custom_call" | custom-call | tf_op jit(solution)/shard_map/pack/pallas_call | solution.py:426
  8.2 0.5 %collective-permute-start = (f32[64,256]{1,0:T(8,128)S(1)}, f32[64,256]{1,0:T(8,128)S(1)}, u32[]{:S(2)}, u32[]{:S(2)}) collective-permute-start(f32[64,256]{1,0:T(8,128)S(1)} %get-tuple-element.16), channel_id=1, source_target_pairs={{0,1},{1,0},{2,3},{3,2},{4,5},{5,4},{6,7},{7,6},{8,9},{9,8},{10,11... | collective-permute-start | bytes 196616 | tf_op jit(solution)/shard_map/ppermute | solution.py:436
  8.7 0.9 %collective-permute-done.refs_7_.got = f32[64,256]{1,0:T(8,128)S(1)} collective-permute-done((f32[64,256]{1,0:T(8,128)S(1)}, f32[64,256]{1,0:T(8,128)S(1)}, u32[]{:S(2)}, u32[]{:S(2)}) %collective-permute-start) | collective-permute-done | bytes 65568 | tf_op jit(solution)/shard_map/ppermute | solution.py:436
  9.6 0.0 copy-start.10
  9.6 0.0 copy-start.11
  9.6 0.0 copy-start.12
  9.6 0.1 corners.1
  9.7 2.9 %collective-permute-start.1 = (f32[176,256]{1,0:T(8,128)S(1)}, f32[176,256]{1,0:T(8,128)S(1)}, u32[]{:S(2)}, u32[]{:S(2)}) collective-permute-start(f32[176,256]{1,0:T(8,128)S(1)} %get-tuple-element.19), channel_id=1, source_target_pairs={{0,2},{2,0},{4,6},{6,4},{8,10},{10,8},{12,14},{14,12},{1,3},{3,1},... | collective-permute-start | bytes 540680 | tf_op jit(solution)/shard_map/ppermute | solution.py:449
  12.6 0.7 %collective-permute-start.2 = (f32[176,256]{1,0:T(8,128)S(1)}, f32[176,256]{1,0:T(8,128)S(1)}, u32[]{:S(2)}, u32[]{:S(2)}) collective-permute-start(f32[176,256]{1,0:T(8,128)S(1)} %get-tuple-element.20), channel_id=1, source_target_pairs={{2,4},{4,2},{6,8},{8,6},{10,12},{12,10},{3,5},{5,3},{7,9},{9,7},{1... | collective-permute-start | bytes 540680 | tf_op jit(solution)/shard_map/ppermute | solution.py:448
  13.2 0.0 copy-done.1
  13.3 0.0 copy-done.4
  13.3 0.0 copy-done.6
  13.3 1.8 %own_planes.1.own.refs_0_ = f32[13,3,64,128]{3,2,1,0:T(8,128)S(1)} custom-call(f32[2,64,256]{2,1,0:T(8,128)S(1)} %copy-done.4, f32[3,64,256]{2,1,0:T(8,128)S(1)} %copy-done.1, f32[2,64,256]{2,1,0:T(8,128)S(1)} %copy-done.6, f32[3,64,256]{2,1,0:T(8,128)S(1)} %copy-done.2, f32[64,256]{1,0:T(8,128)S(1)} %copy-done.7, f32[64,256]{1,0:T(8,128)S(1)} %copy-done.8, ...), custom_call_target="tpu_custom_call" | custom-call | tf_op jit(solution)/shard_map/own_planes/pallas_call | solution.py:451
  15.1 5.5 %collective-permute-done.1.got_even.refs_1_ = f32[176,256]{1,0:T(8,128)S(1)} collective-permute-done((f32[176,256]{1,0:T(8,128)S(1)}, f32[176,256]{1,0:T(8,128)S(1)}, u32[]{:S(2)}, u32[]{:S(2)}) %collective-permute-start.1) | collective-permute-done | bytes 180256 | tf_op jit(solution)/shard_map/ppermute | solution.py:449
  20.6 0.0 collective-permute-done.2.got_odd.refs_2_
  20.6 0.0 copy-done.10
  20.6 0.0 copy-done.11
  20.6 0.0 copy-done.12
  20.6 2.9 %forward.1 = (f32[4,3,96,128]{3,2,1,0:T(8,128)S(1)}, f32[4,3,3,64,128]{4,3,2,1,0:T(8,128)S(1)}, f32[2,64,256]{2,1,0:T(8,128)}, f32[16,24,128]{2,1,0:T(8,128)S(1)}) custom-call(f32[13,3,64,128]{3,2,1,0:T(8,128)S(1)} %own_planes.1.own.refs_0_, f32[176,256]{1,0:T(8,128)S(1)} %collective-permute-done.1.got_even.refs_1_, ...), custom_call_target="tpu_custom_call" | custom-call | tf_op jit(solution)/shard_map/forward/pallas_call | solution.py:462
  23.5 14.9 %all_to_all.5.refs_5_ = f32[16,24,128]{2,1,0:T(8,128)S(1)} all-to-all(f32[16,24,128]{2,1,0:T(8,128)S(1)} %get-tuple-element.23), channel_id=1, replica_groups=mesh['shots'=2,'track'=8,'depth'=2] {'track','depth'}, dimensions={0} | all-to-all | bytes 393216 | tf_op jit(solution)/shard_map/all_to_all | solution.py:477
  38.4 3.0 %adjoint.1 = (f32[64,256]{1,0:T(8,128)}, f32[64,256]{1,0:T(8,128)}, f32[2,256]{1,0:T(2,128)}) custom-call(f32[13,3,64,128]{3,2,1,0:T(8,128)S(1)} %own_planes.1.own.refs_0_, f32[176,256]{1,0:T(8,128)S(1)} %collective-permute-done.1.got_even.refs_1_, f32[176,256]{1,0:T(8,128)S(1)} %collective-permute-done.2.got_odd.refs_2_, ...), custom_call_target="tpu_custom_call" | custom-call | tf_op jit(solution)/shard_map/adjoint/pallas_call | solution.py:479
Async XLA Ops:
  0.6 0.9 %copy-start = (f32[3,64,256]{2,1,0:T(8,128)S(1)}, f32[3,64,256]{2,1,0:T(8,128)}, u32[]{:S(2)}) copy-start(f32[3,64,256]{2,1,0:T(8,128)} %refs_1_.3) | copy-start | bytes 589828
  1.6 0.9 %copy-start.2 = (f32[3,64,256]{2,1,0:T(8,128)S(1)}, f32[3,64,256]{2,1,0:T(8,128)}, u32[]{:S(2)}) copy-start(f32[3,64,256]{2,1,0:T(8,128)} %refs_3_.3) | copy-start | bytes 589828
  2.5 0.9 %copy-start.3 = (f32[2,64,256]{2,1,0:T(8,128)S(1)}, f32[2,64,256]{2,1,0:T(8,128)}, u32[]{:S(2)}) copy-start(f32[2,64,256]{2,1,0:T(8,128)} %refs_0_.3) | copy-start | bytes 393220
  3.4 0.9 %copy-start.5 = (f32[2,64,256]{2,1,0:T(8,128)S(1)}, f32[2,64,256]{2,1,0:T(8,128)}, u32[]{:S(2)}) copy-start(f32[2,64,256]{2,1,0:T(8,128)} %refs_2_.3) | copy-start | bytes 393220
  4.3 0.8 %copy-start.7 = (f32[64,256]{1,0:T(8,128)S(1)}, f32[64,256]{1,0:T(8,128)}, u32[]{:S(2)}) copy-start(f32[64,256]{1,0:T(8,128)} %refs_4_.3) | copy-start | bytes 196612
  5.1 0.8 %copy-start.8 = (f32[64,256]{1,0:T(8,128)S(1)}, f32[64,256]{1,0:T(8,128)}, u32[]{:S(2)}) copy-start(f32[64,256]{1,0:T(8,128)} %refs_5_.3) | copy-start | bytes 196612
  6.0 0.8 %copy-start.9 = (f32[64,256]{1,0:T(8,128)S(1)}, f32[64,256]{1,0:T(8,128)}, u32[]{:S(2)}) copy-start(f32[64,256]{1,0:T(8,128)} %refs_6_.4) | copy-start | bytes 196612
  6.8 6.4 %copy-start.1 = (f32[3,64,256]{2,1,0:T(8,128)S(1)}, f32[3,64,256]{2,1,0:T(8,128)}, u32[]{:S(2)}) copy-start(f32[3,64,256]{2,1,0:T(8,128)} %refs_1_.3) | copy-start | bytes 589828
  6.8 6.4 %copy-start.4 = (f32[2,64,256]{2,1,0:T(8,128)S(1)}, f32[2,64,256]{2,1,0:T(8,128)}, u32[]{:S(2)}) copy-start(f32[2,64,256]{2,1,0:T(8,128)} %refs_0_.3) | copy-start | bytes 393220
  6.8 6.4 %copy-start.6 = (f32[2,64,256]{2,1,0:T(8,128)S(1)}, f32[2,64,256]{2,1,0:T(8,128)}, u32[]{:S(2)}) copy-start(f32[2,64,256]{2,1,0:T(8,128)} %refs_2_.3) | copy-start | bytes 393220
  8.2 1.4 %collective-permute-start = (f32[64,256]{1,0:T(8,128)S(1)}, f32[64,256]{1,0:T(8,128)S(1)}, u32[]{:S(2)}, u32[]{:S(2)}) collective-permute-start(f32[64,256]{1,0:T(8,128)S(1)} %get-tuple-element.16), channel_id=1, source_target_pairs={{0,1},{1,0},{2,3},{3,2},{4,5},{5,4},{6,7},{7,6},{8,9},{9,8},{10,11... | collective-permute-start | bytes 196616 | tf_op jit(solution)/shard_map/ppermute | solution.py:436
  9.6 11.0 %copy-start.10 = (f32[4,256]{1,0:T(4,128)S(1)}, f32[4,256]{1,0:T(4,128)}, u32[]{:S(2)}) copy-start(f32[4,256]{1,0:T(4,128)} %refs_6_.5) | copy-start | bytes 12292
  9.6 11.0 %copy-start.11 = (s32[256,1]{0,1:T(1,128)S(1)}, s32[256,1]{0,1:T(1,128)}, u32[]{:S(2)}) copy-start(s32[256,1]{0,1:T(1,128)} %param.18) | copy-start | bytes 3076
  9.6 11.0 %copy-start.12 = (s32[256]{0:T(256)S(1)}, s32[256]{0:T(256)}, u32[]{:S(2)}) copy-start(s32[256]{0:T(256)} %param.19) | copy-start | bytes 3076
  9.7 10.9 %collective-permute-start.1 = (f32[176,256]{1,0:T(8,128)S(1)}, f32[176,256]{1,0:T(8,128)S(1)}, u32[]{:S(2)}, u32[]{:S(2)}) collective-permute-start(f32[176,256]{1,0:T(8,128)S(1)} %get-tuple-element.19), channel_id=1, source_target_pairs={{0,2},{2,0},{4,6},{6,4},{8,10},{10,8},{12,14},{14,12},{1,3},{3,1},... | collective-permute-start | bytes 540680 | tf_op jit(solution)/shard_map/ppermute | solution.py:449
  12.6 8.0 %collective-permute-start.2 = (f32[176,256]{1,0:T(8,128)S(1)}, f32[176,256]{1,0:T(8,128)S(1)}, u32[]{:S(2)}, u32[]{:S(2)}) collective-permute-start(f32[176,256]{1,0:T(8,128)S(1)} %get-tuple-element.20), channel_id=1, source_target_pairs={{2,4},{4,2},{6,8},{8,6},{10,12},{12,10},{3,5},{5,3},{7,9},{9,7},{1... | collective-permute-start | bytes 540680 | tf_op jit(solution)/shard_map/ppermute | solution.py:448

commit v3 on v2

--- a/solution.py
+++ b/solution.py
@@ -12,7 +12,9 @@
 EDGE = 16
 LANES = 128
 PAD = 8
-FIELDS = 13
+FORWARD = 8
+ADJOINT = 5
+FIELDS = FORWARD + ADJOINT
 MOMENTS = 4
 IMAGE = MOMENTS * FIBRE_ROWS
 NOTE = 24
@@ -33,6 +35,10 @@
     return pltpu.CompilerParams(vmem_limit_bytes=40 * 1024 * 1024)
 
 
+def cost(microseconds):
+    return pl.CostEstimate(flops=0, bytes_accessed=int(microseconds * 3.5e6), transcendentals=0)
+
+
 def turn(value, by):
     return pltpu.roll(value, by % LANES, 1)
 
@@ -52,22 +58,22 @@
     return (
         [velocity.at[i] for i in range(2)]
         + [stress.at[i] for i in range(3)]
+        + [buoyancy, lame, shear]
         + [adj_velocity.at[i] for i in range(2)]
         + [adj_stress.at[i] for i in range(3)]
-        + [buoyancy, lame, shear]
     )
 
 
 def pack_kernel(*refs):
-    sources, (depth_out, even_out, odd_out), held, sems = refs[:7], refs[7:10], refs[10:17], refs[17]
+    sources, depth_out, edge_outs, held, sems = refs[:7], refs[7], refs[8:12], refs[12:19], refs[19]
     copies = fetch(sources, held, sems)
     depth = lax.axis_index("depth")
     even = is_even()
     fields = field_refs(*held)
     rows = fields[0].shape[0]
     lane = lane_ids(rows)
-    tail = EDGE + HALO * FIELDS
-    for out in (even_out, odd_out):
+    for i, out in enumerate(edge_outs):
+        tail = EDGE + HALO * (FORWARD, ADJOINT)[i // 2]
         out[:EDGE, :] = jnp.zeros((EDGE, 2 * LANES), F32)
         out[tail:, :] = jnp.zeros((out.shape[0] - tail, 2 * LANES), F32)
     for copy in copies:
@@ -75,39 +81,40 @@
     packed = [jnp.zeros((rows, LANES), F32) for _ in range(2)]
     for f, ref in enumerate(fields):
         first, last = ref[:, :LANES], ref[:, LANES:]
-        spot = EDGE * (f % 8)
+        group, place = divmod(f, FORWARD)
+        spot = EDGE * place
         here = (lane >= spot) & (lane < spot + EDGE)
         edge = jnp.where(depth == 0, last, first)
         shift = lax.rem(spot + EDGE * (1 - depth), LANES)
-        packed[f // 8] = jnp.where(here, pltpu.roll(edge, shift, 1), packed[f // 8])
+        packed[group] = jnp.where(here, pltpu.roll(edge, shift, 1), packed[group])
         low, high = ref[:HALO, :], ref[rows - HALO :, :]
-        at = EDGE + HALO * f
-        even_out[at : at + HALO, :] = jnp.where(even, high, low)
-        odd_out[at : at + HALO, :] = jnp.where(even, low, high)
+        at = EDGE + HALO * place
+        edge_outs[2 * group][at : at + HALO, :] = jnp.where(even, high, low)
+        edge_outs[2 * group + 1][at : at + HALO, :] = jnp.where(even, low, high)
     depth_out[:, :LANES] = packed[0]
     depth_out[:, LANES:] = packed[1]
 
 
-def corner_kernel(got, even_in, odd_in, even_out, odd_out, sems):
+def corner_kernel(got, *refs):
+    outs, sems = refs[4:8], refs[8]
     rows = got.shape[0]
     is_odd = lax.rem(lax.axis_index("track"), 2)
     high, low = (rows - EDGE) * (1 - is_odd), (rows - EDGE) * is_odd
-    one = pltpu.make_async_copy(
-        got.at[pl.ds(pl.multiple_of(high, EDGE), EDGE), :], even_out.at[pl.ds(0, EDGE), :], sems.at[0]
-    )
-    two = pltpu.make_async_copy(
-        got.at[pl.ds(pl.multiple_of(low, EDGE), EDGE), :], odd_out.at[pl.ds(0, EDGE), :], sems.at[1]
-    )
-    one.start()
-    two.start()
-    one.wait()
-    two.wait()
+    copies = []
+    for i, out in enumerate(outs):
+        row = pl.multiple_of(low if i % 2 else high, EDGE)
+        source = got.at[pl.ds(row, EDGE), pl.ds(LANES * (i // 2), LANES)]
+        copies.append(pltpu.make_async_copy(source, out.at[pl.ds(0, EDGE), pl.ds(0, LANES)], sems.at[i]))
+    for copy in copies:
+        copy.start()
+    for copy in copies:
+        copy.wait()
 
 
 def windows(f, first, last, halo):
     depth = lax.axis_index("depth")
     lane = lane_ids(first.shape[0])
-    shift = lax.rem(LANES - EDGE * (f % 8) + (LANES - EDGE) * (1 - depth), LANES)
+    shift = lax.rem(LANES - EDGE * (f % FORWARD) + (LANES - EDGE) * (1 - depth), LANES)
     beside = pltpu.roll(halo, shift, 1)
     return [
         jnp.where(lane >= EDGE, turn(first, EDGE), jnp.where(depth == 1, beside, 0.0)),
@@ -130,7 +137,7 @@
     for copy in fetch(sources, held, sems):
         copy.wait()
     for f, ref in enumerate(field_refs(*held)):
-        col = LANES * (f // 8)
+        col = LANES * (f // FORWARD)
         planes = windows(f, ref[:, :LANES], ref[:, LANES:], got_depth[:, col : col + LANES])
         for p in range(3):
             planes_out[f, p] = planes[p]
@@ -138,10 +145,9 @@
 
 def halo_windows(f, got_even, got_odd):
     even = is_even()
-    col = LANES * (f // 8)
-    high = EDGE + HALO * f
+    high = EDGE + HALO * (f % FORWARD)
     low = high - (EDGE - HALO)
-    corner_even, corner_odd = got_even[:EDGE, col : col + LANES], got_odd[:EDGE, col : col + LANES]
+    corner_even, corner_odd = got_even[:EDGE, :LANES], got_odd[:EDGE, :LANES]
     left = jnp.where(even, got_odd[low : low + EDGE, :], got_even[low : low + EDGE, :])
     right = jnp.where(even, got_even[high : high + EDGE, :], got_odd[high : high + EDGE, :])
     left_halo = jnp.where(even, corner_odd, corner_even)
@@ -211,14 +217,10 @@
     return inner, inner if step < MOMENTS - 1 else (EDGE // 8, tiles - EDGE // 8)
 
 
-def forward_kernel(
-    own, got_even, got_odd, obs, owner, cell, media, saved, end_out, note_out, state, small, numbers, sems
-):
-    copies = fetch((obs, owner, cell), (small, numbers.at[0], numbers.at[1]), sems)
+def forward_kernel(own, got_even, got_odd, media, saved, end_out, image_out, state):
     rows = own.shape[2]
-    extent = rows + 2 * EDGE
     parts = []
-    for f in (10, 11, 12):
+    for f in (5, 6, 7):
         below, above = halo_windows(f, got_even, got_odd)
         parts.append([(below[p], own[f, p], above[p]) for p in range(3)])
     for p in range(3):
@@ -255,14 +257,20 @@
         here = (lane >= spot) & (lane < spot + FIBRE_ROWS)
         image = jnp.where(here, NEAR * turn(saved[step, 0, 0], spot - EDGE), image)
     turned = image.T
+    half = IMAGE // 2
+    image_out[...] = jnp.concatenate([turned[:half], turned[half:IMAGE]], axis=1)
+
+
+def note_kernel(rows, adj_even, adj_odd, image, image_beside, obs, owner, cell, note_out, small, numbers, sems):
+    copies = fetch((obs, owner, cell), (small, numbers.at[0], numbers.at[1]), sems)
+    depth = lax.axis_index("depth")
     for copy in copies:
         copy.wait()
     along = numbers[0] * rows + lax.shift_right_logical(numbers[1], 2)
     row = numbers[1] & 3
-    half = IMAGE // 2
     block = jnp.concatenate(
         [
-            jnp.concatenate([turned[:half], turned[half:IMAGE]], axis=1),
+            jnp.where(depth == 0, image[...], image_beside[...]),
             jnp.concatenate([small[:, :LANES], small[:, LANES:]], axis=0),
             along[:, :LANES].astype(F32),
             along[:, LANES:].astype(F32),
@@ -301,7 +309,7 @@
         base = number * group
         firsts, lasts = [], []
         for k in range(0, group, 2):
-            a, b = notes[2 * (base + k), :8, :], notes[2 * (base + k + 1), :8, :]
+            a, b = notes[base + k, :8, :], notes[base + k + 1, :8, :]
             firsts.append(jnp.where(lane < half, a, turn(b, half)))
             lasts.append(jnp.where(lane < half, turn(a, half), b))
         strains = jnp.concatenate([jnp.concatenate(firsts, axis=1), jnp.concatenate(lasts, axis=1)], axis=0)
@@ -310,7 +318,7 @@
         rate = rate + jnp.dot(jnp.concatenate(three(strains), axis=0), hot, preferred_element_type=F32)
         weights, hots = [], []
         for k in range(group):
-            who = 2 * (base + k)
+            who = base + k
             for h in range(2):
                 along = notes[who, 16 + h : 17 + h, :]
                 mask = (row16 & 3).astype(F32) == notes[who, 18 + h : 19 + h, :]
@@ -349,7 +357,7 @@
     rows = own.shape[2]
     extent = rows + 2 * EDGE
     depth = lax.axis_index("depth")
-    load_state(state, own, got_even, got_odd, 5)
+    load_state(state, own, got_even, got_odd, FORWARD)
     sums[...] = jnp.zeros(sums.shape, F32)
     for copy in copies:
         copy.wait()
@@ -407,12 +415,15 @@
     moments, channels = observed.shape
     owner = owner_track.reshape(1, channels)
     cell = fibre_cell.reshape(1, channels)
+    pinned = lambda array: pltpu.with_memory_space_constraint(array, pltpu.HBM)
     arrays = (velocity, stress, adjoint_velocity, adjoint_stress, buoyancy, lame_lambda, shear_modulus)
-    length = EDGE + HALO * FIELDS
-    length = length + (-length) % 8
+    arrays = tuple(pinned(array) for array in arrays)
+    channel_arrays = (pinned(observed), pinned(owner), pinned(cell))
     extent = rows + 2 * EDGE
     block = jax.ShapeDtypeStruct((rows, depth_cells), F32)
-    edges = jax.ShapeDtypeStruct((length, depth_cells), F32)
+    lengths = [EDGE + HALO * count + EDGE - HALO for count in (FORWARD, ADJOINT)]
+    edges = [jax.ShapeDtypeStruct((length + (-length) % 8, depth_cells), F32) for length in lengths]
+    edges = (edges[0], edges[0], edges[1], edges[1])
     inside = pl.BlockSpec(memory_space=VMEM)
     outside = pl.BlockSpec(memory_space=pltpu.HBM)
     anywhere = pl.BlockSpec(memory_space=pl.ANY)
@@ -423,30 +434,34 @@
         pltpu.SemaphoreType.DMA((3,)),
     ]
 
-    to_depth, to_even, to_odd = pl.pallas_call(
+    to_depth, *to_track = pl.pallas_call(
         pack_kernel,
-        out_shape=(block, edges, edges),
+        out_shape=(block,) + edges,
         in_specs=[outside] * 7,
-        out_specs=(inside,) * 3,
+        out_specs=(inside,) * 5,
         scratch_shapes=held + [pltpu.SemaphoreType.DMA((7,))],
         compiler_params=params(),
+        cost_estimate=cost(2),
         name="pack",
     )(*arrays)
 
-    got_depth = lax.ppermute(to_depth, "depth", [(0, 1), (1, 0)])
-    to_even, to_odd = pl.pallas_call(
+    depth_swap = [(0, 1), (1, 0)]
+    got_depth = lax.ppermute(to_depth, "depth", depth_swap)
+    to_track = pl.pallas_call(
         corner_kernel,
-        out_shape=(edges, edges),
-        in_specs=[anywhere] * 3,
-        out_specs=(anywhere,) * 2,
-        input_output_aliases={1: 0, 2: 1},
-        scratch_shapes=[pltpu.SemaphoreType.DMA((2,))],
+        out_shape=edges,
+        in_specs=[anywhere] * 5,
+        out_specs=(anywhere,) * 4,
+        input_output_aliases={1: 0, 2: 1, 3: 2, 4: 3},
+        scratch_shapes=[pltpu.SemaphoreType.DMA((4,))],
         compiler_params=params(),
         name="corners",
-    )(got_depth, to_even, to_odd)
+    )(got_depth, *to_track)
     swap = lambda k: [pair for i in range(k, tracks - 1, 2) for pair in ((i, i + 1), (i + 1, i))]
-    got_odd = lax.ppermute(to_odd, "track", swap(1))
-    got_even = lax.ppermute(to_even, "track", swap(0))
+    fwd_odd = lax.ppermute(to_track[1], "track", swap(1))
+    fwd_even = lax.ppermute(to_track[0], "track", swap(0))
+    adj_odd = lax.ppermute(to_track[3], "track", swap(1))
+    adj_even = lax.ppermute(to_track[2], "track", swap(0))
 
     own = pl.pallas_call(
         own_kernel,
@@ -455,26 +470,38 @@
         out_specs=inside,
         scratch_shapes=held + [pltpu.SemaphoreType.DMA((7,))],
         compiler_params=params(),
+        cost_estimate=cost(2),
         name="own_planes",
     )(*arrays, got_depth)
 
-    devices = tracks * lax.axis_size("depth")
-    media, saved, velocity_end, note = pl.pallas_call(
+    media, saved, velocity_end, image = pl.pallas_call(
         forward_kernel,
         out_shape=(
             jax.ShapeDtypeStruct((4, 3, extent, LANES), F32),
             jax.ShapeDtypeStruct((moments, 3, 3, rows, LANES), F32),
             jax.ShapeDtypeStruct(velocity.shape, F32),
-            jax.ShapeDtypeStruct((devices, NOTE, LANES), F32),
+            jax.ShapeDtypeStruct((IMAGE // 2, LANES), F32),
         ),
-        in_specs=[inside] * 3 + [outside] * 3,
+        in_specs=[inside] * 3,
         out_specs=(inside,) * 4,
-        scratch_shapes=[VMEM((5, 3, extent + 2 * PAD, LANES), F32)] + channel_scratch,
+        scratch_shapes=[VMEM((5, 3, extent + 2 * PAD, LANES), F32)],
         compiler_params=params(),
+        cost_estimate=cost(3),
         name="forward",
-    )(own, got_even, got_odd, observed, owner, cell)
-
-    notes = lax.all_to_all(note, ("track", "depth"), split_axis=0, concat_axis=0, tiled=True)
+    )(own, fwd_even, fwd_odd)
+
+    image_beside = lax.ppermute(image, "depth", depth_swap)
+    note = pl.pallas_call(
+        lambda *refs: note_kernel(rows, *refs),
+        out_shape=jax.ShapeDtypeStruct((tracks, NOTE, LANES), F32),
+        in_specs=[anywhere] * 2 + [inside] * 2 + [outside] * 3,
+        out_specs=inside,
+        scratch_shapes=channel_scratch,
+        compiler_params=params(),
+        cost_estimate=cost(1),
+        name="note",
+    )(adj_even, adj_odd, image, image_beside, *channel_arrays)
+    notes = lax.all_to_all(note, "track", split_axis=0, concat_axis=0, tiled=True)
 
     gradient_lambda, gradient_mu, residual = pl.pallas_call(
         lambda *refs: adjoint_kernel(tracks, *refs),
@@ -487,8 +514,9 @@
         ]
         + channel_scratch,
         compiler_params=params(),
+        cost_estimate=cost(4),
         name="adjoint",
-    )(own, got_even, got_odd, media, saved, notes, observed, owner, cell)
+    )(own, adj_even, adj_odd, media, saved, notes, *channel_arrays)
     return gradient_lambda, gradient_mu, velocity_end, residual
 
 

time: 41.8 us -> 36.1 us (0.86)
  local copies, waits for them, and re-layouts: 6.19 us -> 0 us
  starting transfers between devices: 4.09 us -> 9.08 us
  waiting for transfers between devices: 6.4 us -> 2.07 us
  blocking collectives: 14.9 us -> 13.5 us
  Pallas kernels: 9.12 us -> 10.5 us
    unnamed x26 -> x0, local copies, waits for them, and re-layouts: 6.19 us -> none
    ppermute x3 -> x6, starting transfers between devices: 4.09 us -> 9.08 us  [the longest x1 4.34 us: per_device(): adj_even = lax.ppermute(to_track[2], 'track', swap(0))]
    ppermute x3 -> x6, waiting for transfers between devices: 6.4 us -> 2.07 us  [the longest x1 1.15 us: per_device(): image_beside = lax.ppermute(image, 'depth', depth_swap)]
    all_to_all x1, blocking collectives: 14.9 us -> 13.5 us  [per_device(): lax.all_to_all(note, 'track', split_axis=0, concat_axis=0, tiled=True)]
    pallas_call x2 -> x3, Pallas kernels: 1.4 us -> 2.23 us  [the longest x1 1.44 us: per_device(): pl.pallas_call(pack_kernel, out_shape=(block,) + edges, in_specs=[outside...]
    pallas_call x1, Pallas kernels: 2.99 us -> 3.54 us  [per_device(): pl.pallas_call(lambda *refs: adjoint_kernel(tracks, *refs), out_shape=(bl...]
  transfers between devices with their start and end apart: 3 -> 6, of which waited for: 2 -> 2; matrix products, arithmetic and copies ran while one was open for 0% -> 0% of each run, Pallas kernels for 4% -> 13%
where the time goes in v3:
time: 36.1 us; the launch traced here: 35.9 us
  blocking collectives  13.5 us (37%)
  Pallas kernels  10.5 us (29%)
  starting transfers between devices  9.08 us (25%)
  waiting for transfers between devices  2.07 us (6%)
  between operations  0.7 us (2%)
    all_to_all x1, blocking collectives, per_device(): lax.all_to_all(note, 'track', split_axis=0, concat_axis=0, tiled=True)  13.5 us
    ppermute x1, starting transfers between devices, per_device(): adj_even = lax.ppermute(to_track[2], 'track', swap(0))  4.34 us
    pallas_call x1, Pallas kernels, per_device(): pl.pallas_call(lambda *refs: adjoint_kernel(tracks, *refs), out_shape=(bl...  3.54 us
    ppermute x1, starting transfers between devices, per_device(): fwd_even = lax.ppermute(to_track[0], 'track', swap(0))  2.9 us
    pallas_call x1, Pallas kernels, per_device(): pl.pallas_call(forward_kernel, out_shape=(jax.ShapeDtypeStruct((4, 3, ext...  2.88 us
    pallas_call x1, Pallas kernels, per_device(): pl.pallas_call(own_kernel, out_shape=jax.ShapeDtypeStruct((FIELDS, 3, row...  1.88 us
    pallas_call x1, Pallas kernels, per_device(): pl.pallas_call(pack_kernel, out_shape=(block,) + edges, in_specs=[outside...  1.44 us
    ppermute x1, waiting for transfers between devices, per_device(): image_beside = lax.ppermute(image, 'depth', depth_swap)  1.15 us
  transfers between devices with their start and end apart: 6, of which 2 were waited for; matrix products, arithmetic and copies ran while one was open for 0% of the time, Pallas kernels for 13%

profile of v3, /device:TPU:0, one launch (start us, length us, event | category | flops | bytes accessed | tf_op | source)
XLA Modules:
  0.0 35.9 jit_solution(15475215802750992810)
XLA Ops:
  0.6 1.4 %pack.1 = (f32[64,256]{1,0:T(8,128)S(1)}, f32[120,256]{1,0:T(8,128)S(1)}, f32[120,256]{1,0:T(8,128)S(1)}, f32[80,256]{1,0:T(8,128)S(1)}, f32[80,256]{1,0:T(8,128)S(1)}) custom-call(f32[2,64,256]{2,1,0:T(8,128)} %refs_0_.3, f32[3,64,256]{2,1,0:T(8,128)} %refs_1_.3, f32[2,64,256]{2,1,0:T(8,128)} %refs_2_.3, f32[3,64,256]{2,1,0:T(8,128)} %refs_3_.3, ...), custom_call_target="tpu_custom_call" | custom-call | bytes 7000000 | tf_op jit(solution)/shard_map/pack/pallas_call | solution.py:437
  2.1 0.5 %collective-permute-start = (f32[64,256]{1,0:T(8,128)S(1)}, f32[64,256]{1,0:T(8,128)S(1)}, u32[]{:S(2)}, u32[]{:S(2)}) collective-permute-start(f32[64,256]{1,0:T(8,128)S(1)} %get-tuple-element.20), channel_id=1, source_target_pairs={{0,1},{1,0},{2,3},{3,2},{4,5},{5,4},{6,7},{7,6},{8,9},{9,8},{10,11... | collective-permute-start | bytes 196616 | tf_op jit(solution)/shard_map/ppermute | solution.py:449
  2.6 0.9 %collective-permute-done.refs_7_.got = f32[64,256]{1,0:T(8,128)S(1)} collective-permute-done((f32[64,256]{1,0:T(8,128)S(1)}, f32[64,256]{1,0:T(8,128)S(1)}, u32[]{:S(2)}, u32[]{:S(2)}) %collective-permute-start) | collective-permute-done | bytes 65568 | tf_op jit(solution)/shard_map/ppermute | solution.py:449
  3.6 2.9 %collective-permute-start.3 = (f32[120,256]{1,0:T(8,128)S(1)}, f32[120,256]{1,0:T(8,128)S(1)}, u32[]{:S(2)}, u32[]{:S(2)}) collective-permute-start(f32[120,256]{1,0:T(8,128)S(1)} %get-tuple-element.27), channel_id=1, source_target_pairs={{0,2},{2,0},{4,6},{6,4},{8,10},{10,8},{12,14},{14,12},{1,3},{3,1},... | collective-permute-start | bytes 368648 | tf_op jit(solution)/shard_map/ppermute | solution.py:462
  6.5 0.7 %collective-permute-start.4 = (f32[120,256]{1,0:T(8,128)S(1)}, f32[120,256]{1,0:T(8,128)S(1)}, u32[]{:S(2)}, u32[]{:S(2)}) collective-permute-start(f32[120,256]{1,0:T(8,128)S(1)} %get-tuple-element.28), channel_id=1, source_target_pairs={{2,4},{4,2},{6,8},{8,6},{10,12},{12,10},{3,5},{5,3},{7,9},{9,7},{1... | collective-permute-start | bytes 368648 | tf_op jit(solution)/shard_map/ppermute | solution.py:461
  7.1 4.3 %collective-permute-start.1 = (f32[80,256]{1,0:T(8,128)S(1)}, f32[80,256]{1,0:T(8,128)S(1)}, u32[]{:S(2)}, u32[]{:S(2)}) collective-permute-start(f32[80,256]{1,0:T(8,128)S(1)} %get-tuple-element.25), channel_id=1, source_target_pairs={{0,2},{2,0},{4,6},{6,4},{8,10},{10,8},{12,14},{14,12},{1,3},{3,1},... | collective-permute-start | bytes 245768 | tf_op jit(solution)/shard_map/ppermute | solution.py:464
  11.5 0.7 %collective-permute-start.2 = (f32[80,256]{1,0:T(8,128)S(1)}, f32[80,256]{1,0:T(8,128)S(1)}, u32[]{:S(2)}, u32[]{:S(2)}) collective-permute-start(f32[80,256]{1,0:T(8,128)S(1)} %get-tuple-element.26), channel_id=1, source_target_pairs={{2,4},{4,2},{6,8},{8,6},{10,12},{12,10},{3,5},{5,3},{7,9},{9,7},{1... | collective-permute-start | bytes 245768 | tf_op jit(solution)/shard_map/ppermute | solution.py:463
  12.1 1.9 %own_planes.1.own.refs_0_ = f32[13,3,64,128]{3,2,1,0:T(8,128)S(1)} custom-call(f32[2,64,256]{2,1,0:T(8,128)} %refs_0_.3, f32[3,64,256]{2,1,0:T(8,128)} %refs_1_.3, f32[2,64,256]{2,1,0:T(8,128)} %refs_2_.3, f32[3,64,256]{2,1,0:T(8,128)} %refs_3_.3, f32[64,256]{1,0:T(8,128)} %refs_4_.4, f32[64,256]{1,0:T(8,128)} %refs_5_.3, f32[64,256]{1,0:T(8,128)} %refs_6_.4, ...), custom_call_target="tpu_custom_call" | custom-call | bytes 7000000 | tf_op jit(solution)/shard_map/own_planes/pallas_call | solution.py:466
  14.0 0.0 collective-permute-done.3.got_even
  14.0 0.0 collective-permute-done.4.got_odd
  14.0 2.9 %forward.1 = (f32[4,3,96,128]{3,2,1,0:T(8,128)S(1)}, f32[4,3,3,64,128]{4,3,2,1,0:T(8,128)S(1)}, f32[2,64,256]{2,1,0:T(8,128)}, f32[8,128]{1,0:T(8,128)S(1)}) custom-call(f32[13,3,64,128]{3,2,1,0:T(8,128)S(1)} %own_planes.1.own.refs_0_, f32[120,256]{1,0:T(8,128)S(1)} %collective-permute-done.3.got_even, f32[120,256]{1,0:T(8,128)S(1)} %collective-permute-done.4.got_odd), custom_call_target="tpu_custom_call" | custom-call | bytes 10500000 | tf_op jit(solution)/shard_map/forward/pallas_call | solution.py:477
  16.9 0.0 collective-permute-start.5
  16.9 0.0 collective-permute-done.1.refs_0_.refs_1_
  16.9 0.0 collective-permute-done.2.refs_1_.refs_2_
  16.9 1.2 %collective-permute-done.5.refs_3_ = f32[8,128]{1,0:T(8,128)S(1)} collective-permute-done((f32[8,128]{1,0:T(8,128)S(1)}, f32[8,128]{1,0:T(8,128)S(1)}, u32[]{:S(2)}, u32[]{:S(2)}) %collective-permute-start.5) | collective-permute-done | bytes 4128 | tf_op jit(solution)/shard_map/ppermute | solution.py:493
  18.1 0.7 %note.1 = f32[8,24,128]{2,1,0:T(8,128)S(1)} custom-call(f32[80,256]{1,0:T(8,128)S(1)} %collective-permute-done.1.refs_0_.refs_1_, f32[80,256]{1,0:T(8,128)S(1)} %collective-permute-done.2.refs_1_.refs_2_, f32[8,128]{1,0:T(8,128)S(1)} %get-tuple-element.31.refs_2_, f32[8,128]{1,0:T(8,128)S(1)} %collective-permute-done.5.refs_3_, f32[4,256]{1,0:T(4,128)} %refs_6_.5, ...), custom_call_target="tpu_custom_call" | custom-call | bytes 3500000 | tf_op jit(solution)/shard_map/note/pallas_call | solution.py:494
  18.8 13.5 %all_to_all.5.refs_5_ = f32[8,24,128]{2,1,0:T(8,128)S(1)} all-to-all(f32[8,24,128]{2,1,0:T(8,128)S(1)} %note.1), channel_id=1, replica_groups=mesh['shots'=2,'track'=8,'depth'=2] {'track'}, dimensions={0} | all-to-all | bytes 196608 | tf_op jit(solution)/shard_map/all_to_all | solution.py:504
  32.3 3.5 %adjoint.1 = (f32[64,256]{1,0:T(8,128)}, f32[64,256]{1,0:T(8,128)}, f32[2,256]{1,0:T(2,128)}) custom-call(f32[13,3,64,128]{3,2,1,0:T(8,128)S(1)} %own_planes.1.own.refs_0_, f32[80,256]{1,0:T(8,128)S(1)} %collective-permute-done.1.refs_0_.refs_1_, f32[80,256]{1,0:T(8,128)S(1)} %collective-permute-done.2.refs_1_.refs_2_, ...), custom_call_target="tpu_custom_call" | custom-call | bytes 14000000 | tf_op jit(solution)/shard_map/adjoint/pallas_call | solution.py:506
  (1 shorter events, 0.0 us)
Async XLA Ops:
  2.1 1.4 %collective-permute-start = (f32[64,256]{1,0:T(8,128)S(1)}, f32[64,256]{1,0:T(8,128)S(1)}, u32[]{:S(2)}, u32[]{:S(2)}) collective-permute-start(f32[64,256]{1,0:T(8,128)S(1)} %get-tuple-element.20), channel_id=1, source_target_pairs={{0,1},{1,0},{2,3},{3,2},{4,5},{5,4},{6,7},{7,6},{8,9},{9,8},{10,11... | collective-permute-start | bytes 196616 | tf_op jit(solution)/shard_map/ppermute | solution.py:449
  3.6 10.5 %collective-permute-start.3 = (f32[120,256]{1,0:T(8,128)S(1)}, f32[120,256]{1,0:T(8,128)S(1)}, u32[]{:S(2)}, u32[]{:S(2)}) collective-permute-start(f32[120,256]{1,0:T(8,128)S(1)} %get-tuple-element.27), channel_id=1, source_target_pairs={{0,2},{2,0},{4,6},{6,4},{8,10},{10,8},{12,14},{14,12},{1,3},{3,1},... | collective-permute-start | bytes 368648 | tf_op jit(solution)/shard_map/ppermute | solution.py:462
  6.5 7.6 %collective-permute-start.4 = (f32[120,256]{1,0:T(8,128)S(1)}, f32[120,256]{1,0:T(8,128)S(1)}, u32[]{:S(2)}, u32[]{:S(2)}) collective-permute-start(f32[120,256]{1,0:T(8,128)S(1)} %get-tuple-element.28), channel_id=1, source_target_pairs={{2,4},{4,2},{6,8},{8,6},{10,12},{12,10},{3,5},{5,3},{7,9},{9,7},{1... | collective-permute-start | bytes 368648 | tf_op jit(solution)/shard_map/ppermute | solution.py:461
  7.1 9.8 %collective-permute-start.1 = (f32[80,256]{1,0:T(8,128)S(1)}, f32[80,256]{1,0:T(8,128)S(1)}, u32[]{:S(2)}, u32[]{:S(2)}) collective-permute-start(f32[80,256]{1,0:T(8,128)S(1)} %get-tuple-element.25), channel_id=1, source_target_pairs={{0,2},{2,0},{4,6},{6,4},{8,10},{10,8},{12,14},{14,12},{1,3},{3,1},... | collective-permute-start | bytes 245768 | tf_op jit(solution)/shard_map/ppermute | solution.py:464
  11.5 5.5 %collective-permute-start.2 = (f32[80,256]{1,0:T(8,128)S(1)}, f32[80,256]{1,0:T(8,128)S(1)}, u32[]{:S(2)}, u32[]{:S(2)}) collective-permute-start(f32[80,256]{1,0:T(8,128)S(1)} %get-tuple-element.26), channel_id=1, source_target_pairs={{2,4},{4,2},{6,8},{8,6},{10,12},{12,10},{3,5},{5,3},{7,9},{9,7},{1... | collective-permute-start | bytes 245768 | tf_op jit(solution)/shard_map/ppermute | solution.py:463
  16.9 1.2 %collective-permute-start.5 = (f32[8,128]{1,0:T(8,128)S(1)}, f32[8,128]{1,0:T(8,128)S(1)}, u32[]{:S(2)}, u32[]{:S(2)}) collective-permute-start(f32[8,128]{1,0:T(8,128)S(1)} %get-tuple-element.31.refs_2_), channel_id=1, source_target_pairs={{0,1},{1,0},{2,3},{3,2},{4,5},{5,4},{6,7},{7,6},{8,9},{9,8},{10,11... | collective-permute-start | bytes 12296 | tf_op jit(solution)/shard_map/ppermute | solution.py:493

commit v4 on v2

--- a/solution.py
+++ b/solution.py
@@ -12,10 +12,12 @@
 EDGE = 16
 LANES = 128
 PAD = 8
-FIELDS = 13
+FORWARD = 8
+ADJOINT = 5
+FIELDS = FORWARD + ADJOINT
 MOMENTS = 4
 IMAGE = MOMENTS * FIBRE_ROWS
-NOTE = 24
+NOTE = 16
 VMEM = pltpu.VMEM
 F32 = jnp.float32
 BF16 = jnp.bfloat16
@@ -31,6 +33,10 @@
 
 def params():
     return pltpu.CompilerParams(vmem_limit_bytes=40 * 1024 * 1024)
+
+
+def cost(microseconds):
+    return pl.CostEstimate(flops=0, bytes_accessed=int(microseconds * 3.5e6), transcendentals=0)
 
 
 def turn(value, by):
@@ -52,14 +58,14 @@
     return (
         [velocity.at[i] for i in range(2)]
         + [stress.at[i] for i in range(3)]
+        + [buoyancy, lame, shear]
         + [adj_velocity.at[i] for i in range(2)]
         + [adj_stress.at[i] for i in range(3)]
-        + [buoyancy, lame, shear]
     )
 
 
 def pack_kernel(*refs):
-    sources, (depth_out, even_out, odd_out), held, sems = refs[:7], refs[7:10], refs[10:17], refs[17]
+    sources, depth_out, edge_outs, held, sems = refs[:7], refs[7], refs[8:10], refs[10:17], refs[17]
     copies = fetch(sources, held, sems)
     depth = lax.axis_index("depth")
     even = is_even()
@@ -67,7 +73,7 @@
     rows = fields[0].shape[0]
     lane = lane_ids(rows)
     tail = EDGE + HALO * FIELDS
-    for out in (even_out, odd_out):
+    for out in edge_outs:
         out[:EDGE, :] = jnp.zeros((EDGE, 2 * LANES), F32)
         out[tail:, :] = jnp.zeros((out.shape[0] - tail, 2 * LANES), F32)
     for copy in copies:
@@ -75,15 +81,16 @@
     packed = [jnp.zeros((rows, LANES), F32) for _ in range(2)]
     for f, ref in enumerate(fields):
         first, last = ref[:, :LANES], ref[:, LANES:]
-        spot = EDGE * (f % 8)
+        group, place = divmod(f, FORWARD)
+        spot = EDGE * place
         here = (lane >= spot) & (lane < spot + EDGE)
         edge = jnp.where(depth == 0, last, first)
         shift = lax.rem(spot + EDGE * (1 - depth), LANES)
-        packed[f // 8] = jnp.where(here, pltpu.roll(edge, shift, 1), packed[f // 8])
+        packed[group] = jnp.where(here, pltpu.roll(edge, shift, 1), packed[group])
         low, high = ref[:HALO, :], ref[rows - HALO :, :]
         at = EDGE + HALO * f
-        even_out[at : at + HALO, :] = jnp.where(even, high, low)
-        odd_out[at : at + HALO, :] = jnp.where(even, low, high)
+        edge_outs[0][at : at + HALO, :] = jnp.where(even, high, low)
+        edge_outs[1][at : at + HALO, :] = jnp.where(even, low, high)
     depth_out[:, :LANES] = packed[0]
     depth_out[:, LANES:] = packed[1]
 
@@ -107,7 +114,7 @@
 def windows(f, first, last, halo):
     depth = lax.axis_index("depth")
     lane = lane_ids(first.shape[0])
-    shift = lax.rem(LANES - EDGE * (f % 8) + (LANES - EDGE) * (1 - depth), LANES)
+    shift = lax.rem(LANES - EDGE * (f % FORWARD) + (LANES - EDGE) * (1 - depth), LANES)
     beside = pltpu.roll(halo, shift, 1)
     return [
         jnp.where(lane >= EDGE, turn(first, EDGE), jnp.where(depth == 1, beside, 0.0)),
@@ -130,7 +137,7 @@
     for copy in fetch(sources, held, sems):
         copy.wait()
     for f, ref in enumerate(field_refs(*held)):
-        col = LANES * (f // 8)
+        col = LANES * (f // FORWARD)
         planes = windows(f, ref[:, :LANES], ref[:, LANES:], got_depth[:, col : col + LANES])
         for p in range(3):
             planes_out[f, p] = planes[p]
@@ -138,9 +145,9 @@
 
 def halo_windows(f, got_even, got_odd):
     even = is_even()
-    col = LANES * (f // 8)
     high = EDGE + HALO * f
     low = high - (EDGE - HALO)
+    col = LANES * (f // FORWARD)
     corner_even, corner_odd = got_even[:EDGE, col : col + LANES], got_odd[:EDGE, col : col + LANES]
     left = jnp.where(even, got_odd[low : low + EDGE, :], got_even[low : low + EDGE, :])
     right = jnp.where(even, got_even[high : high + EDGE, :], got_odd[high : high + EDGE, :])
@@ -216,9 +223,8 @@
 ):
     copies = fetch((obs, owner, cell), (small, numbers.at[0], numbers.at[1]), sems)
     rows = own.shape[2]
-    extent = rows + 2 * EDGE
     parts = []
-    for f in (10, 11, 12):
+    for f in (5, 6, 7):
         below, above = halo_windows(f, got_even, got_odd)
         parts.append([(below[p], own[f, p], above[p]) for p in range(3)])
     for p in range(3):
@@ -255,24 +261,20 @@
         here = (lane >= spot) & (lane < spot + FIBRE_ROWS)
         image = jnp.where(here, NEAR * turn(saved[step, 0, 0], spot - EDGE), image)
     turned = image.T
+    half = IMAGE // 2
+    rates = jnp.concatenate([turned[:half], turned[half:IMAGE]], axis=1)
     for copy in copies:
         copy.wait()
-    along = numbers[0] * rows + lax.shift_right_logical(numbers[1], 2)
-    row = numbers[1] & 3
-    half = IMAGE // 2
-    block = jnp.concatenate(
-        [
-            jnp.concatenate([turned[:half], turned[half:IMAGE]], axis=1),
-            jnp.concatenate([small[:, :LANES], small[:, LANES:]], axis=0),
-            along[:, :LANES].astype(F32),
-            along[:, LANES:].astype(F32),
-            row[:, :LANES].astype(F32),
-            row[:, LANES:].astype(F32),
-            jnp.zeros((4, LANES), F32),
-        ],
-        axis=0,
-    )
-    note_out[...] = jnp.broadcast_to(block[None], note_out.shape)
+    seen = jnp.concatenate([small[:, :LANES], small[:, LANES:]], axis=0)
+    along, row = channel_cells(numbers, rows)
+    note_out[:half, :] = jnp.where(lax.axis_index("depth") == 0, rates, seen)
+    for i, value in enumerate((along[:, :LANES], along[:, LANES:], row[:, :LANES], row[:, LANES:])):
+        note_out[half + i : half + i + 1, :] = value.astype(F32)
+    note_out[half + 4 :, :] = jnp.zeros((NOTE - half - 4, LANES), F32)
+
+
+def channel_cells(numbers, rows):
+    return numbers[0] * rows + lax.shift_right_logical(numbers[1], 2), numbers[1] & 3
 
 
 def three(value):
@@ -312,9 +314,9 @@
         for k in range(group):
             who = 2 * (base + k)
             for h in range(2):
-                along = notes[who, 16 + h : 17 + h, :]
-                mask = (row16 & 3).astype(F32) == notes[who, 18 + h : 19 + h, :]
-                seen = [notes[who, 8 + 4 * h + t : 9 + 4 * h + t, :] for t in range(MOMENTS)]
+                along = notes[who, 8 + h : 9 + h, :]
+                mask = (row16 & 3).astype(F32) == notes[who, 10 + h : 11 + h, :]
+                seen = [notes[who + 1, 4 * h + t : 4 * h + t + 1, :] for t in range(MOMENTS)]
                 value = jnp.where(
                     row16 < 8,
                     jnp.where(row16 < 4, seen[0], seen[1]),
@@ -349,12 +351,11 @@
     rows = own.shape[2]
     extent = rows + 2 * EDGE
     depth = lax.axis_index("depth")
-    load_state(state, own, got_even, got_odd, 5)
+    load_state(state, own, got_even, got_odd, FORWARD)
     sums[...] = jnp.zeros(sums.shape, F32)
     for copy in copies:
         copy.wait()
-    along = numbers[0] * rows + lax.shift_right_logical(numbers[1], 2)
-    row = numbers[1] & 3
+    along, row = channel_cells(numbers, rows)
     rate, seen, count = channel_sums(tracks, rows, notes, along)
     channels = along.shape[1]
     at_own = jnp.where((row_ids(IMAGE, channels) & 3) == row, rate[:, :channels], 0.0)
@@ -407,12 +408,14 @@
     moments, channels = observed.shape
     owner = owner_track.reshape(1, channels)
     cell = fibre_cell.reshape(1, channels)
+    pinned = lambda array: pltpu.with_memory_space_constraint(array, pltpu.HBM)
     arrays = (velocity, stress, adjoint_velocity, adjoint_stress, buoyancy, lame_lambda, shear_modulus)
-    length = EDGE + HALO * FIELDS
-    length = length + (-length) % 8
+    arrays = tuple(pinned(array) for array in arrays)
+    channel_arrays = (pinned(observed), pinned(owner), pinned(cell))
     extent = rows + 2 * EDGE
     block = jax.ShapeDtypeStruct((rows, depth_cells), F32)
-    edges = jax.ShapeDtypeStruct((length, depth_cells), F32)
+    length = EDGE + HALO * FIELDS + EDGE - HALO
+    edges = jax.ShapeDtypeStruct((length + (-length) % 8, depth_cells), F32)
     inside = pl.BlockSpec(memory_space=VMEM)
     outside = pl.BlockSpec(memory_space=pltpu.HBM)
     anywhere = pl.BlockSpec(memory_space=pl.ANY)
@@ -423,18 +426,20 @@
         pltpu.SemaphoreType.DMA((3,)),
     ]
 
-    to_depth, to_even, to_odd = pl.pallas_call(
+    to_depth, *to_track = pl.pallas_call(
         pack_kernel,
         out_shape=(block, edges, edges),
         in_specs=[outside] * 7,
         out_specs=(inside,) * 3,
         scratch_shapes=held + [pltpu.SemaphoreType.DMA((7,))],
         compiler_params=params(),
+        cost_estimate=cost(2),
         name="pack",
     )(*arrays)
 
-    got_depth = lax.ppermute(to_depth, "depth", [(0, 1), (1, 0)])
-    to_even, to_odd = pl.pallas_call(
+    depth_swap = [(0, 1), (1, 0)]
+    got_depth = lax.ppermute(to_depth, "depth", depth_swap)
+    to_track = pl.pallas_call(
         corner_kernel,
         out_shape=(edges, edges),
         in_specs=[anywhere] * 3,
@@ -443,10 +448,10 @@
         scratch_shapes=[pltpu.SemaphoreType.DMA((2,))],
         compiler_params=params(),
         name="corners",
-    )(got_depth, to_even, to_odd)
+    )(got_depth, *to_track)
     swap = lambda k: [pair for i in range(k, tracks - 1, 2) for pair in ((i, i + 1), (i + 1, i))]
-    got_odd = lax.ppermute(to_odd, "track", swap(1))
-    got_even = lax.ppermute(to_even, "track", swap(0))
+    got_odd = lax.ppermute(to_track[1], "track", swap(1))
+    got_even = lax.ppermute(to_track[0], "track", swap(0))
 
     own = pl.pallas_call(
         own_kernel,
@@ -455,26 +460,27 @@
         out_specs=inside,
         scratch_shapes=held + [pltpu.SemaphoreType.DMA((7,))],
         compiler_params=params(),
+        cost_estimate=cost(2),
         name="own_planes",
     )(*arrays, got_depth)
 
-    devices = tracks * lax.axis_size("depth")
     media, saved, velocity_end, note = pl.pallas_call(
         forward_kernel,
         out_shape=(
             jax.ShapeDtypeStruct((4, 3, extent, LANES), F32),
             jax.ShapeDtypeStruct((moments, 3, 3, rows, LANES), F32),
             jax.ShapeDtypeStruct(velocity.shape, F32),
-            jax.ShapeDtypeStruct((devices, NOTE, LANES), F32),
+            jax.ShapeDtypeStruct((NOTE, LANES), F32),
         ),
         in_specs=[inside] * 3 + [outside] * 3,
         out_specs=(inside,) * 4,
         scratch_shapes=[VMEM((5, 3, extent + 2 * PAD, LANES), F32)] + channel_scratch,
         compiler_params=params(),
+        cost_estimate=cost(3),
         name="forward",
-    )(own, got_even, got_odd, observed, owner, cell)
-
-    notes = lax.all_to_all(note, ("track", "depth"), split_axis=0, concat_axis=0, tiled=True)
+    )(own, got_even, got_odd, *channel_arrays)
+
+    notes = lax.all_gather(note, ("track", "depth"), axis=0, tiled=False)
 
     gradient_lambda, gradient_mu, residual = pl.pallas_call(
         lambda *refs: adjoint_kernel(tracks, *refs),
@@ -487,8 +493,9 @@
         ]
         + channel_scratch,
         compiler_params=params(),
+        cost_estimate=cost(4),
         name="adjoint",
-    )(own, got_even, got_odd, media, saved, notes, observed, owner, cell)
+    )(own, got_even, got_odd, media, saved, notes, *channel_arrays)
     return gradient_lambda, gradient_mu, velocity_end, residual
 
 

time: 41.8 us -> 41.7 us (level)
  local copies, waits for them, and re-layouts: 6.19 us -> 0 us
  blocking collectives: 14.9 us -> 20.1 us
  Pallas kernels: 9.12 us -> 10.2 us
    all_gather x0 -> x1, blocking collectives: none -> 20.1 us  [per_device(): notes = lax.all_gather(note, ('track', 'depth'), axis=0, tiled=False)]
    all_to_all x1 -> x0, blocking collectives: 14.9 us -> none  [per_device(): lax.all_to_all(note, ('track', 'depth'), split_axis=0, concat_axis=0, til...]
    unnamed x26 -> x0, local copies, waits for them, and re-layouts: 6.19 us -> none
    pallas_call x1, Pallas kernels: 2.94 us -> 3.45 us  [per_device(): pl.pallas_call(forward_kernel, out_shape=(jax.ShapeDtypeStruct((4, 3, ext...]
    pallas_call x1, Pallas kernels: 2.99 us -> 3.44 us  [per_device(): pl.pallas_call(lambda *refs: adjoint_kernel(tracks, *refs), out_shape=(bl...]
  transfers between devices with their start and end apart: 3 -> 3, of which waited for: 2 -> 2; matrix products, arithmetic and copies ran while one was open for 0% -> 0% of each run, Pallas kernels for 4% -> 5%
where the time goes in v4:
time: 41.7 us; the launch traced here: 41.5 us
  blocking collectives  20.1 us (48%)
  Pallas kernels  10.2 us (24%)
  waiting for transfers between devices  6.34 us (15%)
  starting transfers between devices  4.08 us (10%)
  between operations  0.67 us (2%)
    all_gather x1, blocking collectives, per_device(): notes = lax.all_gather(note, ('track', 'depth'), axis=0, tiled=False)  20.1 us
    ppermute x1, waiting for transfers between devices, per_device(): got_even = lax.ppermute(to_track[0], 'track', swap(0))  5.44 us
    pallas_call x1, Pallas kernels, per_device(): pl.pallas_call(forward_kernel, out_shape=(jax.ShapeDtypeStruct((4, 3, ext...  3.45 us
    pallas_call x1, Pallas kernels, per_device(): pl.pallas_call(lambda *refs: adjoint_kernel(tracks, *refs), out_shape=(bl...  3.44 us
    ppermute x1, starting transfers between devices, per_device(): got_even = lax.ppermute(to_track[0], 'track', swap(0))  2.91 us
    pallas_call x1, Pallas kernels, per_device(): pl.pallas_call(own_kernel, out_shape=jax.ShapeDtypeStruct((FIELDS, 3, row...  1.88 us
    pallas_call x1, Pallas kernels, per_device(): pl.pallas_call(pack_kernel, out_shape=(block, edges, edges), in_specs=[ou...  1.44 us
    ppermute x1, waiting for transfers between devices, per_device(): got_depth = lax.ppermute(to_depth, 'depth', depth_swap)  0.9 us
  transfers between devices with their start and end apart: 3, of which 2 were waited for; matrix products, arithmetic and copies ran while one was open for 0% of the time, Pallas kernels for 5%

profile of v4, /device:TPU:0, one launch (start us, length us, event | category | flops | bytes accessed | tf_op | source)
XLA Modules:
  0.0 41.5 jit_solution(17213537868546671170)
XLA Ops:
  0.6 1.4 %pack.1 = (f32[64,256]{1,0:T(8,128)S(1)}, f32[176,256]{1,0:T(8,128)S(1)}, f32[176,256]{1,0:T(8,128)S(1)}) custom-call(f32[2,64,256]{2,1,0:T(8,128)} %refs_0_.3, f32[3,64,256]{2,1,0:T(8,128)} %refs_1_.3, f32[2,64,256]{2,1,0:T(8,128)} %refs_2_.3, f32[3,64,256]{2,1,0:T(8,128)} %refs_3_.3, f32[64,256]{1,0:T(8,128)} %refs_4_.3, f32[64,256]{1,0:T(8,128)} %refs_5_.3, ...), custom_call_target="tpu_custom_call" | custom-call | bytes 7000000 | tf_op jit(solution)/shard_map/pack/pallas_call | solution.py:429
  2.1 0.5 %collective-permute-start = (f32[64,256]{1,0:T(8,128)S(1)}, f32[64,256]{1,0:T(8,128)S(1)}, u32[]{:S(2)}, u32[]{:S(2)}) collective-permute-start(f32[64,256]{1,0:T(8,128)S(1)} %get-tuple-element.16), channel_id=1, source_target_pairs={{0,1},{1,0},{2,3},{3,2},{4,5},{5,4},{6,7},{7,6},{8,9},{9,8},{10,11... | collective-permute-start | bytes 196616 | tf_op jit(solution)/shard_map/ppermute | solution.py:441
  2.6 0.9 %collective-permute-done.refs_7_.got = f32[64,256]{1,0:T(8,128)S(1)} collective-permute-done((f32[64,256]{1,0:T(8,128)S(1)}, f32[64,256]{1,0:T(8,128)S(1)}, u32[]{:S(2)}, u32[]{:S(2)}) %collective-permute-start) | collective-permute-done | bytes 65568 | tf_op jit(solution)/shard_map/ppermute | solution.py:441
  3.5 2.9 %collective-permute-start.1 = (f32[176,256]{1,0:T(8,128)S(1)}, f32[176,256]{1,0:T(8,128)S(1)}, u32[]{:S(2)}, u32[]{:S(2)}) collective-permute-start(f32[176,256]{1,0:T(8,128)S(1)} %get-tuple-element.19), channel_id=1, source_target_pairs={{0,2},{2,0},{4,6},{6,4},{8,10},{10,8},{12,14},{14,12},{1,3},{3,1},... | collective-permute-start | bytes 540680 | tf_op jit(solution)/shard_map/ppermute | solution.py:454
  6.4 0.7 %collective-permute-start.2 = (f32[176,256]{1,0:T(8,128)S(1)}, f32[176,256]{1,0:T(8,128)S(1)}, u32[]{:S(2)}, u32[]{:S(2)}) collective-permute-start(f32[176,256]{1,0:T(8,128)S(1)} %get-tuple-element.20), channel_id=1, source_target_pairs={{2,4},{4,2},{6,8},{8,6},{10,12},{12,10},{3,5},{5,3},{7,9},{9,7},{1... | collective-permute-start | bytes 540680 | tf_op jit(solution)/shard_map/ppermute | solution.py:453
  7.1 1.9 %own_planes.1.own.refs_0_ = f32[13,3,64,128]{3,2,1,0:T(8,128)S(1)} custom-call(f32[2,64,256]{2,1,0:T(8,128)} %refs_0_.3, f32[3,64,256]{2,1,0:T(8,128)} %refs_1_.3, f32[2,64,256]{2,1,0:T(8,128)} %refs_2_.3, f32[3,64,256]{2,1,0:T(8,128)} %refs_3_.3, f32[64,256]{1,0:T(8,128)} %refs_4_.3, f32[64,256]{1,0:T(8,128)} %refs_5_.3, f32[64,256]{1,0:T(8,128)} %refs_6_.4, ...), custom_call_target="tpu_custom_call" | custom-call | bytes 7000000 | tf_op jit(solution)/shard_map/own_planes/pallas_call | solution.py:456
  9.0 5.4 %collective-permute-done.1.got_even.refs_1_ = f32[176,256]{1,0:T(8,128)S(1)} collective-permute-done((f32[176,256]{1,0:T(8,128)S(1)}, f32[176,256]{1,0:T(8,128)S(1)}, u32[]{:S(2)}, u32[]{:S(2)}) %collective-permute-start.1) | collective-permute-done | bytes 180256 | tf_op jit(solution)/shard_map/ppermute | solution.py:454
  14.4 0.0 collective-permute-done.2.got_odd.refs_2_
  14.4 3.5 %forward.1 = (f32[4,3,96,128]{3,2,1,0:T(8,128)S(1)}, f32[4,3,3,64,128]{4,3,2,1,0:T(8,128)S(1)}, f32[2,64,256]{2,1,0:T(8,128)}, f32[16,128]{1,0:T(8,128)S(1)}) custom-call(f32[13,3,64,128]{3,2,1,0:T(8,128)S(1)} %own_planes.1.own.refs_0_, f32[176,256]{1,0:T(8,128)S(1)} %collective-permute-done.1.got_even.refs_1_, ...), custom_call_target="tpu_custom_call" | custom-call | bytes 10500000 | tf_op jit(solution)/shard_map/forward/pallas_call | solution.py:467
  17.9 20.1 %all-gather = f32[256,128]{1,0:T(8,128)S(1)} all-gather(f32[16,128]{1,0:T(8,128)S(1)} %get-tuple-element.23), channel_id=2, replica_groups=mesh['shots'=2,'track'=8,'depth'=2] {'track','depth'}, dimensions={0}, use_global_device_ids=true | all-gather | bytes 139264 | tf_op jit(solution)/shard_map/all_gather | solution.py:483
  38.0 3.4 %adjoint.1 = (f32[64,256]{1,0:T(8,128)}, f32[64,256]{1,0:T(8,128)}, f32[2,256]{1,0:T(2,128)}) custom-call(f32[13,3,64,128]{3,2,1,0:T(8,128)S(1)} %own_planes.1.own.refs_0_, f32[176,256]{1,0:T(8,128)S(1)} %collective-permute-done.1.got_even.refs_1_, f32[176,256]{1,0:T(8,128)S(1)} %collective-permute-done.2.got_odd.refs_2_, ...), custom_call_target="tpu_custom_call" | custom-call | bytes 14000000 | tf_op jit(solution)/shard_map/adjoint/pallas_call | solution.py:485
  (1 shorter events, 0.0 us)
Async XLA Ops:
  2.1 1.4 %collective-permute-start = (f32[64,256]{1,0:T(8,128)S(1)}, f32[64,256]{1,0:T(8,128)S(1)}, u32[]{:S(2)}, u32[]{:S(2)}) collective-permute-start(f32[64,256]{1,0:T(8,128)S(1)} %get-tuple-element.16), channel_id=1, source_target_pairs={{0,1},{1,0},{2,3},{3,2},{4,5},{5,4},{6,7},{7,6},{8,9},{9,8},{10,11... | collective-permute-start | bytes 196616 | tf_op jit(solution)/shard_map/ppermute | solution.py:441
  3.5 10.9 %collective-permute-start.1 = (f32[176,256]{1,0:T(8,128)S(1)}, f32[176,256]{1,0:T(8,128)S(1)}, u32[]{:S(2)}, u32[]{:S(2)}) collective-permute-start(f32[176,256]{1,0:T(8,128)S(1)} %get-tuple-element.19), channel_id=1, source_target_pairs={{0,2},{2,0},{4,6},{6,4},{8,10},{10,8},{12,14},{14,12},{1,3},{3,1},... | collective-permute-start | bytes 540680 | tf_op jit(solution)/shard_map/ppermute | solution.py:454
  6.4 8.0 %collective-permute-start.2 = (f32[176,256]{1,0:T(8,128)S(1)}, f32[176,256]{1,0:T(8,128)S(1)}, u32[]{:S(2)}, u32[]{:S(2)}) collective-permute-start(f32[176,256]{1,0:T(8,128)S(1)} %get-tuple-element.20), channel_id=1, source_target_pairs={{2,4},{4,2},{6,8},{8,6},{10,12},{12,10},{3,5},{5,3},{7,9},{9,7},{1... | collective-permute-start | bytes 540680 | tf_op jit(solution)/shard_map/ppermute | solution.py:453

commit v5 on v4

--- a/solution.py
+++ b/solution.py
@@ -17,7 +17,6 @@
 FIELDS = FORWARD + ADJOINT
 MOMENTS = 4
 IMAGE = MOMENTS * FIBRE_ROWS
-NOTE = 16
 VMEM = pltpu.VMEM
 F32 = jnp.float32
 BF16 = jnp.bfloat16
@@ -267,10 +266,10 @@
         copy.wait()
     seen = jnp.concatenate([small[:, :LANES], small[:, LANES:]], axis=0)
     along, row = channel_cells(numbers, rows)
-    note_out[:half, :] = jnp.where(lax.axis_index("depth") == 0, rates, seen)
-    for i, value in enumerate((along[:, :LANES], along[:, LANES:], row[:, :LANES], row[:, LANES:])):
-        note_out[half + i : half + i + 1, :] = value.astype(F32)
-    note_out[half + 4 :, :] = jnp.zeros((NOTE - half - 4, LANES), F32)
+    mine = jnp.where(lax.axis_index("depth") == 0, rates, seen)
+    cells = jnp.concatenate([along[:, :LANES], along[:, LANES:], row[:, :LANES], row[:, LANES:]], axis=0)
+    for i, value in enumerate((mine[:4], mine[4:], cells.astype(F32))):
+        note_out[:, i] = jnp.broadcast_to(value[None], (note_out.shape[0], 4, LANES))
 
 
 def channel_cells(numbers, rows):
@@ -289,8 +288,9 @@
     return (value[2 * IMAGE : 3 * IMAGE] + value[IMAGE : 2 * IMAGE]) + value[:IMAGE]
 
 
-def channel_sums(tracks, rows, notes, own_along):
+def channel_sums(tracks, rows, notes, beside, own_along):
     start = lax.axis_index("track") * rows - EDGE
+    surface = lax.axis_index("depth") == 0
     group = min(8, tracks)
     channels = own_along.shape[1]
     lane = lane_ids(8)
@@ -302,8 +302,14 @@
         rate, image = carry
         base = number * group
         firsts, lasts = [], []
+        mine = [[notes[base + k, i] for i in range(3)] for k in range(group)]
+        other = [[beside[base + k, i] for i in range(3)] for k in range(group)]
+        rates = [
+            jnp.concatenate([jnp.where(surface, m[i], o[i]) for i in range(2)], axis=0) for m, o in zip(mine, other)
+        ]
+        traces = [[jnp.where(surface, o[i], m[i]) for i in range(2)] for m, o in zip(mine, other)]
         for k in range(0, group, 2):
-            a, b = notes[2 * (base + k), :8, :], notes[2 * (base + k + 1), :8, :]
+            a, b = rates[k], rates[k + 1]
             firsts.append(jnp.where(lane < half, a, turn(b, half)))
             lasts.append(jnp.where(lane < half, turn(a, half), b))
         strains = jnp.concatenate([jnp.concatenate(firsts, axis=1), jnp.concatenate(lasts, axis=1)], axis=0)
@@ -312,11 +318,10 @@
         rate = rate + jnp.dot(jnp.concatenate(three(strains), axis=0), hot, preferred_element_type=F32)
         weights, hots = [], []
         for k in range(group):
-            who = 2 * (base + k)
             for h in range(2):
-                along = notes[who, 8 + h : 9 + h, :]
-                mask = (row16 & 3).astype(F32) == notes[who, 10 + h : 11 + h, :]
-                seen = [notes[who + 1, 4 * h + t : 4 * h + t + 1, :] for t in range(MOMENTS)]
+                along = mine[k][2][h : h + 1]
+                mask = (row16 & 3).astype(F32) == mine[k][2][2 + h : 3 + h]
+                seen = [traces[k][h][t : t + 1] for t in range(MOMENTS)]
                 value = jnp.where(
                     row16 < 8,
                     jnp.where(row16 < 4, seen[0], seen[1]),
@@ -344,7 +349,7 @@
 
 
 def adjoint_kernel(
-    tracks, own, got_even, got_odd, media, saved, notes, obs, owner, cell,
+    tracks, own, got_even, got_odd, media, saved, notes, beside, obs, owner, cell,
     lambda_out, mu_out, residual_out, state, sums, small, numbers, sems,
 ):
     copies = fetch((obs, owner, cell), (small, numbers.at[0], numbers.at[1]), sems)
@@ -356,7 +361,7 @@
     for copy in copies:
         copy.wait()
     along, row = channel_cells(numbers, rows)
-    rate, seen, count = channel_sums(tracks, rows, notes, along)
+    rate, seen, count = channel_sums(tracks, rows, notes, beside, along)
     channels = along.shape[1]
     at_own = jnp.where((row_ids(IMAGE, channels) & 3) == row, rate[:, :channels], 0.0)
     traces = [
@@ -470,7 +475,7 @@
             jax.ShapeDtypeStruct((4, 3, extent, LANES), F32),
             jax.ShapeDtypeStruct((moments, 3, 3, rows, LANES), F32),
             jax.ShapeDtypeStruct(velocity.shape, F32),
-            jax.ShapeDtypeStruct((NOTE, LANES), F32),
+            jax.ShapeDtypeStruct((tracks, 3, 4, LANES), F32),
         ),
         in_specs=[inside] * 3 + [outside] * 3,
         out_specs=(inside,) * 4,
@@ -480,12 +485,13 @@
         name="forward",
     )(own, got_even, got_odd, *channel_arrays)
 
-    notes = lax.all_gather(note, ("track", "depth"), axis=0, tiled=False)
+    notes = lax.all_to_all(note, "track", split_axis=0, concat_axis=0, tiled=True)
+    beside = lax.ppermute(notes, "depth", depth_swap)
 
     gradient_lambda, gradient_mu, residual = pl.pallas_call(
         lambda *refs: adjoint_kernel(tracks, *refs),
         out_shape=(block, block, jax.ShapeDtypeStruct((moments // 2, channels), F32)),
-        in_specs=[inside] * 6 + [outside] * 3,
+        in_specs=[inside] * 7 + [outside] * 3,
         out_specs=(inside,) * 3,
         scratch_shapes=[
             VMEM((5, 3, extent + 2 * PAD, LANES), F32),
@@ -495,7 +501,7 @@
         compiler_params=params(),
         cost_estimate=cost(4),
         name="adjoint",
-    )(own, got_even, got_odd, media, saved, notes, *channel_arrays)
+    )(own, got_even, got_odd, media, saved, notes, beside, *channel_arrays)
     return gradient_lambda, gradient_mu, velocity_end, residual
 
 

time: 41.7 us -> 35.4 us (0.85)
  blocking collectives: 20.1 us -> 12.6 us
  waiting for transfers between devices: 6.34 us -> 7.57 us
    all_gather x1 -> x0, blocking collectives: 20.1 us -> none  [per_device(): notes = lax.all_gather(note, ('track', 'depth'), axis=0, tiled=False)]
    all_to_all x0 -> x1, blocking collectives: none -> 12.6 us  [per_device(): lax.all_to_all(note, 'track', split_axis=0, concat_axis=0, tiled=True)]
    ppermute x0 -> x1, waiting for transfers between devices: none -> 1.23 us  [per_device(): beside = lax.ppermute(notes, 'depth', depth_swap)]
  transfers between devices with their start and end apart: 3 -> 4, of which waited for: 2 -> 3; matrix products, arithmetic and copies ran while one was open for 0% -> 0% of each run, Pallas kernels for 5% -> 5%
where the time goes in v5:
time: 35.4 us; the launch traced here: 35.1 us
  blocking collectives  12.6 us (36%)
  Pallas kernels  10.2 us (29%)
  waiting for transfers between devices  7.57 us (21%)
  starting transfers between devices  4.09 us (12%)
  between operations  0.67 us (2%)
    all_to_all x1, blocking collectives, per_device(): lax.all_to_all(note, 'track', split_axis=0, concat_axis=0, tiled=True)  12.6 us
    ppermute x1, waiting for transfers between devices, per_device(): got_even = lax.ppermute(to_track[0], 'track', swap(0))  5.44 us
    pallas_call x1, Pallas kernels, per_device(): pl.pallas_call(forward_kernel, out_shape=(jax.ShapeDtypeStruct((4, 3, ext...  3.45 us
    pallas_call x1, Pallas kernels, per_device(): pl.pallas_call(lambda *refs: adjoint_kernel(tracks, *refs), out_shape=(bl...  3.43 us
    ppermute x1, starting transfers between devices, per_device(): got_even = lax.ppermute(to_track[0], 'track', swap(0))  2.91 us
    pallas_call x1, Pallas kernels, per_device(): pl.pallas_call(own_kernel, out_shape=jax.ShapeDtypeStruct((FIELDS, 3, row...  1.88 us
    pallas_call x1, Pallas kernels, per_device(): pl.pallas_call(pack_kernel, out_shape=(block, edges, edges), in_specs=[ou...  1.44 us
    ppermute x1, waiting for transfers between devices, per_device(): beside = lax.ppermute(notes, 'depth', depth_swap)  1.23 us
  transfers between devices with their start and end apart: 4, of which 3 were waited for; matrix products, arithmetic and copies ran while one was open for 0% of the time, Pallas kernels for 5%

profile of v5, /device:TPU:0, one launch (start us, length us, event | category | flops | bytes accessed | tf_op | source)
XLA Modules:
  0.0 35.1 jit_solution(15969230337693601021)
XLA Ops:
  0.6 1.4 %pack.1 = (f32[64,256]{1,0:T(8,128)S(1)}, f32[176,256]{1,0:T(8,128)S(1)}, f32[176,256]{1,0:T(8,128)S(1)}) custom-call(f32[2,64,256]{2,1,0:T(8,128)} %refs_0_.3, f32[3,64,256]{2,1,0:T(8,128)} %refs_1_.3, f32[2,64,256]{2,1,0:T(8,128)} %refs_2_.3, f32[3,64,256]{2,1,0:T(8,128)} %refs_3_.3, f32[64,256]{1,0:T(8,128)} %refs_4_.3, f32[64,256]{1,0:T(8,128)} %refs_5_.3, ...), custom_call_target="tpu_custom_call" | custom-call | bytes 7000000 | tf_op jit(solution)/shard_map/pack/pallas_call | solution.py:434
  2.1 0.5 %collective-permute-start = (f32[64,256]{1,0:T(8,128)S(1)}, f32[64,256]{1,0:T(8,128)S(1)}, u32[]{:S(2)}, u32[]{:S(2)}) collective-permute-start(f32[64,256]{1,0:T(8,128)S(1)} %get-tuple-element.16), channel_id=1, source_target_pairs={{0,1},{1,0},{2,3},{3,2},{4,5},{5,4},{6,7},{7,6},{8,9},{9,8},{10,11... | collective-permute-start | bytes 196616 | tf_op jit(solution)/shard_map/ppermute | solution.py:446
  2.6 0.9 %collective-permute-done.refs_7_.got = f32[64,256]{1,0:T(8,128)S(1)} collective-permute-done((f32[64,256]{1,0:T(8,128)S(1)}, f32[64,256]{1,0:T(8,128)S(1)}, u32[]{:S(2)}, u32[]{:S(2)}) %collective-permute-start) | collective-permute-done | bytes 65568 | tf_op jit(solution)/shard_map/ppermute | solution.py:446
  3.5 2.9 %collective-permute-start.1 = (f32[176,256]{1,0:T(8,128)S(1)}, f32[176,256]{1,0:T(8,128)S(1)}, u32[]{:S(2)}, u32[]{:S(2)}) collective-permute-start(f32[176,256]{1,0:T(8,128)S(1)} %get-tuple-element.19), channel_id=1, source_target_pairs={{0,2},{2,0},{4,6},{6,4},{8,10},{10,8},{12,14},{14,12},{1,3},{3,1},... | collective-permute-start | bytes 540680 | tf_op jit(solution)/shard_map/ppermute | solution.py:459
  6.4 0.7 %collective-permute-start.2 = (f32[176,256]{1,0:T(8,128)S(1)}, f32[176,256]{1,0:T(8,128)S(1)}, u32[]{:S(2)}, u32[]{:S(2)}) collective-permute-start(f32[176,256]{1,0:T(8,128)S(1)} %get-tuple-element.20), channel_id=1, source_target_pairs={{2,4},{4,2},{6,8},{8,6},{10,12},{12,10},{3,5},{5,3},{7,9},{9,7},{1... | collective-permute-start | bytes 540680 | tf_op jit(solution)/shard_map/ppermute | solution.py:458
  7.1 1.9 %own_planes.1.own.refs_0_ = f32[13,3,64,128]{3,2,1,0:T(8,128)S(1)} custom-call(f32[2,64,256]{2,1,0:T(8,128)} %refs_0_.3, f32[3,64,256]{2,1,0:T(8,128)} %refs_1_.3, f32[2,64,256]{2,1,0:T(8,128)} %refs_2_.3, f32[3,64,256]{2,1,0:T(8,128)} %refs_3_.3, f32[64,256]{1,0:T(8,128)} %refs_4_.3, f32[64,256]{1,0:T(8,128)} %refs_5_.3, f32[64,256]{1,0:T(8,128)} %refs_6_.3, ...), custom_call_target="tpu_custom_call" | custom-call | bytes 7000000 | tf_op jit(solution)/shard_map/own_planes/pallas_call | solution.py:461
  9.0 5.4 %collective-permute-done.1.got_even.refs_1_ = f32[176,256]{1,0:T(8,128)S(1)} collective-permute-done((f32[176,256]{1,0:T(8,128)S(1)}, f32[176,256]{1,0:T(8,128)S(1)}, u32[]{:S(2)}, u32[]{:S(2)}) %collective-permute-start.1) | collective-permute-done | bytes 180256 | tf_op jit(solution)/shard_map/ppermute | solution.py:459
  14.4 0.0 collective-permute-done.2.got_odd.refs_2_
  14.4 3.5 %forward.1 = (f32[4,3,96,128]{3,2,1,0:T(8,128)S(1)}, f32[4,3,3,64,128]{4,3,2,1,0:T(8,128)S(1)}, f32[2,64,256]{2,1,0:T(8,128)}, f32[8,3,4,128]{3,2,1,0:T(4,128)S(1)}) custom-call(f32[13,3,64,128]{3,2,1,0:T(8,128)S(1)} %own_planes.1.own.refs_0_, f32[176,256]{1,0:T(8,128)S(1)} %collective-permute-done.1.got_even.refs_1_, ...), custom_call_target="tpu_custom_call" | custom-call | bytes 10500000 | tf_op jit(solution)/shard_map/forward/pallas_call | solution.py:472
  17.9 12.6 %all_to_all.5.refs_5_ = f32[8,3,4,128]{3,2,1,0:T(4,128)S(1)} all-to-all(f32[8,3,4,128]{3,2,1,0:T(4,128)S(1)} %get-tuple-element.23), channel_id=1, replica_groups=mesh['shots'=2,'track'=8,'depth'=2] {'track'}, dimensions={0} | all-to-all | bytes 98304 | tf_op jit(solution)/shard_map/all_to_all | solution.py:488
  30.5 0.0 collective-permute-start.3
  30.5 1.2 %collective-permute-done.3.refs_6_ = f32[8,3,4,128]{3,2,1,0:T(4,128)S(1)} collective-permute-done((f32[8,3,4,128]{3,2,1,0:T(4,128)S(1)}, f32[8,3,4,128]{3,2,1,0:T(4,128)S(1)}, u32[]{:S(2)}, u32[]{:S(2)}) %collective-permute-start.3) | collective-permute-done | bytes 49184 | tf_op jit(solution)/shard_map/ppermute | solution.py:489
  31.7 3.4 %adjoint.1 = (f32[64,256]{1,0:T(8,128)}, f32[64,256]{1,0:T(8,128)}, f32[2,256]{1,0:T(2,128)}) custom-call(f32[13,3,64,128]{3,2,1,0:T(8,128)S(1)} %own_planes.1.own.refs_0_, f32[176,256]{1,0:T(8,128)S(1)} %collective-permute-done.1.got_even.refs_1_, f32[176,256]{1,0:T(8,128)S(1)} %collective-permute-done.2.got_odd.refs_2_, ...), custom_call_target="tpu_custom_call" | custom-call | bytes 14000000 | tf_op jit(solution)/shard_map/adjoint/pallas_call | solution.py:491
  (1 shorter events, 0.0 us)
Async XLA Ops:
  2.1 1.4 %collective-permute-start = (f32[64,256]{1,0:T(8,128)S(1)}, f32[64,256]{1,0:T(8,128)S(1)}, u32[]{:S(2)}, u32[]{:S(2)}) collective-permute-start(f32[64,256]{1,0:T(8,128)S(1)} %get-tuple-element.16), channel_id=1, source_target_pairs={{0,1},{1,0},{2,3},{3,2},{4,5},{5,4},{6,7},{7,6},{8,9},{9,8},{10,11... | collective-permute-start | bytes 196616 | tf_op jit(solution)/shard_map/ppermute | solution.py:446
  3.5 10.9 %collective-permute-start.1 = (f32[176,256]{1,0:T(8,128)S(1)}, f32[176,256]{1,0:T(8,128)S(1)}, u32[]{:S(2)}, u32[]{:S(2)}) collective-permute-start(f32[176,256]{1,0:T(8,128)S(1)} %get-tuple-element.19), channel_id=1, source_target_pairs={{0,2},{2,0},{4,6},{6,4},{8,10},{10,8},{12,14},{14,12},{1,3},{3,1},... | collective-permute-start | bytes 540680 | tf_op jit(solution)/shard_map/ppermute | solution.py:459
  6.4 8.0 %collective-permute-start.2 = (f32[176,256]{1,0:T(8,128)S(1)}, f32[176,256]{1,0:T(8,128)S(1)}, u32[]{:S(2)}, u32[]{:S(2)}) collective-permute-start(f32[176,256]{1,0:T(8,128)S(1)} %get-tuple-element.20), channel_id=1, source_target_pairs={{2,4},{4,2},{6,8},{8,6},{10,12},{12,10},{3,5},{5,3},{7,9},{9,7},{1... | collective-permute-start | bytes 540680 | tf_op jit(solution)/shard_map/ppermute | solution.py:458
  30.5 1.2 %collective-permute-start.3 = (f32[8,3,4,128]{3,2,1,0:T(4,128)S(1)}, f32[8,3,4,128]{3,2,1,0:T(4,128)S(1)}, u32[]{:S(2)}, u32[]{:S(2)}) collective-permute-start(f32[8,3,4,128]{3,2,1,0:T(4,128)S(1)} %all_to_all.5.refs_5_), channel_id=1, source_target_pairs={{0,1},{1,0},{2,3},{3,2},{4,5},{5,4},{6,7},{7,6},{8,9},{9,8},{10,11... | collective-permute-start | bytes 147464 | tf_op jit(solution)/shard_map/ppermute | solution.py:489

commit v6 on v4

--- a/solution.py
+++ b/solution.py
@@ -17,7 +17,6 @@
 FIELDS = FORWARD + ADJOINT
 MOMENTS = 4
 IMAGE = MOMENTS * FIBRE_ROWS
-NOTE = 16
 VMEM = pltpu.VMEM
 F32 = jnp.float32
 BF16 = jnp.bfloat16
@@ -159,42 +158,42 @@
     )
 
 
-def load_state(state, own, got_even, got_odd, base):
+def load_state(state, own, got_even, got_odd, base, planes):
     rows = own.shape[2]
     extent = rows + 2 * EDGE
     for f in range(5):
         below, above = halo_windows(base + f, got_even, got_odd)
-        for p in range(3):
-            state[f, p, :PAD, :] = jnp.zeros((PAD, LANES), F32)
-            state[f, p, PAD : PAD + EDGE, :] = below[p]
-            state[f, p, PAD + EDGE : PAD + EDGE + rows, :] = own[base + f, p]
-            state[f, p, PAD + EDGE + rows : PAD + extent, :] = above[p]
-            state[f, p, PAD + extent :, :] = jnp.zeros((PAD, LANES), F32)
+        for i, p in enumerate(planes):
+            state[f, i, :PAD, :] = jnp.zeros((PAD, LANES), F32)
+            state[f, i, PAD : PAD + EDGE, :] = below[p]
+            state[f, i, PAD + EDGE : PAD + EDGE + rows, :] = own[base + f, p]
+            state[f, i, PAD + EDGE + rows : PAD + extent, :] = above[p]
+            state[f, i, PAD + extent :, :] = jnp.zeros((PAD, LANES), F32)
 
 
 def velocities(state, media, span):
     for r in range(8 * span[0], 8 * span[1], 8):
-        for p in range(3):
+        for i in range(state.shape[1]):
 
             def at(f, by=0):
-                return state[f, p, r + PAD + by : r + PAD + by + 8, :]
+                return state[f, i, r + PAD + by : r + PAD + by + 8, :]
 
             xx, xz, zz = at(2), at(4), at(3)
-            b = media[0, p, r : r + 8, :]
+            b = media[0, i, r : r + 8, :]
             near = (xx - at(2, -1)) + (xz - turn(xz, 1))
             far = (at(2, 1) - at(2, -2)) + (turn(xz, -1) - turn(xz, 2))
-            state[0, p, r + PAD : r + PAD + 8, :] = at(0) + b * (near + RATIO * far)
+            state[0, i, r + PAD : r + PAD + 8, :] = at(0) + b * (near + RATIO * far)
             near = (at(4, 1) - xz) + (turn(zz, -1) - zz)
             far = (at(4, 2) - at(4, -1)) + (turn(zz, -2) - turn(zz, 1))
-            state[1, p, r + PAD : r + PAD + 8, :] = at(1) + b * (near + RATIO * far)
+            state[1, i, r + PAD : r + PAD + 8, :] = at(1) + b * (near + RATIO * far)
 
 
 def stresses(state, media, span, update, keep):
     for r in range(8 * span[0], 8 * span[1], 8):
-        for p in range(3):
+        for i in range(state.shape[1]):
 
             def at(f, by=0):
-                return state[f, p, r + PAD + by : r + PAD + by + 8, :]
+                return state[f, i, r + PAD + by : r + PAD + by + 8, :]
 
             vx, vz = at(0), at(1)
             exx = (at(0, 1) - vx) + RATIO * (at(0, 2) - at(0, -1))
@@ -202,12 +201,12 @@
             near = (turn(vx, -1) - vx) + (vz - at(1, -1))
             far = (turn(vx, -2) - turn(vx, 1)) + (at(1, 1) - at(1, -2))
             shear = near + RATIO * far
-            keep(p, r - EDGE, exx, ezz, shear)
+            keep(i, r - EDGE, exx, ezz, shear)
             if update:
-                whole, lam, mu = (media[k, p, r : r + 8, :] for k in (1, 2, 3))
-                state[2, p, r + PAD : r + PAD + 8, :] = at(2) + (whole * exx + lam * ezz)
-                state[3, p, r + PAD : r + PAD + 8, :] = at(3) + (lam * exx + whole * ezz)
-                state[4, p, r + PAD : r + PAD + 8, :] = at(4) + mu * shear
+                whole, lam, mu = (media[k, i, r : r + 8, :] for k in (1, 2, 3))
+                state[2, i, r + PAD : r + PAD + 8, :] = at(2) + (whole * exx + lam * ezz)
+                state[3, i, r + PAD : r + PAD + 8, :] = at(3) + (lam * exx + whole * ezz)
+                state[4, i, r + PAD : r + PAD + 8, :] = at(4) + mu * shear
 
 
 def spans(step, rows):
@@ -218,42 +217,40 @@
     return inner, inner if step < MOMENTS - 1 else (EDGE // 8, tiles - EDGE // 8)
 
 
-def forward_kernel(
-    own, got_even, got_odd, obs, owner, cell, media, saved, end_out, note_out, state, small, numbers, sems
-):
-    copies = fetch((obs, owner, cell), (small, numbers.at[0], numbers.at[1]), sems)
+def run_forward(own, got_even, got_odd, media, saved, state, planes):
     rows = own.shape[2]
     parts = []
     for f in (5, 6, 7):
         below, above = halo_windows(f, got_even, got_odd)
-        parts.append([(below[p], own[f, p], above[p]) for p in range(3)])
-    for p in range(3):
+        parts.append([(below[p], own[f, p], above[p]) for p in planes])
+    for i in range(len(planes)):
         for k, at in enumerate((0, EDGE, EDGE + rows)):
-            b, lam, mu = (NEAR * parts[i][p][k] for i in range(3))
+            b, lam, mu = (NEAR * parts[m][i][k] for m in range(3))
             span = slice(at, at + b.shape[0])
-            media[0, p, span, :] = b
-            media[1, p, span, :] = lam + 2.0 * mu
-            media[2, p, span, :] = lam
-            media[3, p, span, :] = mu
-    load_state(state, own, got_even, got_odd, 0)
+            media[0, i, span, :] = b
+            media[1, i, span, :] = lam + 2.0 * mu
+            media[2, i, span, :] = lam
+            media[3, i, span, :] = mu
+    load_state(state, own, got_even, got_odd, 0, planes)
     for step in range(MOMENTS):
         fast, slow = spans(step, rows)
         velocities(state, media, fast)
 
-        def save(p, r, exx, ezz, shear):
+        def save(i, r, exx, ezz, shear):
             if 0 <= r < rows:
-                saved[step, 0, p, r : r + 8, :] = exx
-                saved[step, 1, p, r : r + 8, :] = ezz
-                saved[step, 2, p, r : r + 8, :] = shear
+                saved[step, 0, i, r : r + 8, :] = exx
+                saved[step, 1, i, r : r + 8, :] = ezz
+                saved[step, 2, i, r : r + 8, :] = shear
 
         stresses(state, media, slow, step < MOMENTS - 1, save)
 
+
+def forward_top_kernel(own, got_even, got_odd, media, saved, end_out, image_out, state):
+    run_forward(own, got_even, got_odd, media, saved, state, (0,))
+    rows = own.shape[2]
     top = PAD + EDGE
     for f in range(2):
-        first, last = joined([state[f, p, top : top + rows, :] for p in range(3)])
-        end_out[f, :, :LANES] = first
-        end_out[f, :, LANES:] = last
-
+        end_out[f] = state[f, 0, top : top + rows, :]
     lane = lane_ids(rows)
     image = jnp.zeros((rows, LANES), F32)
     for step in range(MOMENTS):
@@ -262,19 +259,31 @@
         image = jnp.where(here, NEAR * turn(saved[step, 0, 0], spot - EDGE), image)
     turned = image.T
     half = IMAGE // 2
-    rates = jnp.concatenate([turned[:half], turned[half:IMAGE]], axis=1)
-    for copy in copies:
-        copy.wait()
-    seen = jnp.concatenate([small[:, :LANES], small[:, LANES:]], axis=0)
-    along, row = channel_cells(numbers, rows)
-    note_out[:half, :] = jnp.where(lax.axis_index("depth") == 0, rates, seen)
-    for i, value in enumerate((along[:, :LANES], along[:, LANES:], row[:, :LANES], row[:, LANES:])):
-        note_out[half + i : half + i + 1, :] = value.astype(F32)
-    note_out[half + 4 :, :] = jnp.zeros((NOTE - half - 4, LANES), F32)
-
-
-def channel_cells(numbers, rows):
-    return numbers[0] * rows + lax.shift_right_logical(numbers[1], 2), numbers[1] & 3
+    image_out[...] = jnp.concatenate([turned[:half], turned[half:IMAGE]], axis=1)
+
+
+def forward_rest_kernel(own, got_even, got_odd, top_end, media, saved, end_out, state):
+    run_forward(own, got_even, got_odd, media, saved, state, (1, 2))
+    rows = own.shape[2]
+    top = PAD + EDGE
+    for f in range(2):
+        rest = [state[f, i, top : top + rows, :] for i in range(2)]
+        first, last = joined([top_end[f]] + rest)
+        end_out[f, :, :LANES] = first
+        end_out[f, :, LANES:] = last
+
+
+def note_kernel(rows, image, image_beside, obs, owner, cell, note_out):
+    rates = jnp.where(lax.axis_index("depth") == 0, image[...], image_beside[...])
+    seen = obs[...]
+    along, row = channel_cells(owner, cell, rows)
+    cells = jnp.concatenate([along[:, :LANES], along[:, LANES:], row[:, :LANES], row[:, LANES:]], axis=0)
+    for i, value in enumerate((rates[:4], rates[4:], seen[:, :LANES], seen[:, LANES:], cells.astype(F32))):
+        note_out[:, i] = jnp.broadcast_to(value[None], (note_out.shape[0], 4, LANES))
+
+
+def channel_cells(owner, cell, rows):
+    return owner[...] * rows + lax.shift_right_logical(cell[...], 2), cell[...] & 3
 
 
 def three(value):
@@ -302,8 +311,10 @@
         rate, image = carry
         base = number * group
         firsts, lasts = [], []
+        blocks = [[notes[base + k, i] for i in range(5)] for k in range(group)]
+        rates = [jnp.concatenate(block[:2], axis=0) for block in blocks]
         for k in range(0, group, 2):
-            a, b = notes[2 * (base + k), :8, :], notes[2 * (base + k + 1), :8, :]
+            a, b = rates[k], rates[k + 1]
             firsts.append(jnp.where(lane < half, a, turn(b, half)))
             lasts.append(jnp.where(lane < half, turn(a, half), b))
         strains = jnp.concatenate([jnp.concatenate(firsts, axis=1), jnp.concatenate(lasts, axis=1)], axis=0)
@@ -312,11 +323,10 @@
         rate = rate + jnp.dot(jnp.concatenate(three(strains), axis=0), hot, preferred_element_type=F32)
         weights, hots = [], []
         for k in range(group):
-            who = 2 * (base + k)
             for h in range(2):
-                along = notes[who, 8 + h : 9 + h, :]
-                mask = (row16 & 3).astype(F32) == notes[who, 10 + h : 11 + h, :]
-                seen = [notes[who + 1, 4 * h + t : 4 * h + t + 1, :] for t in range(MOMENTS)]
+                along = blocks[k][4][h : h + 1]
+                mask = (row16 & 3).astype(F32) == blocks[k][4][2 + h : 3 + h]
+                seen = [blocks[k][2 + h][t : t + 1] for t in range(MOMENTS)]
                 value = jnp.where(
                     row16 < 8,
                     jnp.where(row16 < 4, seen[0], seen[1]),
@@ -343,24 +353,45 @@
     return add_up(rate), add_up(image), image[3 * IMAGE :]
 
 
-def adjoint_kernel(
-    tracks, own, got_even, got_odd, media, saved, notes, obs, owner, cell,
-    lambda_out, mu_out, residual_out, state, sums, small, numbers, sems,
+def run_adjoint(media, saved, state, sums, inject=None):
+    rows = sums.shape[2]
+    sums[...] = jnp.zeros(sums.shape, F32)
+    for step in range(MOMENTS):
+        fast, slow = spans(step, rows)
+        moment = MOMENTS - 1 - step
+        if inject is not None:
+            inject(moment)
+        velocities(state, media, fast)
+
+        def gather(i, r, exx, ezz, shear):
+            if 0 <= r < rows:
+                fxx, fzz, fxz = (saved[moment, k, i, r : r + 8, :] for k in range(3))
+                sums[0, i, r : r + 8, :] += (fxx + fzz) * (exx + ezz)
+                sums[1, i, r : r + 8, :] += 2.0 * (fxx * exx + fzz * ezz) + fxz * shear
+
+        stresses(state, media, slow, step < MOMENTS - 1, gather)
+
+
+def adjoint_rest_kernel(own, got_even, got_odd, media, saved, note, sums, state):
+    del note
+    load_state(state, own, got_even, got_odd, FORWARD, (1, 2))
+    run_adjoint(media, saved, state, sums)
+
+
+def adjoint_top_kernel(
+    tracks, own, got_even, got_odd, media, saved, notes, rest, obs, owner, cell,
+    lambda_out, mu_out, residual_out, state, sums,
 ):
-    copies = fetch((obs, owner, cell), (small, numbers.at[0], numbers.at[1]), sems)
     rows = own.shape[2]
     extent = rows + 2 * EDGE
     depth = lax.axis_index("depth")
-    load_state(state, own, got_even, got_odd, FORWARD)
-    sums[...] = jnp.zeros(sums.shape, F32)
-    for copy in copies:
-        copy.wait()
-    along, row = channel_cells(numbers, rows)
+    load_state(state, own, got_even, got_odd, FORWARD, (0,))
+    along, row = channel_cells(owner, cell, rows)
     rate, seen, count = channel_sums(tracks, rows, notes, along)
     channels = along.shape[1]
     at_own = jnp.where((row_ids(IMAGE, channels) & 3) == row, rate[:, :channels], 0.0)
     traces = [
-        jnp.sum(at_own[4 * t : 4 * t + 4], axis=0, keepdims=True) - small[t : t + 1, :] for t in range(MOMENTS)
+        jnp.sum(at_own[4 * t : 4 * t + 4], axis=0, keepdims=True) - obs[t : t + 1, :] for t in range(MOMENTS)
     ]
     residual_out[...] = jnp.where(
         depth == 0, jnp.concatenate(traces[:2], axis=0), jnp.concatenate(traces[2:], axis=0)
@@ -370,23 +401,13 @@
     lane = lane_ids(extent)
     here = (lane >= EDGE) & (lane < EDGE + FIBRE_ROWS) & (depth == 0)
 
-    for step in range(MOMENTS):
-        fast, slow = spans(step, rows)
-        moment = MOMENTS - 1 - step
+    def inject(moment):
         added = jnp.where(here, turn(turned, EDGE - FIBRE_ROWS * moment), 0.0)
         state[2, 0, PAD : PAD + extent, :] += added
-        velocities(state, media, fast)
-
-        def gather(p, r, exx, ezz, shear):
-            if 0 <= r < rows:
-                fxx, fzz, fxz = (saved[moment, k, p, r : r + 8, :] for k in range(3))
-                sums[0, p, r : r + 8, :] += (fxx + fzz) * (exx + ezz)
-                sums[1, p, r : r + 8, :] += 2.0 * (fxx * exx + fzz * ezz) + fxz * shear
-
-        stresses(state, media, slow, step < MOMENTS - 1, gather)
-
+
+    run_adjoint(media, saved, state, sums, inject)
     for k, out in enumerate((lambda_out, mu_out)):
-        first, last = joined([sums[k, p] for p in range(3)])
+        first, last = joined([sums[k, 0], rest[k, 0], rest[k, 1]])
         out[:, :LANES] = (NEAR * NEAR) * first
         out[:, LANES:] = (NEAR * NEAR) * last
 
@@ -411,7 +432,7 @@
     pinned = lambda array: pltpu.with_memory_space_constraint(array, pltpu.HBM)
     arrays = (velocity, stress, adjoint_velocity, adjoint_stress, buoyancy, lame_lambda, shear_modulus)
     arrays = tuple(pinned(array) for array in arrays)
-    channel_arrays = (pinned(observed), pinned(owner), pinned(cell))
+    channel_arrays = (observed, owner, cell)
     extent = rows + 2 * EDGE
     block = jax.ShapeDtypeStruct((rows, depth_cells), F32)
     length = EDGE + HALO * FIELDS + EDGE - HALO
@@ -420,12 +441,6 @@
     outside = pl.BlockSpec(memory_space=pltpu.HBM)
     anywhere = pl.BlockSpec(memory_space=pl.ANY)
     held = [VMEM(a.shape, F32) for a in arrays]
-    channel_scratch = [
-        VMEM((moments, channels), F32),
-        VMEM((2, 1, channels), jnp.int32),
-        pltpu.SemaphoreType.DMA((3,)),
-    ]
-
     to_depth, *to_track = pl.pallas_call(
         pack_kernel,
         out_shape=(block, edges, edges),
@@ -464,38 +479,70 @@
         name="own_planes",
     )(*arrays, got_depth)
 
-    media, saved, velocity_end, note = pl.pallas_call(
-        forward_kernel,
+    def media_of(planes):
+        return jax.ShapeDtypeStruct((4, planes, extent, LANES), F32)
+
+    def saved_of(planes):
+        return jax.ShapeDtypeStruct((moments, 3, planes, rows, LANES), F32)
+
+    def state_of(planes):
+        return VMEM((5, planes, extent + 2 * PAD, LANES), F32)
+
+    media_top, saved_top, top_end, image = pl.pallas_call(
+        forward_top_kernel,
         out_shape=(
-            jax.ShapeDtypeStruct((4, 3, extent, LANES), F32),
-            jax.ShapeDtypeStruct((moments, 3, 3, rows, LANES), F32),
-            jax.ShapeDtypeStruct(velocity.shape, F32),
-            jax.ShapeDtypeStruct((NOTE, LANES), F32),
+            media_of(1),
+            saved_of(1),
+            jax.ShapeDtypeStruct((2, rows, LANES), F32),
+            jax.ShapeDtypeStruct((IMAGE // 2, LANES), F32),
         ),
-        in_specs=[inside] * 3 + [outside] * 3,
+        in_specs=[inside] * 3,
         out_specs=(inside,) * 4,
-        scratch_shapes=[VMEM((5, 3, extent + 2 * PAD, LANES), F32)] + channel_scratch,
+        scratch_shapes=[state_of(1)],
+        compiler_params=params(),
+        cost_estimate=cost(1),
+        name="forward_top",
+    )(own, got_even, got_odd)
+    image_beside = lax.ppermute(image, "depth", depth_swap)
+    media_rest, saved_rest, velocity_end = pl.pallas_call(
+        forward_rest_kernel,
+        out_shape=(media_of(2), saved_of(2), jax.ShapeDtypeStruct(velocity.shape, F32)),
+        in_specs=[inside] * 4,
+        out_specs=(inside,) * 3,
+        scratch_shapes=[state_of(2)],
+        compiler_params=params(),
+        cost_estimate=cost(2),
+        name="forward_rest",
+    )(own, got_even, got_odd, top_end)
+    note = pl.pallas_call(
+        lambda *refs: note_kernel(rows, *refs),
+        out_shape=jax.ShapeDtypeStruct((tracks, 5, 4, LANES), F32),
+        in_specs=[inside] * 5,
+        out_specs=inside,
+        compiler_params=params(),
+        name="note",
+    )(image, image_beside, *channel_arrays)
+    notes = lax.all_to_all(note, "track", split_axis=0, concat_axis=0, tiled=True)
+    rest = pl.pallas_call(
+        adjoint_rest_kernel,
+        out_shape=jax.ShapeDtypeStruct((2, 2, rows, LANES), F32),
+        in_specs=[inside] * 5 + [anywhere],
+        out_specs=inside,
+        scratch_shapes=[state_of(2)],
         compiler_params=params(),
         cost_estimate=cost(3),
-        name="forward",
-    )(own, got_even, got_odd, *channel_arrays)
-
-    notes = lax.all_gather(note, ("track", "depth"), axis=0, tiled=False)
-
+        name="adjoint_rest",
+    )(own, got_even, got_odd, media_rest, saved_rest, note)
     gradient_lambda, gradient_mu, residual = pl.pallas_call(
-        lambda *refs: adjoint_kernel(tracks, *refs),
+        lambda *refs: adjoint_top_kernel(tracks, *refs),
         out_shape=(block, block, jax.ShapeDtypeStruct((moments // 2, channels), F32)),
-        in_specs=[inside] * 6 + [outside] * 3,
+        in_specs=[inside] * 10,
         out_specs=(inside,) * 3,
-        scratch_shapes=[
-            VMEM((5, 3, extent + 2 * PAD, LANES), F32),
-            VMEM((2, 3, rows, LANES), F32),
-        ]
-        + channel_scratch,
-        compiler_params=params(),
-        cost_estimate=cost(4),
-        name="adjoint",
-    )(own, got_even, got_odd, media, saved, notes, *channel_arrays)
+        scratch_shapes=[state_of(1), VMEM((2, 1, rows, LANES), F32)],
+        compiler_params=params(),
+        cost_estimate=cost(2),
+        name="adjoint_top",
+    )(own, got_even, got_odd, media_top, saved_top, notes, rest, *channel_arrays)
     return gradient_lambda, gradient_mu, velocity_end, residual
 
 

time: 41.7 us -> 32.5 us (0.78)
  blocking collectives: 20.1 us -> 0 us
  starting transfers between devices: 4.08 us -> 10.1 us
  waiting for transfers between devices: 6.34 us -> 11.1 us
    all_gather x1 -> x0, blocking collectives: 20.1 us -> none  [per_device(): notes = lax.all_gather(note, ('track', 'depth'), axis=0, tiled=False)]
    all_to_all x0 -> x1, starting transfers between devices: none -> 5.99 us  [per_device(): lax.all_to_all(note, 'track', split_axis=0, concat_axis=0, tiled=True)]
    all_to_all x0 -> x1, waiting for transfers between devices: none -> 3.65 us  [per_device(): lax.all_to_all(note, 'track', split_axis=0, concat_axis=0, tiled=True)]
    ppermute x0 -> x1, waiting for transfers between devices: none -> 1.19 us  [per_device(): image_beside = lax.ppermute(image, 'depth', depth_swap)]
    pallas_call x2 -> x5, Pallas kernels: 6.89 us -> 6.96 us  [the longest x1 2.11 us: per_device(): pl.pallas_call(forward_rest_kernel, out_shape=(media_of(2), saved_of(2),...]
  transfers between devices with their start and end apart: 3 -> 5, of which waited for: 2 -> 4; matrix products, arithmetic and copies ran while one was open for 0% -> 0% of each run, Pallas kernels for 5% -> 16%
where the time goes in v6:
time: 32.5 us; the launch traced here: 32.3 us
  waiting for transfers between devices  11.1 us (34%)
  Pallas kernels  10.3 us (32%)
  starting transfers between devices  10.1 us (31%)
  between operations  0.71 us (2%)
    all_to_all x1, starting transfers between devices, per_device(): lax.all_to_all(note, 'track', split_axis=0, concat_axis=0, tiled=True)  5.99 us
    ppermute x1, waiting for transfers between devices, per_device(): got_even = lax.ppermute(to_track[0], 'track', swap(0))  5.4 us
    all_to_all x1, waiting for transfers between devices, per_device(): lax.all_to_all(note, 'track', split_axis=0, concat_axis=0, tiled=True)  3.65 us
    ppermute x1, starting transfers between devices, per_device(): got_even = lax.ppermute(to_track[0], 'track', swap(0))  2.91 us
    pallas_call x1, Pallas kernels, per_device(): pl.pallas_call(forward_rest_kernel, out_shape=(media_of(2), saved_of(2),...  2.11 us
    pallas_call x1, Pallas kernels, per_device(): pl.pallas_call(lambda *refs: adjoint_top_kernel(tracks, *refs), out_shape...  1.94 us
    pallas_call x1, Pallas kernels, per_device(): pl.pallas_call(own_kernel, out_shape=jax.ShapeDtypeStruct((FIELDS, 3, row...  1.88 us
    pallas_call x1, Pallas kernels, per_device(): pl.pallas_call(pack_kernel, out_shape=(block, edges, edges), in_specs=[ou...  1.44 us
  transfers between devices with their start and end apart: 5, of which 4 were waited for; matrix products, arithmetic and copies ran while one was open for 0% of the time, Pallas kernels for 16%

profile of v6, /device:TPU:0, one launch (start us, length us, event | category | flops | bytes accessed | tf_op | source)
XLA Modules:
  0.0 32.3 jit_solution(11393887620731664227)
XLA Ops:
  0.6 1.4 %pack.1 = (f32[64,256]{1,0:T(8,128)S(1)}, f32[176,256]{1,0:T(8,128)S(1)}, f32[176,256]{1,0:T(8,128)S(1)}) custom-call(f32[2,64,256]{2,1,0:T(8,128)} %refs_0_.3, f32[3,64,256]{2,1,0:T(8,128)} %refs_1_.3, f32[2,64,256]{2,1,0:T(8,128)} %refs_2_.4, f32[3,64,256]{2,1,0:T(8,128)} %refs_3_.3, f32[64,256]{1,0:T(8,128)} %refs_4_.3, f32[64,256]{1,0:T(8,128)} %refs_5_.3, ...), custom_call_target="tpu_custom_call" | custom-call | bytes 7000000 | tf_op jit(solution)/shard_map/pack/pallas_call | solution.py:444
  2.1 0.5 %collective-permute-start = (f32[64,256]{1,0:T(8,128)S(1)}, f32[64,256]{1,0:T(8,128)S(1)}, u32[]{:S(2)}, u32[]{:S(2)}) collective-permute-start(f32[64,256]{1,0:T(8,128)S(1)} %get-tuple-element.19), channel_id=1, source_target_pairs={{0,1},{1,0},{2,3},{3,2},{4,5},{5,4},{6,7},{7,6},{8,9},{9,8},{10,11... | collective-permute-start | bytes 196616 | tf_op jit(solution)/shard_map/ppermute | solution.py:456
  2.6 0.9 %collective-permute-done.refs_7_.got = f32[64,256]{1,0:T(8,128)S(1)} collective-permute-done((f32[64,256]{1,0:T(8,128)S(1)}, f32[64,256]{1,0:T(8,128)S(1)}, u32[]{:S(2)}, u32[]{:S(2)}) %collective-permute-start) | collective-permute-done | bytes 65568 | tf_op jit(solution)/shard_map/ppermute | solution.py:456
  3.5 2.9 %collective-permute-start.1 = (f32[176,256]{1,0:T(8,128)S(1)}, f32[176,256]{1,0:T(8,128)S(1)}, u32[]{:S(2)}, u32[]{:S(2)}) collective-permute-start(f32[176,256]{1,0:T(8,128)S(1)} %get-tuple-element.22), channel_id=1, source_target_pairs={{0,2},{2,0},{4,6},{6,4},{8,10},{10,8},{12,14},{14,12},{1,3},{3,1},... | collective-permute-start | bytes 540680 | tf_op jit(solution)/shard_map/ppermute | solution.py:469
  6.4 0.7 %collective-permute-start.2 = (f32[176,256]{1,0:T(8,128)S(1)}, f32[176,256]{1,0:T(8,128)S(1)}, u32[]{:S(2)}, u32[]{:S(2)}) collective-permute-start(f32[176,256]{1,0:T(8,128)S(1)} %get-tuple-element.23), channel_id=1, source_target_pairs={{2,4},{4,2},{6,8},{8,6},{10,12},{12,10},{3,5},{5,3},{7,9},{9,7},{1... | collective-permute-start | bytes 540680 | tf_op jit(solution)/shard_map/ppermute | solution.py:468
  7.1 1.9 %own_planes.1.own.refs_0_ = f32[13,3,64,128]{3,2,1,0:T(8,128)S(1)} custom-call(f32[2,64,256]{2,1,0:T(8,128)} %refs_0_.3, f32[3,64,256]{2,1,0:T(8,128)} %refs_1_.3, f32[2,64,256]{2,1,0:T(8,128)} %refs_2_.4, f32[3,64,256]{2,1,0:T(8,128)} %refs_3_.3, f32[64,256]{1,0:T(8,128)} %refs_4_.3, f32[64,256]{1,0:T(8,128)} %refs_5_.3, f32[64,256]{1,0:T(8,128)} %refs_6_.3, ...), custom_call_target="tpu_custom_call" | custom-call | bytes 7000000 | tf_op jit(solution)/shard_map/own_planes/pallas_call | solution.py:471
  9.0 0.0 copy-start
  9.0 0.0 copy-start.1
  9.0 0.0 copy-start.2
  9.0 5.4 %collective-permute-done.1.got_even.refs_1_ = f32[176,256]{1,0:T(8,128)S(1)} collective-permute-done((f32[176,256]{1,0:T(8,128)S(1)}, f32[176,256]{1,0:T(8,128)S(1)}, u32[]{:S(2)}, u32[]{:S(2)}) %collective-permute-start.1) | collective-permute-done | bytes 180256 | tf_op jit(solution)/shard_map/ppermute | solution.py:469
  14.4 0.0 collective-permute-done.2.got_odd.refs_2_
  14.4 1.0 %forward_top.1 = (f32[4,1,96,128]{3,2,1,0:T(8,128)S(1)}, f32[4,3,1,64,128]{4,3,2,1,0:T(8,128)S(1)}, f32[2,64,128]{2,1,0:T(8,128)S(1)}, f32[8,128]{1,0:T(8,128)S(1)}) custom-call(f32[13,3,64,128]{3,2,1,0:T(8,128)S(1)} %own_planes.1.own.refs_0_, f32[176,256]{1,0:T(8,128)S(1)} %collective-permute-done.1.got_even.refs_1_, ...), custom_call_target="tpu_custom_call" | custom-call | bytes 3500000 | tf_op jit(solution)/shard_map/forward_top/pallas_call | solution.py:491
  15.5 0.0 collective-permute-start.3
  15.5 1.2 %collective-permute-done.3.refs_1_ = f32[8,128]{1,0:T(8,128)S(1)} collective-permute-done((f32[8,128]{1,0:T(8,128)S(1)}, f32[8,128]{1,0:T(8,128)S(1)}, u32[]{:S(2)}, u32[]{:S(2)}) %collective-permute-start.3) | collective-permute-done | bytes 4128 | tf_op jit(solution)/shard_map/ppermute | solution.py:506
  16.7 0.0 copy-done
  16.7 0.0 copy-done.1
  16.7 0.0 copy-done.2
  16.7 0.6 %note.1 = f32[8,5,4,128]{3,2,1,0:T(4,128)} custom-call(f32[8,128]{1,0:T(8,128)S(1)} %get-tuple-element.26.refs_0_, f32[8,128]{1,0:T(8,128)S(1)} %collective-permute-done.3.refs_1_, f32[4,256]{1,0:T(4,128)S(1)} %copy-done, s32[1,256]{1,0:T(1,128)S(1)} %bitcast.2, s32[1,256]{1,0:T(1,128)S(1)} %bitcast.4), custom_call_target="tpu_custom_call" | custom-call | tf_op jit(solution)/shard_map/note/pallas_call | solution.py:517
  17.3 6.0 %all-to-all-start = ((f32[8,5,4,128]{3,2,1,0:T(4,128)}), f32[8,5,4,128]{3,2,1,0:T(4,128)S(1)}, u32[]{:S(2)}, u32[]{:S(2)}) async-start(f32[8,5,4,128]{3,2,1,0:T(4,128)} %note.1), calls=%async_computation | async-start | bytes 163840 | tf_op jit(solution)/shard_map/all_to_all | solution.py:525
  23.3 2.1 %forward_rest.1 = (f32[4,2,96,128]{3,2,1,0:T(8,128)S(1)}, f32[4,3,2,64,128]{4,3,2,1,0:T(8,128)S(1)}, f32[2,64,256]{2,1,0:T(8,128)}) custom-call(f32[13,3,64,128]{3,2,1,0:T(8,128)S(1)} %own_planes.1.own.refs_0_, f32[176,256]{1,0:T(8,128)S(1)} %collective-permute-done.1.got_even.refs_1_, f32[176,256]{1,0:T(8,128)S(1)} %collective-permute-done.2.got_odd.refs_2_, ...), custom_call_target="tpu_custom_call" | custom-call | bytes 7000000 | tf_op jit(solution)/shard_map/forward_rest/pallas_call | solution.py:507
  25.4 1.2 %adjoint_rest.1.refs_6_ = f32[2,2,64,128]{3,2,1,0:T(8,128)S(1)} custom-call(f32[13,3,64,128]{3,2,1,0:T(8,128)S(1)} %own_planes.1.own.refs_0_, f32[176,256]{1,0:T(8,128)S(1)} %collective-permute-done.1.got_even.refs_1_, f32[176,256]{1,0:T(8,128)S(1)} %collective-permute-done.2.got_odd.refs_2_, f32[4,2,96,128]{3,2,1,0:T(8,128)S(1)} %get-tuple-element.28.media, ...), custom_call_target="tpu_custom_call" | custom-call | bytes 10500000 | tf_op jit(solution)/shard_map/adjoint_rest/pallas_call | solution.py:526
  26.7 3.7 %all-to-all-done.refs_5_ = f32[8,5,4,128]{3,2,1,0:T(4,128)S(1)} async-done(((f32[8,5,4,128]{3,2,1,0:T(4,128)}), f32[8,5,4,128]{3,2,1,0:T(4,128)S(1)}, u32[]{:S(2)}, u32[]{:S(2)}) %all-to-all-start) | async-done | bytes 81952 | tf_op jit(solution)/shard_map/all_to_all | solution.py:525
  30.3 1.9 %adjoint_top.1 = (f32[64,256]{1,0:T(8,128)}, f32[64,256]{1,0:T(8,128)}, f32[2,256]{1,0:T(2,128)}) custom-call(f32[13,3,64,128]{3,2,1,0:T(8,128)S(1)} %own_planes.1.own.refs_0_, f32[176,256]{1,0:T(8,128)S(1)} %collective-permute-done.1.got_even.refs_1_, f32[176,256]{1,0:T(8,128)S(1)} %collective-permute-done.2.got_odd.refs_2_, ...), custom_call_target="tpu_custom_call" | custom-call | bytes 7000000 | tf_op jit(solution)/shard_map/adjoint_top/pallas_call | solution.py:536
  (1 shorter events, 0.0 us)
Async XLA Ops:
  2.1 1.4 %collective-permute-start = (f32[64,256]{1,0:T(8,128)S(1)}, f32[64,256]{1,0:T(8,128)S(1)}, u32[]{:S(2)}, u32[]{:S(2)}) collective-permute-start(f32[64,256]{1,0:T(8,128)S(1)} %get-tuple-element.19), channel_id=1, source_target_pairs={{0,1},{1,0},{2,3},{3,2},{4,5},{5,4},{6,7},{7,6},{8,9},{9,8},{10,11... | collective-permute-start | bytes 196616 | tf_op jit(solution)/shard_map/ppermute | solution.py:456
  3.5 10.9 %collective-permute-start.1 = (f32[176,256]{1,0:T(8,128)S(1)}, f32[176,256]{1,0:T(8,128)S(1)}, u32[]{:S(2)}, u32[]{:S(2)}) collective-permute-start(f32[176,256]{1,0:T(8,128)S(1)} %get-tuple-element.22), channel_id=1, source_target_pairs={{0,2},{2,0},{4,6},{6,4},{8,10},{10,8},{12,14},{14,12},{1,3},{3,1},... | collective-permute-start | bytes 540680 | tf_op jit(solution)/shard_map/ppermute | solution.py:469
  6.4 8.0 %collective-permute-start.2 = (f32[176,256]{1,0:T(8,128)S(1)}, f32[176,256]{1,0:T(8,128)S(1)}, u32[]{:S(2)}, u32[]{:S(2)}) collective-permute-start(f32[176,256]{1,0:T(8,128)S(1)} %get-tuple-element.23), channel_id=1, source_target_pairs={{2,4},{4,2},{6,8},{8,6},{10,12},{12,10},{3,5},{5,3},{7,9},{9,7},{1... | collective-permute-start | bytes 540680 | tf_op jit(solution)/shard_map/ppermute | solution.py:468
  9.0 7.7 %copy-start = (f32[4,256]{1,0:T(4,128)S(1)}, f32[4,256]{1,0:T(4,128)}, u32[]{:S(2)}) copy-start(f32[4,256]{1,0:T(4,128)} %refs_7_.1) | copy-start | bytes 12292
  9.0 7.7 %copy-start.1 = (s32[256,1]{0,1:T(1,128)S(1)}, s32[256,1]{0,1:T(1,128)}, u32[]{:S(2)}) copy-start(s32[256,1]{0,1:T(1,128)} %param.18) | copy-start | bytes 3076
  9.0 7.7 %copy-start.2 = (s32[256]{0:T(256)S(1)}, s32[256]{0:T(256)}, u32[]{:S(2)}) copy-start(s32[256]{0:T(256)} %param.19) | copy-start | bytes 3076
  15.5 1.2 %collective-permute-start.3 = (f32[8,128]{1,0:T(8,128)S(1)}, f32[8,128]{1,0:T(8,128)S(1)}, u32[]{:S(2)}, u32[]{:S(2)}) collective-permute-start(f32[8,128]{1,0:T(8,128)S(1)} %get-tuple-element.26.refs_0_), channel_id=1, source_target_pairs={{0,1},{1,0},{2,3},{3,2},{4,5},{5,4},{6,7},{7,6},{8,9},{9,8},{10,11... | collective-permute-start | bytes 12296 | tf_op jit(solution)/shard_map/ppermute | solution.py:506
  17.3 13.0 %all-to-all-start = ((f32[8,5,4,128]{3,2,1,0:T(4,128)}), f32[8,5,4,128]{3,2,1,0:T(4,128)S(1)}, u32[]{:S(2)}, u32[]{:S(2)}) async-start(f32[8,5,4,128]{3,2,1,0:T(4,128)} %note.1), calls=%async_computation | async-start | bytes 163840 | tf_op jit(solution)/shard_map/all_to_all | solution.py:525

commit v7 on v6

--- a/solution.py
+++ b/solution.py
@@ -15,6 +15,8 @@
 FORWARD = 8
 ADJOINT = 5
 FIELDS = FORWARD + ADJOINT
+OUTER = EDGE - HALO
+INNER = EDGE + HALO * ADJOINT
 MOMENTS = 4
 IMAGE = MOMENTS * FIBRE_ROWS
 VMEM = pltpu.VMEM
@@ -53,43 +55,75 @@
     return copies
 
 
-def field_refs(velocity, stress, adj_velocity, adj_stress, buoyancy, lame, shear):
-    return (
-        [velocity.at[i] for i in range(2)]
-        + [stress.at[i] for i in range(3)]
-        + [buoyancy, lame, shear]
-        + [adj_velocity.at[i] for i in range(2)]
-        + [adj_stress.at[i] for i in range(3)]
+def field_copies(arrays, held, sems):
+    velocity, stress, adj_velocity, adj_stress, buoyancy, lame, shear = arrays
+    sources = (velocity, stress, buoyancy, lame, shear, adj_velocity, adj_stress)
+    targets = (
+        held.at[pl.ds(0, 2)],
+        held.at[pl.ds(2, 3)],
+        held.at[5],
+        held.at[6],
+        held.at[7],
+        held.at[pl.ds(8, 2)],
+        held.at[pl.ds(10, 3)],
     )
-
-
-def pack_kernel(*refs):
-    sources, depth_out, edge_outs, held, sems = refs[:7], refs[7], refs[8:10], refs[10:17], refs[17]
-    copies = fetch(sources, held, sems)
+    return fetch(sources, targets, sems)
+
+
+def outer_kernel(velocity, stress, buoyancy, lame, shear, even_out, odd_out, strips, sems):
     depth = lax.axis_index("depth")
     even = is_even()
-    fields = field_refs(*held)
-    rows = fields[0].shape[0]
+    rows = buoyancy.shape[0]
+    lanes = pl.ds(pl.multiple_of(depth * LANES, LANES), LANES)
+    sources, targets = [], []
+    for side, row in enumerate((0, rows - EDGE)):
+        span = pl.ds(row, EDGE)
+        sources += [array.at[:, span, lanes] for array in (velocity, stress)]
+        targets += [strips.at[side, pl.ds(0, 2)], strips.at[side, pl.ds(2, 3)]]
+        sources += [array.at[span, lanes] for array in (buoyancy, lame, shear)]
+        targets += [strips.at[side, f] for f in (5, 6, 7)]
+    copies = fetch(sources, targets, sems)
+    for out in (even_out, odd_out):
+        out[:OUTER, :] = jnp.zeros((OUTER, LANES), F32)
+        out[OUTER + HALO * FORWARD :, :] = jnp.zeros((EDGE - HALO, LANES), F32)
+    for copy in copies:
+        copy.wait()
+    for f in range(FORWARD):
+        low, high = strips[0, f, :HALO, :], strips[1, f, EDGE - HALO :, :]
+        at = OUTER + HALO * f
+        even_out[at : at + HALO, :] = jnp.where(even, high, low)
+        odd_out[at : at + HALO, :] = jnp.where(even, low, high)
+
+
+def pack_kernel(*refs):
+    arrays, (held, depth_out, even_out, odd_out), sems = refs[:7], refs[8:12], refs[12]
+    copies = field_copies(arrays, held, sems)
+    depth = lax.axis_index("depth")
+    even = is_even()
+    rows = held.shape[1]
     lane = lane_ids(rows)
-    tail = EDGE + HALO * FIELDS
-    for out in edge_outs:
+    tail = INNER + HALO * 4
+    for out in (even_out, odd_out):
         out[:EDGE, :] = jnp.zeros((EDGE, 2 * LANES), F32)
         out[tail:, :] = jnp.zeros((out.shape[0] - tail, 2 * LANES), F32)
     for copy in copies:
         copy.wait()
     packed = [jnp.zeros((rows, LANES), F32) for _ in range(2)]
-    for f, ref in enumerate(fields):
-        first, last = ref[:, :LANES], ref[:, LANES:]
+    for f in range(FIELDS):
         group, place = divmod(f, FORWARD)
         spot = EDGE * place
         here = (lane >= spot) & (lane < spot + EDGE)
-        edge = jnp.where(depth == 0, last, first)
+        edge = jnp.where(depth == 0, held[f, :, LANES:], held[f, :, :LANES])
         shift = lax.rem(spot + EDGE * (1 - depth), LANES)
         packed[group] = jnp.where(here, pltpu.roll(edge, shift, 1), packed[group])
-        low, high = ref[:HALO, :], ref[rows - HALO :, :]
-        at = EDGE + HALO * f
-        edge_outs[0][at : at + HALO, :] = jnp.where(even, high, low)
-        edge_outs[1][at : at + HALO, :] = jnp.where(even, low, high)
+        if f < FORWARD:
+            low, high = edge[:HALO], edge[rows - HALO :]
+            at, lanes = INNER + HALO * (f % 4), slice(LANES * (f // 4), LANES * (f // 4) + LANES)
+        else:
+            low, high = held[f, :HALO, :], held[f, rows - HALO :, :]
+            at, lanes = EDGE + HALO * place, slice(0, 2 * LANES)
+        even_out[at : at + HALO, lanes] = jnp.where(even, high, low)
+        odd_out[at : at + HALO, lanes] = jnp.where(even, low, high)
     depth_out[:, :LANES] = packed[0]
     depth_out[:, LANES:] = packed[1]
 
@@ -110,65 +144,86 @@
     two.wait()
 
 
-def windows(f, first, last, halo):
+def window(plane, f, outer, other, halo):
     depth = lax.axis_index("depth")
-    lane = lane_ids(first.shape[0])
-    shift = lax.rem(LANES - EDGE * (f % FORWARD) + (LANES - EDGE) * (1 - depth), LANES)
-    beside = pltpu.roll(halo, shift, 1)
-    return [
-        jnp.where(lane >= EDGE, turn(first, EDGE), jnp.where(depth == 1, beside, 0.0)),
-        jnp.where(lane < LANES // 2, turn(first, LANES // 2), turn(last, LANES // 2)),
-        jnp.where(lane < LANES - EDGE, turn(last, -EDGE), jnp.where(depth == 0, beside, 0.0)),
-    ]
-
-
-def joined(planes):
-    lane = lane_ids(planes[0].shape[0])
-    middle = turn(planes[1], LANES // 2)
-    return (
-        jnp.where(lane < 88, turn(planes[0], -EDGE), middle),
-        jnp.where(lane < 40, middle, turn(planes[2], EDGE)),
-    )
-
-
-def own_kernel(*refs):
-    sources, got_depth, planes_out, held, sems = refs[:7], refs[7], refs[8], refs[9:16], refs[16]
-    for copy in fetch(sources, held, sems):
-        copy.wait()
-    for f, ref in enumerate(field_refs(*held)):
-        col = LANES * (f // FORWARD)
-        planes = windows(f, ref[:, :LANES], ref[:, LANES:], got_depth[:, col : col + LANES])
-        for p in range(3):
-            planes_out[f, p] = planes[p]
-
-
-def halo_windows(f, got_even, got_odd):
-    even = is_even()
-    high = EDGE + HALO * f
-    low = high - (EDGE - HALO)
-    col = LANES * (f // FORWARD)
-    corner_even, corner_odd = got_even[:EDGE, col : col + LANES], got_odd[:EDGE, col : col + LANES]
-    left = jnp.where(even, got_odd[low : low + EDGE, :], got_even[low : low + EDGE, :])
-    right = jnp.where(even, got_even[high : high + EDGE, :], got_odd[high : high + EDGE, :])
-    left_halo = jnp.where(even, corner_odd, corner_even)
-    right_halo = jnp.where(even, corner_even, corner_odd)
-    return (
-        windows(f, left[:, :LANES], left[:, LANES:], left_halo),
-        windows(f, right[:, :LANES], right[:, LANES:], right_halo),
-    )
-
-
-def load_state(state, own, got_even, got_odd, base, planes):
-    rows = own.shape[2]
-    extent = rows + 2 * EDGE
+    surface = depth == 0
+    lane = lane_ids(outer.shape[0])
+    low = jnp.where(surface, lane, LANES - 1 - lane)
+    if plane == 0:
+        shift = jnp.where(surface, EDGE, LANES - EDGE)
+        return jnp.where(low >= EDGE, pltpu.roll(outer, shift, 1), 0.0)
+    if plane == 1:
+        return jnp.where(low < LANES // 2, turn(outer, LANES // 2), turn(other, LANES // 2))
+    shift = jnp.where(surface, LANES - EDGE, EDGE)
+    beside = lax.rem(LANES - EDGE * (f % FORWARD) + (LANES - EDGE) * (1 - depth), LANES)
+    return jnp.where(low < LANES - EDGE, pltpu.roll(other, shift, 1), pltpu.roll(halo, beside, 1))
+
+
+def split(value):
+    surface = lax.axis_index("depth") == 0
+    first, last = value[:, :LANES], value[:, LANES:]
+    return jnp.where(surface, first, last), jnp.where(surface, last, first)
+
+
+def joined(outer, middle, inner):
+    surface = lax.axis_index("depth") == 0
+    lane = lane_ids(outer.shape[0])
+    first, last = jnp.where(surface, outer, inner), jnp.where(surface, inner, outer)
+    middle = turn(middle, LANES // 2)
+    return jnp.where(lane < 88, turn(first, -EDGE), middle), jnp.where(lane < 40, middle, turn(last, EDGE))
+
+
+class Blocks:
+    def __init__(self, held, got_depth, outer, bulk):
+        self.held, self.got_depth, self.outer, self.bulk = held, got_depth, outer, bulk
+
+    def from_edges(self, pair, side, at, lanes):
+        even_got, odd_got = pair
+        span = slice(at - (EDGE - HALO), at + HALO) if side == 0 else slice(at, at + EDGE)
+        use_odd = is_even() if side == 0 else ~is_even()
+        return jnp.where(use_odd, odd_got[span, lanes], even_got[span, lanes])
+
+    def edge_windows(self, f, side, planes):
+        whole = slice(0, LANES)
+        inner = planes != (0,)
+        outer = other = halo = None
+        if f < FORWARD:
+            outer = self.from_edges(self.outer, side, OUTER + HALO * f, whole)
+            if inner:
+                lanes = slice(LANES * (f // 4), LANES * (f // 4) + LANES)
+                other = self.from_edges(self.bulk, side, INNER + HALO * (f % 4), lanes)
+        else:
+            at = EDGE + HALO * (f - FORWARD)
+            outer, other = split(self.from_edges(self.bulk, side, at, slice(0, 2 * LANES)))
+        if inner:
+            even_got, odd_got = self.bulk
+            lanes = slice(LANES * (f // FORWARD), LANES * (f // FORWARD) + LANES)
+            use_odd = is_even() if side == 0 else ~is_even()
+            halo = jnp.where(use_odd, odd_got[:EDGE, lanes], even_got[:EDGE, lanes])
+        return [window(p, f, outer, other, halo) for p in planes]
+
+    def own_windows(self, f, planes):
+        outer, other = split(self.held[f])
+        halo = None
+        if planes != (0,):
+            col = LANES * (f // FORWARD)
+            halo = self.got_depth[:, col : col + LANES]
+        return [window(p, f, outer, other, halo) for p in planes]
+
+    def windows(self, f, planes):
+        rows = self.held.shape[1]
+        sets = self.edge_windows(f, 0, planes), self.own_windows(f, planes), self.edge_windows(f, 1, planes)
+        return [[(at, part[i]) for at, part in zip((0, EDGE, EDGE + rows), sets)] for i in range(len(planes))]
+
+
+def load_state(state, blocks, base, planes):
+    extent = blocks.held.shape[1] + 2 * EDGE
     for f in range(5):
-        below, above = halo_windows(base + f, got_even, got_odd)
-        for i, p in enumerate(planes):
+        for i, parts in enumerate(blocks.windows(base + f, planes)):
             state[f, i, :PAD, :] = jnp.zeros((PAD, LANES), F32)
-            state[f, i, PAD : PAD + EDGE, :] = below[p]
-            state[f, i, PAD + EDGE : PAD + EDGE + rows, :] = own[base + f, p]
-            state[f, i, PAD + EDGE + rows : PAD + extent, :] = above[p]
             state[f, i, PAD + extent :, :] = jnp.zeros((PAD, LANES), F32)
+            for at, part in parts:
+                state[f, i, PAD + at : PAD + at + part.shape[0], :] = part
 
 
 def velocities(state, media, span):
@@ -217,21 +272,19 @@
     return inner, inner if step < MOMENTS - 1 else (EDGE // 8, tiles - EDGE // 8)
 
 
-def run_forward(own, got_even, got_odd, media, saved, state, planes):
-    rows = own.shape[2]
-    parts = []
-    for f in (5, 6, 7):
-        below, above = halo_windows(f, got_even, got_odd)
-        parts.append([(below[p], own[f, p], above[p]) for p in planes])
+def run_forward(blocks, media, saved, state, planes):
+    rows = blocks.held.shape[1]
+    given = [blocks.windows(f, planes) for f in (5, 6, 7)]
     for i in range(len(planes)):
-        for k, at in enumerate((0, EDGE, EDGE + rows)):
-            b, lam, mu = (NEAR * parts[m][i][k] for m in range(3))
+        for k in range(3):
+            at = given[0][i][k][0]
+            b, lam, mu = (NEAR * given[m][i][k][1] for m in range(3))
             span = slice(at, at + b.shape[0])
             media[0, i, span, :] = b
             media[1, i, span, :] = lam + 2.0 * mu
             media[2, i, span, :] = lam
             media[3, i, span, :] = mu
-    load_state(state, own, got_even, got_odd, 0, planes)
+    load_state(state, blocks, 0, planes)
     for step in range(MOMENTS):
         fast, slow = spans(step, rows)
         velocities(state, media, fast)
@@ -245,9 +298,10 @@
         stresses(state, media, slow, step < MOMENTS - 1, save)
 
 
-def forward_top_kernel(own, got_even, got_odd, media, saved, end_out, image_out, state):
-    run_forward(own, got_even, got_odd, media, saved, state, (0,))
-    rows = own.shape[2]
+def forward_top_kernel(held, outer_even, outer_odd, media, saved, end_out, image_out, state):
+    blocks = Blocks(held, None, (outer_even, outer_odd), None)
+    run_forward(blocks, media, saved, state, (0,))
+    rows = held.shape[1]
     top = PAD + EDGE
     for f in range(2):
         end_out[f] = state[f, 0, top : top + rows, :]
@@ -262,13 +316,15 @@
     image_out[...] = jnp.concatenate([turned[:half], turned[half:IMAGE]], axis=1)
 
 
-def forward_rest_kernel(own, got_even, got_odd, top_end, media, saved, end_out, state):
-    run_forward(own, got_even, got_odd, media, saved, state, (1, 2))
-    rows = own.shape[2]
+def forward_rest_kernel(
+    held, got_depth, outer_even, outer_odd, even, odd, top_end, media, saved, end_out, state
+):
+    blocks = Blocks(held, got_depth, (outer_even, outer_odd), (even, odd))
+    run_forward(blocks, media, saved, state, (1, 2))
+    rows = held.shape[1]
     top = PAD + EDGE
     for f in range(2):
-        rest = [state[f, i, top : top + rows, :] for i in range(2)]
-        first, last = joined([top_end[f]] + rest)
+        first, last = joined(top_end[f], *(state[f, i, top : top + rows, :] for i in range(2)))
         end_out[f, :, :LANES] = first
         end_out[f, :, LANES:] = last
 
@@ -372,20 +428,20 @@
         stresses(state, media, slow, step < MOMENTS - 1, gather)
 
 
-def adjoint_rest_kernel(own, got_even, got_odd, media, saved, note, sums, state):
+def adjoint_rest_kernel(held, got_depth, even, odd, media, saved, note, sums, state):
     del note
-    load_state(state, own, got_even, got_odd, FORWARD, (1, 2))
+    load_state(state, Blocks(held, got_depth, None, (even, odd)), FORWARD, (1, 2))
     run_adjoint(media, saved, state, sums)
 
 
 def adjoint_top_kernel(
-    tracks, own, got_even, got_odd, media, saved, notes, rest, obs, owner, cell,
+    tracks, held, even, odd, media, saved, notes, rest, obs, owner, cell,
     lambda_out, mu_out, residual_out, state, sums,
 ):
-    rows = own.shape[2]
+    rows = held.shape[1]
     extent = rows + 2 * EDGE
     depth = lax.axis_index("depth")
-    load_state(state, own, got_even, got_odd, FORWARD, (0,))
+    load_state(state, Blocks(held, None, None, (even, odd)), FORWARD, (0,))
     along, row = channel_cells(owner, cell, rows)
     rate, seen, count = channel_sums(tracks, rows, notes, along)
     channels = along.shape[1]
@@ -407,7 +463,7 @@
 
     run_adjoint(media, saved, state, sums, inject)
     for k, out in enumerate((lambda_out, mu_out)):
-        first, last = joined([sums[k, 0], rest[k, 0], rest[k, 1]])
+        first, last = joined(sums[k, 0], rest[k, 0], rest[k, 1])
         out[:, :LANES] = (NEAR * NEAR) * first
         out[:, LANES:] = (NEAR * NEAR) * last
 
@@ -435,26 +491,38 @@
     channel_arrays = (observed, owner, cell)
     extent = rows + 2 * EDGE
     block = jax.ShapeDtypeStruct((rows, depth_cells), F32)
-    length = EDGE + HALO * FIELDS + EDGE - HALO
-    edges = jax.ShapeDtypeStruct((length + (-length) % 8, depth_cells), F32)
+    outer_edges = jax.ShapeDtypeStruct((OUTER + HALO * FORWARD + EDGE - HALO, LANES), F32)
+    edges = jax.ShapeDtypeStruct((INNER + HALO * 4 + EDGE - HALO, depth_cells), F32)
     inside = pl.BlockSpec(memory_space=VMEM)
     outside = pl.BlockSpec(memory_space=pltpu.HBM)
     anywhere = pl.BlockSpec(memory_space=pl.ANY)
-    held = [VMEM(a.shape, F32) for a in arrays]
-    to_depth, *to_track = pl.pallas_call(
+    swap = lambda k: [pair for i in range(k, tracks - 1, 2) for pair in ((i, i + 1), (i + 1, i))]
+    to_even, to_odd = pl.pallas_call(
+        outer_kernel,
+        out_shape=(outer_edges, outer_edges),
+        in_specs=[outside] * 5,
+        out_specs=(inside,) * 2,
+        scratch_shapes=[VMEM((2, FORWARD, EDGE, LANES), F32), pltpu.SemaphoreType.DMA((10,))],
+        compiler_params=params(),
+        cost_estimate=cost(1),
+        name="outer",
+    )(*arrays[:2], *arrays[4:])
+    outer_odd = lax.ppermute(to_odd, "track", swap(1))
+    outer_even = lax.ppermute(to_even, "track", swap(0))
+
+    held, to_depth, to_even, to_odd = pl.pallas_call(
         pack_kernel,
-        out_shape=(block, edges, edges),
-        in_specs=[outside] * 7,
-        out_specs=(inside,) * 3,
-        scratch_shapes=held + [pltpu.SemaphoreType.DMA((7,))],
+        out_shape=(jax.ShapeDtypeStruct((FIELDS, rows, depth_cells), F32), block, edges, edges),
+        in_specs=[outside] * 7 + [anywhere],
+        out_specs=(inside,) * 4,
+        scratch_shapes=[pltpu.SemaphoreType.DMA((7,))],
         compiler_params=params(),
         cost_estimate=cost(2),
         name="pack",
-    )(*arrays)
-
+    )(*arrays, to_even)
     depth_swap = [(0, 1), (1, 0)]
     got_depth = lax.ppermute(to_depth, "depth", depth_swap)
-    to_track = pl.pallas_call(
+    to_even, to_odd = pl.pallas_call(
         corner_kernel,
         out_shape=(edges, edges),
         in_specs=[anywhere] * 3,
@@ -463,21 +531,9 @@
         scratch_shapes=[pltpu.SemaphoreType.DMA((2,))],
         compiler_params=params(),
         name="corners",
-    )(got_depth, *to_track)
-    swap = lambda k: [pair for i in range(k, tracks - 1, 2) for pair in ((i, i + 1), (i + 1, i))]
-    got_odd = lax.ppermute(to_track[1], "track", swap(1))
-    got_even = lax.ppermute(to_track[0], "track", swap(0))
-
-    own = pl.pallas_call(
-        own_kernel,
-        out_shape=jax.ShapeDtypeStruct((FIELDS, 3, rows, LANES), F32),
-        in_specs=[outside] * 7 + [inside],
-        out_specs=inside,
-        scratch_shapes=held + [pltpu.SemaphoreType.DMA((7,))],
-        compiler_params=params(),
-        cost_estimate=cost(2),
-        name="own_planes",
-    )(*arrays, got_depth)
+    )(got_depth, to_even, to_odd)
+    got_odd = lax.ppermute(to_odd, "track", swap(1))
+    got_even = lax.ppermute(to_even, "track", swap(0))
 
     def media_of(planes):
         return jax.ShapeDtypeStruct((4, planes, extent, LANES), F32)
@@ -502,18 +558,18 @@
         compiler_params=params(),
         cost_estimate=cost(1),
         name="forward_top",
-    )(own, got_even, got_odd)
+    )(held, outer_even, outer_odd)
     image_beside = lax.ppermute(image, "depth", depth_swap)
     media_rest, saved_rest, velocity_end = pl.pallas_call(
         forward_rest_kernel,
         out_shape=(media_of(2), saved_of(2), jax.ShapeDtypeStruct(velocity.shape, F32)),
-        in_specs=[inside] * 4,
+        in_specs=[inside] * 7,
         out_specs=(inside,) * 3,
         scratch_shapes=[state_of(2)],
         compiler_params=params(),
         cost_estimate=cost(2),
         name="forward_rest",
-    )(own, got_even, got_odd, top_end)
+    )(held, got_depth, outer_even, outer_odd, got_even, got_odd, top_end)
     note = pl.pallas_call(
         lambda *refs: note_kernel(rows, *refs),
         out_shape=jax.ShapeDtypeStruct((tracks, 5, 4, LANES), F32),
@@ -526,13 +582,13 @@
     rest = pl.pallas_call(
         adjoint_rest_kernel,
         out_shape=jax.ShapeDtypeStruct((2, 2, rows, LANES), F32),
-        in_specs=[inside] * 5 + [anywhere],
+        in_specs=[inside] * 6 + [anywhere],
         out_specs=inside,
         scratch_shapes=[state_of(2)],
         compiler_params=params(),
         cost_estimate=cost(3),
         name="adjoint_rest",
-    )(own, got_even, got_odd, media_rest, saved_rest, note)
+    )(held, got_depth, got_even, got_odd, media_rest, saved_rest, note)
     gradient_lambda, gradient_mu, residual = pl.pallas_call(
         lambda *refs: adjoint_top_kernel(tracks, *refs),
         out_shape=(block, block, jax.ShapeDtypeStruct((moments // 2, channels), F32)),
@@ -542,7 +598,7 @@
         compiler_params=params(),
         cost_estimate=cost(2),
         name="adjoint_top",
-    )(own, got_even, got_odd, media_top, saved_top, notes, rest, *channel_arrays)
+    )(held, got_even, got_odd, media_top, saved_top, notes, rest, *channel_arrays)
     return gradient_lambda, gradient_mu, velocity_end, residual
 
 

time: 32.5 us -> 34.5 us (1.062); the launches traced: 32.3 us -> 33.9 us
  starting transfers between devices: 10.1 us -> 16.4 us
  waiting for transfers between devices: 11.1 us -> 6.09 us
  local copies, waits for them, and re-layouts: 0.02 us -> 0.68 us
    all_to_all x1, waiting for transfers between devices: 3.65 us -> 0.01 us  [per_device(): lax.all_to_all(note, 'track', split_axis=0, concat_axis=0, tiled=True)]
    all_to_all x1, starting transfers between devices: 5.99 us -> 9.41 us  [per_device(): lax.all_to_all(note, 'track', split_axis=0, concat_axis=0, tiled=True)]
    ppermute x2 -> x4, starting transfers between devices: 3.57 us -> 6.37 us  [the longest x1 3 us: per_device(): outer_even = lax.ppermute(to_even, 'track', swap(0))]
    ppermute x1, waiting for transfers between devices: 0.9 us -> 0.01 us  [per_device(): got_depth = lax.ppermute(to_depth, 'depth', depth_swap)]
    pallas_call x2, Pallas kernels: 3.31 us -> 2.43 us  [the longest x1 1.47 us: per_device(): pl.pallas_call(pack_kernel, out_shape=(jax.ShapeDtypeStruct((FIELDS, rows...]
    unnamed x6, local copies, waits for them, and re-layouts: 0.02 us -> 0.68 us
    ppermute x1, starting transfers between devices: 0.01 us -> 0.5 us  [per_device(): image_beside = lax.ppermute(image, 'depth', depth_swap)]
    ppermute x1, starting transfers between devices: 0.52 us -> 0.07 us  [per_device(): got_depth = lax.ppermute(to_depth, 'depth', depth_swap)]
  transfers between devices with their start and end apart: 5 -> 7, of which waited for: 4 -> 2; matrix products, arithmetic and copies ran while one was open for 0% -> 0% of each run, Pallas kernels for 16% -> 21%
where the time goes in v7:
time: 34.5 us; the launch traced here: 33.9 us
  starting transfers between devices  16.4 us (48%)
  Pallas kernels  10 us (29%)
  waiting for transfers between devices  6.09 us (18%)
  between operations  0.73 us (2%)
  local copies, waits for them, and re-layouts  0.68 us (2%)
    all_to_all x1, starting transfers between devices, per_device(): lax.all_to_all(note, 'track', split_axis=0, concat_axis=0, tiled=True)  9.41 us
    ppermute x1, waiting for transfers between devices, per_device(): got_even = lax.ppermute(to_even, 'track', swap(0))  5.25 us
    ppermute x1, starting transfers between devices, per_device(): outer_even = lax.ppermute(to_even, 'track', swap(0))  3 us
    pallas_call x1, Pallas kernels, per_device(): pl.pallas_call(forward_rest_kernel, out_shape=(media_of(2), saved_of(2),...  2.38 us
    ppermute x1, starting transfers between devices, per_device(): got_even = lax.ppermute(to_even, 'track', swap(0))  2.06 us
    pallas_call x1, Pallas kernels, per_device(): pl.pallas_call(lambda *refs: adjoint_top_kernel(tracks, *refs), out_shape...  1.97 us
    pallas_call x1, Pallas kernels, per_device(): pl.pallas_call(pack_kernel, out_shape=(jax.ShapeDtypeStruct((FIELDS, rows...  1.47 us
    pallas_call x1, Pallas kernels, per_device(): pl.pallas_call(adjoint_rest_kernel, out_shape=jax.ShapeDtypeStruct((2, 2,...  1.47 us
  transfers between devices with their start and end apart: 7, of which 2 were waited for; matrix products, arithmetic and copies ran while one was open for 0% of the time, Pallas kernels for 21%

profile of v7, /device:TPU:0, one launch (start us, length us, event | category | flops | bytes accessed | tf_op | source)
XLA Modules:
  0.0 33.9 jit_solution(7071619385870133128)
XLA Ops:
  0.6 1.0 %outer.1 = (f32[104,128]{1,0:T(8,128)S(1)}, f32[104,128]{1,0:T(8,128)S(1)}) custom-call(f32[2,64,256]{2,1,0:T(8,128)} %refs_0_.1, f32[3,64,256]{2,1,0:T(8,128)} %refs_1_.1, f32[64,256]{1,0:T(8,128)} %refs_4_.1, f32[64,256]{1,0:T(8,128)} %refs_5_.1, f32[64,256]{1,0:T(8,128)} %refs_6_.1), custom_call_target="tpu_custom_call" | custom-call | bytes 3500000 | tf_op jit(solution)/shard_map/outer/pallas_call | solution.py:500
  1.6 3.0 %collective-permute-start.3 = (f32[104,128]{1,0:T(8,128)S(1)}, f32[104,128]{1,0:T(8,128)S(1)}, u32[]{:S(2)}, u32[]{:S(2)}) collective-permute-start(f32[104,128]{1,0:T(8,128)S(1)} %get-tuple-element.22.refs_7_), channel_id=1, source_target_pairs={{0,2},{2,0},{4,6},{6,4},{8,10},{10,8},{12,14},{14,12},{1,3},{3,1},... | collective-permute-start | bytes 159752 | tf_op jit(solution)/shard_map/ppermute | solution.py:511
  4.6 0.7 %collective-permute-start.4 = (f32[104,128]{1,0:T(8,128)S(1)}, f32[104,128]{1,0:T(8,128)S(1)}, u32[]{:S(2)}, u32[]{:S(2)}) collective-permute-start(f32[104,128]{1,0:T(8,128)S(1)} %get-tuple-element.29), channel_id=1, source_target_pairs={{2,4},{4,2},{6,8},{8,6},{10,12},{12,10},{3,5},{5,3},{7,9},{9,7},{1... | collective-permute-start | bytes 159752 | tf_op jit(solution)/shard_map/ppermute | solution.py:510
  5.3 1.5 %pack.1 = (f32[13,64,256]{2,1,0:T(8,128)S(1)}, f32[64,256]{1,0:T(8,128)S(1)}, f32[128,256]{1,0:T(8,128)S(1)}, f32[128,256]{1,0:T(8,128)S(1)}) custom-call(f32[2,64,256]{2,1,0:T(8,128)} %refs_0_.1, f32[3,64,256]{2,1,0:T(8,128)} %refs_1_.1, f32[2,64,256]{2,1,0:T(8,128)} %refs_2_.2, f32[3,64,256]{2,1,0:T(8,128)} %refs_3_.1, f32[64,256]{1,0:T(8,128)} %refs_4_.1, ...), custom_call_target="tpu_custom_call" | custom-call | bytes 7000000 | tf_op jit(solution)/shard_map/pack/pallas_call | solution.py:513
  6.7 0.1 collective-permute-start
  6.8 0.0 collective-permute-done.3.outer_even
  6.8 0.0 collective-permute-done.4.outer_odd
  6.8 0.0 copy-start.2
  6.9 1.0 %forward_top.1 = (f32[4,1,96,128]{3,2,1,0:T(8,128)S(1)}, f32[4,3,1,64,128]{4,3,2,1,0:T(8,128)S(1)}, f32[2,64,128]{2,1,0:T(8,128)S(1)}, f32[8,128]{1,0:T(8,128)S(1)}) custom-call(f32[13,64,256]{2,1,0:T(8,128)S(1)} %get-tuple-element.23.held.refs_0_, f32[104,128]{1,0:T(8,128)S(1)} %collective-permute-done.3.outer_even, ...), custom_call_target="tpu_custom_call" | custom-call | bytes 3500000 | tf_op jit(solution)/shard_map/forward_top/pallas_call | solution.py:547
  7.9 0.0 copy-start
  7.9 0.5 %collective-permute-start.5 = (f32[8,128]{1,0:T(8,128)S(1)}, f32[8,128]{1,0:T(8,128)S(1)}, u32[]{:S(2)}, u32[]{:S(2)}) collective-permute-start(f32[8,128]{1,0:T(8,128)S(1)} %get-tuple-element.32.refs_0_), channel_id=1, source_target_pairs={{0,1},{1,0},{2,3},{3,2},{4,5},{5,4},{6,7},{7,6},{8,9},{9,8},{10,11... | collective-permute-start | bytes 12296 | tf_op jit(solution)/shard_map/ppermute | solution.py:562
  8.4 0.8 %collective-permute-done.5.refs_1_ = f32[8,128]{1,0:T(8,128)S(1)} collective-permute-done((f32[8,128]{1,0:T(8,128)S(1)}, f32[8,128]{1,0:T(8,128)S(1)}, u32[]{:S(2)}, u32[]{:S(2)}) %collective-permute-start.5) | collective-permute-done | bytes 4128 | tf_op jit(solution)/shard_map/ppermute | solution.py:562
  9.2 0.0 copy-start.1
  9.2 0.0 copy-done.2
  9.2 0.0 copy-done
  9.2 0.7 %copy-done.1 = s32[256,1]{0,1:T(1,128)S(1)} copy-done((s32[256,1]{0,1:T(1,128)S(1)}, s32[256,1]{0,1:T(1,128)}, u32[]{:S(2)}) %copy-start.1) | copy-done | bytes 1048
  9.9 0.7 %note.1 = f32[8,5,4,128]{3,2,1,0:T(4,128)} custom-call(f32[8,128]{1,0:T(8,128)S(1)} %get-tuple-element.32.refs_0_, f32[8,128]{1,0:T(8,128)S(1)} %collective-permute-done.5.refs_1_, f32[4,256]{1,0:T(4,128)S(1)} %copy-done, s32[1,256]{1,0:T(1,128)S(1)} %bitcast.2, s32[1,256]{1,0:T(1,128)S(1)} %bitcast.4), custom_call_target="tpu_custom_call" | custom-call | tf_op jit(solution)/shard_map/note/pallas_call | solution.py:573
  10.6 9.4 %all-to-all-start = ((f32[8,5,4,128]{3,2,1,0:T(4,128)}), f32[8,5,4,128]{3,2,1,0:T(4,128)S(1)}, u32[]{:S(2)}, u32[]{:S(2)}) async-start(f32[8,5,4,128]{3,2,1,0:T(4,128)} %note.1), calls=%async_computation | async-start | bytes 163840 | tf_op jit(solution)/shard_map/all_to_all | solution.py:581
  20.0 0.0 collective-permute-done.got.got_depth
  20.0 0.1 corners.1
  20.1 2.1 %collective-permute-start.1 = (f32[128,256]{1,0:T(8,128)S(1)}, f32[128,256]{1,0:T(8,128)S(1)}, u32[]{:S(2)}, u32[]{:S(2)}) collective-permute-start(f32[128,256]{1,0:T(8,128)S(1)} %get-tuple-element.27), channel_id=1, source_target_pairs={{0,2},{2,0},{4,6},{6,4},{8,10},{10,8},{12,14},{14,12},{1,3},{3,1},... | collective-permute-start | bytes 393224 | tf_op jit(solution)/shard_map/ppermute | solution.py:536
  22.1 0.7 %collective-permute-start.2 = (f32[128,256]{1,0:T(8,128)S(1)}, f32[128,256]{1,0:T(8,128)S(1)}, u32[]{:S(2)}, u32[]{:S(2)}) collective-permute-start(f32[128,256]{1,0:T(8,128)S(1)} %get-tuple-element.28), channel_id=1, source_target_pairs={{2,4},{4,2},{6,8},{8,6},{10,12},{12,10},{3,5},{5,3},{7,9},{9,7},{1... | collective-permute-start | bytes 393224 | tf_op jit(solution)/shard_map/ppermute | solution.py:535
  22.8 5.3 %collective-permute-done.1.even.refs_1_ = f32[128,256]{1,0:T(8,128)S(1)} collective-permute-done((f32[128,256]{1,0:T(8,128)S(1)}, f32[128,256]{1,0:T(8,128)S(1)}, u32[]{:S(2)}, u32[]{:S(2)}) %collective-permute-start.1) | collective-permute-done | bytes 131104 | tf_op jit(solution)/shard_map/ppermute | solution.py:536
  28.0 0.0 collective-permute-done.2.odd.refs_2_
  28.0 2.4 %forward_rest.1 = (f32[4,2,96,128]{3,2,1,0:T(8,128)S(1)}, f32[4,3,2,64,128]{4,3,2,1,0:T(8,128)S(1)}, f32[2,64,256]{2,1,0:T(8,128)}) custom-call(f32[13,64,256]{2,1,0:T(8,128)S(1)} %get-tuple-element.23.held.refs_0_, f32[64,256]{1,0:T(8,128)S(1)} %collective-permute-done.got.got_depth, f32[104,128]{1,0:T(8,128)S(1)} %collective-permute-done.3.outer_even, ...), custom_call_target="tpu_custom_call" | custom-call | bytes 7000000 | tf_op jit(solution)/shard_map/forward_rest/pallas_call | solution.py:563
  30.4 1.5 %adjoint_rest.1.refs_6_ = f32[2,2,64,128]{3,2,1,0:T(8,128)S(1)} custom-call(f32[13,64,256]{2,1,0:T(8,128)S(1)} %get-tuple-element.23.held.refs_0_, f32[64,256]{1,0:T(8,128)S(1)} %collective-permute-done.got.got_depth, f32[128,256]{1,0:T(8,128)S(1)} %collective-permute-done.1.even.refs_1_, f32[128,256]{1,0:T(8,128)S(1)} %collective-permute-done.2.odd.refs_2_, ...), custom_call_target="tpu_custom_call" | custom-call | bytes 10500000 | tf_op jit(solution)/shard_map/adjoint_rest/pallas_call | solution.py:582
  31.9 0.0 all-to-all-done.refs_5_
  31.9 2.0 %adjoint_top.1 = (f32[64,256]{1,0:T(8,128)}, f32[64,256]{1,0:T(8,128)}, f32[2,256]{1,0:T(2,128)}) custom-call(f32[13,64,256]{2,1,0:T(8,128)S(1)} %get-tuple-element.23.held.refs_0_, f32[128,256]{1,0:T(8,128)S(1)} %collective-permute-done.1.even.refs_1_, f32[128,256]{1,0:T(8,128)S(1)} %collective-permute-done.2.odd.refs_2_, ...), custom_call_target="tpu_custom_call" | custom-call | bytes 7000000 | tf_op jit(solution)/shard_map/adjoint_top/pallas_call | solution.py:592
Async XLA Ops:
  1.6 5.2 %collective-permute-start.3 = (f32[104,128]{1,0:T(8,128)S(1)}, f32[104,128]{1,0:T(8,128)S(1)}, u32[]{:S(2)}, u32[]{:S(2)}) collective-permute-start(f32[104,128]{1,0:T(8,128)S(1)} %get-tuple-element.22.refs_7_), channel_id=1, source_target_pairs={{0,2},{2,0},{4,6},{6,4},{8,10},{10,8},{12,14},{14,12},{1,3},{3,1},... | collective-permute-start | bytes 159752 | tf_op jit(solution)/shard_map/ppermute | solution.py:511
  4.6 2.2 %collective-permute-start.4 = (f32[104,128]{1,0:T(8,128)S(1)}, f32[104,128]{1,0:T(8,128)S(1)}, u32[]{:S(2)}, u32[]{:S(2)}) collective-permute-start(f32[104,128]{1,0:T(8,128)S(1)} %get-tuple-element.29), channel_id=1, source_target_pairs={{2,4},{4,2},{6,8},{8,6},{10,12},{12,10},{3,5},{5,3},{7,9},{9,7},{1... | collective-permute-start | bytes 159752 | tf_op jit(solution)/shard_map/ppermute | solution.py:510
  6.7 13.2 %collective-permute-start = (f32[64,256]{1,0:T(8,128)S(1)}, f32[64,256]{1,0:T(8,128)S(1)}, u32[]{:S(2)}, u32[]{:S(2)}) collective-permute-start(f32[64,256]{1,0:T(8,128)S(1)} %get-tuple-element.24), channel_id=1, source_target_pairs={{0,1},{1,0},{2,3},{3,2},{4,5},{5,4},{6,7},{7,6},{8,9},{9,8},{10,11... | collective-permute-start | bytes 196616 | tf_op jit(solution)/shard_map/ppermute | solution.py:524
  6.8 2.4 %copy-start.2 = (s32[256]{0:T(256)S(1)}, s32[256]{0:T(256)}, u32[]{:S(2)}) copy-start(s32[256]{0:T(256)} %param.19) | copy-start | bytes 3076
  7.9 1.3 %copy-start = (f32[4,256]{1,0:T(4,128)S(1)}, f32[4,256]{1,0:T(4,128)}, u32[]{:S(2)}) copy-start(f32[4,256]{1,0:T(4,128)} %refs_7_.1) | copy-start | bytes 12292
  7.9 1.3 %collective-permute-start.5 = (f32[8,128]{1,0:T(8,128)S(1)}, f32[8,128]{1,0:T(8,128)S(1)}, u32[]{:S(2)}, u32[]{:S(2)}) collective-permute-start(f32[8,128]{1,0:T(8,128)S(1)} %get-tuple-element.32.refs_0_), channel_id=1, source_target_pairs={{0,1},{1,0},{2,3},{3,2},{4,5},{5,4},{6,7},{7,6},{8,9},{9,8},{10,11... | collective-permute-start | bytes 12296 | tf_op jit(solution)/shard_map/ppermute | solution.py:562
  9.2 0.7 %copy-start.1 = (s32[256,1]{0,1:T(1,128)S(1)}, s32[256,1]{0,1:T(1,128)}, u32[]{:S(2)}) copy-start(s32[256,1]{0,1:T(1,128)} %param.18) | copy-start | bytes 3076
  10.6 21.3 %all-to-all-start = ((f32[8,5,4,128]{3,2,1,0:T(4,128)}), f32[8,5,4,128]{3,2,1,0:T(4,128)S(1)}, u32[]{:S(2)}, u32[]{:S(2)}) async-start(f32[8,5,4,128]{3,2,1,0:T(4,128)} %note.1), calls=%async_computation | async-start | bytes 163840 | tf_op jit(solution)/shard_map/all_to_all | solution.py:581
  20.1 8.0 %collective-permute-start.1 = (f32[128,256]{1,0:T(8,128)S(1)}, f32[128,256]{1,0:T(8,128)S(1)}, u32[]{:S(2)}, u32[]{:S(2)}) collective-permute-start(f32[128,256]{1,0:T(8,128)S(1)} %get-tuple-element.27), channel_id=1, source_target_pairs={{0,2},{2,0},{4,6},{6,4},{8,10},{10,8},{12,14},{14,12},{1,3},{3,1},... | collective-permute-start | bytes 393224 | tf_op jit(solution)/shard_map/ppermute | solution.py:536
  22.1 5.9 %collective-permute-start.2 = (f32[128,256]{1,0:T(8,128)S(1)}, f32[128,256]{1,0:T(8,128)S(1)}, u32[]{:S(2)}, u32[]{:S(2)}) collective-permute-start(f32[128,256]{1,0:T(8,128)S(1)} %get-tuple-element.28), channel_id=1, source_target_pairs={{2,4},{4,2},{6,8},{8,6},{10,12},{12,10},{3,5},{5,3},{7,9},{9,7},{1... | collective-permute-start | bytes 393224 | tf_op jit(solution)/shard_map/ppermute | solution.py:535

commit v8 on v7

--- a/solution.py
+++ b/solution.py
@@ -96,8 +96,17 @@
 
 
 def pack_kernel(*refs):
-    arrays, (held, depth_out, even_out, odd_out), sems = refs[:7], refs[8:12], refs[12]
+    arrays, channel_arrays = refs[:7], refs[7:10]
+    held, depth_out, even_out, odd_out, traces_out, cells_out = refs[11:17]
+    numbers, sems = refs[17:]
     copies = field_copies(arrays, held, sems)
+    targets = (traces_out, numbers.at[0], numbers.at[1])
+    channel_copies = [
+        pltpu.make_async_copy(source, target, sems.at[7 + i])
+        for i, (source, target) in enumerate(zip(channel_arrays, targets))
+    ]
+    for copy in channel_copies:
+        copy.start()
     depth = lax.axis_index("depth")
     even = is_even()
     rows = held.shape[1]
@@ -126,6 +135,10 @@
         odd_out[at : at + HALO, lanes] = jnp.where(even, low, high)
     depth_out[:, :LANES] = packed[0]
     depth_out[:, LANES:] = packed[1]
+    for copy in channel_copies:
+        copy.wait()
+    cells_out[0] = numbers[0] * rows + lax.shift_right_logical(numbers[1], 2)
+    cells_out[1] = numbers[1] & 3
 
 
 def corner_kernel(got, even_in, odd_in, even_out, odd_out, sems):
@@ -298,7 +311,10 @@
         stresses(state, media, slow, step < MOMENTS - 1, save)
 
 
-def forward_top_kernel(held, outer_even, outer_odd, media, saved, end_out, image_out, state):
+def forward_top_kernel(
+    held, outer_even, outer_odd, traces, cells, bulk, media, saved, end_out, note_out, state
+):
+    del bulk
     blocks = Blocks(held, None, (outer_even, outer_odd), None)
     run_forward(blocks, media, saved, state, (0,))
     rows = held.shape[1]
@@ -313,7 +329,13 @@
         image = jnp.where(here, NEAR * turn(saved[step, 0, 0], spot - EDGE), image)
     turned = image.T
     half = IMAGE // 2
-    image_out[...] = jnp.concatenate([turned[:half], turned[half:IMAGE]], axis=1)
+    rates = jnp.concatenate([turned[:half], turned[half:IMAGE]], axis=1)
+    seen = jnp.concatenate([traces[:, :LANES], traces[:, LANES:]], axis=0)
+    mine = jnp.where(lax.axis_index("depth") == 0, rates, seen)
+    along, row = cells[0], cells[1]
+    places = jnp.concatenate([along[:, :LANES], along[:, LANES:], row[:, :LANES], row[:, LANES:]], axis=0)
+    for i, value in enumerate((mine[:4], mine[4:], places.astype(F32))):
+        note_out[:, i] = jnp.broadcast_to(value[None], (note_out.shape[0], 4, LANES))
 
 
 def forward_rest_kernel(
@@ -329,19 +351,6 @@
         end_out[f, :, LANES:] = last
 
 
-def note_kernel(rows, image, image_beside, obs, owner, cell, note_out):
-    rates = jnp.where(lax.axis_index("depth") == 0, image[...], image_beside[...])
-    seen = obs[...]
-    along, row = channel_cells(owner, cell, rows)
-    cells = jnp.concatenate([along[:, :LANES], along[:, LANES:], row[:, :LANES], row[:, LANES:]], axis=0)
-    for i, value in enumerate((rates[:4], rates[4:], seen[:, :LANES], seen[:, LANES:], cells.astype(F32))):
-        note_out[:, i] = jnp.broadcast_to(value[None], (note_out.shape[0], 4, LANES))
-
-
-def channel_cells(owner, cell, rows):
-    return owner[...] * rows + lax.shift_right_logical(cell[...], 2), cell[...] & 3
-
-
 def three(value):
     high = value.astype(BF16)
     rest = value - high.astype(F32)
@@ -354,8 +363,9 @@
     return (value[2 * IMAGE : 3 * IMAGE] + value[IMAGE : 2 * IMAGE]) + value[:IMAGE]
 
 
-def channel_sums(tracks, rows, notes, own_along):
+def channel_sums(tracks, rows, notes, beside, own_along):
     start = lax.axis_index("track") * rows - EDGE
+    surface = lax.axis_index("depth") == 0
     group = min(8, tracks)
     channels = own_along.shape[1]
     lane = lane_ids(8)
@@ -367,8 +377,12 @@
         rate, image = carry
         base = number * group
         firsts, lasts = [], []
-        blocks = [[notes[base + k, i] for i in range(5)] for k in range(group)]
-        rates = [jnp.concatenate(block[:2], axis=0) for block in blocks]
+        mine = [[notes[base + k, i] for i in range(3)] for k in range(group)]
+        other = [[beside[base + k, i] for i in range(3)] for k in range(group)]
+        rates = [
+            jnp.concatenate([jnp.where(surface, m[i], o[i]) for i in range(2)], axis=0) for m, o in zip(mine, other)
+        ]
+        traces = [[jnp.where(surface, o[i], m[i]) for i in range(2)] for m, o in zip(mine, other)]
         for k in range(0, group, 2):
             a, b = rates[k], rates[k + 1]
             firsts.append(jnp.where(lane < half, a, turn(b, half)))
@@ -380,9 +394,9 @@
         weights, hots = [], []
         for k in range(group):
             for h in range(2):
-                along = blocks[k][4][h : h + 1]
-                mask = (row16 & 3).astype(F32) == blocks[k][4][2 + h : 3 + h]
-                seen = [blocks[k][2 + h][t : t + 1] for t in range(MOMENTS)]
+                along = mine[k][2][h : h + 1]
+                mask = (row16 & 3).astype(F32) == mine[k][2][2 + h : 3 + h]
+                seen = [traces[k][h][t : t + 1] for t in range(MOMENTS)]
                 value = jnp.where(
                     row16 < 8,
                     jnp.where(row16 < 4, seen[0], seen[1]),
@@ -428,22 +442,22 @@
         stresses(state, media, slow, step < MOMENTS - 1, gather)
 
 
-def adjoint_rest_kernel(held, got_depth, even, odd, media, saved, note, sums, state):
-    del note
+def adjoint_rest_kernel(held, got_depth, even, odd, media, saved, notes, sums, state):
+    del notes
     load_state(state, Blocks(held, got_depth, None, (even, odd)), FORWARD, (1, 2))
     run_adjoint(media, saved, state, sums)
 
 
 def adjoint_top_kernel(
-    tracks, held, even, odd, media, saved, notes, rest, obs, owner, cell,
+    tracks, held, even, odd, media, saved, notes, beside, rest, obs, cells,
     lambda_out, mu_out, residual_out, state, sums,
 ):
     rows = held.shape[1]
     extent = rows + 2 * EDGE
     depth = lax.axis_index("depth")
     load_state(state, Blocks(held, None, None, (even, odd)), FORWARD, (0,))
-    along, row = channel_cells(owner, cell, rows)
-    rate, seen, count = channel_sums(tracks, rows, notes, along)
+    along, row = cells[0], cells[1]
+    rate, seen, count = channel_sums(tracks, rows, notes, beside, along)
     channels = along.shape[1]
     at_own = jnp.where((row_ids(IMAGE, channels) & 3) == row, rate[:, :channels], 0.0)
     traces = [
@@ -488,7 +502,7 @@
     pinned = lambda array: pltpu.with_memory_space_constraint(array, pltpu.HBM)
     arrays = (velocity, stress, adjoint_velocity, adjoint_stress, buoyancy, lame_lambda, shear_modulus)
     arrays = tuple(pinned(array) for array in arrays)
-    channel_arrays = (observed, owner, cell)
+    channel_arrays = (pinned(observed), pinned(owner), pinned(cell))
     extent = rows + 2 * EDGE
     block = jax.ShapeDtypeStruct((rows, depth_cells), F32)
     outer_edges = jax.ShapeDtypeStruct((OUTER + HALO * FORWARD + EDGE - HALO, LANES), F32)
@@ -510,16 +524,23 @@
     outer_odd = lax.ppermute(to_odd, "track", swap(1))
     outer_even = lax.ppermute(to_even, "track", swap(0))
 
-    held, to_depth, to_even, to_odd = pl.pallas_call(
+    held, to_depth, to_even, to_odd, traces, cells = pl.pallas_call(
         pack_kernel,
-        out_shape=(jax.ShapeDtypeStruct((FIELDS, rows, depth_cells), F32), block, edges, edges),
-        in_specs=[outside] * 7 + [anywhere],
-        out_specs=(inside,) * 4,
-        scratch_shapes=[pltpu.SemaphoreType.DMA((7,))],
+        out_shape=(
+            jax.ShapeDtypeStruct((FIELDS, rows, depth_cells), F32),
+            block,
+            edges,
+            edges,
+            jax.ShapeDtypeStruct((moments, channels), F32),
+            jax.ShapeDtypeStruct((2, 1, channels), jnp.int32),
+        ),
+        in_specs=[outside] * 10 + [anywhere],
+        out_specs=(inside,) * 6,
+        scratch_shapes=[VMEM((2, 1, channels), jnp.int32), pltpu.SemaphoreType.DMA((10,))],
         compiler_params=params(),
         cost_estimate=cost(2),
         name="pack",
-    )(*arrays, to_even)
+    )(*arrays, *channel_arrays, to_even)
     depth_swap = [(0, 1), (1, 0)]
     got_depth = lax.ppermute(to_depth, "depth", depth_swap)
     to_even, to_odd = pl.pallas_call(
@@ -544,22 +565,23 @@
     def state_of(planes):
         return VMEM((5, planes, extent + 2 * PAD, LANES), F32)
 
-    media_top, saved_top, top_end, image = pl.pallas_call(
+    media_top, saved_top, top_end, note = pl.pallas_call(
         forward_top_kernel,
         out_shape=(
             media_of(1),
             saved_of(1),
             jax.ShapeDtypeStruct((2, rows, LANES), F32),
-            jax.ShapeDtypeStruct((IMAGE // 2, LANES), F32),
+            jax.ShapeDtypeStruct((tracks, 3, 4, LANES), F32),
         ),
-        in_specs=[inside] * 3,
+        in_specs=[inside] * 5 + [anywhere],
         out_specs=(inside,) * 4,
         scratch_shapes=[state_of(1)],
         compiler_params=params(),
-        cost_estimate=cost(1),
+        cost_estimate=cost(20),
         name="forward_top",
-    )(held, outer_even, outer_odd)
-    image_beside = lax.ppermute(image, "depth", depth_swap)
+    )(held, outer_even, outer_odd, traces, cells, to_even)
+    notes = lax.all_to_all(note, "track", split_axis=0, concat_axis=0, tiled=True)
+    beside = lax.ppermute(notes, "depth", depth_swap)
     media_rest, saved_rest, velocity_end = pl.pallas_call(
         forward_rest_kernel,
         out_shape=(media_of(2), saved_of(2), jax.ShapeDtypeStruct(velocity.shape, F32)),
@@ -567,18 +589,9 @@
         out_specs=(inside,) * 3,
         scratch_shapes=[state_of(2)],
         compiler_params=params(),
-        cost_estimate=cost(2),
+        cost_estimate=cost(20),
         name="forward_rest",
     )(held, got_depth, outer_even, outer_odd, got_even, got_odd, top_end)
-    note = pl.pallas_call(
-        lambda *refs: note_kernel(rows, *refs),
-        out_shape=jax.ShapeDtypeStruct((tracks, 5, 4, LANES), F32),
-        in_specs=[inside] * 5,
-        out_specs=inside,
-        compiler_params=params(),
-        name="note",
-    )(image, image_beside, *channel_arrays)
-    notes = lax.all_to_all(note, "track", split_axis=0, concat_axis=0, tiled=True)
     rest = pl.pallas_call(
         adjoint_rest_kernel,
         out_shape=jax.ShapeDtypeStruct((2, 2, rows, LANES), F32),
@@ -586,9 +599,9 @@
         out_specs=inside,
         scratch_shapes=[state_of(2)],
         compiler_params=params(),
-        cost_estimate=cost(3),
+        cost_estimate=cost(20),
         name="adjoint_rest",
-    )(held, got_depth, got_even, got_odd, media_rest, saved_rest, note)
+    )(held, got_depth, got_even, got_odd, media_rest, saved_rest, notes)
     gradient_lambda, gradient_mu, residual = pl.pallas_call(
         lambda *refs: adjoint_top_kernel(tracks, *refs),
         out_shape=(block, block, jax.ShapeDtypeStruct((moments // 2, channels), F32)),
@@ -598,7 +611,7 @@
         compiler_params=params(),
         cost_estimate=cost(2),
         name="adjoint_top",
-    )(held, got_even, got_odd, media_top, saved_top, notes, rest, *channel_arrays)
+    )(held, got_even, got_odd, media_top, saved_top, notes, beside, rest, traces, cells)
     return gradient_lambda, gradient_mu, velocity_end, residual
 
 

time: 34.5 us -> 34.1 us (0.988)
  the two profiles are of different devices: /device:TPU:0 before, /device:TPU:8 now
where the time goes in v8:
time: 34.1 us; the launch traced here: 33.8 us
  starting transfers between devices  12.2 us (36%)
  waiting for transfers between devices  10.7 us (31%)
  Pallas kernels  10.1 us (30%)
  between operations  0.71 us (2%)
    all_to_all x1, starting transfers between devices, per_device(): lax.all_to_all(note, 'track', split_axis=0, concat_axis=0, tiled=True)  5.32 us
    ppermute x1, waiting for transfers between devices, per_device(): outer_odd = lax.ppermute(to_odd, 'track', swap(1))  4.23 us
    ppermute x1, waiting for transfers between devices, per_device(): got_odd = lax.ppermute(to_odd, 'track', swap(1))  3.76 us
    pallas_call x1, Pallas kernels, per_device(): pl.pallas_call(forward_rest_kernel, out_shape=(media_of(2), saved_of(2),...  2.38 us
    pallas_call x1, Pallas kernels, per_device(): pl.pallas_call(lambda *refs: adjoint_top_kernel(tracks, *refs), out_shape...  2.02 us
    ppermute x1, starting transfers between devices, per_device(): got_odd = lax.ppermute(to_odd, 'track', swap(1))  1.92 us
    ppermute x1, starting transfers between devices, per_device(): outer_odd = lax.ppermute(to_odd, 'track', swap(1))  1.91 us
    all_to_all x1, waiting for transfers between devices, per_device(): lax.all_to_all(note, 'track', split_axis=0, concat_axis=0, tiled=True)  1.76 us
  transfers between devices with their start and end apart: 7, of which 5 were waited for; matrix products, arithmetic and copies ran while one was open for 0% of the time, Pallas kernels for 12%

profile of v8, /device:TPU:8, one launch (start us, length us, event | category | flops | bytes accessed | tf_op | source)
XLA Modules:
  0.0 33.8 jit_solution(12704191044659851516)
XLA Ops:
  0.6 1.0 %outer.1 = (f32[104,128]{1,0:T(8,128)S(1)}, f32[104,128]{1,0:T(8,128)S(1)}) custom-call(f32[2,64,256]{2,1,0:T(8,128)} %refs_0_.1, f32[3,64,256]{2,1,0:T(8,128)} %refs_1_.1, f32[64,256]{1,0:T(8,128)} %refs_4_.1, f32[64,256]{1,0:T(8,128)} %refs_5_.1, f32[64,256]{1,0:T(8,128)} %refs_6_.1), custom_call_target="tpu_custom_call" | custom-call | bytes 3500000 | tf_op jit(solution)/shard_map/outer/pallas_call | solution.py:514
  1.6 1.5 %pack.1 = (f32[13,64,256]{2,1,0:T(8,128)S(1)}, f32[64,256]{1,0:T(8,128)S(1)}, f32[128,256]{1,0:T(8,128)S(1)}, f32[128,256]{1,0:T(8,128)S(1)}, f32[4,256]{1,0:T(4,128)S(1)}, /*index=5*/s32[2,1,256]{2,1,0:T(1,128)S(1)}) custom-call(f32[2,64,256]{2,1,0:T(8,128)} %refs_0_.1, f32[3,64,256]{2,1,0:T(8,128)} %refs_1_.1, f32[2,64,256]{2,1,0:T(8,128)} %refs_2_.1, ...), custom_call_target="tpu_custom_call" | custom-call | bytes 7000000 | tf_op jit(solution)/shard_map/pack/pallas_call | solution.py:527
  3.1 0.1 collective-permute-start
  3.2 1.6 %collective-permute-start.3 = (f32[104,128]{1,0:T(8,128)S(1)}, f32[104,128]{1,0:T(8,128)S(1)}, u32[]{:S(2)}, u32[]{:S(2)}) collective-permute-start(f32[104,128]{1,0:T(8,128)S(1)} %get-tuple-element.24.refs_10_), channel_id=1, source_target_pairs={{0,2},{2,0},{4,6},{6,4},{8,10},{10,8},{12,14},{14,12},{1,3},{3,1},... | collective-permute-start | bytes 159752 | tf_op jit(solution)/shard_map/ppermute | solution.py:525
  4.8 1.9 %collective-permute-start.4 = (f32[104,128]{1,0:T(8,128)S(1)}, f32[104,128]{1,0:T(8,128)S(1)}, u32[]{:S(2)}, u32[]{:S(2)}) collective-permute-start(f32[104,128]{1,0:T(8,128)S(1)} %get-tuple-element.31), channel_id=1, source_target_pairs={{2,4},{4,2},{6,8},{8,6},{10,12},{12,10},{3,5},{5,3},{7,9},{9,7},{1... | collective-permute-start | bytes 159752 | tf_op jit(solution)/shard_map/ppermute | solution.py:524
  6.7 0.0 collective-permute-done.got.got_depth
  6.7 0.1 corners.1
  6.8 0.7 %collective-permute-done.3.outer_even = f32[104,128]{1,0:T(8,128)S(1)} collective-permute-done((f32[104,128]{1,0:T(8,128)S(1)}, f32[104,128]{1,0:T(8,128)S(1)}, u32[]{:S(2)}, u32[]{:S(2)}) %collective-permute-start.3) | collective-permute-done | bytes 53280 | tf_op jit(solution)/shard_map/ppermute | solution.py:525
  7.4 4.2 %collective-permute-done.4.outer_odd = f32[104,128]{1,0:T(8,128)S(1)} collective-permute-done((f32[104,128]{1,0:T(8,128)S(1)}, f32[104,128]{1,0:T(8,128)S(1)}, u32[]{:S(2)}, u32[]{:S(2)}) %collective-permute-start.4) | collective-permute-done | bytes 53280 | tf_op jit(solution)/shard_map/ppermute | solution.py:524
  11.7 1.7 %forward_top.1 = (f32[4,1,96,128]{3,2,1,0:T(8,128)S(1)}, f32[4,3,1,64,128]{4,3,2,1,0:T(8,128)S(1)}, f32[2,64,128]{2,1,0:T(8,128)S(1)}, f32[8,3,4,128]{3,2,1,0:T(4,128)}) custom-call(f32[13,64,256]{2,1,0:T(8,128)S(1)} %get-tuple-element.25.held.refs_0_, f32[104,128]{1,0:T(8,128)S(1)} %collective-permute-done.3.outer_even, ...), custom_call_target="tpu_custom_call" | custom-call | bytes 70000000 | tf_op jit(solution)/shard_map/forward_top/pallas_call | solution.py:568
  13.4 5.3 %all-to-all-start = ((f32[8,3,4,128]{3,2,1,0:T(4,128)}), f32[8,3,4,128]{3,2,1,0:T(4,128)S(1)}, u32[]{:S(2)}, u32[]{:S(2)}) async-start(f32[8,3,4,128]{3,2,1,0:T(4,128)} %get-tuple-element.36), calls=%async_computation | async-start | bytes 98304 | tf_op jit(solution)/shard_map/all_to_all | solution.py:583
  18.7 1.5 %collective-permute-start.1 = (f32[128,256]{1,0:T(8,128)S(1)}, f32[128,256]{1,0:T(8,128)S(1)}, u32[]{:S(2)}, u32[]{:S(2)}) collective-permute-start(f32[128,256]{1,0:T(8,128)S(1)} %get-tuple-element.29.bulk), channel_id=1, source_target_pairs={{0,2},{2,0},{4,6},{6,4},{8,10},{10,8},{12,14},{14,12},{1,3},{3,1},... | collective-permute-start | bytes 393224 | tf_op jit(solution)/shard_map/ppermute | solution.py:557
  20.1 1.9 %collective-permute-start.2 = (f32[128,256]{1,0:T(8,128)S(1)}, f32[128,256]{1,0:T(8,128)S(1)}, u32[]{:S(2)}, u32[]{:S(2)}) collective-permute-start(f32[128,256]{1,0:T(8,128)S(1)} %get-tuple-element.30), channel_id=1, source_target_pairs={{2,4},{4,2},{6,8},{8,6},{10,12},{12,10},{3,5},{5,3},{7,9},{9,7},{1... | collective-permute-start | bytes 393224 | tf_op jit(solution)/shard_map/ppermute | solution.py:556
  22.1 1.8 %all-to-all-done.notes.refs_5_ = f32[8,3,4,128]{3,2,1,0:T(4,128)S(1)} async-done(((f32[8,3,4,128]{3,2,1,0:T(4,128)}), f32[8,3,4,128]{3,2,1,0:T(4,128)S(1)}, u32[]{:S(2)}, u32[]{:S(2)}) %all-to-all-start) | async-done | bytes 49184 | tf_op jit(solution)/shard_map/all_to_all | solution.py:583
  23.8 0.0 collective-permute-start.5
  23.8 0.3 collective-permute-done.1.even.refs_1_
  24.1 3.8 %collective-permute-done.2.odd.refs_2_ = f32[128,256]{1,0:T(8,128)S(1)} collective-permute-done((f32[128,256]{1,0:T(8,128)S(1)}, f32[128,256]{1,0:T(8,128)S(1)}, u32[]{:S(2)}, u32[]{:S(2)}) %collective-permute-start.2) | collective-permute-done | bytes 131104 | tf_op jit(solution)/shard_map/ppermute | solution.py:556
  27.9 2.4 %forward_rest.1 = (f32[4,2,96,128]{3,2,1,0:T(8,128)S(1)}, f32[4,3,2,64,128]{4,3,2,1,0:T(8,128)S(1)}, f32[2,64,256]{2,1,0:T(8,128)}) custom-call(f32[13,64,256]{2,1,0:T(8,128)S(1)} %get-tuple-element.25.held.refs_0_, f32[64,256]{1,0:T(8,128)S(1)} %collective-permute-done.got.got_depth, f32[104,128]{1,0:T(8,128)S(1)} %collective-permute-done.3.outer_even, ...), custom_call_target="tpu_custom_call" | custom-call | bytes 70000000 | tf_op jit(solution)/shard_map/forward_rest/pallas_call | solution.py:585
  30.3 1.5 %adjoint_rest.1.refs_7_ = f32[2,2,64,128]{3,2,1,0:T(8,128)S(1)} custom-call(f32[13,64,256]{2,1,0:T(8,128)S(1)} %get-tuple-element.25.held.refs_0_, f32[64,256]{1,0:T(8,128)S(1)} %collective-permute-done.got.got_depth, f32[128,256]{1,0:T(8,128)S(1)} %collective-permute-done.1.even.refs_1_, f32[128,256]{1,0:T(8,128)S(1)} %collective-permute-done.2.odd.refs_2_, ...), custom_call_target="tpu_custom_call" | custom-call | bytes 70000000 | tf_op jit(solution)/shard_map/adjoint_rest/pallas_call | solution.py:595
  31.8 0.0 collective-permute-done.5.refs_6_
  31.8 2.0 %adjoint_top.1 = (f32[64,256]{1,0:T(8,128)}, f32[64,256]{1,0:T(8,128)}, f32[2,256]{1,0:T(2,128)}) custom-call(f32[13,64,256]{2,1,0:T(8,128)S(1)} %get-tuple-element.25.held.refs_0_, f32[128,256]{1,0:T(8,128)S(1)} %collective-permute-done.1.even.refs_1_, f32[128,256]{1,0:T(8,128)S(1)} %collective-permute-done.2.odd.refs_2_, ...), custom_call_target="tpu_custom_call" | custom-call | bytes 7000000 | tf_op jit(solution)/shard_map/adjoint_top/pallas_call | solution.py:605
Async XLA Ops:
  3.1 3.6 %collective-permute-start = (f32[64,256]{1,0:T(8,128)S(1)}, f32[64,256]{1,0:T(8,128)S(1)}, u32[]{:S(2)}, u32[]{:S(2)}) collective-permute-start(f32[64,256]{1,0:T(8,128)S(1)} %get-tuple-element.26), channel_id=1, source_target_pairs={{0,1},{1,0},{2,3},{3,2},{4,5},{5,4},{6,7},{7,6},{8,9},{9,8},{10,11... | collective-permute-start | bytes 196616 | tf_op jit(solution)/shard_map/ppermute | solution.py:545
  3.2 4.2 %collective-permute-start.3 = (f32[104,128]{1,0:T(8,128)S(1)}, f32[104,128]{1,0:T(8,128)S(1)}, u32[]{:S(2)}, u32[]{:S(2)}) collective-permute-start(f32[104,128]{1,0:T(8,128)S(1)} %get-tuple-element.24.refs_10_), channel_id=1, source_target_pairs={{0,2},{2,0},{4,6},{6,4},{8,10},{10,8},{12,14},{14,12},{1,3},{3,1},... | collective-permute-start | bytes 159752 | tf_op jit(solution)/shard_map/ppermute | solution.py:525
  4.8 6.9 %collective-permute-start.4 = (f32[104,128]{1,0:T(8,128)S(1)}, f32[104,128]{1,0:T(8,128)S(1)}, u32[]{:S(2)}, u32[]{:S(2)}) collective-permute-start(f32[104,128]{1,0:T(8,128)S(1)} %get-tuple-element.31), channel_id=1, source_target_pairs={{2,4},{4,2},{6,8},{8,6},{10,12},{12,10},{3,5},{5,3},{7,9},{9,7},{1... | collective-permute-start | bytes 159752 | tf_op jit(solution)/shard_map/ppermute | solution.py:524
  13.4 10.5 %all-to-all-start = ((f32[8,3,4,128]{3,2,1,0:T(4,128)}), f32[8,3,4,128]{3,2,1,0:T(4,128)S(1)}, u32[]{:S(2)}, u32[]{:S(2)}) async-start(f32[8,3,4,128]{3,2,1,0:T(4,128)} %get-tuple-element.36), calls=%async_computation | async-start | bytes 98304 | tf_op jit(solution)/shard_map/all_to_all | solution.py:583
  18.7 5.5 %collective-permute-start.1 = (f32[128,256]{1,0:T(8,128)S(1)}, f32[128,256]{1,0:T(8,128)S(1)}, u32[]{:S(2)}, u32[]{:S(2)}) collective-permute-start(f32[128,256]{1,0:T(8,128)S(1)} %get-tuple-element.29.bulk), channel_id=1, source_target_pairs={{0,2},{2,0},{4,6},{6,4},{8,10},{10,8},{12,14},{14,12},{1,3},{3,1},... | collective-permute-start | bytes 393224 | tf_op jit(solution)/shard_map/ppermute | solution.py:557
  20.1 7.7 %collective-permute-start.2 = (f32[128,256]{1,0:T(8,128)S(1)}, f32[128,256]{1,0:T(8,128)S(1)}, u32[]{:S(2)}, u32[]{:S(2)}) collective-permute-start(f32[128,256]{1,0:T(8,128)S(1)} %get-tuple-element.30), channel_id=1, source_target_pairs={{2,4},{4,2},{6,8},{8,6},{10,12},{12,10},{3,5},{5,3},{7,9},{9,7},{1... | collective-permute-start | bytes 393224 | tf_op jit(solution)/shard_map/ppermute | solution.py:556
  23.8 7.9 %collective-permute-start.5 = (f32[8,3,4,128]{3,2,1,0:T(4,128)S(1)}, f32[8,3,4,128]{3,2,1,0:T(4,128)S(1)}, u32[]{:S(2)}, u32[]{:S(2)}) collective-permute-start(f32[8,3,4,128]{3,2,1,0:T(4,128)S(1)} %all-to-all-done.notes.refs_5_), channel_id=1, source_target_pairs={{0,1},{1,0},{2,3},{3,2},{4,5},{5,4},{6,7},{7,6},{8,9},{9,8},{10,11... | collective-permute-start | bytes 147464 | tf_op jit(solution)/shard_map/ppermute | solution.py:584

commit v9 on v8

--- a/solution.py
+++ b/solution.py
@@ -312,9 +312,8 @@
 
 
 def forward_top_kernel(
-    held, outer_even, outer_odd, traces, cells, bulk, media, saved, end_out, note_out, state
+    held, outer_even, outer_odd, traces, cells, media, saved, end_out, note_out, state
 ):
-    del bulk
     blocks = Blocks(held, None, (outer_even, outer_odd), None)
     run_forward(blocks, media, saved, state, (0,))
     rows = held.shape[1]
@@ -538,7 +537,7 @@
         out_specs=(inside,) * 6,
         scratch_shapes=[VMEM((2, 1, channels), jnp.int32), pltpu.SemaphoreType.DMA((10,))],
         compiler_params=params(),
-        cost_estimate=cost(2),
+        cost_estimate=cost(500),
         name="pack",
     )(*arrays, *channel_arrays, to_even)
     depth_swap = [(0, 1), (1, 0)]
@@ -573,13 +572,13 @@
             jax.ShapeDtypeStruct((2, rows, LANES), F32),
             jax.ShapeDtypeStruct((tracks, 3, 4, LANES), F32),
         ),
-        in_specs=[inside] * 5 + [anywhere],
+        in_specs=[inside] * 5,
         out_specs=(inside,) * 4,
         scratch_shapes=[state_of(1)],
         compiler_params=params(),
-        cost_estimate=cost(20),
+        cost_estimate=cost(500),
         name="forward_top",
-    )(held, outer_even, outer_odd, traces, cells, to_even)
+    )(held, outer_even, outer_odd, traces, cells)
     notes = lax.all_to_all(note, "track", split_axis=0, concat_axis=0, tiled=True)
     beside = lax.ppermute(notes, "depth", depth_swap)
     media_rest, saved_rest, velocity_end = pl.pallas_call(
@@ -589,7 +588,7 @@
         out_specs=(inside,) * 3,
         scratch_shapes=[state_of(2)],
         compiler_params=params(),
-        cost_estimate=cost(20),
+        cost_estimate=cost(500),
         name="forward_rest",
     )(held, got_depth, outer_even, outer_odd, got_even, got_odd, top_end)
     rest = pl.pallas_call(
@@ -599,7 +598,7 @@
         out_specs=inside,
         scratch_shapes=[state_of(2)],
         compiler_params=params(),
-        cost_estimate=cost(20),
+        cost_estimate=cost(500),
         name="adjoint_rest",
     )(held, got_depth, got_even, got_odd, media_rest, saved_rest, notes)
     gradient_lambda, gradient_mu, residual = pl.pallas_call(

time: 34.1 us -> 34.2 us (level)
    ppermute x1, waiting for transfers between devices: 0.3 us -> 1.45 us  [per_device(): got_even = lax.ppermute(to_even, 'track', swap(0))]
    ppermute x1, waiting for transfers between devices: 3.76 us -> 2.71 us  [per_device(): got_odd = lax.ppermute(to_odd, 'track', swap(1))]
  transfers between devices with their start and end apart: 7 -> 7, of which waited for: 5 -> 5; matrix products, arithmetic and copies ran while one was open for 0% -> 0% of each run, Pallas kernels for 12% -> 17%
where the time goes in v9:
time: 34.2 us; the launch traced here: 33.9 us
  starting transfers between devices  12.3 us (36%)
  waiting for transfers between devices  10.8 us (32%)
  Pallas kernels  10.1 us (30%)
  between operations  0.7 us (2%)
    all_to_all x1, starting transfers between devices, per_device(): lax.all_to_all(note, 'track', split_axis=0, concat_axis=0, tiled=True)  5.32 us
    ppermute x1, waiting for transfers between devices, per_device(): outer_odd = lax.ppermute(to_odd, 'track', swap(1))  4.23 us
    ppermute x1, waiting for transfers between devices, per_device(): got_odd = lax.ppermute(to_odd, 'track', swap(1))  2.71 us
    pallas_call x1, Pallas kernels, per_device(): pl.pallas_call(forward_rest_kernel, out_shape=(media_of(2), saved_of(2),...  2.38 us
    pallas_call x1, Pallas kernels, per_device(): pl.pallas_call(lambda *refs: adjoint_top_kernel(tracks, *refs), out_shape...  2.02 us
    ppermute x1, starting transfers between devices, per_device(): got_odd = lax.ppermute(to_odd, 'track', swap(1))  1.93 us
    ppermute x1, starting transfers between devices, per_device(): outer_odd = lax.ppermute(to_odd, 'track', swap(1))  1.91 us
    pallas_call x1, Pallas kernels, per_device(): pl.pallas_call(forward_top_kernel, out_shape=(media_of(1), saved_of(1), j...  1.69 us
  transfers between devices with their start and end apart: 7, of which 5 were waited for; matrix products, arithmetic and copies ran while one was open for 0% of the time, Pallas kernels for 17%

profile of v9, /device:TPU:8, one launch (start us, length us, event | category | flops | bytes accessed | tf_op | source)
XLA Modules:
  0.0 33.9 jit_solution(2287017717824154528)
XLA Ops:
  0.6 1.0 %outer.1 = (f32[104,128]{1,0:T(8,128)S(1)}, f32[104,128]{1,0:T(8,128)S(1)}) custom-call(f32[2,64,256]{2,1,0:T(8,128)} %refs_0_.1, f32[3,64,256]{2,1,0:T(8,128)} %refs_1_.1, f32[64,256]{1,0:T(8,128)} %refs_4_.1, f32[64,256]{1,0:T(8,128)} %refs_5_.1, f32[64,256]{1,0:T(8,128)} %refs_6_.1), custom_call_target="tpu_custom_call" | custom-call | bytes 3500000 | tf_op jit(solution)/shard_map/outer/pallas_call | solution.py:513
  1.6 1.5 %pack.1 = (f32[13,64,256]{2,1,0:T(8,128)S(1)}, f32[64,256]{1,0:T(8,128)S(1)}, f32[128,256]{1,0:T(8,128)S(1)}, f32[128,256]{1,0:T(8,128)S(1)}, f32[4,256]{1,0:T(4,128)S(1)}, /*index=5*/s32[2,1,256]{2,1,0:T(1,128)S(1)}) custom-call(f32[2,64,256]{2,1,0:T(8,128)} %refs_0_.1, f32[3,64,256]{2,1,0:T(8,128)} %refs_1_.1, f32[2,64,256]{2,1,0:T(8,128)} %refs_2_.1, ...), custom_call_target="tpu_custom_call" | custom-call | bytes 1750000000 | tf_op jit(solution)/shard_map/pack/pallas_call | solution.py:526
  3.1 0.1 collective-permute-start
  3.2 1.6 %collective-permute-start.3 = (f32[104,128]{1,0:T(8,128)S(1)}, f32[104,128]{1,0:T(8,128)S(1)}, u32[]{:S(2)}, u32[]{:S(2)}) collective-permute-start(f32[104,128]{1,0:T(8,128)S(1)} %get-tuple-element.24.refs_10_), channel_id=1, source_target_pairs={{0,2},{2,0},{4,6},{6,4},{8,10},{10,8},{12,14},{14,12},{1,3},{3,1},... | collective-permute-start | bytes 159752 | tf_op jit(solution)/shard_map/ppermute | solution.py:524
  4.8 1.9 %collective-permute-start.4 = (f32[104,128]{1,0:T(8,128)S(1)}, f32[104,128]{1,0:T(8,128)S(1)}, u32[]{:S(2)}, u32[]{:S(2)}) collective-permute-start(f32[104,128]{1,0:T(8,128)S(1)} %get-tuple-element.31), channel_id=1, source_target_pairs={{2,4},{4,2},{6,8},{8,6},{10,12},{12,10},{3,5},{5,3},{7,9},{9,7},{1... | collective-permute-start | bytes 159752 | tf_op jit(solution)/shard_map/ppermute | solution.py:523
  6.7 0.8 %collective-permute-done.3.outer_even = f32[104,128]{1,0:T(8,128)S(1)} collective-permute-done((f32[104,128]{1,0:T(8,128)S(1)}, f32[104,128]{1,0:T(8,128)S(1)}, u32[]{:S(2)}, u32[]{:S(2)}) %collective-permute-start.3) | collective-permute-done | bytes 53280 | tf_op jit(solution)/shard_map/ppermute | solution.py:524
  7.4 4.2 %collective-permute-done.4.outer_odd = f32[104,128]{1,0:T(8,128)S(1)} collective-permute-done((f32[104,128]{1,0:T(8,128)S(1)}, f32[104,128]{1,0:T(8,128)S(1)}, u32[]{:S(2)}, u32[]{:S(2)}) %collective-permute-start.4) | collective-permute-done | bytes 53280 | tf_op jit(solution)/shard_map/ppermute | solution.py:523
  11.7 1.7 %forward_top.1 = (f32[4,1,96,128]{3,2,1,0:T(8,128)S(1)}, f32[4,3,1,64,128]{4,3,2,1,0:T(8,128)S(1)}, f32[2,64,128]{2,1,0:T(8,128)S(1)}, f32[8,3,4,128]{3,2,1,0:T(4,128)}) custom-call(f32[13,64,256]{2,1,0:T(8,128)S(1)} %get-tuple-element.25.held.refs_0_, f32[104,128]{1,0:T(8,128)S(1)} %collective-permute-done.3.outer_even, ...), custom_call_target="tpu_custom_call" | custom-call | bytes 1750000000 | tf_op jit(solution)/shard_map/forward_top/pallas_call | solution.py:567
  13.4 5.3 %all-to-all-start = ((f32[8,3,4,128]{3,2,1,0:T(4,128)}), f32[8,3,4,128]{3,2,1,0:T(4,128)S(1)}, u32[]{:S(2)}, u32[]{:S(2)}) async-start(f32[8,3,4,128]{3,2,1,0:T(4,128)} %get-tuple-element.36), calls=%async_computation | async-start | bytes 98304 | tf_op jit(solution)/shard_map/all_to_all | solution.py:582
  18.7 0.0 collective-permute-done.got.got_depth
  18.7 0.1 corners.1
  18.8 1.5 %collective-permute-start.1 = (f32[128,256]{1,0:T(8,128)S(1)}, f32[128,256]{1,0:T(8,128)S(1)}, u32[]{:S(2)}, u32[]{:S(2)}) collective-permute-start(f32[128,256]{1,0:T(8,128)S(1)} %get-tuple-element.29), channel_id=1, source_target_pairs={{0,2},{2,0},{4,6},{6,4},{8,10},{10,8},{12,14},{14,12},{1,3},{3,1},... | collective-permute-start | bytes 393224 | tf_op jit(solution)/shard_map/ppermute | solution.py:556
  20.3 1.9 %collective-permute-start.2 = (f32[128,256]{1,0:T(8,128)S(1)}, f32[128,256]{1,0:T(8,128)S(1)}, u32[]{:S(2)}, u32[]{:S(2)}) collective-permute-start(f32[128,256]{1,0:T(8,128)S(1)} %get-tuple-element.30), channel_id=1, source_target_pairs={{2,4},{4,2},{6,8},{8,6},{10,12},{12,10},{3,5},{5,3},{7,9},{9,7},{1... | collective-permute-start | bytes 393224 | tf_op jit(solution)/shard_map/ppermute | solution.py:555
  22.2 1.6 %all-to-all-done.notes.refs_5_ = f32[8,3,4,128]{3,2,1,0:T(4,128)S(1)} async-done(((f32[8,3,4,128]{3,2,1,0:T(4,128)}), f32[8,3,4,128]{3,2,1,0:T(4,128)S(1)}, u32[]{:S(2)}, u32[]{:S(2)}) %all-to-all-start) | async-done | bytes 49184 | tf_op jit(solution)/shard_map/all_to_all | solution.py:582
  23.9 0.0 collective-permute-start.5
  23.9 1.4 %collective-permute-done.1.even.refs_1_ = f32[128,256]{1,0:T(8,128)S(1)} collective-permute-done((f32[128,256]{1,0:T(8,128)S(1)}, f32[128,256]{1,0:T(8,128)S(1)}, u32[]{:S(2)}, u32[]{:S(2)}) %collective-permute-start.1) | collective-permute-done | bytes 131104 | tf_op jit(solution)/shard_map/ppermute | solution.py:556
  25.3 2.7 %collective-permute-done.2.odd.refs_2_ = f32[128,256]{1,0:T(8,128)S(1)} collective-permute-done((f32[128,256]{1,0:T(8,128)S(1)}, f32[128,256]{1,0:T(8,128)S(1)}, u32[]{:S(2)}, u32[]{:S(2)}) %collective-permute-start.2) | collective-permute-done | bytes 131104 | tf_op jit(solution)/shard_map/ppermute | solution.py:555
  28.0 2.4 %forward_rest.1 = (f32[4,2,96,128]{3,2,1,0:T(8,128)S(1)}, f32[4,3,2,64,128]{4,3,2,1,0:T(8,128)S(1)}, f32[2,64,256]{2,1,0:T(8,128)}) custom-call(f32[13,64,256]{2,1,0:T(8,128)S(1)} %get-tuple-element.25.held.refs_0_, f32[64,256]{1,0:T(8,128)S(1)} %collective-permute-done.got.got_depth, f32[104,128]{1,0:T(8,128)S(1)} %collective-permute-done.3.outer_even, ...), custom_call_target="tpu_custom_call" | custom-call | bytes 1750000000 | tf_op jit(solution)/shard_map/forward_rest/pallas_call | solution.py:584
  30.4 1.5 %adjoint_rest.1.refs_7_ = f32[2,2,64,128]{3,2,1,0:T(8,128)S(1)} custom-call(f32[13,64,256]{2,1,0:T(8,128)S(1)} %get-tuple-element.25.held.refs_0_, f32[64,256]{1,0:T(8,128)S(1)} %collective-permute-done.got.got_depth, f32[128,256]{1,0:T(8,128)S(1)} %collective-permute-done.1.even.refs_1_, f32[128,256]{1,0:T(8,128)S(1)} %collective-permute-done.2.odd.refs_2_, ...), custom_call_target="tpu_custom_call" | custom-call | bytes 1750000000 | tf_op jit(solution)/shard_map/adjoint_rest/pallas_call | solution.py:594
  31.9 0.0 collective-permute-done.5.refs_6_
  31.9 2.0 %adjoint_top.1 = (f32[64,256]{1,0:T(8,128)}, f32[64,256]{1,0:T(8,128)}, f32[2,256]{1,0:T(2,128)}) custom-call(f32[13,64,256]{2,1,0:T(8,128)S(1)} %get-tuple-element.25.held.refs_0_, f32[128,256]{1,0:T(8,128)S(1)} %collective-permute-done.1.even.refs_1_, f32[128,256]{1,0:T(8,128)S(1)} %collective-permute-done.2.odd.refs_2_, ...), custom_call_target="tpu_custom_call" | custom-call | bytes 7000000 | tf_op jit(solution)/shard_map/adjoint_top/pallas_call | solution.py:604
Async XLA Ops:
  3.1 15.6 %collective-permute-start = (f32[64,256]{1,0:T(8,128)S(1)}, f32[64,256]{1,0:T(8,128)S(1)}, u32[]{:S(2)}, u32[]{:S(2)}) collective-permute-start(f32[64,256]{1,0:T(8,128)S(1)} %get-tuple-element.26), channel_id=1, source_target_pairs={{0,1},{1,0},{2,3},{3,2},{4,5},{5,4},{6,7},{7,6},{8,9},{9,8},{10,11... | collective-permute-start | bytes 196616 | tf_op jit(solution)/shard_map/ppermute | solution.py:544
  3.2 4.2 %collective-permute-start.3 = (f32[104,128]{1,0:T(8,128)S(1)}, f32[104,128]{1,0:T(8,128)S(1)}, u32[]{:S(2)}, u32[]{:S(2)}) collective-permute-start(f32[104,128]{1,0:T(8,128)S(1)} %get-tuple-element.24.refs_10_), channel_id=1, source_target_pairs={{0,2},{2,0},{4,6},{6,4},{8,10},{10,8},{12,14},{14,12},{1,3},{3,1},... | collective-permute-start | bytes 159752 | tf_op jit(solution)/shard_map/ppermute | solution.py:524
  4.8 6.9 %collective-permute-start.4 = (f32[104,128]{1,0:T(8,128)S(1)}, f32[104,128]{1,0:T(8,128)S(1)}, u32[]{:S(2)}, u32[]{:S(2)}) collective-permute-start(f32[104,128]{1,0:T(8,128)S(1)} %get-tuple-element.31), channel_id=1, source_target_pairs={{2,4},{4,2},{6,8},{8,6},{10,12},{12,10},{3,5},{5,3},{7,9},{9,7},{1... | collective-permute-start | bytes 159752 | tf_op jit(solution)/shard_map/ppermute | solution.py:523
  13.4 10.5 %all-to-all-start = ((f32[8,3,4,128]{3,2,1,0:T(4,128)}), f32[8,3,4,128]{3,2,1,0:T(4,128)S(1)}, u32[]{:S(2)}, u32[]{:S(2)}) async-start(f32[8,3,4,128]{3,2,1,0:T(4,128)} %get-tuple-element.36), calls=%async_computation | async-start | bytes 98304 | tf_op jit(solution)/shard_map/all_to_all | solution.py:582
  18.8 6.6 %collective-permute-start.1 = (f32[128,256]{1,0:T(8,128)S(1)}, f32[128,256]{1,0:T(8,128)S(1)}, u32[]{:S(2)}, u32[]{:S(2)}) collective-permute-start(f32[128,256]{1,0:T(8,128)S(1)} %get-tuple-element.29), channel_id=1, source_target_pairs={{0,2},{2,0},{4,6},{6,4},{8,10},{10,8},{12,14},{14,12},{1,3},{3,1},... | collective-permute-start | bytes 393224 | tf_op jit(solution)/shard_map/ppermute | solution.py:556
  20.3 7.7 %collective-permute-start.2 = (f32[128,256]{1,0:T(8,128)S(1)}, f32[128,256]{1,0:T(8,128)S(1)}, u32[]{:S(2)}, u32[]{:S(2)}) collective-permute-start(f32[128,256]{1,0:T(8,128)S(1)} %get-tuple-element.30), channel_id=1, source_target_pairs={{2,4},{4,2},{6,8},{8,6},{10,12},{12,10},{3,5},{5,3},{7,9},{9,7},{1... | collective-permute-start | bytes 393224 | tf_op jit(solution)/shard_map/ppermute | solution.py:555
  23.9 8.0 %collective-permute-start.5 = (f32[8,3,4,128]{3,2,1,0:T(4,128)S(1)}, f32[8,3,4,128]{3,2,1,0:T(4,128)S(1)}, u32[]{:S(2)}, u32[]{:S(2)}) collective-permute-start(f32[8,3,4,128]{3,2,1,0:T(4,128)S(1)} %all-to-all-done.notes.refs_5_), channel_id=1, source_target_pairs={{0,1},{1,0},{2,3},{3,2},{4,5},{5,4},{6,7},{7,6},{8,9},{9,8},{10,11... | collective-permute-start | bytes 147464 | tf_op jit(solution)/shard_map/ppermute | solution.py:583

commit v10 on v7

--- a/solution.py
+++ b/solution.py
@@ -96,8 +96,17 @@
 
 
 def pack_kernel(*refs):
-    arrays, (held, depth_out, even_out, odd_out), sems = refs[:7], refs[8:12], refs[12]
+    arrays, channel_arrays = refs[:7], refs[7:10]
+    held, depth_out, even_out, odd_out, traces_out, cells_out = refs[11:17]
+    numbers, sems = refs[17:]
     copies = field_copies(arrays, held, sems)
+    targets = (traces_out, numbers.at[0], numbers.at[1])
+    channel_copies = [
+        pltpu.make_async_copy(source, target, sems.at[7 + i])
+        for i, (source, target) in enumerate(zip(channel_arrays, targets))
+    ]
+    for copy in channel_copies:
+        copy.start()
     depth = lax.axis_index("depth")
     even = is_even()
     rows = held.shape[1]
@@ -126,6 +135,10 @@
         odd_out[at : at + HALO, lanes] = jnp.where(even, low, high)
     depth_out[:, :LANES] = packed[0]
     depth_out[:, LANES:] = packed[1]
+    for copy in channel_copies:
+        copy.wait()
+    cells_out[0] = numbers[0] * rows + lax.shift_right_logical(numbers[1], 2)
+    cells_out[1] = numbers[1] & 3
 
 
 def corner_kernel(got, even_in, odd_in, even_out, odd_out, sems):
@@ -329,17 +342,13 @@
         end_out[f, :, LANES:] = last
 
 
-def note_kernel(rows, image, image_beside, obs, owner, cell, note_out):
+def note_kernel(image, image_beside, obs, cells, note_out):
     rates = jnp.where(lax.axis_index("depth") == 0, image[...], image_beside[...])
     seen = obs[...]
-    along, row = channel_cells(owner, cell, rows)
-    cells = jnp.concatenate([along[:, :LANES], along[:, LANES:], row[:, :LANES], row[:, LANES:]], axis=0)
-    for i, value in enumerate((rates[:4], rates[4:], seen[:, :LANES], seen[:, LANES:], cells.astype(F32))):
+    along, row = cells[0], cells[1]
+    places = jnp.concatenate([along[:, :LANES], along[:, LANES:], row[:, :LANES], row[:, LANES:]], axis=0)
+    for i, value in enumerate((rates[:4], rates[4:], seen[:, :LANES], seen[:, LANES:], places.astype(F32))):
         note_out[:, i] = jnp.broadcast_to(value[None], (note_out.shape[0], 4, LANES))
-
-
-def channel_cells(owner, cell, rows):
-    return owner[...] * rows + lax.shift_right_logical(cell[...], 2), cell[...] & 3
 
 
 def three(value):
@@ -435,14 +444,14 @@
 
 
 def adjoint_top_kernel(
-    tracks, held, even, odd, media, saved, notes, rest, obs, owner, cell,
+    tracks, held, even, odd, media, saved, notes, rest, obs, cells,
     lambda_out, mu_out, residual_out, state, sums,
 ):
     rows = held.shape[1]
     extent = rows + 2 * EDGE
     depth = lax.axis_index("depth")
     load_state(state, Blocks(held, None, None, (even, odd)), FORWARD, (0,))
-    along, row = channel_cells(owner, cell, rows)
+    along, row = cells[0], cells[1]
     rate, seen, count = channel_sums(tracks, rows, notes, along)
     channels = along.shape[1]
     at_own = jnp.where((row_ids(IMAGE, channels) & 3) == row, rate[:, :channels], 0.0)
@@ -488,7 +497,7 @@
     pinned = lambda array: pltpu.with_memory_space_constraint(array, pltpu.HBM)
     arrays = (velocity, stress, adjoint_velocity, adjoint_stress, buoyancy, lame_lambda, shear_modulus)
     arrays = tuple(pinned(array) for array in arrays)
-    channel_arrays = (observed, owner, cell)
+    channel_arrays = (pinned(observed), pinned(owner), pinned(cell))
     extent = rows + 2 * EDGE
     block = jax.ShapeDtypeStruct((rows, depth_cells), F32)
     outer_edges = jax.ShapeDtypeStruct((OUTER + HALO * FORWARD + EDGE - HALO, LANES), F32)
@@ -510,16 +519,23 @@
     outer_odd = lax.ppermute(to_odd, "track", swap(1))
     outer_even = lax.ppermute(to_even, "track", swap(0))
 
-    held, to_depth, to_even, to_odd = pl.pallas_call(
+    held, to_depth, to_even, to_odd, traces, cells = pl.pallas_call(
         pack_kernel,
-        out_shape=(jax.ShapeDtypeStruct((FIELDS, rows, depth_cells), F32), block, edges, edges),
-        in_specs=[outside] * 7 + [anywhere],
-        out_specs=(inside,) * 4,
-        scratch_shapes=[pltpu.SemaphoreType.DMA((7,))],
+        out_shape=(
+            jax.ShapeDtypeStruct((FIELDS, rows, depth_cells), F32),
+            block,
+            edges,
+            edges,
+            jax.ShapeDtypeStruct((moments, channels), F32),
+            jax.ShapeDtypeStruct((2, 1, channels), jnp.int32),
+        ),
+        in_specs=[outside] * 10 + [anywhere],
+        out_specs=(inside,) * 6,
+        scratch_shapes=[VMEM((2, 1, channels), jnp.int32), pltpu.SemaphoreType.DMA((10,))],
         compiler_params=params(),
         cost_estimate=cost(2),
         name="pack",
-    )(*arrays, to_even)
+    )(*arrays, *channel_arrays, to_even)
     depth_swap = [(0, 1), (1, 0)]
     got_depth = lax.ppermute(to_depth, "depth", depth_swap)
     to_even, to_odd = pl.pallas_call(
@@ -556,7 +572,7 @@
         out_specs=(inside,) * 4,
         scratch_shapes=[state_of(1)],
         compiler_params=params(),
-        cost_estimate=cost(1),
+        cost_estimate=cost(500),
         name="forward_top",
     )(held, outer_even, outer_odd)
     image_beside = lax.ppermute(image, "depth", depth_swap)
@@ -567,17 +583,17 @@
         out_specs=(inside,) * 3,
         scratch_shapes=[state_of(2)],
         compiler_params=params(),
-        cost_estimate=cost(2),
+        cost_estimate=cost(500),
         name="forward_rest",
     )(held, got_depth, outer_even, outer_odd, got_even, got_odd, top_end)
     note = pl.pallas_call(
-        lambda *refs: note_kernel(rows, *refs),
+        note_kernel,
         out_shape=jax.ShapeDtypeStruct((tracks, 5, 4, LANES), F32),
-        in_specs=[inside] * 5,
+        in_specs=[inside] * 4,
         out_specs=inside,
         compiler_params=params(),
         name="note",
-    )(image, image_beside, *channel_arrays)
+    )(image, image_beside, traces, cells)
     notes = lax.all_to_all(note, "track", split_axis=0, concat_axis=0, tiled=True)
     rest = pl.pallas_call(
         adjoint_rest_kernel,
@@ -586,19 +602,19 @@
         out_specs=inside,
         scratch_shapes=[state_of(2)],
         compiler_params=params(),
-        cost_estimate=cost(3),
+        cost_estimate=cost(500),
         name="adjoint_rest",
     )(held, got_depth, got_even, got_odd, media_rest, saved_rest, note)
     gradient_lambda, gradient_mu, residual = pl.pallas_call(
         lambda *refs: adjoint_top_kernel(tracks, *refs),
         out_shape=(block, block, jax.ShapeDtypeStruct((moments // 2, channels), F32)),
-        in_specs=[inside] * 10,
+        in_specs=[inside] * 9,
         out_specs=(inside,) * 3,
         scratch_shapes=[state_of(1), VMEM((2, 1, rows, LANES), F32)],
         compiler_params=params(),
         cost_estimate=cost(2),
         name="adjoint_top",
-    )(held, got_even, got_odd, media_top, saved_top, notes, rest, *channel_arrays)
+    )(held, got_even, got_odd, media_top, saved_top, notes, rest, traces, cells)
     return gradient_lambda, gradient_mu, velocity_end, residual
 
 

time: 34.5 us -> 33.7 us (0.977)
  local copies, waits for them, and re-layouts: 0.68 us -> 0 us
    unnamed x6 -> x0, local copies, waits for them, and re-layouts: 0.68 us -> none
where the time goes in v10:
time: 33.7 us; the launch traced here: 33.2 us
  starting transfers between devices  16.3 us (48%)
  Pallas kernels  10 us (30%)
  waiting for transfers between devices  6.09 us (18%)
  between operations  0.72 us (2%)
    all_to_all x1, starting transfers between devices, per_device(): lax.all_to_all(note, 'track', split_axis=0, concat_axis=0, tiled=True)  9.37 us
    ppermute x1, waiting for transfers between devices, per_device(): got_even = lax.ppermute(to_even, 'track', swap(0))  5.25 us
    ppermute x1, starting transfers between devices, per_device(): outer_even = lax.ppermute(to_even, 'track', swap(0))  3 us
    pallas_call x1, Pallas kernels, per_device(): pl.pallas_call(forward_rest_kernel, out_shape=(media_of(2), saved_of(2),...  2.38 us
    ppermute x1, starting transfers between devices, per_device(): got_even = lax.ppermute(to_even, 'track', swap(0))  2.06 us
    pallas_call x1, Pallas kernels, per_device(): pl.pallas_call(lambda *refs: adjoint_top_kernel(tracks, *refs), out_shape...  1.97 us
    pallas_call x1, Pallas kernels, per_device(): pl.pallas_call(pack_kernel, out_shape=(jax.ShapeDtypeStruct((FIELDS, rows...  1.51 us
    pallas_call x1, Pallas kernels, per_device(): pl.pallas_call(adjoint_rest_kernel, out_shape=jax.ShapeDtypeStruct((2, 2,...  1.47 us
  transfers between devices with their start and end apart: 7, of which 2 were waited for; matrix products, arithmetic and copies ran while one was open for 0% of the time, Pallas kernels for 21%

profile of v10, /device:TPU:0, one launch (start us, length us, event | category | flops | bytes accessed | tf_op | source)
XLA Modules:
  0.0 33.2 jit_solution(12755905230956047193)
XLA Ops:
  0.6 1.0 %outer.1 = (f32[104,128]{1,0:T(8,128)S(1)}, f32[104,128]{1,0:T(8,128)S(1)}) custom-call(f32[2,64,256]{2,1,0:T(8,128)} %refs_0_.1, f32[3,64,256]{2,1,0:T(8,128)} %refs_1_.1, f32[64,256]{1,0:T(8,128)} %refs_4_.1, f32[64,256]{1,0:T(8,128)} %refs_5_.1, f32[64,256]{1,0:T(8,128)} %refs_6_.1), custom_call_target="tpu_custom_call" | custom-call | bytes 3500000 | tf_op jit(solution)/shard_map/outer/pallas_call | solution.py:509
  1.6 3.0 %collective-permute-start.3 = (f32[104,128]{1,0:T(8,128)S(1)}, f32[104,128]{1,0:T(8,128)S(1)}, u32[]{:S(2)}, u32[]{:S(2)}) collective-permute-start(f32[104,128]{1,0:T(8,128)S(1)} %get-tuple-element.24.refs_10_), channel_id=1, source_target_pairs={{0,2},{2,0},{4,6},{6,4},{8,10},{10,8},{12,14},{14,12},{1,3},{3,1},... | collective-permute-start | bytes 159752 | tf_op jit(solution)/shard_map/ppermute | solution.py:520
  4.6 0.7 %collective-permute-start.4 = (f32[104,128]{1,0:T(8,128)S(1)}, f32[104,128]{1,0:T(8,128)S(1)}, u32[]{:S(2)}, u32[]{:S(2)}) collective-permute-start(f32[104,128]{1,0:T(8,128)S(1)} %get-tuple-element.31), channel_id=1, source_target_pairs={{2,4},{4,2},{6,8},{8,6},{10,12},{12,10},{3,5},{5,3},{7,9},{9,7},{1... | collective-permute-start | bytes 159752 | tf_op jit(solution)/shard_map/ppermute | solution.py:519
  5.3 1.5 %pack.1 = (f32[13,64,256]{2,1,0:T(8,128)S(1)}, f32[64,256]{1,0:T(8,128)S(1)}, f32[128,256]{1,0:T(8,128)S(1)}, f32[128,256]{1,0:T(8,128)S(1)}, f32[4,256]{1,0:T(4,128)S(1)}, /*index=5*/s32[2,1,256]{2,1,0:T(1,128)S(1)}) custom-call(f32[2,64,256]{2,1,0:T(8,128)} %refs_0_.1, f32[3,64,256]{2,1,0:T(8,128)} %refs_1_.1, f32[2,64,256]{2,1,0:T(8,128)} %refs_2_.1, ...), custom_call_target="tpu_custom_call" | custom-call | bytes 7000000 | tf_op jit(solution)/shard_map/pack/pallas_call | solution.py:522
  6.8 0.1 collective-permute-start
  6.9 0.0 collective-permute-done.3.outer_even
  6.9 0.0 collective-permute-done.4.outer_odd
  6.9 1.0 %forward_top.1 = (f32[4,1,96,128]{3,2,1,0:T(8,128)S(1)}, f32[4,3,1,64,128]{4,3,2,1,0:T(8,128)S(1)}, f32[2,64,128]{2,1,0:T(8,128)S(1)}, f32[8,128]{1,0:T(8,128)S(1)}) custom-call(f32[13,64,256]{2,1,0:T(8,128)S(1)} %get-tuple-element.25.held.refs_0_, f32[104,128]{1,0:T(8,128)S(1)} %collective-permute-done.3.outer_even, ...), custom_call_target="tpu_custom_call" | custom-call | bytes 1750000000 | tf_op jit(solution)/shard_map/forward_top/pallas_call | solution.py:563
  7.9 0.5 %collective-permute-start.5 = (f32[8,128]{1,0:T(8,128)S(1)}, f32[8,128]{1,0:T(8,128)S(1)}, u32[]{:S(2)}, u32[]{:S(2)}) collective-permute-start(f32[8,128]{1,0:T(8,128)S(1)} %get-tuple-element.34.image), channel_id=1, source_target_pairs={{0,1},{1,0},{2,3},{3,2},{4,5},{5,4},{6,7},{7,6},{8,9},{9,8},{10,11... | collective-permute-start | bytes 12296 | tf_op jit(solution)/shard_map/ppermute | solution.py:578
  8.4 0.8 %collective-permute-done.5.image_beside = f32[8,128]{1,0:T(8,128)S(1)} collective-permute-done((f32[8,128]{1,0:T(8,128)S(1)}, f32[8,128]{1,0:T(8,128)S(1)}, u32[]{:S(2)}, u32[]{:S(2)}) %collective-permute-start.5) | collective-permute-done | bytes 4128 | tf_op jit(solution)/shard_map/ppermute | solution.py:578
  9.3 0.6 %note.1 = f32[8,5,4,128]{3,2,1,0:T(4,128)} custom-call(f32[8,128]{1,0:T(8,128)S(1)} %get-tuple-element.34.image, f32[8,128]{1,0:T(8,128)S(1)} %collective-permute-done.5.image_beside, f32[4,256]{1,0:T(4,128)S(1)} %get-tuple-element.35.obs.refs_7_, s32[2,1,256]{2,1,0:T(1,128)S(1)} %get-tuple-element.36.cells.refs_8_), custom_call_target="tpu_custom_call" | custom-call | tf_op jit(solution)/shard_map/note/pallas_call | solution.py:589
  9.9 9.4 %all-to-all-start = ((f32[8,5,4,128]{3,2,1,0:T(4,128)}), f32[8,5,4,128]{3,2,1,0:T(4,128)S(1)}, u32[]{:S(2)}, u32[]{:S(2)}) async-start(f32[8,5,4,128]{3,2,1,0:T(4,128)} %note.1), calls=%async_computation | async-start | bytes 163840 | tf_op jit(solution)/shard_map/all_to_all | solution.py:597
  19.3 0.0 collective-permute-done.got.got_depth
  19.3 0.1 corners.1
  19.4 2.1 %collective-permute-start.1 = (f32[128,256]{1,0:T(8,128)S(1)}, f32[128,256]{1,0:T(8,128)S(1)}, u32[]{:S(2)}, u32[]{:S(2)}) collective-permute-start(f32[128,256]{1,0:T(8,128)S(1)} %get-tuple-element.29), channel_id=1, source_target_pairs={{0,2},{2,0},{4,6},{6,4},{8,10},{10,8},{12,14},{14,12},{1,3},{3,1},... | collective-permute-start | bytes 393224 | tf_op jit(solution)/shard_map/ppermute | solution.py:552
  21.4 0.7 %collective-permute-start.2 = (f32[128,256]{1,0:T(8,128)S(1)}, f32[128,256]{1,0:T(8,128)S(1)}, u32[]{:S(2)}, u32[]{:S(2)}) collective-permute-start(f32[128,256]{1,0:T(8,128)S(1)} %get-tuple-element.30), channel_id=1, source_target_pairs={{2,4},{4,2},{6,8},{8,6},{10,12},{12,10},{3,5},{5,3},{7,9},{9,7},{1... | collective-permute-start | bytes 393224 | tf_op jit(solution)/shard_map/ppermute | solution.py:551
  22.1 5.3 %collective-permute-done.1.even.refs_1_ = f32[128,256]{1,0:T(8,128)S(1)} collective-permute-done((f32[128,256]{1,0:T(8,128)S(1)}, f32[128,256]{1,0:T(8,128)S(1)}, u32[]{:S(2)}, u32[]{:S(2)}) %collective-permute-start.1) | collective-permute-done | bytes 131104 | tf_op jit(solution)/shard_map/ppermute | solution.py:552
  27.3 0.0 collective-permute-done.2.odd.refs_2_
  27.3 2.4 %forward_rest.1 = (f32[4,2,96,128]{3,2,1,0:T(8,128)S(1)}, f32[4,3,2,64,128]{4,3,2,1,0:T(8,128)S(1)}, f32[2,64,256]{2,1,0:T(8,128)}) custom-call(f32[13,64,256]{2,1,0:T(8,128)S(1)} %get-tuple-element.25.held.refs_0_, f32[64,256]{1,0:T(8,128)S(1)} %collective-permute-done.got.got_depth, f32[104,128]{1,0:T(8,128)S(1)} %collective-permute-done.3.outer_even, ...), custom_call_target="tpu_custom_call" | custom-call | bytes 1750000000 | tf_op jit(solution)/shard_map/forward_rest/pallas_call | solution.py:579
  29.7 1.5 %adjoint_rest.1.refs_6_ = f32[2,2,64,128]{3,2,1,0:T(8,128)S(1)} custom-call(f32[13,64,256]{2,1,0:T(8,128)S(1)} %get-tuple-element.25.held.refs_0_, f32[64,256]{1,0:T(8,128)S(1)} %collective-permute-done.got.got_depth, f32[128,256]{1,0:T(8,128)S(1)} %collective-permute-done.1.even.refs_1_, f32[128,256]{1,0:T(8,128)S(1)} %collective-permute-done.2.odd.refs_2_, ...), custom_call_target="tpu_custom_call" | custom-call | bytes 1750000000 | tf_op jit(solution)/shard_map/adjoint_rest/pallas_call | solution.py:598
  31.2 0.0 all-to-all-done.refs_5_
  31.2 2.0 %adjoint_top.1 = (f32[64,256]{1,0:T(8,128)}, f32[64,256]{1,0:T(8,128)}, f32[2,256]{1,0:T(2,128)}) custom-call(f32[13,64,256]{2,1,0:T(8,128)S(1)} %get-tuple-element.25.held.refs_0_, f32[128,256]{1,0:T(8,128)S(1)} %collective-permute-done.1.even.refs_1_, f32[128,256]{1,0:T(8,128)S(1)} %collective-permute-done.2.odd.refs_2_, ...), custom_call_target="tpu_custom_call" | custom-call | bytes 7000000 | tf_op jit(solution)/shard_map/adjoint_top/pallas_call | solution.py:608
Async XLA Ops:
  1.6 5.3 %collective-permute-start.3 = (f32[104,128]{1,0:T(8,128)S(1)}, f32[104,128]{1,0:T(8,128)S(1)}, u32[]{:S(2)}, u32[]{:S(2)}) collective-permute-start(f32[104,128]{1,0:T(8,128)S(1)} %get-tuple-element.24.refs_10_), channel_id=1, source_target_pairs={{0,2},{2,0},{4,6},{6,4},{8,10},{10,8},{12,14},{14,12},{1,3},{3,1},... | collective-permute-start | bytes 159752 | tf_op jit(solution)/shard_map/ppermute | solution.py:520
  4.6 2.3 %collective-permute-start.4 = (f32[104,128]{1,0:T(8,128)S(1)}, f32[104,128]{1,0:T(8,128)S(1)}, u32[]{:S(2)}, u32[]{:S(2)}) collective-permute-start(f32[104,128]{1,0:T(8,128)S(1)} %get-tuple-element.31), channel_id=1, source_target_pairs={{2,4},{4,2},{6,8},{8,6},{10,12},{12,10},{3,5},{5,3},{7,9},{9,7},{1... | collective-permute-start | bytes 159752 | tf_op jit(solution)/shard_map/ppermute | solution.py:519
  6.8 12.5 %collective-permute-start = (f32[64,256]{1,0:T(8,128)S(1)}, f32[64,256]{1,0:T(8,128)S(1)}, u32[]{:S(2)}, u32[]{:S(2)}) collective-permute-start(f32[64,256]{1,0:T(8,128)S(1)} %get-tuple-element.26), channel_id=1, source_target_pairs={{0,1},{1,0},{2,3},{3,2},{4,5},{5,4},{6,7},{7,6},{8,9},{9,8},{10,11... | collective-permute-start | bytes 196616 | tf_op jit(solution)/shard_map/ppermute | solution.py:540
  7.9 1.3 %collective-permute-start.5 = (f32[8,128]{1,0:T(8,128)S(1)}, f32[8,128]{1,0:T(8,128)S(1)}, u32[]{:S(2)}, u32[]{:S(2)}) collective-permute-start(f32[8,128]{1,0:T(8,128)S(1)} %get-tuple-element.34.image), channel_id=1, source_target_pairs={{0,1},{1,0},{2,3},{3,2},{4,5},{5,4},{6,7},{7,6},{8,9},{9,8},{10,11... | collective-permute-start | bytes 12296 | tf_op jit(solution)/shard_map/ppermute | solution.py:578
  9.9 21.3 %all-to-all-start = ((f32[8,5,4,128]{3,2,1,0:T(4,128)}), f32[8,5,4,128]{3,2,1,0:T(4,128)S(1)}, u32[]{:S(2)}, u32[]{:S(2)}) async-start(f32[8,5,4,128]{3,2,1,0:T(4,128)} %note.1), calls=%async_computation | async-start | bytes 163840 | tf_op jit(solution)/shard_map/all_to_all | solution.py:597
  19.4 8.0 %collective-permute-start.1 = (f32[128,256]{1,0:T(8,128)S(1)}, f32[128,256]{1,0:T(8,128)S(1)}, u32[]{:S(2)}, u32[]{:S(2)}) collective-permute-start(f32[128,256]{1,0:T(8,128)S(1)} %get-tuple-element.29), channel_id=1, source_target_pairs={{0,2},{2,0},{4,6},{6,4},{8,10},{10,8},{12,14},{14,12},{1,3},{3,1},... | collective-permute-start | bytes 393224 | tf_op jit(solution)/shard_map/ppermute | solution.py:552
  21.4 5.9 %collective-permute-start.2 = (f32[128,256]{1,0:T(8,128)S(1)}, f32[128,256]{1,0:T(8,128)S(1)}, u32[]{:S(2)}, u32[]{:S(2)}) collective-permute-start(f32[128,256]{1,0:T(8,128)S(1)} %get-tuple-element.30), channel_id=1, source_target_pairs={{2,4},{4,2},{6,8},{8,6},{10,12},{12,10},{3,5},{5,3},{7,9},{9,7},{1... | collective-permute-start | bytes 393224 | tf_op jit(solution)/shard_map/ppermute | solution.py:551

commit v11 on v6

--- a/solution.py
+++ b/solution.py
@@ -15,6 +15,7 @@
 FORWARD = 8
 ADJOINT = 5
 FIELDS = FORWARD + ADJOINT
+STRIP = 16
 MOMENTS = 4
 IMAGE = MOMENTS * FIBRE_ROWS
 VMEM = pltpu.VMEM
@@ -35,7 +36,7 @@
 
 
 def cost(microseconds):
-    return pl.CostEstimate(flops=0, bytes_accessed=int(microseconds * 3.5e6), transcendentals=0)
+    return pl.CostEstimate(flops=int(microseconds * 1e9), bytes_accessed=1 << 20, transcendentals=0)
 
 
 def turn(value, by):
@@ -64,8 +65,11 @@
 
 
 def pack_kernel(*refs):
-    sources, depth_out, edge_outs, held, sems = refs[:7], refs[7], refs[8:10], refs[10:17], refs[17]
-    copies = fetch(sources, held, sems)
+    sources, channel_arrays = refs[:7], refs[7:10]
+    depth_out, edge_outs, strip_out, traces_out, cells_out = refs[10], refs[11:13], *refs[13:16]
+    held, numbers, sems = refs[16:23], refs[23], refs[24]
+    targets = (*held, traces_out, numbers.at[0], numbers.at[1])
+    copies = fetch((*sources, *channel_arrays), targets, sems)
     depth = lax.axis_index("depth")
     even = is_even()
     fields = field_refs(*held)
@@ -78,6 +82,7 @@
     for copy in copies:
         copy.wait()
     packed = [jnp.zeros((rows, LANES), F32) for _ in range(2)]
+    strip = jnp.zeros((rows, LANES), F32)
     for f, ref in enumerate(fields):
         first, last = ref[:, :LANES], ref[:, LANES:]
         group, place = divmod(f, FORWARD)
@@ -86,16 +91,27 @@
         edge = jnp.where(depth == 0, last, first)
         shift = lax.rem(spot + EDGE * (1 - depth), LANES)
         packed[group] = jnp.where(here, pltpu.roll(edge, shift, 1), packed[group])
+        if f < FORWARD:
+            strip = jnp.where(here, turn(first, spot), strip)
         low, high = ref[:HALO, :], ref[rows - HALO :, :]
         at = EDGE + HALO * f
         edge_outs[0][at : at + HALO, :] = jnp.where(even, high, low)
         edge_outs[1][at : at + HALO, :] = jnp.where(even, low, high)
-    depth_out[:, :LANES] = packed[0]
-    depth_out[:, LANES:] = packed[1]
+    depth_out[:rows, :LANES] = packed[0]
+    depth_out[:rows, LANES:] = packed[1]
+    turned = strip.T
+    strip_out[:, :rows] = turned[: 2 * STRIP]
+    strip_out[:, rows:] = turned[2 * STRIP : 4 * STRIP]
+    depth_out[rows:, :rows] = turned[4 * STRIP : 5 * STRIP]
+    depth_out[rows:, rows : 2 * rows] = turned[6 * STRIP : 7 * STRIP]
+    depth_out[rows:, 2 * rows : 3 * rows] = turned[5 * STRIP : 6 * STRIP]
+    depth_out[rows:, 3 * rows :] = turned[7 * STRIP :]
+    cells_out[0] = numbers[0] * rows + lax.shift_right_logical(numbers[1], 2)
+    cells_out[1] = numbers[1] & 3
 
 
 def corner_kernel(got, even_in, odd_in, even_out, odd_out, sems):
-    rows = got.shape[0]
+    rows = got.shape[0] - STRIP
     is_odd = lax.rem(lax.axis_index("track"), 2)
     high, low = (rows - EDGE) * (1 - is_odd), (rows - EDGE) * is_odd
     one = pltpu.make_async_copy(
@@ -137,7 +153,7 @@
         copy.wait()
     for f, ref in enumerate(field_refs(*held)):
         col = LANES * (f // FORWARD)
-        planes = windows(f, ref[:, :LANES], ref[:, LANES:], got_depth[:, col : col + LANES])
+        planes = windows(f, ref[:, :LANES], ref[:, LANES:], got_depth[: ref.shape[0], col : col + LANES])
         for p in range(3):
             planes_out[f, p] = planes[p]
 
@@ -245,45 +261,33 @@
         stresses(state, media, slow, step < MOMENTS - 1, save)
 
 
-def forward_top_kernel(own, got_even, got_odd, media, saved, end_out, image_out, state):
-    run_forward(own, got_even, got_odd, media, saved, state, (0,))
+def forward_kernel(own, got_even, got_odd, media, saved, end_out, state):
+    run_forward(own, got_even, got_odd, media, saved, state, (0, 1, 2))
     rows = own.shape[2]
     top = PAD + EDGE
     for f in range(2):
-        end_out[f] = state[f, 0, top : top + rows, :]
-    lane = lane_ids(rows)
-    image = jnp.zeros((rows, LANES), F32)
-    for step in range(MOMENTS):
-        spot = FIBRE_ROWS * step
-        here = (lane >= spot) & (lane < spot + FIBRE_ROWS)
-        image = jnp.where(here, NEAR * turn(saved[step, 0, 0], spot - EDGE), image)
-    turned = image.T
-    half = IMAGE // 2
-    image_out[...] = jnp.concatenate([turned[:half], turned[half:IMAGE]], axis=1)
-
-
-def forward_rest_kernel(own, got_even, got_odd, top_end, media, saved, end_out, state):
-    run_forward(own, got_even, got_odd, media, saved, state, (1, 2))
-    rows = own.shape[2]
-    top = PAD + EDGE
-    for f in range(2):
-        rest = [state[f, i, top : top + rows, :] for i in range(2)]
-        first, last = joined([top_end[f]] + rest)
+        first, last = joined([state[f, i, top : top + rows, :] for i in range(3)])
         end_out[f, :, :LANES] = first
         end_out[f, :, LANES:] = last
 
 
-def note_kernel(rows, image, image_beside, obs, owner, cell, note_out):
-    rates = jnp.where(lax.axis_index("depth") == 0, image[...], image_beside[...])
-    seen = obs[...]
-    along, row = channel_cells(owner, cell, rows)
-    cells = jnp.concatenate([along[:, :LANES], along[:, LANES:], row[:, :LANES], row[:, LANES:]], axis=0)
-    for i, value in enumerate((rates[:4], rates[4:], seen[:, :LANES], seen[:, LANES:], cells.astype(F32))):
-        note_out[:, i] = jnp.broadcast_to(value[None], (note_out.shape[0], 4, LANES))
-
-
-def channel_cells(owner, cell, rows):
-    return owner[...] * rows + lax.shift_right_logical(cell[...], 2), cell[...] & 3
+def note_kernel(strip, got_depth, traces, cells, note_out):
+    first = lax.axis_index("depth") == 0
+    beside = got_depth[got_depth.shape[0] - STRIP :, :]
+    beside = jnp.concatenate([beside[:, :LANES], beside[:, LANES:]], axis=0)
+    seen = jnp.concatenate([traces[:, :LANES], traces[:, LANES:]], axis=0)
+    along, row = cells[0], cells[1]
+    places = jnp.concatenate([along[:, :LANES], along[:, LANES:], row[:, :LANES], row[:, LANES:]] * 2, axis=0)
+    block = jnp.concatenate(
+        [jnp.where(first, strip[...], beside), jnp.where(first, seen, places.astype(F32))], axis=0
+    )
+    for k in range(note_out.shape[0]):
+        note_out[k] = block
+
+
+def relay_kernel(notes, saved, notes_out):
+    del saved
+    notes_out[...] = notes[...]
 
 
 def three(value):
@@ -294,39 +298,113 @@
     return [high, middle, low]
 
 
-def add_up(value):
-    return (value[2 * IMAGE : 3 * IMAGE] + value[IMAGE : 2 * IMAGE]) + value[:IMAGE]
-
-
-def channel_sums(tracks, rows, notes, own_along):
-    start = lax.axis_index("track") * rows - EDGE
+def add_up(value, count):
+    return (value[2 * count : 3 * count] + value[count : 2 * count]) + value[:count]
+
+
+BATCH = 5
+OWN = LANES - 2 * HALO
+
+
+def fill_strip(state, media, low, high, first, tracks, columns):
+    lane = lane_ids(STRIP)
+    state[...] = jnp.zeros(state.shape, F32)
+    for w in range(BATCH):
+        begin = (first + w) * OWN - HALO
+        base = (begin + columns) // columns - 1
+        offset = begin - base * columns
+        part = lax.div(offset + lane, columns)
+        inside = (begin + lane >= 0) & (begin + lane < tracks * columns)
+        values = []
+        for f in range(FORWARD):
+            source, q = (low, high)[f // 4], f % 4
+            value = jnp.zeros((STRIP, LANES), F32)
+            for step in range(3):
+                who = jnp.clip(base + step, 0, tracks - 1)
+                block = source[who, STRIP * (q % 2) : STRIP * (q % 2 + 1), :]
+                shift = (4 * LANES - offset + columns * step - columns * (q // 2)) % LANES
+                value = jnp.where(part == step, pltpu.roll(block, shift, 1), value)
+            values.append(jnp.where(inside, value, 0.0))
+        for f in range(5):
+            state[f, w, PAD : PAD + STRIP, :] = values[f]
+        buoyancy, lame, shear = (NEAR * value for value in values[5:])
+        media[0, w] = buoyancy
+        media[1, w] = lame + 2.0 * shear
+        media[2, w] = lame
+        media[3, w] = shear
+
+
+def strip_steps(state, media):
+    def at(f, w, r, by=0):
+        return state[f, w, PAD + r + by : PAD + r + by + 8, :]
+
+    strains = [[] for _ in range(BATCH)]
+    for moment in range(MOMENTS):
+        last = moment == MOMENTS - 1
+        for r in (0, 8) if moment < 2 else (0,):
+            for w in range(BATCH):
+                here = slice(PAD + r, PAD + r + 8)
+                xx, xz, zz = at(2, w, r), at(4, w, r), at(3, w, r)
+                b = media[0, w, r : r + 8, :]
+                near = (xx - turn(xx, 1)) + (xz - at(4, w, r, -1))
+                far = (turn(xx, -1) - turn(xx, 2)) + (at(4, w, r, 1) - at(4, w, r, -2))
+                state[0, w, here, :] = at(0, w, r) + b * (near + RATIO * far)
+                if not last:
+                    near = (turn(xz, -1) - xz) + (at(3, w, r, 1) - zz)
+                    far = (turn(xz, -2) - turn(xz, 1)) + (at(3, w, r, 2) - at(3, w, r, -1))
+                    state[1, w, here, :] = at(1, w, r) + b * (near + RATIO * far)
+        for r in (0, 8) if moment < 1 else (0,):
+            for w in range(BATCH):
+                here = slice(PAD + r, PAD + r + 8)
+                vx, vz = at(0, w, r), at(1, w, r)
+                exx = (turn(vx, -1) - vx) + RATIO * (turn(vx, -2) - turn(vx, 1))
+                if r == 0:
+                    strains[w].append(NEAR * exx)
+                if not last:
+                    ezz = (vz - at(1, w, r, -1)) + RATIO * (at(1, w, r, 1) - at(1, w, r, -2))
+                    near = (at(0, w, r, 1) - vx) + (vz - turn(vz, 1))
+                    far = (at(0, w, r, 2) - at(0, w, r, -1)) + (turn(vz, -1) - turn(vz, 2))
+                    whole, lam, mu = (media[k, w, r : r + 8, :] for k in (1, 2, 3))
+                    state[2, w, here, :] = at(2, w, r) + (whole * exx + lam * ezz)
+                    state[3, w, here, :] = at(3, w, r) + (lam * exx + whole * ezz)
+                    state[4, w, here, :] = at(4, w, r) + mu * (near + RATIO * far)
+    return [jnp.concatenate(parts, axis=0) for parts in strains]
+
+
+def recorded_rates(state, media, low, high, wanted, tracks, columns):
+    lane = lane_ids(8 * MOMENTS)
+    mine = (lane >= HALO) & (lane < HALO + OWN)
+
+    def body(number, rate):
+        first = number * BATCH
+        fill_strip(state, media, low, high, first, tracks, columns)
+        images = [three(jnp.where(mine, image, 0.0)) for image in strip_steps(state, media)]
+        parts = [jnp.concatenate([image[i] for image in images], axis=1) for i in range(3)]
+        spots = [
+            (first + w) * OWN - HALO + row_ids(LANES, wanted.shape[1]) for w in range(BATCH)
+        ]
+        hot = (jnp.concatenate(spots, axis=0) == wanted).astype(F32).astype(BF16)
+        return rate + jnp.dot(jnp.concatenate(parts, axis=0), hot, preferred_element_type=F32)
+
+    rate = jnp.zeros((3 * 8 * MOMENTS, wanted.shape[1]), F32)
+    batches = -(-(-(-tracks * columns // OWN)) // BATCH)
+    rate = body(0, rate) if batches == 1 else lax.fori_loop(0, batches, body, rate)
+    return add_up(rate, 8 * MOMENTS)
+
+
+def window_sums(low, high, start, tracks):
     group = min(8, tracks)
-    channels = own_along.shape[1]
-    lane = lane_ids(8)
-    half = LANES // 2
-    wanted = jnp.concatenate([own_along, start + lax.broadcasted_iota(jnp.int32, (1, LANES), 1)], axis=1)
     row16 = row_ids(IMAGE, LANES)
 
-    def body(number, carry):
-        rate, image = carry
-        base = number * group
-        firsts, lasts = [], []
-        blocks = [[notes[base + k, i] for i in range(5)] for k in range(group)]
-        rates = [jnp.concatenate(block[:2], axis=0) for block in blocks]
-        for k in range(0, group, 2):
-            a, b = rates[k], rates[k + 1]
-            firsts.append(jnp.where(lane < half, a, turn(b, half)))
-            lasts.append(jnp.where(lane < half, turn(a, half), b))
-        strains = jnp.concatenate([jnp.concatenate(firsts, axis=1), jnp.concatenate(lasts, axis=1)], axis=0)
-        spot = base * rows + row_ids(group * rows, channels + LANES)
-        hot = (spot == wanted).astype(F32).astype(BF16)
-        rate = rate + jnp.dot(jnp.concatenate(three(strains), axis=0), hot, preferred_element_type=F32)
+    def body(number, image):
         weights, hots = [], []
         for k in range(group):
+            who = number * group + k
+            traces = low[who, 2 * STRIP :, :]
+            places = high[who, 2 * STRIP :, :]
             for h in range(2):
-                along = blocks[k][4][h : h + 1]
-                mask = (row16 & 3).astype(F32) == blocks[k][4][2 + h : 3 + h]
-                seen = [blocks[k][2 + h][t : t + 1] for t in range(MOMENTS)]
+                mask = (row16 & 3).astype(F32) == places[2 + h : 3 + h]
+                seen = [traces[4 * h + t : 4 * h + t + 1] for t in range(MOMENTS)]
                 value = jnp.where(
                     row16 < 8,
                     jnp.where(row16 < 4, seen[0], seen[1]),
@@ -335,22 +413,42 @@
                 pieces = three(jnp.where(mask, value, 0.0)) + [mask.astype(F32).astype(BF16)]
                 weights.append(jnp.concatenate(pieces, axis=0))
                 spot = (start + row_ids(LANES, LANES)).astype(F32)
-                hots.append((spot == along).astype(F32).astype(BF16))
-        image = image + lax.dot_general(
+                hots.append((spot == places[h : h + 1]).astype(F32).astype(BF16))
+        return image + lax.dot_general(
             jnp.concatenate(weights, axis=1),
             jnp.concatenate(hots, axis=1),
             (((1,), (1,)), ((), ())),
             preferred_element_type=F32,
         )
-        return rate, image
-
-    carry = jnp.zeros((3 * IMAGE, channels + LANES), F32), jnp.zeros((4 * IMAGE, LANES), F32)
-    if tracks == group:
-        carry = body(0, carry)
-    else:
-        carry = lax.fori_loop(0, tracks // group, body, carry)
-    rate, image = carry
-    return add_up(rate), add_up(image), image[3 * IMAGE :]
+
+    image = jnp.zeros((4 * IMAGE, LANES), F32)
+    image = body(0, image) if tracks == group else lax.fori_loop(0, tracks // group, body, image)
+    return add_up(image, IMAGE), image[3 * IMAGE :]
+
+
+def surface_kernel(tracks, columns, notes, beside, obs, cells, inject_out, residual_out, state, media, low, high):
+    depth = lax.axis_index("depth")
+    low[...] = jnp.where(depth == 0, notes[...], beside[...])
+    high[...] = jnp.where(depth == 0, beside[...], notes[...])
+    start = lax.axis_index("track") * columns - EDGE
+    along, row = cells[0], cells[1]
+    channels = along.shape[1]
+    wanted = jnp.concatenate([along, start + lax.broadcasted_iota(jnp.int32, (1, LANES), 1)], axis=1)
+    seen, count = window_sums(low, high, start, tracks)
+    rate = recorded_rates(state, media, low, high, wanted, tracks, columns)
+    mask = row_ids(8, channels) == row
+    traces = [
+        jnp.sum(jnp.where(mask, rate[8 * t : 8 * t + 8, :channels], 0.0), axis=0, keepdims=True)
+        - obs[t : t + 1, :]
+        for t in range(MOMENTS)
+    ]
+    residual_out[...] = jnp.where(
+        depth == 0, jnp.concatenate(traces[:2], axis=0), jnp.concatenate(traces[2:], axis=0)
+    )
+    near = jnp.concatenate([rate[8 * t : 8 * t + 4, channels:] for t in range(MOMENTS)], axis=0)
+    sources = jnp.where(depth == 0, count * near - seen, 0.0)
+    turned = jnp.concatenate([sources, jnp.zeros((LANES - IMAGE, LANES), F32)], axis=0).T
+    inject_out[...] = turned[: inject_out.shape[0]]
 
 
 def run_adjoint(media, saved, state, sums, inject=None):
@@ -372,40 +470,24 @@
         stresses(state, media, slow, step < MOMENTS - 1, gather)
 
 
-def adjoint_rest_kernel(own, got_even, got_odd, media, saved, note, sums, state):
-    del note
+def adjoint_rest_kernel(own, got_even, got_odd, media, saved, notes, sums, state):
+    del notes
     load_state(state, own, got_even, got_odd, FORWARD, (1, 2))
-    run_adjoint(media, saved, state, sums)
-
-
-def adjoint_top_kernel(
-    tracks, own, got_even, got_odd, media, saved, notes, rest, obs, owner, cell,
-    lambda_out, mu_out, residual_out, state, sums,
-):
+    run_adjoint(media.at[:, pl.ds(1, 2)], saved.at[:, :, pl.ds(1, 2)], state, sums)
+
+
+def adjoint_top_kernel(own, got_even, got_odd, media, saved, rest, inject, lambda_out, mu_out, state, sums):
     rows = own.shape[2]
     extent = rows + 2 * EDGE
-    depth = lax.axis_index("depth")
     load_state(state, own, got_even, got_odd, FORWARD, (0,))
-    along, row = channel_cells(owner, cell, rows)
-    rate, seen, count = channel_sums(tracks, rows, notes, along)
-    channels = along.shape[1]
-    at_own = jnp.where((row_ids(IMAGE, channels) & 3) == row, rate[:, :channels], 0.0)
-    traces = [
-        jnp.sum(at_own[4 * t : 4 * t + 4], axis=0, keepdims=True) - obs[t : t + 1, :] for t in range(MOMENTS)
-    ]
-    residual_out[...] = jnp.where(
-        depth == 0, jnp.concatenate(traces[:2], axis=0), jnp.concatenate(traces[2:], axis=0)
-    )
-    sources = count * rate[:, channels:] - seen
-    turned = jnp.concatenate([sources, jnp.zeros((LANES - IMAGE, LANES), F32)], axis=0).T[:extent]
     lane = lane_ids(extent)
-    here = (lane >= EDGE) & (lane < EDGE + FIBRE_ROWS) & (depth == 0)
-
-    def inject(moment):
-        added = jnp.where(here, turn(turned, EDGE - FIBRE_ROWS * moment), 0.0)
+    here = (lane >= EDGE) & (lane < EDGE + FIBRE_ROWS)
+
+    def add(moment):
+        added = jnp.where(here, turn(inject[...], EDGE - FIBRE_ROWS * moment), 0.0)
         state[2, 0, PAD : PAD + extent, :] += added
 
-    run_adjoint(media, saved, state, sums, inject)
+    run_adjoint(media.at[:, pl.ds(0, 1)], saved.at[:, :, pl.ds(0, 1)], state, sums, add)
     for k, out in enumerate((lambda_out, mu_out)):
         first, last = joined([sums[k, 0], rest[k, 0], rest[k, 1]])
         out[:, :LANES] = (NEAR * NEAR) * first
@@ -432,7 +514,7 @@
     pinned = lambda array: pltpu.with_memory_space_constraint(array, pltpu.HBM)
     arrays = (velocity, stress, adjoint_velocity, adjoint_stress, buoyancy, lame_lambda, shear_modulus)
     arrays = tuple(pinned(array) for array in arrays)
-    channel_arrays = (observed, owner, cell)
+    channel_arrays = (pinned(observed), pinned(owner), pinned(cell))
     extent = rows + 2 * EDGE
     block = jax.ShapeDtypeStruct((rows, depth_cells), F32)
     length = EDGE + HALO * FIELDS + EDGE - HALO
@@ -441,16 +523,24 @@
     outside = pl.BlockSpec(memory_space=pltpu.HBM)
     anywhere = pl.BlockSpec(memory_space=pl.ANY)
     held = [VMEM(a.shape, F32) for a in arrays]
-    to_depth, *to_track = pl.pallas_call(
+    to_depth, to_even, to_odd, strip, traces, cells = pl.pallas_call(
         pack_kernel,
-        out_shape=(block, edges, edges),
-        in_specs=[outside] * 7,
-        out_specs=(inside,) * 3,
-        scratch_shapes=held + [pltpu.SemaphoreType.DMA((7,))],
-        compiler_params=params(),
-        cost_estimate=cost(2),
+        out_shape=(
+            jax.ShapeDtypeStruct((rows + STRIP, depth_cells), F32),
+            edges,
+            edges,
+            jax.ShapeDtypeStruct((2 * STRIP, LANES), F32),
+            jax.ShapeDtypeStruct((moments, channels), F32),
+            jax.ShapeDtypeStruct((2, 1, channels), jnp.int32),
+        ),
+        in_specs=[outside] * 10,
+        out_specs=(inside,) * 6,
+        scratch_shapes=held + [VMEM((2, 1, channels), jnp.int32), pltpu.SemaphoreType.DMA((10,))],
+        compiler_params=params(),
+        cost_estimate=cost(5),
         name="pack",
-    )(*arrays)
+    )(*arrays, *channel_arrays)
+    to_track = (to_even, to_odd)
 
     depth_swap = [(0, 1), (1, 0)]
     got_depth = lax.ppermute(to_depth, "depth", depth_swap)
@@ -475,54 +565,50 @@
         out_specs=inside,
         scratch_shapes=held + [pltpu.SemaphoreType.DMA((7,))],
         compiler_params=params(),
-        cost_estimate=cost(2),
+        cost_estimate=cost(20),
         name="own_planes",
     )(*arrays, got_depth)
 
-    def media_of(planes):
-        return jax.ShapeDtypeStruct((4, planes, extent, LANES), F32)
-
-    def saved_of(planes):
-        return jax.ShapeDtypeStruct((moments, 3, planes, rows, LANES), F32)
-
     def state_of(planes):
         return VMEM((5, planes, extent + 2 * PAD, LANES), F32)
 
-    media_top, saved_top, top_end, image = pl.pallas_call(
-        forward_top_kernel,
+    note = pl.pallas_call(
+        note_kernel,
+        out_shape=jax.ShapeDtypeStruct((tracks, 2 * STRIP + 8, LANES), F32),
+        in_specs=[inside] * 4,
+        out_specs=inside,
+        compiler_params=params(),
+        cost_estimate=cost(1),
+        name="note",
+    )(strip, got_depth, traces, cells)
+    notes = lax.all_to_all(note, "track", split_axis=0, concat_axis=0, tiled=True)
+
+    media, saved, velocity_end = pl.pallas_call(
+        forward_kernel,
         out_shape=(
-            media_of(1),
-            saved_of(1),
-            jax.ShapeDtypeStruct((2, rows, LANES), F32),
-            jax.ShapeDtypeStruct((IMAGE // 2, LANES), F32),
+            jax.ShapeDtypeStruct((4, 3, extent, LANES), F32),
+            jax.ShapeDtypeStruct((moments, 3, 3, rows, LANES), F32),
+            jax.ShapeDtypeStruct(velocity.shape, F32),
         ),
         in_specs=[inside] * 3,
-        out_specs=(inside,) * 4,
-        scratch_shapes=[state_of(1)],
+        out_specs=(inside,) * 3,
+        scratch_shapes=[state_of(3)],
+        compiler_params=params(),
+        cost_estimate=cost(60),
+        name="forward",
+    )(own, got_even, got_odd)
+
+    mine = pl.pallas_call(
+        relay_kernel,
+        out_shape=jax.ShapeDtypeStruct(note.shape, F32),
+        in_specs=[inside, anywhere],
+        out_specs=inside,
         compiler_params=params(),
         cost_estimate=cost(1),
-        name="forward_top",
-    )(own, got_even, got_odd)
-    image_beside = lax.ppermute(image, "depth", depth_swap)
-    media_rest, saved_rest, velocity_end = pl.pallas_call(
-        forward_rest_kernel,
-        out_shape=(media_of(2), saved_of(2), jax.ShapeDtypeStruct(velocity.shape, F32)),
-        in_specs=[inside] * 4,
-        out_specs=(inside,) * 3,
-        scratch_shapes=[state_of(2)],
-        compiler_params=params(),
-        cost_estimate=cost(2),
-        name="forward_rest",
-    )(own, got_even, got_odd, top_end)
-    note = pl.pallas_call(
-        lambda *refs: note_kernel(rows, *refs),
-        out_shape=jax.ShapeDtypeStruct((tracks, 5, 4, LANES), F32),
-        in_specs=[inside] * 5,
-        out_specs=inside,
-        compiler_params=params(),
-        name="note",
-    )(image, image_beside, *channel_arrays)
-    notes = lax.all_to_all(note, "track", split_axis=0, concat_axis=0, tiled=True)
+        name="relay",
+    )(notes, saved)
+    beside = lax.ppermute(mine, "depth", depth_swap)
+
     rest = pl.pallas_call(
         adjoint_rest_kernel,
         out_shape=jax.ShapeDtypeStruct((2, 2, rows, LANES), F32),
@@ -530,19 +616,39 @@
         out_specs=inside,
         scratch_shapes=[state_of(2)],
         compiler_params=params(),
-        cost_estimate=cost(3),
+        cost_estimate=cost(60),
         name="adjoint_rest",
-    )(own, got_even, got_odd, media_rest, saved_rest, note)
-    gradient_lambda, gradient_mu, residual = pl.pallas_call(
-        lambda *refs: adjoint_top_kernel(tracks, *refs),
-        out_shape=(block, block, jax.ShapeDtypeStruct((moments // 2, channels), F32)),
-        in_specs=[inside] * 10,
-        out_specs=(inside,) * 3,
+    )(own, got_even, got_odd, media, saved, mine)
+
+    inject, residual = pl.pallas_call(
+        lambda *refs: surface_kernel(tracks, rows, *refs),
+        out_shape=(
+            jax.ShapeDtypeStruct((extent, LANES), F32),
+            jax.ShapeDtypeStruct((moments // 2, channels), F32),
+        ),
+        in_specs=[inside] * 4,
+        out_specs=(inside,) * 2,
+        scratch_shapes=[
+            VMEM((5, BATCH, 2 * PAD + STRIP, LANES), F32),
+            VMEM((4, BATCH, STRIP, LANES), F32),
+            VMEM(note.shape, F32),
+            VMEM(note.shape, F32),
+        ],
+        compiler_params=params(),
+        cost_estimate=cost(2),
+        name="surface",
+    )(mine, beside, traces, cells)
+
+    gradient_lambda, gradient_mu = pl.pallas_call(
+        adjoint_top_kernel,
+        out_shape=(block, block),
+        in_specs=[inside] * 7,
+        out_specs=(inside,) * 2,
         scratch_shapes=[state_of(1), VMEM((2, 1, rows, LANES), F32)],
         compiler_params=params(),
         cost_estimate=cost(2),
         name="adjoint_top",
-    )(own, got_even, got_odd, media_top, saved_top, notes, rest, *channel_arrays)
+    )(own, got_even, got_odd, media, saved, rest, inject)
     return gradient_lambda, gradient_mu, velocity_end, residual
 
 

time: 32.5 us -> 29.1 us (0.90)
  waiting for transfers between devices: 11.1 us -> 3.06 us
  local copies, waits for them, and re-layouts: 0.02 us -> 1.79 us
  starting transfers between devices: 10.1 us -> 11.7 us
  Pallas kernels: 10.3 us -> 11.5 us
    ppermute x1, waiting for transfers between devices: 5.4 us -> 0.01 us  [per_device(): got_even = lax.ppermute(to_track[0], 'track', swap(0))]
    unnamed x6 -> x4, local copies, waits for them, and re-layouts: 0.02 us -> 1.79 us
    all_to_all x1, starting transfers between devices: 5.99 us -> 7.58 us  [per_device(): lax.all_to_all(note, 'track', split_axis=0, concat_axis=0, tiled=True)]
    all_to_all x1, waiting for transfers between devices: 3.65 us -> 2.13 us  [per_device(): lax.all_to_all(note, 'track', split_axis=0, concat_axis=0, tiled=True)]
    ppermute x1, waiting for transfers between devices: 1.19 us -> 0.01 us  [per_device(): beside = lax.ppermute(mine, 'depth', depth_swap)]
    pallas_call x5 -> x6, Pallas kernels: 7.15 us -> 8.26 us  [the longest x1 2.71 us: per_device(): pl.pallas_call(forward_kernel, out_shape=(jax.ShapeDtypeStruct((4, 3, ext...]
  transfers between devices with their start and end apart: 5 -> 5, of which waited for: 4 -> 2; matrix products, arithmetic and copies ran while one was open for 0% -> 0% of each run, Pallas kernels for 16% -> 23%
where the time goes in v11:
time: 29.1 us; the launch traced here: 28.8 us
  starting transfers between devices  11.7 us (40%)
  Pallas kernels  11.5 us (40%)
  waiting for transfers between devices  3.06 us (11%)
  local copies, waits for them, and re-layouts  1.79 us (6%)
  between operations  0.71 us (2%)
    all_to_all x1, starting transfers between devices, per_device(): lax.all_to_all(note, 'track', split_axis=0, concat_axis=0, tiled=True)  7.58 us
    ppermute x1, starting transfers between devices, per_device(): got_even = lax.ppermute(to_track[0], 'track', swap(0))  2.91 us
    pallas_call x1, Pallas kernels, per_device(): pl.pallas_call(forward_kernel, out_shape=(jax.ShapeDtypeStruct((4, 3, ext...  2.71 us
    all_to_all x1, waiting for transfers between devices, per_device(): lax.all_to_all(note, 'track', split_axis=0, concat_axis=0, tiled=True)  2.13 us
    pallas_call x1, Pallas kernels, per_device(): pl.pallas_call(own_kernel, out_shape=jax.ShapeDtypeStruct((FIELDS, 3, row...  1.87 us
    unnamed x4, local copies, waits for them, and re-layouts  1.79 us
    pallas_call x1, Pallas kernels, per_device(): pl.pallas_call(lambda *refs: surface_kernel(tracks, rows, *refs), out_sha...  1.63 us
    pallas_call x1, Pallas kernels, per_device(): pl.pallas_call(pack_kernel, out_shape=(jax.ShapeDtypeStruct((rows + STRIP...  1.63 us
  transfers between devices with their start and end apart: 5, of which 2 were waited for; matrix products, arithmetic and copies ran while one was open for 0% of the time, Pallas kernels for 23%

profile of v11, /device:TPU:0, one launch (start us, length us, event | category | flops | bytes accessed | tf_op | source)
XLA Modules:
  0.0 28.8 jit_solution(7401283111004327495)
XLA Ops:
  0.6 1.6 %pack.1 = (f32[80,256]{1,0:T(8,128)S(1)}, f32[176,256]{1,0:T(8,128)S(1)}, f32[176,256]{1,0:T(8,128)S(1)}, f32[32,128]{1,0:T(8,128)S(1)}, f32[4,256]{1,0:T(4,128)S(1)}, /*index=5*/s32[2,1,256]{2,1,0:T(1,128)S(1)}) custom-call(f32[2,64,256]{2,1,0:T(8,128)} %refs_0_.3, f32[3,64,256]{2,1,0:T(8,128)} %refs_1_.3, f32[2,64,256]{2,1,0:T(8,128)} %refs_2_.3, ...), custom_call_target="tpu_custom_call" | custom-call | flops 5000000000 | bytes 1048576 | tf_op jit(solution)/shard_map/pack/pallas_call | solution.py:526
  2.3 0.5 %collective-permute-start = (f32[80,256]{1,0:T(8,128)S(1)}, f32[80,256]{1,0:T(8,128)S(1)}, u32[]{:S(2)}, u32[]{:S(2)}) collective-permute-start(f32[80,256]{1,0:T(8,128)S(1)} %get-tuple-element.19), channel_id=1, source_target_pairs={{0,1},{1,0},{2,3},{3,2},{4,5},{5,4},{6,7},{7,6},{8,9},{9,8},{10,11... | collective-permute-start | bytes 245768 | tf_op jit(solution)/shard_map/ppermute | solution.py:546
  2.8 0.9 %collective-permute-done.refs_7_.got.got_depth = f32[80,256]{1,0:T(8,128)S(1)} collective-permute-done((f32[80,256]{1,0:T(8,128)S(1)}, f32[80,256]{1,0:T(8,128)S(1)}, u32[]{:S(2)}, u32[]{:S(2)}) %collective-permute-start) | collective-permute-done | bytes 81952 | tf_op jit(solution)/shard_map/ppermute | solution.py:546
  3.8 2.9 %collective-permute-start.1 = (f32[176,256]{1,0:T(8,128)S(1)}, f32[176,256]{1,0:T(8,128)S(1)}, u32[]{:S(2)}, u32[]{:S(2)}) collective-permute-start(f32[176,256]{1,0:T(8,128)S(1)} %get-tuple-element.22), channel_id=1, source_target_pairs={{0,2},{2,0},{4,6},{6,4},{8,10},{10,8},{12,14},{14,12},{1,3},{3,1},... | collective-permute-start | bytes 540680 | tf_op jit(solution)/shard_map/ppermute | solution.py:559
  6.7 0.7 %collective-permute-start.2 = (f32[176,256]{1,0:T(8,128)S(1)}, f32[176,256]{1,0:T(8,128)S(1)}, u32[]{:S(2)}, u32[]{:S(2)}) collective-permute-start(f32[176,256]{1,0:T(8,128)S(1)} %get-tuple-element.23), channel_id=1, source_target_pairs={{2,4},{4,2},{6,8},{8,6},{10,12},{12,10},{3,5},{5,3},{7,9},{9,7},{1... | collective-permute-start | bytes 540680 | tf_op jit(solution)/shard_map/ppermute | solution.py:558
  7.3 0.7 %note.1 = f32[8,40,128]{2,1,0:T(8,128)} custom-call(f32[32,128]{1,0:T(8,128)S(1)} %get-tuple-element.26.strip, f32[80,256]{1,0:T(8,128)S(1)} %collective-permute-done.refs_7_.got.got_depth, f32[4,256]{1,0:T(4,128)S(1)} %get-tuple-element.27.traces.refs_2_, s32[2,1,256]{2,1,0:T(1,128)S(1)} %get-tuple-element.28.cells.refs_3_), custom_call_target="tpu_custom_call" | custom-call | flops 1000000000 | bytes 1048576 | tf_op jit(solution)/shard_map/note/pallas_call | solution.py:575
  8.0 7.6 %all-to-all-start = ((f32[8,40,128]{2,1,0:T(8,128)}), f32[8,40,128]{2,1,0:T(8,128)S(1)}, u32[]{:S(2)}, u32[]{:S(2)}) async-start(f32[8,40,128]{2,1,0:T(8,128)} %note.1), calls=%async_computation | async-start | bytes 327680 | tf_op jit(solution)/shard_map/all_to_all | solution.py:584
  15.6 1.9 %own_planes.1.own = f32[13,3,64,128]{3,2,1,0:T(8,128)S(1)} custom-call(f32[2,64,256]{2,1,0:T(8,128)} %refs_0_.3, f32[3,64,256]{2,1,0:T(8,128)} %refs_1_.3, f32[2,64,256]{2,1,0:T(8,128)} %refs_2_.3, f32[3,64,256]{2,1,0:T(8,128)} %refs_3_.3, f32[64,256]{1,0:T(8,128)} %refs_4_.3, f32[64,256]{1,0:T(8,128)} %refs_5_.3, f32[64,256]{1,0:T(8,128)} %refs_6_.3, ...), custom_call_target="tpu_custom_call" | custom-call | flops 20000000000 | bytes 1048576 | tf_op jit(solution)/shard_map/own_planes/pallas_call | solution.py:561
  17.5 0.0 collective-permute-done.1.got_even
  17.5 0.0 collective-permute-done.2.got_odd
  17.5 2.7 %forward.1 = (f32[4,3,96,128]{3,2,1,0:T(8,128)S(1)}, f32[4,3,3,64,128]{4,3,2,1,0:T(8,128)S(1)}, f32[2,64,256]{2,1,0:T(8,128)}) custom-call(f32[13,3,64,128]{3,2,1,0:T(8,128)S(1)} %own_planes.1.own, f32[176,256]{1,0:T(8,128)S(1)} %collective-permute-done.1.got_even, f32[176,256]{1,0:T(8,128)S(1)} %collective-permute-done.2.got_odd), custom_call_target="tpu_custom_call" | custom-call | flops 60000002048 | bytes 1048576 | tf_op jit(solution)/shard_map/forward/pallas_call | solution.py:586
  20.2 0.0 copy-start
  20.2 0.8 %copy-done = f32[4,3,96,128]{3,2,1,0:T(8,128)} copy-done((f32[4,3,96,128]{3,2,1,0:T(8,128)}, f32[4,3,96,128]{3,2,1,0:T(8,128)S(1)}, u32[]{:S(2)}) %copy-start) | copy-done | bytes 589848
  21.0 2.1 %all-to-all-done.notes = f32[8,40,128]{2,1,0:T(8,128)S(1)} async-done(((f32[8,40,128]{2,1,0:T(8,128)}), f32[8,40,128]{2,1,0:T(8,128)S(1)}, u32[]{:S(2)}, u32[]{:S(2)}) %all-to-all-start) | async-done | bytes 163872 | tf_op jit(solution)/shard_map/all_to_all | solution.py:584
  23.2 0.0 copy-start.1
  23.2 0.1 collective-permute-start.3
  23.3 1.0 %copy-done.1 = f32[4,3,96,128]{3,2,1,0:T(8,128)S(1)} copy-done((f32[4,3,96,128]{3,2,1,0:T(8,128)S(1)}, f32[4,3,96,128]{3,2,1,0:T(8,128)}, u32[]{:S(2)}) %copy-start.1) | copy-done | bytes 589848
  24.2 1.3 %adjoint_rest.1.rest = f32[2,2,64,128]{3,2,1,0:T(8,128)S(1)} custom-call(f32[13,3,64,128]{3,2,1,0:T(8,128)S(1)} %own_planes.1.own, f32[176,256]{1,0:T(8,128)S(1)} %collective-permute-done.1.got_even, f32[176,256]{1,0:T(8,128)S(1)} %collective-permute-done.2.got_odd, f32[4,3,96,128]{3,2,1,0:T(8,128)S(1)} %copy-done.1, ...), custom_call_target="tpu_custom_call" | custom-call | flops 60000002048 | bytes 1048576 | tf_op jit(solution)/shard_map/adjoint_rest/pallas_call | solution.py:612
  25.6 0.0 collective-permute-done.3.refs_1_
  25.6 1.6 %surface.1 = (f32[96,128]{1,0:T(8,128)S(1)}, f32[2,256]{1,0:T(2,128)}) custom-call(f32[8,40,128]{2,1,0:T(8,128)S(1)} %relay.1.notes.refs_0_, f32[8,40,128]{2,1,0:T(8,128)S(1)} %collective-permute-done.3.refs_1_, f32[4,256]{1,0:T(4,128)S(1)} %get-tuple-element.27.traces.refs_2_, s32[2,1,256]{2,1,0:T(1,128)S(1)} %get-tuple-element.28.cells.refs_3_), custom_call_target="tpu_custom_call" | custom-call | flops 2000000000 | bytes 1048576 | tf_op jit(solution)/shard_map/surface/pallas_call | solution.py:623
  27.2 1.6 %adjoint_top.1 = (f32[64,256]{1,0:T(8,128)}, f32[64,256]{1,0:T(8,128)}) custom-call(f32[13,3,64,128]{3,2,1,0:T(8,128)S(1)} %own_planes.1.own, f32[176,256]{1,0:T(8,128)S(1)} %collective-permute-done.1.got_even, f32[176,256]{1,0:T(8,128)S(1)} %collective-permute-done.2.got_odd, f32[4,3,96,128]{3,2,1,0:T(8,128)S(1)} %copy-done.1, ...), custom_call_target="tpu_custom_call" | custom-call | flops 2000000000 | bytes 1048576 | tf_op jit(solution)/shard_map/adjoint_top/pallas_call | solution.py:642
  (2 shorter events, 0.0 us)
Async XLA Ops:
  2.3 1.4 %collective-permute-start = (f32[80,256]{1,0:T(8,128)S(1)}, f32[80,256]{1,0:T(8,128)S(1)}, u32[]{:S(2)}, u32[]{:S(2)}) collective-permute-start(f32[80,256]{1,0:T(8,128)S(1)} %get-tuple-element.19), channel_id=1, source_target_pairs={{0,1},{1,0},{2,3},{3,2},{4,5},{5,4},{6,7},{7,6},{8,9},{9,8},{10,11... | collective-permute-start | bytes 245768 | tf_op jit(solution)/shard_map/ppermute | solution.py:546
  3.8 13.7 %collective-permute-start.1 = (f32[176,256]{1,0:T(8,128)S(1)}, f32[176,256]{1,0:T(8,128)S(1)}, u32[]{:S(2)}, u32[]{:S(2)}) collective-permute-start(f32[176,256]{1,0:T(8,128)S(1)} %get-tuple-element.22), channel_id=1, source_target_pairs={{0,2},{2,0},{4,6},{6,4},{8,10},{10,8},{12,14},{14,12},{1,3},{3,1},... | collective-permute-start | bytes 540680 | tf_op jit(solution)/shard_map/ppermute | solution.py:559
  6.7 10.8 %collective-permute-start.2 = (f32[176,256]{1,0:T(8,128)S(1)}, f32[176,256]{1,0:T(8,128)S(1)}, u32[]{:S(2)}, u32[]{:S(2)}) collective-permute-start(f32[176,256]{1,0:T(8,128)S(1)} %get-tuple-element.23), channel_id=1, source_target_pairs={{2,4},{4,2},{6,8},{8,6},{10,12},{12,10},{3,5},{5,3},{7,9},{9,7},{1... | collective-permute-start | bytes 540680 | tf_op jit(solution)/shard_map/ppermute | solution.py:558
  8.0 15.1 %all-to-all-start = ((f32[8,40,128]{2,1,0:T(8,128)}), f32[8,40,128]{2,1,0:T(8,128)S(1)}, u32[]{:S(2)}, u32[]{:S(2)}) async-start(f32[8,40,128]{2,1,0:T(8,128)} %note.1), calls=%async_computation | async-start | bytes 327680 | tf_op jit(solution)/shard_map/all_to_all | solution.py:584
  20.2 0.8 %copy-start = (f32[4,3,96,128]{3,2,1,0:T(8,128)}, f32[4,3,96,128]{3,2,1,0:T(8,128)S(1)}, u32[]{:S(2)}) copy-start(f32[4,3,96,128]{3,2,1,0:T(8,128)S(1)} %get-tuple-element.24.media) | copy-start | bytes 1769476
  23.2 1.1 %copy-start.1 = (f32[4,3,96,128]{3,2,1,0:T(8,128)S(1)}, f32[4,3,96,128]{3,2,1,0:T(8,128)}, u32[]{:S(2)}) copy-start(f32[4,3,96,128]{3,2,1,0:T(8,128)} %copy-done) | copy-start | bytes 1769476
  23.2 2.4 %collective-permute-start.3 = (f32[8,40,128]{2,1,0:T(8,128)S(1)}, f32[8,40,128]{2,1,0:T(8,128)S(1)}, u32[]{:S(2)}, u32[]{:S(2)}) collective-permute-start(f32[8,40,128]{2,1,0:T(8,128)S(1)} %relay.1.notes.refs_0_), channel_id=1, source_target_pairs={{0,1},{1,0},{2,3},{3,2},{4,5},{5,4},{6,7},{7,6},{8,9},{9,8},{10,11... | collective-permute-start | bytes 491528 | tf_op jit(solution)/shard_map/ppermute | solution.py:610

commit v12 on v11

--- a/solution.py
+++ b/solution.py
@@ -32,7 +32,7 @@
 
 
 def params():
-    return pltpu.CompilerParams(vmem_limit_bytes=40 * 1024 * 1024)
+    return pltpu.CompilerParams(vmem_limit_bytes=16 * 1024 * 1024)
 
 
 def cost(microseconds):
@@ -54,37 +54,38 @@
     return copies
 
 
-def field_refs(velocity, stress, adj_velocity, adj_stress, buoyancy, lame, shear):
-    return (
-        [velocity.at[i] for i in range(2)]
-        + [stress.at[i] for i in range(3)]
-        + [buoyancy, lame, shear]
-        + [adj_velocity.at[i] for i in range(2)]
-        + [adj_stress.at[i] for i in range(3)]
-    )
-
-
 def pack_kernel(*refs):
     sources, channel_arrays = refs[:7], refs[7:10]
-    depth_out, edge_outs, strip_out, traces_out, cells_out = refs[10], refs[11:13], *refs[13:16]
-    held, numbers, sems = refs[16:23], refs[23], refs[24]
-    targets = (*held, traces_out, numbers.at[0], numbers.at[1])
-    copies = fetch((*sources, *channel_arrays), targets, sems)
+    held, depth_out, edge_outs, strip_out, traces_out, cells_out = refs[10], refs[11], refs[12:14], *refs[14:17]
+    numbers, sems = refs[17:]
+    targets = (
+        held.at[pl.ds(0, 2)],
+        held.at[pl.ds(2, 3)],
+        held.at[5],
+        held.at[6],
+        held.at[7],
+        held.at[pl.ds(8, 2)],
+        held.at[pl.ds(10, 3)],
+        traces_out,
+        numbers.at[0],
+        numbers.at[1],
+    )
+    copies = fetch((*sources[:2], *sources[4:], *sources[2:4], *channel_arrays), targets, sems)
+    arriving = {0: copies[0], 2: copies[1], 5: copies[2], 6: copies[3], 7: copies[4], 8: copies[5], 10: copies[6]}
     depth = lax.axis_index("depth")
     even = is_even()
-    fields = field_refs(*held)
-    rows = fields[0].shape[0]
+    rows = held.shape[1]
     lane = lane_ids(rows)
     tail = EDGE + HALO * FIELDS
     for out in edge_outs:
         out[:EDGE, :] = jnp.zeros((EDGE, 2 * LANES), F32)
         out[tail:, :] = jnp.zeros((out.shape[0] - tail, 2 * LANES), F32)
-    for copy in copies:
-        copy.wait()
     packed = [jnp.zeros((rows, LANES), F32) for _ in range(2)]
     strip = jnp.zeros((rows, LANES), F32)
-    for f, ref in enumerate(fields):
-        first, last = ref[:, :LANES], ref[:, LANES:]
+    for f in range(FIELDS):
+        if f in arriving:
+            arriving[f].wait()
+        first, last = held[f, :, :LANES], held[f, :, LANES:]
         group, place = divmod(f, FORWARD)
         spot = EDGE * place
         here = (lane >= spot) & (lane < spot + EDGE)
@@ -93,7 +94,7 @@
         packed[group] = jnp.where(here, pltpu.roll(edge, shift, 1), packed[group])
         if f < FORWARD:
             strip = jnp.where(here, turn(first, spot), strip)
-        low, high = ref[:HALO, :], ref[rows - HALO :, :]
+        low, high = held[f, :HALO, :], held[f, rows - HALO :, :]
         at = EDGE + HALO * f
         edge_outs[0][at : at + HALO, :] = jnp.where(even, high, low)
         edge_outs[1][at : at + HALO, :] = jnp.where(even, low, high)
@@ -106,6 +107,8 @@
     depth_out[rows:, rows : 2 * rows] = turned[6 * STRIP : 7 * STRIP]
     depth_out[rows:, 2 * rows : 3 * rows] = turned[5 * STRIP : 6 * STRIP]
     depth_out[rows:, 3 * rows :] = turned[7 * STRIP :]
+    for copy in copies[7:]:
+        copy.wait()
     cells_out[0] = numbers[0] * rows + lax.shift_right_logical(numbers[1], 2)
     cells_out[1] = numbers[1] & 3
 
@@ -147,15 +150,9 @@
     )
 
 
-def own_kernel(*refs):
-    sources, got_depth, planes_out, held, sems = refs[:7], refs[7], refs[8], refs[9:16], refs[16]
-    for copy in fetch(sources, held, sems):
-        copy.wait()
-    for f, ref in enumerate(field_refs(*held)):
-        col = LANES * (f // FORWARD)
-        planes = windows(f, ref[:, :LANES], ref[:, LANES:], got_depth[: ref.shape[0], col : col + LANES])
-        for p in range(3):
-            planes_out[f, p] = planes[p]
+def own_windows(f, held, got_depth):
+    col = LANES * (f // FORWARD)
+    return windows(f, held[f, :, :LANES], held[f, :, LANES:], got_depth[: held.shape[1], col : col + LANES])
 
 
 def halo_windows(f, got_even, got_odd):
@@ -174,15 +171,16 @@
     )
 
 
-def load_state(state, own, got_even, got_odd, base, planes):
-    rows = own.shape[2]
+def load_state(state, held, got_depth, got_even, got_odd, base, planes):
+    rows = held.shape[1]
     extent = rows + 2 * EDGE
     for f in range(5):
         below, above = halo_windows(base + f, got_even, got_odd)
+        own = own_windows(base + f, held, got_depth)
         for i, p in enumerate(planes):
             state[f, i, :PAD, :] = jnp.zeros((PAD, LANES), F32)
             state[f, i, PAD : PAD + EDGE, :] = below[p]
-            state[f, i, PAD + EDGE : PAD + EDGE + rows, :] = own[base + f, p]
+            state[f, i, PAD + EDGE : PAD + EDGE + rows, :] = own[p]
             state[f, i, PAD + EDGE + rows : PAD + extent, :] = above[p]
             state[f, i, PAD + extent :, :] = jnp.zeros((PAD, LANES), F32)
 
@@ -233,12 +231,13 @@
     return inner, inner if step < MOMENTS - 1 else (EDGE // 8, tiles - EDGE // 8)
 
 
-def run_forward(own, got_even, got_odd, media, saved, state, planes):
-    rows = own.shape[2]
+def run_forward(held, got_depth, got_even, got_odd, media, saved, state, planes):
+    rows = held.shape[1]
     parts = []
     for f in (5, 6, 7):
         below, above = halo_windows(f, got_even, got_odd)
-        parts.append([(below[p], own[f, p], above[p]) for p in planes])
+        own = own_windows(f, held, got_depth)
+        parts.append([(below[p], own[p], above[p]) for p in planes])
     for i in range(len(planes)):
         for k, at in enumerate((0, EDGE, EDGE + rows)):
             b, lam, mu = (NEAR * parts[m][i][k] for m in range(3))
@@ -247,7 +246,7 @@
             media[1, i, span, :] = lam + 2.0 * mu
             media[2, i, span, :] = lam
             media[3, i, span, :] = mu
-    load_state(state, own, got_even, got_odd, 0, planes)
+    load_state(state, held, got_depth, got_even, got_odd, 0, planes)
     for step in range(MOMENTS):
         fast, slow = spans(step, rows)
         velocities(state, media, fast)
@@ -261,9 +260,9 @@
         stresses(state, media, slow, step < MOMENTS - 1, save)
 
 
-def forward_kernel(own, got_even, got_odd, media, saved, end_out, state):
-    run_forward(own, got_even, got_odd, media, saved, state, (0, 1, 2))
-    rows = own.shape[2]
+def forward_kernel(held, got_depth, got_even, got_odd, media, saved, end_out, state):
+    run_forward(held, got_depth, got_even, got_odd, media, saved, state, (0, 1, 2))
+    rows = held.shape[1]
     top = PAD + EDGE
     for f in range(2):
         first, last = joined([state[f, i, top : top + rows, :] for i in range(3)])
@@ -470,16 +469,20 @@
         stresses(state, media, slow, step < MOMENTS - 1, gather)
 
 
-def adjoint_rest_kernel(own, got_even, got_odd, media, saved, notes, sums, state):
+def adjoint_rest_kernel(held, got_depth, got_even, got_odd, media, saved, notes, sums, state):
     del notes
-    load_state(state, own, got_even, got_odd, FORWARD, (1, 2))
+    load_state(state, held, got_depth, got_even, got_odd, FORWARD, (1, 2))
     run_adjoint(media.at[:, pl.ds(1, 2)], saved.at[:, :, pl.ds(1, 2)], state, sums)
 
 
-def adjoint_top_kernel(own, got_even, got_odd, media, saved, rest, inject, lambda_out, mu_out, state, sums):
-    rows = own.shape[2]
+def adjoint_top_kernel(
+    held, got_depth, got_even, got_odd, media, saved, rest, inject, end, residual,
+    lambda_out, mu_out, end_out, residual_out, state, sums, sems,
+):
+    copies = fetch((end, residual), (end_out, residual_out), sems)
+    rows = held.shape[1]
     extent = rows + 2 * EDGE
-    load_state(state, own, got_even, got_odd, FORWARD, (0,))
+    load_state(state, held, got_depth, got_even, got_odd, FORWARD, (0,))
     lane = lane_ids(extent)
     here = (lane >= EDGE) & (lane < EDGE + FIBRE_ROWS)
 
@@ -492,6 +495,8 @@
         first, last = joined([sums[k, 0], rest[k, 0], rest[k, 1]])
         out[:, :LANES] = (NEAR * NEAR) * first
         out[:, LANES:] = (NEAR * NEAR) * last
+    for copy in copies:
+        copy.wait()
 
 
 def per_device(
@@ -522,10 +527,10 @@
     inside = pl.BlockSpec(memory_space=VMEM)
     outside = pl.BlockSpec(memory_space=pltpu.HBM)
     anywhere = pl.BlockSpec(memory_space=pl.ANY)
-    held = [VMEM(a.shape, F32) for a in arrays]
-    to_depth, to_even, to_odd, strip, traces, cells = pl.pallas_call(
+    held, to_depth, to_even, to_odd, strip, traces, cells = pl.pallas_call(
         pack_kernel,
         out_shape=(
+            jax.ShapeDtypeStruct((FIELDS, rows, depth_cells), F32),
             jax.ShapeDtypeStruct((rows + STRIP, depth_cells), F32),
             edges,
             edges,
@@ -534,8 +539,8 @@
             jax.ShapeDtypeStruct((2, 1, channels), jnp.int32),
         ),
         in_specs=[outside] * 10,
-        out_specs=(inside,) * 6,
-        scratch_shapes=held + [VMEM((2, 1, channels), jnp.int32), pltpu.SemaphoreType.DMA((10,))],
+        out_specs=(inside,) * 7,
+        scratch_shapes=[VMEM((2, 1, channels), jnp.int32), pltpu.SemaphoreType.DMA((10,))],
         compiler_params=params(),
         cost_estimate=cost(5),
         name="pack",
@@ -558,17 +563,6 @@
     got_odd = lax.ppermute(to_track[1], "track", swap(1))
     got_even = lax.ppermute(to_track[0], "track", swap(0))
 
-    own = pl.pallas_call(
-        own_kernel,
-        out_shape=jax.ShapeDtypeStruct((FIELDS, 3, rows, LANES), F32),
-        in_specs=[outside] * 7 + [inside],
-        out_specs=inside,
-        scratch_shapes=held + [pltpu.SemaphoreType.DMA((7,))],
-        compiler_params=params(),
-        cost_estimate=cost(20),
-        name="own_planes",
-    )(*arrays, got_depth)
-
     def state_of(planes):
         return VMEM((5, planes, extent + 2 * PAD, LANES), F32)
 
@@ -583,20 +577,20 @@
     )(strip, got_depth, traces, cells)
     notes = lax.all_to_all(note, "track", split_axis=0, concat_axis=0, tiled=True)
 
-    media, saved, velocity_end = pl.pallas_call(
+    media, saved, end = pl.pallas_call(
         forward_kernel,
         out_shape=(
             jax.ShapeDtypeStruct((4, 3, extent, LANES), F32),
             jax.ShapeDtypeStruct((moments, 3, 3, rows, LANES), F32),
             jax.ShapeDtypeStruct(velocity.shape, F32),
         ),
-        in_specs=[inside] * 3,
+        in_specs=[inside] * 4,
         out_specs=(inside,) * 3,
         scratch_shapes=[state_of(3)],
         compiler_params=params(),
-        cost_estimate=cost(60),
+        cost_estimate=cost(20),
         name="forward",
-    )(own, got_even, got_odd)
+    )(held, got_depth, got_even, got_odd)
 
     mine = pl.pallas_call(
         relay_kernel,
@@ -612,13 +606,13 @@
     rest = pl.pallas_call(
         adjoint_rest_kernel,
         out_shape=jax.ShapeDtypeStruct((2, 2, rows, LANES), F32),
-        in_specs=[inside] * 5 + [anywhere],
+        in_specs=[inside] * 6 + [anywhere],
         out_specs=inside,
         scratch_shapes=[state_of(2)],
         compiler_params=params(),
-        cost_estimate=cost(60),
+        cost_estimate=cost(20),
         name="adjoint_rest",
-    )(own, got_even, got_odd, media, saved, mine)
+    )(held, got_depth, got_even, got_odd, media, saved, mine)
 
     inject, residual = pl.pallas_call(
         lambda *refs: surface_kernel(tracks, rows, *refs),
@@ -639,16 +633,21 @@
         name="surface",
     )(mine, beside, traces, cells)
 
-    gradient_lambda, gradient_mu = pl.pallas_call(
+    gradient_lambda, gradient_mu, velocity_end, residual = pl.pallas_call(
         adjoint_top_kernel,
-        out_shape=(block, block),
-        in_specs=[inside] * 7,
-        out_specs=(inside,) * 2,
-        scratch_shapes=[state_of(1), VMEM((2, 1, rows, LANES), F32)],
+        out_shape=(
+            block,
+            block,
+            jax.ShapeDtypeStruct(velocity.shape, F32),
+            jax.ShapeDtypeStruct((moments // 2, channels), F32),
+        ),
+        in_specs=[inside] * 10,
+        out_specs=(inside, inside, outside, outside),
+        scratch_shapes=[state_of(1), VMEM((2, 1, rows, LANES), F32), pltpu.SemaphoreType.DMA((2,))],
         compiler_params=params(),
         cost_estimate=cost(2),
         name="adjoint_top",
-    )(own, got_even, got_odd, media, saved, rest, inject)
+    )(held, got_depth, got_even, got_odd, media, saved, rest, inject, end, residual)
     return gradient_lambda, gradient_mu, velocity_end, residual
 
 

time: 29.1 us -> 29 us (level)
  Pallas kernels: 11.5 us -> 9.14 us
  waiting for transfers between devices: 3.06 us -> 5.31 us
    all_to_all x1, waiting for transfers between devices: 2.13 us -> 4.38 us  [per_device(): lax.all_to_all(note, 'track', split_axis=0, concat_axis=0, tiled=True)]
    pallas_call x3 -> x2, Pallas kernels: 5.08 us -> 3.42 us  [the longest x1 1.73 us: per_device(): pl.pallas_call(pack_kernel, out_shape=(jax.ShapeDtypeStruct((FIELDS, rows...]
    pallas_call x1, Pallas kernels: 1.63 us -> 1.18 us  [per_device(): pl.pallas_call(lambda *refs: surface_kernel(tracks, rows, *refs), out_sha...]
    pallas_call x1, Pallas kernels: 2.71 us -> 2.35 us  [per_device(): pl.pallas_call(forward_kernel, out_shape=(jax.ShapeDtypeStruct((4, 3, ext...]
  transfers between devices with their start and end apart: 5 -> 5, of which waited for: 2 -> 2; matrix products, arithmetic and copies ran while one was open for 0% -> 0% of each run, Pallas kernels for 23% -> 16%
where the time goes in v12:
time: 29 us; the launch traced here: 28.7 us
  starting transfers between devices  11.7 us (40%)
  Pallas kernels  9.14 us (32%)
  waiting for transfers between devices  5.31 us (18%)
  local copies, waits for them, and re-layouts  1.77 us (6%)
  between operations  0.72 us (2%)
    all_to_all x1, starting transfers between devices, per_device(): lax.all_to_all(note, 'track', split_axis=0, concat_axis=0, tiled=True)  7.58 us
    all_to_all x1, waiting for transfers between devices, per_device(): lax.all_to_all(note, 'track', split_axis=0, concat_axis=0, tiled=True)  4.38 us
    ppermute x1, starting transfers between devices, per_device(): got_even = lax.ppermute(to_track[0], 'track', swap(0))  2.91 us
    pallas_call x1, Pallas kernels, per_device(): pl.pallas_call(forward_kernel, out_shape=(jax.ShapeDtypeStruct((4, 3, ext...  2.35 us
    unnamed x4, local copies, waits for them, and re-layouts  1.77 us
    pallas_call x1, Pallas kernels, per_device(): pl.pallas_call(pack_kernel, out_shape=(jax.ShapeDtypeStruct((FIELDS, rows...  1.73 us
    pallas_call x1, Pallas kernels, per_device(): pl.pallas_call(adjoint_top_kernel, out_shape=(block, block, jax.ShapeDtyp...  1.69 us
    pallas_call x1, Pallas kernels, per_device(): pl.pallas_call(adjoint_rest_kernel, out_shape=jax.ShapeDtypeStruct((2, 2,...  1.45 us
  transfers between devices with their start and end apart: 5, of which 2 were waited for; matrix products, arithmetic and copies ran while one was open for 0% of the time, Pallas kernels for 16%

profile of v12, /device:TPU:0, one launch (start us, length us, event | category | flops | bytes accessed | tf_op | source)
XLA Modules:
  0.0 28.7 jit_solution(2673419520053493587)
XLA Ops:
  0.6 1.7 %pack.1 = (f32[13,64,256]{2,1,0:T(8,128)S(1)}, f32[80,256]{1,0:T(8,128)S(1)}, f32[176,256]{1,0:T(8,128)S(1)}, f32[176,256]{1,0:T(8,128)S(1)}, f32[32,128]{1,0:T(...) custom-call(f32[2,64,256]{2,1,0:T(8,128)} %refs_0_.1, f32[3,64,256]{2,1,0:T(8,128)} %refs_1_.1, ...), custom_call_target="tpu_custom_call" | custom-call | flops 5000000000 | bytes 1048576 | tf_op jit(solution)/shard_map/pack/pallas_call | solution.py:530
  2.4 0.5 %collective-permute-start = (f32[80,256]{1,0:T(8,128)S(1)}, f32[80,256]{1,0:T(8,128)S(1)}, u32[]{:S(2)}, u32[]{:S(2)}) collective-permute-start(f32[80,256]{1,0:T(8,128)S(1)} %get-tuple-element.19), channel_id=1, source_target_pairs={{0,1},{1,0},{2,3},{3,2},{4,5},{5,4},{6,7},{7,6},{8,9},{9,8},{10,11... | collective-permute-start | bytes 245768 | tf_op jit(solution)/shard_map/ppermute | solution.py:551
  2.9 0.9 %collective-permute-done.got.got_depth = f32[80,256]{1,0:T(8,128)S(1)} collective-permute-done((f32[80,256]{1,0:T(8,128)S(1)}, f32[80,256]{1,0:T(8,128)S(1)}, u32[]{:S(2)}, u32[]{:S(2)}) %collective-permute-start) | collective-permute-done | bytes 81952 | tf_op jit(solution)/shard_map/ppermute | solution.py:551
  3.9 2.9 %collective-permute-start.1 = (f32[176,256]{1,0:T(8,128)S(1)}, f32[176,256]{1,0:T(8,128)S(1)}, u32[]{:S(2)}, u32[]{:S(2)}) collective-permute-start(f32[176,256]{1,0:T(8,128)S(1)} %get-tuple-element.22), channel_id=1, source_target_pairs={{0,2},{2,0},{4,6},{6,4},{8,10},{10,8},{12,14},{14,12},{1,3},{3,1},... | collective-permute-start | bytes 540680 | tf_op jit(solution)/shard_map/ppermute | solution.py:564
  6.8 0.7 %collective-permute-start.2 = (f32[176,256]{1,0:T(8,128)S(1)}, f32[176,256]{1,0:T(8,128)S(1)}, u32[]{:S(2)}, u32[]{:S(2)}) collective-permute-start(f32[176,256]{1,0:T(8,128)S(1)} %get-tuple-element.23), channel_id=1, source_target_pairs={{2,4},{4,2},{6,8},{8,6},{10,12},{12,10},{3,5},{5,3},{7,9},{9,7},{1... | collective-permute-start | bytes 540680 | tf_op jit(solution)/shard_map/ppermute | solution.py:563
  7.4 0.7 %note.1 = f32[8,40,128]{2,1,0:T(8,128)} custom-call(f32[32,128]{1,0:T(8,128)S(1)} %get-tuple-element.26.strip, f32[80,256]{1,0:T(8,128)S(1)} %collective-permute-done.got.got_depth, f32[4,256]{1,0:T(4,128)S(1)} %get-tuple-element.27.traces.refs_2_, s32[2,1,256]{2,1,0:T(1,128)S(1)} %get-tuple-element.28.cells.refs_3_), custom_call_target="tpu_custom_call" | custom-call | flops 1000000000 | bytes 1048576 | tf_op jit(solution)/shard_map/note/pallas_call | solution.py:569
  8.1 7.6 %all-to-all-start = ((f32[8,40,128]{2,1,0:T(8,128)}), f32[8,40,128]{2,1,0:T(8,128)S(1)}, u32[]{:S(2)}, u32[]{:S(2)}) async-start(f32[8,40,128]{2,1,0:T(8,128)} %note.1), calls=%async_computation | async-start | bytes 327680 | tf_op jit(solution)/shard_map/all_to_all | solution.py:578
  15.7 0.0 collective-permute-done.1.got_even
  15.7 0.0 collective-permute-done.2.got_odd
  15.7 2.3 %forward.1 = (f32[4,3,96,128]{3,2,1,0:T(8,128)S(1)}, f32[4,3,3,64,128]{4,3,2,1,0:T(8,128)S(1)}, f32[2,64,256]{2,1,0:T(8,128)S(1)}) custom-call(f32[13,64,256]{2,1,0:T(8,128)S(1)} %get-tuple-element.18.held, f32[80,256]{1,0:T(8,128)S(1)} %collective-permute-done.got.got_depth, f32[176,256]{1,0:T(8,128)S(1)} %collective-permute-done.1.got_even, ...), custom_call_target="tpu_custom_call" | custom-call | flops 20000000000 | bytes 1048576 | tf_op jit(solution)/shard_map/forward/pallas_call | solution.py:580
  18.1 0.0 copy-start
  18.1 0.8 %copy-done = f32[4,3,96,128]{3,2,1,0:T(8,128)} copy-done((f32[4,3,96,128]{3,2,1,0:T(8,128)}, f32[4,3,96,128]{3,2,1,0:T(8,128)S(1)}, u32[]{:S(2)}) %copy-start) | copy-done | bytes 589848
  18.9 4.4 %all-to-all-done.notes = f32[8,40,128]{2,1,0:T(8,128)S(1)} async-done(((f32[8,40,128]{2,1,0:T(8,128)}), f32[8,40,128]{2,1,0:T(8,128)S(1)}, u32[]{:S(2)}, u32[]{:S(2)}) %all-to-all-start) | async-done | bytes 163872 | tf_op jit(solution)/shard_map/all_to_all | solution.py:578
  23.3 0.0 copy-start.1
  23.3 0.1 collective-permute-start.3
  23.4 1.0 %copy-done.1 = f32[4,3,96,128]{3,2,1,0:T(8,128)S(1)} copy-done((f32[4,3,96,128]{3,2,1,0:T(8,128)S(1)}, f32[4,3,96,128]{3,2,1,0:T(8,128)}, u32[]{:S(2)}) %copy-start.1) | copy-done | bytes 589848
  24.3 1.5 %adjoint_rest.1.rest = f32[2,2,64,128]{3,2,1,0:T(8,128)S(1)} custom-call(f32[13,64,256]{2,1,0:T(8,128)S(1)} %get-tuple-element.18.held, f32[80,256]{1,0:T(8,128)S(1)} %collective-permute-done.got.got_depth, f32[176,256]{1,0:T(8,128)S(1)} %collective-permute-done.1.got_even, f32[176,256]{1,0:T(8,128)S(1)} %collective-permute-done.2.got_odd, ...), custom_call_target="tpu_custom_call" | custom-call | flops 20000000000 | bytes 1048576 | tf_op jit(solution)/shard_map/adjoint_rest/pallas_call | solution.py:606
  25.8 0.0 collective-permute-done.3.refs_1_
  25.8 1.2 %surface.1 = (f32[96,128]{1,0:T(8,128)S(1)}, f32[2,256]{1,0:T(2,128)S(1)}) custom-call(f32[8,40,128]{2,1,0:T(8,128)S(1)} %relay.1.notes.refs_0_, f32[8,40,128]{2,1,0:T(8,128)S(1)} %collective-permute-done.3.refs_1_, f32[4,256]{1,0:T(4,128)S(1)} %get-tuple-element.27.traces.refs_2_, s32[2,1,256]{2,1,0:T(1,128)S(1)} %get-tuple-element.28.cells.refs_3_), custom_call_target="tpu_custom_call" | custom-call | flops 2000000000 | bytes 1048576 | tf_op jit(solution)/shard_map/surface/pallas_call | solution.py:617
  27.0 1.7 %adjoint_top.1 = (f32[64,256]{1,0:T(8,128)}, f32[64,256]{1,0:T(8,128)}, f32[2,64,256]{2,1,0:T(8,128)}, f32[2,256]{1,0:T(2,128)}) custom-call(f32[13,64,256]{2,1,0:T(8,128)S(1)} %get-tuple-element.18.held, f32[80,256]{1,0:T(8,128)S(1)} %collective-permute-done.got.got_depth, f32[176,256]{1,0:T(8,128)S(1)} %collective-permute-done.1.got_even, ...), custom_call_target="tpu_custom_call" | custom-call | flops 2000000000 | bytes 1048576 | tf_op jit(solution)/shard_map/adjoint_top/pallas_call | solution.py:636
  (2 shorter events, 0.0 us)
Async XLA Ops:
  2.4 1.4 %collective-permute-start = (f32[80,256]{1,0:T(8,128)S(1)}, f32[80,256]{1,0:T(8,128)S(1)}, u32[]{:S(2)}, u32[]{:S(2)}) collective-permute-start(f32[80,256]{1,0:T(8,128)S(1)} %get-tuple-element.19), channel_id=1, source_target_pairs={{0,1},{1,0},{2,3},{3,2},{4,5},{5,4},{6,7},{7,6},{8,9},{9,8},{10,11... | collective-permute-start | bytes 245768 | tf_op jit(solution)/shard_map/ppermute | solution.py:551
  3.9 11.8 %collective-permute-start.1 = (f32[176,256]{1,0:T(8,128)S(1)}, f32[176,256]{1,0:T(8,128)S(1)}, u32[]{:S(2)}, u32[]{:S(2)}) collective-permute-start(f32[176,256]{1,0:T(8,128)S(1)} %get-tuple-element.22), channel_id=1, source_target_pairs={{0,2},{2,0},{4,6},{6,4},{8,10},{10,8},{12,14},{14,12},{1,3},{3,1},... | collective-permute-start | bytes 540680 | tf_op jit(solution)/shard_map/ppermute | solution.py:564
  6.8 8.9 %collective-permute-start.2 = (f32[176,256]{1,0:T(8,128)S(1)}, f32[176,256]{1,0:T(8,128)S(1)}, u32[]{:S(2)}, u32[]{:S(2)}) collective-permute-start(f32[176,256]{1,0:T(8,128)S(1)} %get-tuple-element.23), channel_id=1, source_target_pairs={{2,4},{4,2},{6,8},{8,6},{10,12},{12,10},{3,5},{5,3},{7,9},{9,7},{1... | collective-permute-start | bytes 540680 | tf_op jit(solution)/shard_map/ppermute | solution.py:563
  8.1 15.1 %all-to-all-start = ((f32[8,40,128]{2,1,0:T(8,128)}), f32[8,40,128]{2,1,0:T(8,128)S(1)}, u32[]{:S(2)}, u32[]{:S(2)}) async-start(f32[8,40,128]{2,1,0:T(8,128)} %note.1), calls=%async_computation | async-start | bytes 327680 | tf_op jit(solution)/shard_map/all_to_all | solution.py:578
  18.1 0.8 %copy-start = (f32[4,3,96,128]{3,2,1,0:T(8,128)}, f32[4,3,96,128]{3,2,1,0:T(8,128)S(1)}, u32[]{:S(2)}) copy-start(f32[4,3,96,128]{3,2,1,0:T(8,128)S(1)} %get-tuple-element.24.media) | copy-start | bytes 1769476
  23.3 1.1 %copy-start.1 = (f32[4,3,96,128]{3,2,1,0:T(8,128)S(1)}, f32[4,3,96,128]{3,2,1,0:T(8,128)}, u32[]{:S(2)}) copy-start(f32[4,3,96,128]{3,2,1,0:T(8,128)} %copy-done) | copy-start | bytes 1769476
  23.3 2.5 %collective-permute-start.3 = (f32[8,40,128]{2,1,0:T(8,128)S(1)}, f32[8,40,128]{2,1,0:T(8,128)S(1)}, u32[]{:S(2)}, u32[]{:S(2)}) collective-permute-start(f32[8,40,128]{2,1,0:T(8,128)S(1)} %relay.1.notes.refs_0_), channel_id=1, source_target_pairs={{0,1},{1,0},{2,3},{3,2},{4,5},{5,4},{6,7},{7,6},{8,9},{9,8},{10,11... | collective-permute-start | bytes 491528 | tf_op jit(solution)/shard_map/ppermute | solution.py:604

commit v13 on v12

--- a/solution.py
+++ b/solution.py
@@ -16,6 +16,7 @@
 ADJOINT = 5
 FIELDS = FORWARD + ADJOINT
 STRIP = 16
+BASE = EDGE - HALO
 MOMENTS = 4
 IMAGE = MOMENTS * FIBRE_ROWS
 VMEM = pltpu.VMEM
@@ -56,16 +57,16 @@
 
 def pack_kernel(*refs):
     sources, channel_arrays = refs[:7], refs[7:10]
-    held, depth_out, edge_outs, strip_out, traces_out, cells_out = refs[10], refs[11], refs[12:14], *refs[14:17]
-    numbers, sems = refs[17:]
+    held, held_adj, depth_out, edge_outs, strip_out, traces_out, cells_out = *refs[10:13], refs[13:15], *refs[15:18]
+    numbers, sems = refs[18:]
     targets = (
         held.at[pl.ds(0, 2)],
         held.at[pl.ds(2, 3)],
         held.at[5],
         held.at[6],
         held.at[7],
-        held.at[pl.ds(8, 2)],
-        held.at[pl.ds(10, 3)],
+        held_adj.at[pl.ds(0, 2)],
+        held_adj.at[pl.ds(2, 3)],
         traces_out,
         numbers.at[0],
         numbers.at[1],
@@ -76,16 +77,17 @@
     even = is_even()
     rows = held.shape[1]
     lane = lane_ids(rows)
-    tail = EDGE + HALO * FIELDS
+    tail = BASE + HALO * FIELDS
     for out in edge_outs:
-        out[:EDGE, :] = jnp.zeros((EDGE, 2 * LANES), F32)
+        out[:BASE, :] = jnp.zeros((BASE, 2 * LANES), F32)
         out[tail:, :] = jnp.zeros((out.shape[0] - tail, 2 * LANES), F32)
     packed = [jnp.zeros((rows, LANES), F32) for _ in range(2)]
     strip = jnp.zeros((rows, LANES), F32)
     for f in range(FIELDS):
         if f in arriving:
             arriving[f].wait()
-        first, last = held[f, :, :LANES], held[f, :, LANES:]
+        ref = held.at[f] if f < FORWARD else held_adj.at[f - FORWARD]
+        first, last = ref[:, :LANES], ref[:, LANES:]
         group, place = divmod(f, FORWARD)
         spot = EDGE * place
         here = (lane >= spot) & (lane < spot + EDGE)
@@ -94,8 +96,8 @@
         packed[group] = jnp.where(here, pltpu.roll(edge, shift, 1), packed[group])
         if f < FORWARD:
             strip = jnp.where(here, turn(first, spot), strip)
-        low, high = held[f, :HALO, :], held[f, rows - HALO :, :]
-        at = EDGE + HALO * f
+        low, high = ref[:HALO, :], ref[rows - HALO :, :]
+        at = BASE + HALO * f
         edge_outs[0][at : at + HALO, :] = jnp.where(even, high, low)
         edge_outs[1][at : at + HALO, :] = jnp.where(even, low, high)
     depth_out[:rows, :LANES] = packed[0]
@@ -113,101 +115,105 @@
     cells_out[1] = numbers[1] & 3
 
 
-def corner_kernel(got, even_in, odd_in, even_out, odd_out, sems):
-    rows = got.shape[0] - STRIP
-    is_odd = lax.rem(lax.axis_index("track"), 2)
-    high, low = (rows - EDGE) * (1 - is_odd), (rows - EDGE) * is_odd
-    one = pltpu.make_async_copy(
-        got.at[pl.ds(pl.multiple_of(high, EDGE), EDGE), :], even_out.at[pl.ds(0, EDGE), :], sems.at[0]
+def edge_rows(f, side, got_even, got_odd):
+    at = BASE + HALO * f
+    span = slice(at - BASE, at + HALO) if side == 0 else slice(at, at + EDGE)
+    use_odd = is_even() if side == 0 else ~is_even()
+    return jnp.where(use_odd, got_odd[span, :], got_even[span, :])
+
+
+def corner_kernel(got_even, got_odd, corner_out):
+    depth = lax.axis_index("depth")
+    lane = lane_ids(EDGE)
+    for side in range(2):
+        packed = [jnp.zeros((EDGE, LANES), F32) for _ in range(2)]
+        for f in range(FIELDS):
+            group, place = divmod(f, FORWARD)
+            spot = EDGE * place
+            value = edge_rows(f, side, got_even, got_odd)
+            edge = jnp.where(depth == 0, value[:, LANES:], value[:, :LANES])
+            shift = lax.rem(spot + EDGE * (1 - depth), LANES)
+            here = (lane >= spot) & (lane < spot + EDGE)
+            packed[group] = jnp.where(here, pltpu.roll(edge, shift, 1), packed[group])
+        corner_out[EDGE * side : EDGE * (side + 1), :LANES] = packed[0]
+        corner_out[EDGE * side : EDGE * (side + 1), LANES:] = packed[1]
+
+
+def window(plane, f, value, halo):
+    depth = lax.axis_index("depth")
+    surface = depth == 0
+    first, last = value[:, :LANES], value[:, LANES:]
+    lane = lane_ids(first.shape[0])
+    low = jnp.where(surface, lane, LANES - 1 - lane)
+    if plane == 0:
+        shift = jnp.where(surface, EDGE, LANES - EDGE)
+        return jnp.where(low >= EDGE, pltpu.roll(jnp.where(surface, first, last), shift, 1), 0.0)
+    if plane == 1:
+        return jnp.where(lane < LANES // 2, turn(first, LANES // 2), turn(last, LANES // 2))
+    shift = jnp.where(surface, LANES - EDGE, EDGE)
+    beside = lax.rem(LANES - EDGE * (f % FORWARD) + (LANES - EDGE) * (1 - depth), LANES)
+    own = pltpu.roll(jnp.where(surface, last, first), shift, 1)
+    return jnp.where(low < LANES - EDGE, own, pltpu.roll(halo, beside, 1))
+
+
+def field_windows(f, planes, held, got_even, got_odd, got_depth=None, corner=None):
+    rows = held.shape[1]
+    col = LANES * (f // FORWARD)
+    blocks = (
+        (0, edge_rows(f, 0, got_even, got_odd), corner, 0),
+        (EDGE, held[f % FORWARD], got_depth, 0),
+        (EDGE + rows, edge_rows(f, 1, got_even, got_odd), corner, EDGE),
     )
-    two = pltpu.make_async_copy(
-        got.at[pl.ds(pl.multiple_of(low, EDGE), EDGE), :], odd_out.at[pl.ds(0, EDGE), :], sems.at[1]
-    )
-    one.start()
-    two.start()
-    one.wait()
-    two.wait()
-
-
-def windows(f, first, last, halo):
-    depth = lax.axis_index("depth")
-    lane = lane_ids(first.shape[0])
-    shift = lax.rem(LANES - EDGE * (f % FORWARD) + (LANES - EDGE) * (1 - depth), LANES)
-    beside = pltpu.roll(halo, shift, 1)
-    return [
-        jnp.where(lane >= EDGE, turn(first, EDGE), jnp.where(depth == 1, beside, 0.0)),
-        jnp.where(lane < LANES // 2, turn(first, LANES // 2), turn(last, LANES // 2)),
-        jnp.where(lane < LANES - EDGE, turn(last, -EDGE), jnp.where(depth == 0, beside, 0.0)),
-    ]
-
-
-def joined(planes):
-    lane = lane_ids(planes[0].shape[0])
-    middle = turn(planes[1], LANES // 2)
-    return (
-        jnp.where(lane < 88, turn(planes[0], -EDGE), middle),
-        jnp.where(lane < 40, middle, turn(planes[2], EDGE)),
-    )
-
-
-def own_windows(f, held, got_depth):
-    col = LANES * (f // FORWARD)
-    return windows(f, held[f, :, :LANES], held[f, :, LANES:], got_depth[: held.shape[1], col : col + LANES])
-
-
-def halo_windows(f, got_even, got_odd):
-    even = is_even()
-    high = EDGE + HALO * f
-    low = high - (EDGE - HALO)
-    col = LANES * (f // FORWARD)
-    corner_even, corner_odd = got_even[:EDGE, col : col + LANES], got_odd[:EDGE, col : col + LANES]
-    left = jnp.where(even, got_odd[low : low + EDGE, :], got_even[low : low + EDGE, :])
-    right = jnp.where(even, got_even[high : high + EDGE, :], got_odd[high : high + EDGE, :])
-    left_halo = jnp.where(even, corner_odd, corner_even)
-    right_halo = jnp.where(even, corner_even, corner_odd)
-    return (
-        windows(f, left[:, :LANES], left[:, LANES:], left_halo),
-        windows(f, right[:, :LANES], right[:, LANES:], right_halo),
-    )
-
-
-def load_state(state, held, got_depth, got_even, got_odd, base, planes):
-    rows = held.shape[1]
-    extent = rows + 2 * EDGE
+    found = [[] for _ in planes]
+    for at, value, halo, start in blocks:
+        if halo is not None:
+            halo = halo[start : start + value.shape[0], col : col + LANES]
+        for parts, p in zip(found, planes):
+            parts.append((at, window(p, f, value, halo)))
+    return found
+
+
+def joined(outer, middle, inner):
+    surface = lax.axis_index("depth") == 0
+    lane = lane_ids(outer.shape[0])
+    first, last = jnp.where(surface, outer, inner), jnp.where(surface, inner, outer)
+    middle = turn(middle, LANES // 2)
+    return jnp.where(lane < 88, turn(first, -EDGE), middle), jnp.where(lane < 40, middle, turn(last, EDGE))
+
+
+def load_state(states, base, planes, held, *got):
+    extent = held.shape[1] + 2 * EDGE
     for f in range(5):
-        below, above = halo_windows(base + f, got_even, got_odd)
-        own = own_windows(base + f, held, got_depth)
-        for i, p in enumerate(planes):
-            state[f, i, :PAD, :] = jnp.zeros((PAD, LANES), F32)
-            state[f, i, PAD : PAD + EDGE, :] = below[p]
-            state[f, i, PAD + EDGE : PAD + EDGE + rows, :] = own[p]
-            state[f, i, PAD + EDGE + rows : PAD + extent, :] = above[p]
-            state[f, i, PAD + extent :, :] = jnp.zeros((PAD, LANES), F32)
-
-
-def velocities(state, media, span):
+        for state, parts in zip(states, field_windows(base + f, planes, held, *got)):
+            state[f, :PAD, :] = jnp.zeros((PAD, LANES), F32)
+            state[f, PAD + extent :, :] = jnp.zeros((PAD, LANES), F32)
+            for at, part in parts:
+                state[f, PAD + at : PAD + at + part.shape[0], :] = part
+
+
+def velocities(states, medias, span):
     for r in range(8 * span[0], 8 * span[1], 8):
-        for i in range(state.shape[1]):
+        for state, media in zip(states, medias):
 
             def at(f, by=0):
-                return state[f, i, r + PAD + by : r + PAD + by + 8, :]
+                return state[f, r + PAD + by : r + PAD + by + 8, :]
 
             xx, xz, zz = at(2), at(4), at(3)
-            b = media[0, i, r : r + 8, :]
+            b = media[0, r : r + 8, :]
             near = (xx - at(2, -1)) + (xz - turn(xz, 1))
             far = (at(2, 1) - at(2, -2)) + (turn(xz, -1) - turn(xz, 2))
-            state[0, i, r + PAD : r + PAD + 8, :] = at(0) + b * (near + RATIO * far)
+            state[0, r + PAD : r + PAD + 8, :] = at(0) + b * (near + RATIO * far)
             near = (at(4, 1) - xz) + (turn(zz, -1) - zz)
             far = (at(4, 2) - at(4, -1)) + (turn(zz, -2) - turn(zz, 1))
-            state[1, i, r + PAD : r + PAD + 8, :] = at(1) + b * (near + RATIO * far)
-
-
-def stresses(state, media, span, update, keep):
+            state[1, r + PAD : r + PAD + 8, :] = at(1) + b * (near + RATIO * far)
+
+
+def stresses(states, medias, span, update, keep):
     for r in range(8 * span[0], 8 * span[1], 8):
-        for i in range(state.shape[1]):
+        for i, (state, media) in enumerate(zip(states, medias)):
 
             def at(f, by=0):
-                return state[f, i, r + PAD + by : r + PAD + by + 8, :]
+                return state[f, r + PAD + by : r + PAD + by + 8, :]
 
             vx, vz = at(0), at(1)
             exx = (at(0, 1) - vx) + RATIO * (at(0, 2) - at(0, -1))
@@ -217,10 +223,10 @@
             shear = near + RATIO * far
             keep(i, r - EDGE, exx, ezz, shear)
             if update:
-                whole, lam, mu = (media[k, i, r : r + 8, :] for k in (1, 2, 3))
-                state[2, i, r + PAD : r + PAD + 8, :] = at(2) + (whole * exx + lam * ezz)
-                state[3, i, r + PAD : r + PAD + 8, :] = at(3) + (lam * exx + whole * ezz)
-                state[4, i, r + PAD : r + PAD + 8, :] = at(4) + mu * shear
+                whole, lam, mu = (media[k, r : r + 8, :] for k in (1, 2, 3))
+                state[2, r + PAD : r + PAD + 8, :] = at(2) + (whole * exx + lam * ezz)
+                state[3, r + PAD : r + PAD + 8, :] = at(3) + (lam * exx + whole * ezz)
+                state[4, r + PAD : r + PAD + 8, :] = at(4) + mu * shear
 
 
 def spans(step, rows):
@@ -231,41 +237,53 @@
     return inner, inner if step < MOMENTS - 1 else (EDGE // 8, tiles - EDGE // 8)
 
 
-def run_forward(held, got_depth, got_even, got_odd, media, saved, state, planes):
+def run_forward(states, medias, saveds, planes, held, *got):
     rows = held.shape[1]
-    parts = []
-    for f in (5, 6, 7):
-        below, above = halo_windows(f, got_even, got_odd)
-        own = own_windows(f, held, got_depth)
-        parts.append([(below[p], own[p], above[p]) for p in planes])
-    for i in range(len(planes)):
-        for k, at in enumerate((0, EDGE, EDGE + rows)):
-            b, lam, mu = (NEAR * parts[m][i][k] for m in range(3))
+    given = [field_windows(f, planes, held, *got) for f in (5, 6, 7)]
+    for i, media in enumerate(medias):
+        for k in range(3):
+            at = given[0][i][k][0]
+            b, lam, mu = (NEAR * given[m][i][k][1] for m in range(3))
             span = slice(at, at + b.shape[0])
-            media[0, i, span, :] = b
-            media[1, i, span, :] = lam + 2.0 * mu
-            media[2, i, span, :] = lam
-            media[3, i, span, :] = mu
-    load_state(state, held, got_depth, got_even, got_odd, 0, planes)
+            media[0, span, :] = b
+            media[1, span, :] = lam + 2.0 * mu
+            media[2, span, :] = lam
+            media[3, span, :] = mu
+    load_state(states, 0, planes, held, *got)
     for step in range(MOMENTS):
         fast, slow = spans(step, rows)
-        velocities(state, media, fast)
+        velocities(states, medias, fast)
 
         def save(i, r, exx, ezz, shear):
             if 0 <= r < rows:
-                saved[step, 0, i, r : r + 8, :] = exx
-                saved[step, 1, i, r : r + 8, :] = ezz
-                saved[step, 2, i, r : r + 8, :] = shear
-
-        stresses(state, media, slow, step < MOMENTS - 1, save)
-
-
-def forward_kernel(held, got_depth, got_even, got_odd, media, saved, end_out, state):
-    run_forward(held, got_depth, got_even, got_odd, media, saved, state, (0, 1, 2))
-    rows = held.shape[1]
-    top = PAD + EDGE
+                saveds[i][step, 0, r : r + 8, :] = exx
+                saveds[i][step, 1, r : r + 8, :] = ezz
+                saveds[i][step, 2, r : r + 8, :] = shear
+
+        stresses(states, medias, slow, step < MOMENTS - 1, save)
+
+
+def each(ref, count, axis):
+    return [ref.at[(slice(None),) * axis + (i,)] for i in range(count)]
+
+
+def forward_kernel(held, got_even, got_odd, media, saved, end_out, state):
+    states = each(state, 2, 1)
+    run_forward(states, each(media, 2, 1), each(saved, 2, 2), (0, 1), held, got_even, got_odd)
+    top, rows = PAD + EDGE, held.shape[1]
     for f in range(2):
-        first, last = joined([state[f, i, top : top + rows, :] for i in range(3)])
+        for i in range(2):
+            end_out[f, i] = states[i][f, top : top + rows, :]
+
+
+def forward_inner_kernel(held, got_even, got_odd, got_depth, corner, end, media, saved, end_out, state):
+    states = each(state, 1, 1)
+    run_forward(
+        states, each(media, 1, 1), each(saved, 1, 2), (2,), held, got_even, got_odd, got_depth, corner
+    )
+    top, rows = PAD + EDGE, held.shape[1]
+    for f in range(2):
+        first, last = joined(end[f, 0], end[f, 1], states[0][f, top : top + rows, :])
         end_out[f, :, :LANES] = first
         end_out[f, :, LANES:] = last
 
@@ -284,8 +302,8 @@
         note_out[k] = block
 
 
-def relay_kernel(notes, saved, notes_out):
-    del saved
+def relay_kernel(notes, rest, notes_out):
+    del rest
     notes_out[...] = notes[...]
 
 
@@ -450,49 +468,55 @@
     inject_out[...] = turned[: inject_out.shape[0]]
 
 
-def run_adjoint(media, saved, state, sums, inject=None):
-    rows = sums.shape[2]
-    sums[...] = jnp.zeros(sums.shape, F32)
+def run_adjoint(states, medias, saveds, sums, inject=None):
+    rows = sums[0].shape[1]
+    for total in sums:
+        total[...] = jnp.zeros(total.shape, F32)
     for step in range(MOMENTS):
         fast, slow = spans(step, rows)
         moment = MOMENTS - 1 - step
         if inject is not None:
             inject(moment)
-        velocities(state, media, fast)
+        velocities(states, medias, fast)
 
         def gather(i, r, exx, ezz, shear):
             if 0 <= r < rows:
-                fxx, fzz, fxz = (saved[moment, k, i, r : r + 8, :] for k in range(3))
-                sums[0, i, r : r + 8, :] += (fxx + fzz) * (exx + ezz)
-                sums[1, i, r : r + 8, :] += 2.0 * (fxx * exx + fzz * ezz) + fxz * shear
-
-        stresses(state, media, slow, step < MOMENTS - 1, gather)
-
-
-def adjoint_rest_kernel(held, got_depth, got_even, got_odd, media, saved, notes, sums, state):
-    del notes
-    load_state(state, held, got_depth, got_even, got_odd, FORWARD, (1, 2))
-    run_adjoint(media.at[:, pl.ds(1, 2)], saved.at[:, :, pl.ds(1, 2)], state, sums)
+                fxx, fzz, fxz = (saveds[i][moment, k, r : r + 8, :] for k in range(3))
+                sums[i][0, r : r + 8, :] += (fxx + fzz) * (exx + ezz)
+                sums[i][1, r : r + 8, :] += 2.0 * (fxx * exx + fzz * ezz) + fxz * shear
+
+        stresses(states, medias, slow, step < MOMENTS - 1, gather)
+
+
+def adjoint_rest_kernel(
+    held, got_even, got_odd, got_depth, corner, media, saved, inner_media, inner_saved, sums, state
+):
+    states = each(state, 2, 1)
+    load_state(states, FORWARD, (1, 2), held, got_even, got_odd, got_depth, corner)
+    medias = [media.at[:, 1], inner_media.at[:, 0]]
+    saveds = [saved.at[:, :, 1], inner_saved.at[:, :, 0]]
+    run_adjoint(states, medias, saveds, each(sums, 2, 1))
 
 
 def adjoint_top_kernel(
-    held, got_depth, got_even, got_odd, media, saved, rest, inject, end, residual,
+    held, got_even, got_odd, media, saved, rest, inject, end, residual,
     lambda_out, mu_out, end_out, residual_out, state, sums, sems,
 ):
     copies = fetch((end, residual), (end_out, residual_out), sems)
     rows = held.shape[1]
     extent = rows + 2 * EDGE
-    load_state(state, held, got_depth, got_even, got_odd, FORWARD, (0,))
+    states = each(state, 1, 1)
+    load_state(states, FORWARD, (0,), held, got_even, got_odd)
     lane = lane_ids(extent)
     here = (lane >= EDGE) & (lane < EDGE + FIBRE_ROWS)
 
     def add(moment):
         added = jnp.where(here, turn(inject[...], EDGE - FIBRE_ROWS * moment), 0.0)
-        state[2, 0, PAD : PAD + extent, :] += added
-
-    run_adjoint(media.at[:, pl.ds(0, 1)], saved.at[:, :, pl.ds(0, 1)], state, sums, add)
+        states[0][2, PAD : PAD + extent, :] += added
+
+    run_adjoint(states, [media.at[:, 0]], [saved.at[:, :, 0]], each(sums, 1, 1), add)
     for k, out in enumerate((lambda_out, mu_out)):
-        first, last = joined([sums[k, 0], rest[k, 0], rest[k, 1]])
+        first, last = joined(sums[k, 0], rest[k, 0], rest[k, 1])
         out[:, :LANES] = (NEAR * NEAR) * first
         out[:, LANES:] = (NEAR * NEAR) * last
     for copy in copies:
@@ -522,15 +546,16 @@
     channel_arrays = (pinned(observed), pinned(owner), pinned(cell))
     extent = rows + 2 * EDGE
     block = jax.ShapeDtypeStruct((rows, depth_cells), F32)
-    length = EDGE + HALO * FIELDS + EDGE - HALO
+    length = BASE + HALO * FIELDS + BASE
     edges = jax.ShapeDtypeStruct((length + (-length) % 8, depth_cells), F32)
     inside = pl.BlockSpec(memory_space=VMEM)
     outside = pl.BlockSpec(memory_space=pltpu.HBM)
     anywhere = pl.BlockSpec(memory_space=pl.ANY)
-    held, to_depth, to_even, to_odd, strip, traces, cells = pl.pallas_call(
+    held, held_adj, to_depth, to_even, to_odd, strip, traces, cells = pl.pallas_call(
         pack_kernel,
         out_shape=(
-            jax.ShapeDtypeStruct((FIELDS, rows, depth_cells), F32),
+            jax.ShapeDtypeStruct((FORWARD, rows, depth_cells), F32),
+            jax.ShapeDtypeStruct((ADJOINT, rows, depth_cells), F32),
             jax.ShapeDtypeStruct((rows + STRIP, depth_cells), F32),
             edges,
             edges,
@@ -539,29 +564,17 @@
             jax.ShapeDtypeStruct((2, 1, channels), jnp.int32),
         ),
         in_specs=[outside] * 10,
-        out_specs=(inside,) * 7,
+        out_specs=(inside,) * 8,
         scratch_shapes=[VMEM((2, 1, channels), jnp.int32), pltpu.SemaphoreType.DMA((10,))],
         compiler_params=params(),
         cost_estimate=cost(5),
         name="pack",
     )(*arrays, *channel_arrays)
-    to_track = (to_even, to_odd)
-
     depth_swap = [(0, 1), (1, 0)]
     got_depth = lax.ppermute(to_depth, "depth", depth_swap)
-    to_track = pl.pallas_call(
-        corner_kernel,
-        out_shape=(edges, edges),
-        in_specs=[anywhere] * 3,
-        out_specs=(anywhere,) * 2,
-        input_output_aliases={1: 0, 2: 1},
-        scratch_shapes=[pltpu.SemaphoreType.DMA((2,))],
-        compiler_params=params(),
-        name="corners",
-    )(got_depth, *to_track)
     swap = lambda k: [pair for i in range(k, tracks - 1, 2) for pair in ((i, i + 1), (i + 1, i))]
-    got_odd = lax.ppermute(to_track[1], "track", swap(1))
-    got_even = lax.ppermute(to_track[0], "track", swap(0))
+    got_odd = lax.ppermute(to_odd, "track", swap(1))
+    got_even = lax.ppermute(to_even, "track", swap(0))
 
     def state_of(planes):
         return VMEM((5, planes, extent + 2 * PAD, LANES), F32)
@@ -577,20 +590,55 @@
     )(strip, got_depth, traces, cells)
     notes = lax.all_to_all(note, "track", split_axis=0, concat_axis=0, tiled=True)
 
+    corner = pl.pallas_call(
+        corner_kernel,
+        out_shape=jax.ShapeDtypeStruct((2 * EDGE, depth_cells), F32),
+        in_specs=[inside] * 2,
+        out_specs=inside,
+        compiler_params=params(),
+        cost_estimate=cost(1),
+        name="corners",
+    )(got_even, got_odd)
+    got_corner = lax.ppermute(corner, "depth", depth_swap)
+
+    def media_of(planes):
+        return jax.ShapeDtypeStruct((4, planes, extent, LANES), F32)
+
+    def saved_of(planes):
+        return jax.ShapeDtypeStruct((moments, 3, planes, rows, LANES), F32)
+
     media, saved, end = pl.pallas_call(
         forward_kernel,
-        out_shape=(
-            jax.ShapeDtypeStruct((4, 3, extent, LANES), F32),
-            jax.ShapeDtypeStruct((moments, 3, 3, rows, LANES), F32),
-            jax.ShapeDtypeStruct(velocity.shape, F32),
-        ),
-        in_specs=[inside] * 4,
+        out_shape=(media_of(2), saved_of(2), jax.ShapeDtypeStruct((2, 2, rows, LANES), F32)),
+        in_specs=[inside] * 3,
         out_specs=(inside,) * 3,
-        scratch_shapes=[state_of(3)],
+        scratch_shapes=[state_of(2)],
         compiler_params=params(),
         cost_estimate=cost(20),
         name="forward",
-    )(held, got_depth, got_even, got_odd)
+    )(held, got_even, got_odd)
+
+    inner_media, inner_saved, end = pl.pallas_call(
+        forward_inner_kernel,
+        out_shape=(media_of(1), saved_of(1), jax.ShapeDtypeStruct(velocity.shape, F32)),
+        in_specs=[inside] * 6,
+        out_specs=(inside,) * 3,
+        scratch_shapes=[state_of(1)],
+        compiler_params=params(),
+        cost_estimate=cost(20),
+        name="forward_inner",
+    )(held, got_even, got_odd, got_depth, got_corner, end)
+
+    rest = pl.pallas_call(
+        adjoint_rest_kernel,
+        out_shape=jax.ShapeDtypeStruct((2, 2, rows, LANES), F32),
+        in_specs=[inside] * 9,
+        out_specs=inside,
+        scratch_shapes=[state_of(2)],
+        compiler_params=params(),
+        cost_estimate=cost(20),
+        name="adjoint_rest",
+    )(held_adj, got_even, got_odd, got_depth, got_corner, media, saved, inner_media, inner_saved)
 
     mine = pl.pallas_call(
         relay_kernel,
@@ -600,19 +648,8 @@
         compiler_params=params(),
         cost_estimate=cost(1),
         name="relay",
-    )(notes, saved)
+    )(notes, rest)
     beside = lax.ppermute(mine, "depth", depth_swap)
-
-    rest = pl.pallas_call(
-        adjoint_rest_kernel,
-        out_shape=jax.ShapeDtypeStruct((2, 2, rows, LANES), F32),
-        in_specs=[inside] * 6 + [anywhere],
-        out_specs=inside,
-        scratch_shapes=[state_of(2)],
-        compiler_params=params(),
-        cost_estimate=cost(20),
-        name="adjoint_rest",
-    )(held, got_depth, got_even, got_odd, media, saved, mine)
 
     inject, residual = pl.pallas_call(
         lambda *refs: surface_kernel(tracks, rows, *refs),
@@ -641,13 +678,13 @@
             jax.ShapeDtypeStruct(velocity.shape, F32),
             jax.ShapeDtypeStruct((moments // 2, channels), F32),
         ),
-        in_specs=[inside] * 10,
+        in_specs=[inside] * 9,
         out_specs=(inside, inside, outside, outside),
         scratch_shapes=[state_of(1), VMEM((2, 1, rows, LANES), F32), pltpu.SemaphoreType.DMA((2,))],
         compiler_params=params(),
         cost_estimate=cost(2),
         name="adjoint_top",
-    )(held, got_depth, got_even, got_odd, media, saved, rest, inject, end, residual)
+    )(held_adj, got_even, got_odd, media, saved, rest, inject, end, residual)
     return gradient_lambda, gradient_mu, velocity_end, residual
 
 

time: 29 us -> 26.5 us (0.914)
  local copies, waits for them, and re-layouts: 1.77 us -> 0 us
  waiting for transfers between devices: 5.31 us -> 4.73 us
    unnamed x4 -> x0, local copies, waits for them, and re-layouts: 1.77 us -> none
    ppermute x1, waiting for transfers between devices: 0.01 us -> 1.38 us  [per_device(): beside = lax.ppermute(mine, 'depth', depth_swap)]
    all_to_all x1, waiting for transfers between devices: 4.38 us -> 3.34 us  [per_device(): lax.all_to_all(note, 'track', split_axis=0, concat_axis=0, tiled=True)]
    ppermute x1, waiting for transfers between devices: 0.92 us -> 0.01 us  [per_device(): got_depth = lax.ppermute(to_depth, 'depth', depth_swap)]
    pallas_call x3 -> x4, Pallas kernels: 4.11 us -> 4.44 us  [the longest x1 1.73 us: per_device(): pl.pallas_call(pack_kernel, out_shape=(jax.ShapeDtypeStruct((FORWARD, row...]
    ppermute x2 -> x3, starting transfers between devices: 3.57 us -> 3.29 us  [the longest x1 2.56 us: per_device(): got_even = lax.ppermute(to_even, 'track', swap(0))]
  transfers between devices with their start and end apart: 5 -> 6, of which waited for: 2 -> 2; matrix products, arithmetic and copies ran while one was open for 0% -> 0% of each run, Pallas kernels for 16% -> 18%
where the time goes in v13:
time: 26.5 us; the launch traced here: 26.3 us
  starting transfers between devices  11.5 us (43%)
  Pallas kernels  9.34 us (35%)
  waiting for transfers between devices  4.73 us (18%)
  between operations  0.73 us (3%)
    all_to_all x1, starting transfers between devices, per_device(): lax.all_to_all(note, 'track', split_axis=0, concat_axis=0, tiled=True)  7.58 us
    all_to_all x1, waiting for transfers between devices, per_device(): lax.all_to_all(note, 'track', split_axis=0, concat_axis=0, tiled=True)  3.34 us
    ppermute x1, starting transfers between devices, per_device(): got_even = lax.ppermute(to_even, 'track', swap(0))  2.56 us
    pallas_call x1, Pallas kernels, per_device(): pl.pallas_call(pack_kernel, out_shape=(jax.ShapeDtypeStruct((FORWARD, row...  1.73 us
    pallas_call x1, Pallas kernels, per_device(): pl.pallas_call(adjoint_top_kernel, out_shape=(block, block, jax.ShapeDtyp...  1.64 us
    pallas_call x1, Pallas kernels, per_device(): pl.pallas_call(forward_kernel, out_shape=(media_of(2), saved_of(2), jax.S...  1.54 us
    pallas_call x1, Pallas kernels, per_device(): pl.pallas_call(adjoint_rest_kernel, out_shape=jax.ShapeDtypeStruct((2, 2,...  1.39 us
    ppermute x1, waiting for transfers between devices, per_device(): beside = lax.ppermute(mine, 'depth', depth_swap)  1.38 us
  transfers between devices with their start and end apart: 6, of which 2 were waited for; matrix products, arithmetic and copies ran while one was open for 0% of the time, Pallas kernels for 18%

profile of v13, /device:TPU:0, one launch (start us, length us, event | category | flops | bytes accessed | tf_op | source)
XLA Modules:
  0.0 26.3 jit_solution(16368527376999610355)
XLA Ops:
  0.6 1.7 %pack.1 = (f32[8,64,256]{2,1,0:T(8,128)S(1)}, f32[5,64,256]{2,1,0:T(8,128)S(1)}, f32[80,256]{1,0:T(8,128)S(1)}, f32[168,256]{1,0:T(8,128)S(1)}, f32[168,256]{1,0...) custom-call(f32[2,64,256]{2,1,0:T(8,128)} %refs_0_.1, ...), custom_call_target="tpu_custom_call" | custom-call | flops 5000000000 | bytes 1048576 | tf_op jit(solution)/shard_map/pack/pallas_call | solution.py:554
  2.4 0.5 %collective-permute-start.2 = (f32[80,256]{1,0:T(8,128)S(1)}, f32[80,256]{1,0:T(8,128)S(1)}, u32[]{:S(2)}, u32[]{:S(2)}) collective-permute-start(f32[80,256]{1,0:T(8,128)S(1)} %get-tuple-element.26), channel_id=1, source_target_pairs={{0,1},{1,0},{2,3},{3,2},{4,5},{5,4},{6,7},{7,6},{8,9},{9,8},{10,11... | collective-permute-start | bytes 245768 | tf_op jit(solution)/shard_map/ppermute | solution.py:574
  2.9 2.6 %collective-permute-start = (f32[168,256]{1,0:T(8,128)S(1)}, f32[168,256]{1,0:T(8,128)S(1)}, u32[]{:S(2)}, u32[]{:S(2)}) collective-permute-start(f32[168,256]{1,0:T(8,128)S(1)} %get-tuple-element.21), channel_id=1, source_target_pairs={{0,2},{2,0},{4,6},{6,4},{8,10},{10,8},{12,14},{14,12},{1,3},{3,1},... | collective-permute-start | bytes 516104 | tf_op jit(solution)/shard_map/ppermute | solution.py:577
  5.5 0.7 %collective-permute-start.1 = (f32[168,256]{1,0:T(8,128)S(1)}, f32[168,256]{1,0:T(8,128)S(1)}, u32[]{:S(2)}, u32[]{:S(2)}) collective-permute-start(f32[168,256]{1,0:T(8,128)S(1)} %get-tuple-element.22), channel_id=1, source_target_pairs={{2,4},{4,2},{6,8},{8,6},{10,12},{12,10},{3,5},{5,3},{7,9},{9,7},{1... | collective-permute-start | bytes 516104 | tf_op jit(solution)/shard_map/ppermute | solution.py:576
  6.1 0.0 collective-permute-done.2.got_depth
  6.1 0.7 %note.1 = f32[8,40,128]{2,1,0:T(8,128)} custom-call(f32[32,128]{1,0:T(8,128)S(1)} %get-tuple-element.30.strip, f32[80,256]{1,0:T(8,128)S(1)} %collective-permute-done.2.got_depth, f32[4,256]{1,0:T(4,128)S(1)} %get-tuple-element.31.traces.refs_2_, s32[2,1,256]{2,1,0:T(1,128)S(1)} %get-tuple-element.32.cells.refs_3_), custom_call_target="tpu_custom_call" | custom-call | flops 1000000000 | bytes 1048576 | tf_op jit(solution)/shard_map/note/pallas_call | solution.py:582
  6.8 7.6 %all-to-all-start = ((f32[8,40,128]{2,1,0:T(8,128)}), f32[8,40,128]{2,1,0:T(8,128)S(1)}, u32[]{:S(2)}, u32[]{:S(2)}) async-start(f32[8,40,128]{2,1,0:T(8,128)} %note.1), calls=%async_computation | async-start | bytes 327680 | tf_op jit(solution)/shard_map/all_to_all | solution.py:591
  14.4 0.0 collective-permute-done.got_even
  14.4 0.0 collective-permute-done.1.got_odd
  14.4 0.1 corners.1
  14.6 0.1 collective-permute-start.3
  14.6 1.5 %forward.1 = (f32[4,2,96,128]{3,2,1,0:T(8,128)S(1)}, f32[4,3,2,64,128]{4,3,2,1,0:T(8,128)S(1)}, f32[2,2,64,128]{3,2,1,0:T(8,128)S(1)}) custom-call(f32[8,64,256]{2,1,0:T(8,128)S(1)} %get-tuple-element.23.held, f32[168,256]{1,0:T(8,128)S(1)} %collective-permute-done.got_even, f32[168,256]{1,0:T(8,128)S(1)} %collective-permute-done.1.got_odd), custom_call_target="tpu_custom_call" | custom-call | flops 20000000000 | bytes 1048576 | tf_op jit(solution)/shard_map/forward/pallas_call | solution.py:610
  16.2 0.0 collective-permute-done.3.corner
  16.2 1.0 %forward_inner.1 = (f32[4,1,96,128]{3,2,1,0:T(8,128)S(1)}, f32[4,3,1,64,128]{4,3,2,1,0:T(8,128)S(1)}, f32[2,64,256]{2,1,0:T(8,128)S(1)}) custom-call(f32[8,64,256]{2,1,0:T(8,128)S(1)} %get-tuple-element.23.held, f32[168,256]{1,0:T(8,128)S(1)} %collective-permute-done.got_even, f32[168,256]{1,0:T(8,128)S(1)} %collective-permute-done.1.got_odd, ...), custom_call_target="tpu_custom_call" | custom-call | flops 20000000000 | bytes 1048576 | tf_op jit(solution)/shard_map/forward_inner/pallas_call | solution.py:621
  17.2 1.4 %adjoint_rest.1.rest = f32[2,2,64,128]{3,2,1,0:T(8,128)S(1)} custom-call(f32[5,64,256]{2,1,0:T(8,128)S(1)} %get-tuple-element.20.held, f32[168,256]{1,0:T(8,128)S(1)} %collective-permute-done.got_even, f32[168,256]{1,0:T(8,128)S(1)} %collective-permute-done.1.got_odd, f32[80,256]{1,0:T(8,128)S(1)} %collective-permute-done.2.got_depth, ...), custom_call_target="tpu_custom_call" | custom-call | flops 20000000000 | bytes 1048576 | tf_op jit(solution)/shard_map/adjoint_rest/pallas_call | solution.py:632
  18.6 3.3 %all-to-all-done.notes = f32[8,40,128]{2,1,0:T(8,128)S(1)} async-done(((f32[8,40,128]{2,1,0:T(8,128)}), f32[8,40,128]{2,1,0:T(8,128)S(1)}, u32[]{:S(2)}, u32[]{:S(2)}) %all-to-all-start) | async-done | bytes 163872 | tf_op jit(solution)/shard_map/all_to_all | solution.py:591
  22.0 0.1 collective-permute-start.4
  22.1 1.4 %collective-permute-done.4.refs_1_ = f32[8,40,128]{2,1,0:T(8,128)S(1)} collective-permute-done((f32[8,40,128]{2,1,0:T(8,128)S(1)}, f32[8,40,128]{2,1,0:T(8,128)S(1)}, u32[]{:S(2)}, u32[]{:S(2)}) %collective-permute-start.4) | collective-permute-done | bytes 163872 | tf_op jit(solution)/shard_map/ppermute | solution.py:652
  23.4 1.2 %surface.1 = (f32[96,128]{1,0:T(8,128)S(1)}, f32[2,256]{1,0:T(2,128)S(1)}) custom-call(f32[8,40,128]{2,1,0:T(8,128)S(1)} %relay.1.refs_0_, f32[8,40,128]{2,1,0:T(8,128)S(1)} %collective-permute-done.4.refs_1_, f32[4,256]{1,0:T(4,128)S(1)} %get-tuple-element.31.traces.refs_2_, s32[2,1,256]{2,1,0:T(1,128)S(1)} %get-tuple-element.32.cells.refs_3_), custom_call_target="tpu_custom_call" | custom-call | flops 2000000000 | bytes 1048576 | tf_op jit(solution)/shard_map/surface/pallas_call | solution.py:654
  24.6 1.6 %adjoint_top.1 = (f32[64,256]{1,0:T(8,128)}, f32[64,256]{1,0:T(8,128)}, f32[2,64,256]{2,1,0:T(8,128)}, f32[2,256]{1,0:T(2,128)}) custom-call(f32[5,64,256]{2,1,0:T(8,128)S(1)} %get-tuple-element.20.held, f32[168,256]{1,0:T(8,128)S(1)} %collective-permute-done.got_even, f32[168,256]{1,0:T(8,128)S(1)} %collective-permute-done.1.got_odd, ...), custom_call_target="tpu_custom_call" | custom-call | flops 2000000000 | bytes 1048576 | tf_op jit(solution)/shard_map/adjoint_top/pallas_call | solution.py:673
  (1 shorter events, 0.0 us)
Async XLA Ops:
  2.4 3.8 %collective-permute-start.2 = (f32[80,256]{1,0:T(8,128)S(1)}, f32[80,256]{1,0:T(8,128)S(1)}, u32[]{:S(2)}, u32[]{:S(2)}) collective-permute-start(f32[80,256]{1,0:T(8,128)S(1)} %get-tuple-element.26), channel_id=1, source_target_pairs={{0,1},{1,0},{2,3},{3,2},{4,5},{5,4},{6,7},{7,6},{8,9},{9,8},{10,11... | collective-permute-start | bytes 245768 | tf_op jit(solution)/shard_map/ppermute | solution.py:574
  2.9 11.5 %collective-permute-start = (f32[168,256]{1,0:T(8,128)S(1)}, f32[168,256]{1,0:T(8,128)S(1)}, u32[]{:S(2)}, u32[]{:S(2)}) collective-permute-start(f32[168,256]{1,0:T(8,128)S(1)} %get-tuple-element.21), channel_id=1, source_target_pairs={{0,2},{2,0},{4,6},{6,4},{8,10},{10,8},{12,14},{14,12},{1,3},{3,1},... | collective-permute-start | bytes 516104 | tf_op jit(solution)/shard_map/ppermute | solution.py:577
  5.5 8.9 %collective-permute-start.1 = (f32[168,256]{1,0:T(8,128)S(1)}, f32[168,256]{1,0:T(8,128)S(1)}, u32[]{:S(2)}, u32[]{:S(2)}) collective-permute-start(f32[168,256]{1,0:T(8,128)S(1)} %get-tuple-element.22), channel_id=1, source_target_pairs={{2,4},{4,2},{6,8},{8,6},{10,12},{12,10},{3,5},{5,3},{7,9},{9,7},{1... | collective-permute-start | bytes 516104 | tf_op jit(solution)/shard_map/ppermute | solution.py:576
  6.8 15.1 %all-to-all-start = ((f32[8,40,128]{2,1,0:T(8,128)}), f32[8,40,128]{2,1,0:T(8,128)S(1)}, u32[]{:S(2)}, u32[]{:S(2)}) async-start(f32[8,40,128]{2,1,0:T(8,128)} %note.1), calls=%async_computation | async-start | bytes 327680 | tf_op jit(solution)/shard_map/all_to_all | solution.py:591
  14.6 1.6 %collective-permute-start.3 = (f32[32,256]{1,0:T(8,128)S(1)}, f32[32,256]{1,0:T(8,128)S(1)}, u32[]{:S(2)}, u32[]{:S(2)}) collective-permute-start(f32[32,256]{1,0:T(8,128)S(1)} %corners.1), channel_id=1, source_target_pairs={{0,1},{1,0},{2,3},{3,2},{4,5},{5,4},{6,7},{7,6},{8,9},{9,8},{10,11... | collective-permute-start | bytes 98312 | tf_op jit(solution)/shard_map/ppermute | solution.py:602
  22.0 1.5 %collective-permute-start.4 = (f32[8,40,128]{2,1,0:T(8,128)S(1)}, f32[8,40,128]{2,1,0:T(8,128)S(1)}, u32[]{:S(2)}, u32[]{:S(2)}) collective-permute-start(f32[8,40,128]{2,1,0:T(8,128)S(1)} %relay.1.refs_0_), channel_id=1, source_target_pairs={{0,1},{1,0},{2,3},{3,2},{4,5},{5,4},{6,7},{7,6},{8,9},{9,8},{10,11... | collective-permute-start | bytes 491528 | tf_op jit(solution)/shard_map/ppermute | solution.py:652

commit v14 on v13

--- a/solution.py
+++ b/solution.py
@@ -16,7 +16,9 @@
 ADJOINT = 5
 FIELDS = FORWARD + ADJOINT
 STRIP = 16
-BASE = EDGE - HALO
+LAYERS = (11, 11, 12, 11, 12, 11, 9, 9, 11, 11, 12, 11, 12)
+PLACES = tuple(5 + sum(LAYERS[:f]) for f in range(FIELDS))
+EDGE_ROWS = 5 + sum(LAYERS) + 4
 MOMENTS = 4
 IMAGE = MOMENTS * FIBRE_ROWS
 VMEM = pltpu.VMEM
@@ -59,33 +61,24 @@
     sources, channel_arrays = refs[:7], refs[7:10]
     held, held_adj, depth_out, edge_outs, strip_out, traces_out, cells_out = *refs[10:13], refs[13:15], *refs[15:18]
     numbers, sems = refs[18:]
-    targets = (
-        held.at[pl.ds(0, 2)],
-        held.at[pl.ds(2, 3)],
-        held.at[5],
-        held.at[6],
-        held.at[7],
-        held_adj.at[pl.ds(0, 2)],
-        held_adj.at[pl.ds(2, 3)],
-        traces_out,
-        numbers.at[0],
-        numbers.at[1],
-    )
-    copies = fetch((*sources[:2], *sources[4:], *sources[2:4], *channel_arrays), targets, sems)
-    arriving = {0: copies[0], 2: copies[1], 5: copies[2], 6: copies[3], 7: copies[4], 8: copies[5], 10: copies[6]}
+    velocity, stress, adj_velocity, adj_stress, buoyancy, lame, shear = sources
+    fields = [velocity.at[i] for i in range(2)] + [stress.at[i] for i in range(3)] + [buoyancy, lame, shear]
+    fields += [adj_velocity.at[i] for i in range(2)] + [adj_stress.at[i] for i in range(3)]
+    targets = [held.at[f] for f in range(FORWARD)] + [held_adj.at[f] for f in range(ADJOINT)]
+    targets += [traces_out, numbers.at[0], numbers.at[1]]
+    copies = fetch((*fields, *channel_arrays), targets, sems)
     depth = lax.axis_index("depth")
     even = is_even()
     rows = held.shape[1]
     lane = lane_ids(rows)
-    tail = BASE + HALO * FIELDS
+    tail = PLACES[-1] + LAYERS[-1]
     for out in edge_outs:
-        out[:BASE, :] = jnp.zeros((BASE, 2 * LANES), F32)
+        out[: PLACES[0], :] = jnp.zeros((PLACES[0], 2 * LANES), F32)
         out[tail:, :] = jnp.zeros((out.shape[0] - tail, 2 * LANES), F32)
     packed = [jnp.zeros((rows, LANES), F32) for _ in range(2)]
     strip = jnp.zeros((rows, LANES), F32)
     for f in range(FIELDS):
-        if f in arriving:
-            arriving[f].wait()
+        copies[f].wait()
         ref = held.at[f] if f < FORWARD else held_adj.at[f - FORWARD]
         first, last = ref[:, :LANES], ref[:, LANES:]
         group, place = divmod(f, FORWARD)
@@ -96,10 +89,10 @@
         packed[group] = jnp.where(here, pltpu.roll(edge, shift, 1), packed[group])
         if f < FORWARD:
             strip = jnp.where(here, turn(first, spot), strip)
-        low, high = ref[:HALO, :], ref[rows - HALO :, :]
-        at = BASE + HALO * f
-        edge_outs[0][at : at + HALO, :] = jnp.where(even, high, low)
-        edge_outs[1][at : at + HALO, :] = jnp.where(even, low, high)
+        count, at = LAYERS[f], PLACES[f]
+        low, high = ref[:count, :], ref[rows - count :, :]
+        edge_outs[0][at : at + count, :] = jnp.where(even, high, low)
+        edge_outs[1][at : at + count, :] = jnp.where(even, low, high)
     depth_out[:rows, :LANES] = packed[0]
     depth_out[:rows, LANES:] = packed[1]
     turned = strip.T
@@ -109,15 +102,15 @@
     depth_out[rows:, rows : 2 * rows] = turned[6 * STRIP : 7 * STRIP]
     depth_out[rows:, 2 * rows : 3 * rows] = turned[5 * STRIP : 6 * STRIP]
     depth_out[rows:, 3 * rows :] = turned[7 * STRIP :]
-    for copy in copies[7:]:
+    for copy in copies[FIELDS:]:
         copy.wait()
     cells_out[0] = numbers[0] * rows + lax.shift_right_logical(numbers[1], 2)
     cells_out[1] = numbers[1] & 3
 
 
 def edge_rows(f, side, got_even, got_odd):
-    at = BASE + HALO * f
-    span = slice(at - BASE, at + HALO) if side == 0 else slice(at, at + EDGE)
+    at = PLACES[f]
+    span = slice(at + LAYERS[f] - EDGE, at + LAYERS[f]) if side == 0 else slice(at, at + EDGE)
     use_odd = is_even() if side == 0 else ~is_even()
     return jnp.where(use_odd, got_odd[span, :], got_even[span, :])
 
@@ -288,18 +281,18 @@
         end_out[f, :, LANES:] = last
 
 
-def note_kernel(strip, got_depth, traces, cells, note_out):
+def note_kernel(strip, got_depth, traces, cells, note_out, block, sems):
     first = lax.axis_index("depth") == 0
     beside = got_depth[got_depth.shape[0] - STRIP :, :]
     beside = jnp.concatenate([beside[:, :LANES], beside[:, LANES:]], axis=0)
     seen = jnp.concatenate([traces[:, :LANES], traces[:, LANES:]], axis=0)
     along, row = cells[0], cells[1]
     places = jnp.concatenate([along[:, :LANES], along[:, LANES:], row[:, :LANES], row[:, LANES:]] * 2, axis=0)
-    block = jnp.concatenate(
-        [jnp.where(first, strip[...], beside), jnp.where(first, seen, places.astype(F32))], axis=0
-    )
-    for k in range(note_out.shape[0]):
-        note_out[k] = block
+    block[: 2 * STRIP, :] = jnp.where(first, strip[...], beside)
+    block[2 * STRIP :, :] = jnp.where(first, seen, places.astype(F32))
+    count = note_out.shape[0]
+    for copy in fetch([block] * count, [note_out.at[k] for k in range(count)], sems):
+        copy.wait()
 
 
 def relay_kernel(notes, rest, notes_out):
@@ -546,8 +539,7 @@
     channel_arrays = (pinned(observed), pinned(owner), pinned(cell))
     extent = rows + 2 * EDGE
     block = jax.ShapeDtypeStruct((rows, depth_cells), F32)
-    length = BASE + HALO * FIELDS + BASE
-    edges = jax.ShapeDtypeStruct((length + (-length) % 8, depth_cells), F32)
+    edges = jax.ShapeDtypeStruct((EDGE_ROWS, depth_cells), F32)
     inside = pl.BlockSpec(memory_space=VMEM)
     outside = pl.BlockSpec(memory_space=pltpu.HBM)
     anywhere = pl.BlockSpec(memory_space=pl.ANY)
@@ -565,7 +557,7 @@
         ),
         in_specs=[outside] * 10,
         out_specs=(inside,) * 8,
-        scratch_shapes=[VMEM((2, 1, channels), jnp.int32), pltpu.SemaphoreType.DMA((10,))],
+        scratch_shapes=[VMEM((2, 1, channels), jnp.int32), pltpu.SemaphoreType.DMA((FIELDS + 3,))],
         compiler_params=params(),
         cost_estimate=cost(5),
         name="pack",
@@ -583,7 +575,8 @@
         note_kernel,
         out_shape=jax.ShapeDtypeStruct((tracks, 2 * STRIP + 8, LANES), F32),
         in_specs=[inside] * 4,
-        out_specs=inside,
+        out_specs=outside,
+        scratch_shapes=[VMEM((2 * STRIP + 8, LANES), F32), pltpu.SemaphoreType.DMA((tracks,))],
         compiler_params=params(),
         cost_estimate=cost(1),
         name="note",

time: 26.5 us -> 27 us (1.019)
  Pallas kernels: 9.34 us -> 9.84 us
    pallas_call x1, Pallas kernels: 1.73 us -> 2.15 us  [per_device(): pl.pallas_call(pack_kernel, out_shape=(jax.ShapeDtypeStruct((FORWARD, row...]
where the time goes in v14:
time: 27 us; the launch traced here: 26.8 us
  starting transfers between devices  11.5 us (43%)
  Pallas kernels  9.84 us (36%)
  waiting for transfers between devices  4.71 us (17%)
  between operations  0.74 us (3%)
    all_to_all x1, starting transfers between devices, per_device(): lax.all_to_all(note, 'track', split_axis=0, concat_axis=0, tiled=True)  7.59 us
    all_to_all x1, waiting for transfers between devices, per_device(): lax.all_to_all(note, 'track', split_axis=0, concat_axis=0, tiled=True)  3.32 us
    ppermute x1, starting transfers between devices, per_device(): got_even = lax.ppermute(to_even, 'track', swap(0))  2.56 us
    pallas_call x1, Pallas kernels, per_device(): pl.pallas_call(pack_kernel, out_shape=(jax.ShapeDtypeStruct((FORWARD, row...  2.15 us
    pallas_call x1, Pallas kernels, per_device(): pl.pallas_call(adjoint_top_kernel, out_shape=(block, block, jax.ShapeDtyp...  1.65 us
    pallas_call x1, Pallas kernels, per_device(): pl.pallas_call(forward_kernel, out_shape=(media_of(2), saved_of(2), jax.S...  1.55 us
    pallas_call x1, Pallas kernels, per_device(): pl.pallas_call(adjoint_rest_kernel, out_shape=jax.ShapeDtypeStruct((2, 2,...  1.39 us
    ppermute x1, waiting for transfers between devices, per_device(): beside = lax.ppermute(mine, 'depth', depth_swap)  1.38 us
  transfers between devices with their start and end apart: 6, of which 2 were waited for; matrix products, arithmetic and copies ran while one was open for 0% of the time, Pallas kernels for 18%

profile of v14, /device:TPU:0, one launch (start us, length us, event | category | flops | bytes accessed | tf_op | source)
XLA Modules:
  0.0 26.8 jit_solution(2247973244497119919)
XLA Ops:
  0.6 2.1 %pack.1 = (f32[8,64,256]{2,1,0:T(8,128)S(1)}, f32[5,64,256]{2,1,0:T(8,128)S(1)}, f32[80,256]{1,0:T(8,128)S(1)}, f32[152,256]{1,0:T(8,128)S(1)}, f32[152,256]{1,0...) custom-call(f32[2,64,256]{2,1,0:T(8,128)} %refs_0_.1, ...), custom_call_target="tpu_custom_call" | custom-call | flops 5000000000 | bytes 1048576 | tf_op jit(solution)/shard_map/pack/pallas_call | solution.py:546
  2.8 0.5 %collective-permute-start.2 = (f32[80,256]{1,0:T(8,128)S(1)}, f32[80,256]{1,0:T(8,128)S(1)}, u32[]{:S(2)}, u32[]{:S(2)}) collective-permute-start(f32[80,256]{1,0:T(8,128)S(1)} %get-tuple-element.26), channel_id=1, source_target_pairs={{0,1},{1,0},{2,3},{3,2},{4,5},{5,4},{6,7},{7,6},{8,9},{9,8},{10,11... | collective-permute-start | bytes 245768 | tf_op jit(solution)/shard_map/ppermute | solution.py:566
  3.3 2.6 %collective-permute-start = (f32[152,256]{1,0:T(8,128)S(1)}, f32[152,256]{1,0:T(8,128)S(1)}, u32[]{:S(2)}, u32[]{:S(2)}) collective-permute-start(f32[152,256]{1,0:T(8,128)S(1)} %get-tuple-element.21), channel_id=1, source_target_pairs={{0,2},{2,0},{4,6},{6,4},{8,10},{10,8},{12,14},{14,12},{1,3},{3,1},... | collective-permute-start | bytes 466952 | tf_op jit(solution)/shard_map/ppermute | solution.py:569
  5.9 0.7 %collective-permute-start.1 = (f32[152,256]{1,0:T(8,128)S(1)}, f32[152,256]{1,0:T(8,128)S(1)}, u32[]{:S(2)}, u32[]{:S(2)}) collective-permute-start(f32[152,256]{1,0:T(8,128)S(1)} %get-tuple-element.22), channel_id=1, source_target_pairs={{2,4},{4,2},{6,8},{8,6},{10,12},{12,10},{3,5},{5,3},{7,9},{9,7},{1... | collective-permute-start | bytes 466952 | tf_op jit(solution)/shard_map/ppermute | solution.py:568
  6.5 0.0 collective-permute-done.2.got_depth
  6.5 0.7 %note.1 = f32[8,40,128]{2,1,0:T(8,128)} custom-call(f32[32,128]{1,0:T(8,128)S(1)} %get-tuple-element.30.strip, f32[80,256]{1,0:T(8,128)S(1)} %collective-permute-done.2.got_depth, f32[4,256]{1,0:T(4,128)S(1)} %get-tuple-element.31.traces.refs_2_, s32[2,1,256]{2,1,0:T(1,128)S(1)} %get-tuple-element.32.cells.refs_3_), custom_call_target="tpu_custom_call" | custom-call | flops 1000000000 | bytes 1048576 | tf_op jit(solution)/shard_map/note/pallas_call | solution.py:574
  7.3 7.6 %all-to-all-start = ((f32[8,40,128]{2,1,0:T(8,128)}), f32[8,40,128]{2,1,0:T(8,128)S(1)}, u32[]{:S(2)}, u32[]{:S(2)}) async-start(f32[8,40,128]{2,1,0:T(8,128)} %note.1), calls=%async_computation | async-start | bytes 327680 | tf_op jit(solution)/shard_map/all_to_all | solution.py:584
  14.9 0.0 collective-permute-done.got_even
  14.9 0.0 collective-permute-done.1.got_odd
  14.9 0.1 corners.1
  15.1 0.1 collective-permute-start.3
  15.1 1.5 %forward.1 = (f32[4,2,96,128]{3,2,1,0:T(8,128)S(1)}, f32[4,3,2,64,128]{4,3,2,1,0:T(8,128)S(1)}, f32[2,2,64,128]{3,2,1,0:T(8,128)S(1)}) custom-call(f32[8,64,256]{2,1,0:T(8,128)S(1)} %get-tuple-element.23.held, f32[152,256]{1,0:T(8,128)S(1)} %collective-permute-done.got_even, f32[152,256]{1,0:T(8,128)S(1)} %collective-permute-done.1.got_odd), custom_call_target="tpu_custom_call" | custom-call | flops 20000000000 | bytes 1048576 | tf_op jit(solution)/shard_map/forward/pallas_call | solution.py:603
  16.7 0.0 collective-permute-done.3.corner
  16.7 1.0 %forward_inner.1 = (f32[4,1,96,128]{3,2,1,0:T(8,128)S(1)}, f32[4,3,1,64,128]{4,3,2,1,0:T(8,128)S(1)}, f32[2,64,256]{2,1,0:T(8,128)S(1)}) custom-call(f32[8,64,256]{2,1,0:T(8,128)S(1)} %get-tuple-element.23.held, f32[152,256]{1,0:T(8,128)S(1)} %collective-permute-done.got_even, f32[152,256]{1,0:T(8,128)S(1)} %collective-permute-done.1.got_odd, ...), custom_call_target="tpu_custom_call" | custom-call | flops 20000000000 | bytes 1048576 | tf_op jit(solution)/shard_map/forward_inner/pallas_call | solution.py:614
  17.7 1.4 %adjoint_rest.1.rest = f32[2,2,64,128]{3,2,1,0:T(8,128)S(1)} custom-call(f32[5,64,256]{2,1,0:T(8,128)S(1)} %get-tuple-element.20.held, f32[152,256]{1,0:T(8,128)S(1)} %collective-permute-done.got_even, f32[152,256]{1,0:T(8,128)S(1)} %collective-permute-done.1.got_odd, f32[80,256]{1,0:T(8,128)S(1)} %collective-permute-done.2.got_depth, ...), custom_call_target="tpu_custom_call" | custom-call | flops 20000000000 | bytes 1048576 | tf_op jit(solution)/shard_map/adjoint_rest/pallas_call | solution.py:625
  19.1 3.3 %all-to-all-done.notes = f32[8,40,128]{2,1,0:T(8,128)S(1)} async-done(((f32[8,40,128]{2,1,0:T(8,128)}), f32[8,40,128]{2,1,0:T(8,128)S(1)}, u32[]{:S(2)}, u32[]{:S(2)}) %all-to-all-start) | async-done | bytes 163872 | tf_op jit(solution)/shard_map/all_to_all | solution.py:584
  22.5 0.1 collective-permute-start.4
  22.5 1.4 %collective-permute-done.4.refs_1_ = f32[8,40,128]{2,1,0:T(8,128)S(1)} collective-permute-done((f32[8,40,128]{2,1,0:T(8,128)S(1)}, f32[8,40,128]{2,1,0:T(8,128)S(1)}, u32[]{:S(2)}, u32[]{:S(2)}) %collective-permute-start.4) | collective-permute-done | bytes 163872 | tf_op jit(solution)/shard_map/ppermute | solution.py:645
  23.9 1.2 %surface.1 = (f32[96,128]{1,0:T(8,128)S(1)}, f32[2,256]{1,0:T(2,128)S(1)}) custom-call(f32[8,40,128]{2,1,0:T(8,128)S(1)} %relay.1.refs_0_, f32[8,40,128]{2,1,0:T(8,128)S(1)} %collective-permute-done.4.refs_1_, f32[4,256]{1,0:T(4,128)S(1)} %get-tuple-element.31.traces.refs_2_, s32[2,1,256]{2,1,0:T(1,128)S(1)} %get-tuple-element.32.cells.refs_3_), custom_call_target="tpu_custom_call" | custom-call | flops 2000000000 | bytes 1048576 | tf_op jit(solution)/shard_map/surface/pallas_call | solution.py:647
  25.1 1.6 %adjoint_top.1 = (f32[64,256]{1,0:T(8,128)}, f32[64,256]{1,0:T(8,128)}, f32[2,64,256]{2,1,0:T(8,128)}, f32[2,256]{1,0:T(2,128)}) custom-call(f32[5,64,256]{2,1,0:T(8,128)S(1)} %get-tuple-element.20.held, f32[152,256]{1,0:T(8,128)S(1)} %collective-permute-done.got_even, f32[152,256]{1,0:T(8,128)S(1)} %collective-permute-done.1.got_odd, ...), custom_call_target="tpu_custom_call" | custom-call | flops 2000000000 | bytes 1048576 | tf_op jit(solution)/shard_map/adjoint_top/pallas_call | solution.py:666
  (1 shorter events, 0.0 us)
Async XLA Ops:
  2.8 3.8 %collective-permute-start.2 = (f32[80,256]{1,0:T(8,128)S(1)}, f32[80,256]{1,0:T(8,128)S(1)}, u32[]{:S(2)}, u32[]{:S(2)}) collective-permute-start(f32[80,256]{1,0:T(8,128)S(1)} %get-tuple-element.26), channel_id=1, source_target_pairs={{0,1},{1,0},{2,3},{3,2},{4,5},{5,4},{6,7},{7,6},{8,9},{9,8},{10,11... | collective-permute-start | bytes 245768 | tf_op jit(solution)/shard_map/ppermute | solution.py:566
  3.3 11.6 %collective-permute-start = (f32[152,256]{1,0:T(8,128)S(1)}, f32[152,256]{1,0:T(8,128)S(1)}, u32[]{:S(2)}, u32[]{:S(2)}) collective-permute-start(f32[152,256]{1,0:T(8,128)S(1)} %get-tuple-element.21), channel_id=1, source_target_pairs={{0,2},{2,0},{4,6},{6,4},{8,10},{10,8},{12,14},{14,12},{1,3},{3,1},... | collective-permute-start | bytes 466952 | tf_op jit(solution)/shard_map/ppermute | solution.py:569
  5.9 9.0 %collective-permute-start.1 = (f32[152,256]{1,0:T(8,128)S(1)}, f32[152,256]{1,0:T(8,128)S(1)}, u32[]{:S(2)}, u32[]{:S(2)}) collective-permute-start(f32[152,256]{1,0:T(8,128)S(1)} %get-tuple-element.22), channel_id=1, source_target_pairs={{2,4},{4,2},{6,8},{8,6},{10,12},{12,10},{3,5},{5,3},{7,9},{9,7},{1... | collective-permute-start | bytes 466952 | tf_op jit(solution)/shard_map/ppermute | solution.py:568
  7.3 15.2 %all-to-all-start = ((f32[8,40,128]{2,1,0:T(8,128)}), f32[8,40,128]{2,1,0:T(8,128)S(1)}, u32[]{:S(2)}, u32[]{:S(2)}) async-start(f32[8,40,128]{2,1,0:T(8,128)} %note.1), calls=%async_computation | async-start | bytes 327680 | tf_op jit(solution)/shard_map/all_to_all | solution.py:584
  15.1 1.6 %collective-permute-start.3 = (f32[32,256]{1,0:T(8,128)S(1)}, f32[32,256]{1,0:T(8,128)S(1)}, u32[]{:S(2)}, u32[]{:S(2)}) collective-permute-start(f32[32,256]{1,0:T(8,128)S(1)} %corners.1), channel_id=1, source_target_pairs={{0,1},{1,0},{2,3},{3,2},{4,5},{5,4},{6,7},{7,6},{8,9},{9,8},{10,11... | collective-permute-start | bytes 98312 | tf_op jit(solution)/shard_map/ppermute | solution.py:595
  22.5 1.5 %collective-permute-start.4 = (f32[8,40,128]{2,1,0:T(8,128)S(1)}, f32[8,40,128]{2,1,0:T(8,128)S(1)}, u32[]{:S(2)}, u32[]{:S(2)}) collective-permute-start(f32[8,40,128]{2,1,0:T(8,128)S(1)} %relay.1.refs_0_), channel_id=1, source_target_pairs={{0,1},{1,0},{2,3},{3,2},{4,5},{5,4},{6,7},{7,6},{8,9},{9,8},{10,11... | collective-permute-start | bytes 491528 | tf_op jit(solution)/shard_map/ppermute | solution.py:645

commit v15 on v13

--- a/solution.py
+++ b/solution.py
@@ -323,25 +323,27 @@
 OWN = LANES - 2 * HALO
 
 
+def strip_window(f, low, high, base, offset, tracks, columns):
+    lane = lane_ids(STRIP)
+    part = lax.div(offset + lane, columns)
+    spot = base * columns + offset + lane
+    source, q = (low, high)[f // 4], f % 4
+    value = jnp.zeros((STRIP, LANES), F32)
+    for step in range(3):
+        who = jnp.clip(base + step, 0, tracks - 1)
+        block = source[who, STRIP * (q % 2) : STRIP * (q % 2 + 1), :]
+        shift = (4 * LANES - offset + columns * step - columns * (q // 2)) % LANES
+        value = jnp.where(part == step, pltpu.roll(block, shift, 1), value)
+    return jnp.where((spot >= 0) & (spot < tracks * columns), value, 0.0)
+
+
 def fill_strip(state, media, low, high, first, tracks, columns):
-    lane = lane_ids(STRIP)
     state[...] = jnp.zeros(state.shape, F32)
     for w in range(BATCH):
         begin = (first + w) * OWN - HALO
         base = (begin + columns) // columns - 1
         offset = begin - base * columns
-        part = lax.div(offset + lane, columns)
-        inside = (begin + lane >= 0) & (begin + lane < tracks * columns)
-        values = []
-        for f in range(FORWARD):
-            source, q = (low, high)[f // 4], f % 4
-            value = jnp.zeros((STRIP, LANES), F32)
-            for step in range(3):
-                who = jnp.clip(base + step, 0, tracks - 1)
-                block = source[who, STRIP * (q % 2) : STRIP * (q % 2 + 1), :]
-                shift = (4 * LANES - offset + columns * step - columns * (q // 2)) % LANES
-                value = jnp.where(part == step, pltpu.roll(block, shift, 1), value)
-            values.append(jnp.where(inside, value, 0.0))
+        values = [strip_window(f, low, high, base, offset, tracks, columns) for f in range(FORWARD)]
         for f in range(5):
             state[f, w, PAD : PAD + STRIP, :] = values[f]
         buoyancy, lame, shear = (NEAR * value for value in values[5:])
@@ -443,11 +445,60 @@
     return add_up(image, IMAGE), image[3 * IMAGE :]
 
 
-def surface_kernel(tracks, columns, notes, beside, obs, cells, inject_out, residual_out, state, media, low, high):
+def response(state, media, sources, strains):
+    state[...] = jnp.zeros(state.shape, F32)
+    tiles = (0, 8)
+    sums = [[jnp.zeros((8, LANES), F32) for _ in tiles] for _ in range(2)]
+
+    def at(f, r, by=0):
+        return state[f, PAD + r + by : PAD + r + by + 8, :]
+
+    def put(f, r, value):
+        state[f, PAD + r : PAD + r + 8, :] = value
+
+    for moment in reversed(range(MOMENTS)):
+        put(2, 0, at(2, 0) + sources[moment])
+        for r in tiles:
+            xx, xz, zz = at(2, r), at(4, r), at(3, r)
+            b = media[0, r : r + 8, :]
+            near = (xx - turn(xx, 1)) + (xz - at(4, r, -1))
+            far = (turn(xx, -1) - turn(xx, 2)) + (at(4, r, 1) - at(4, r, -2))
+            put(0, r, at(0, r) + b * (near + RATIO * far))
+            near = (turn(xz, -1) - xz) + (at(3, r, 1) - zz)
+            far = (turn(xz, -2) - turn(xz, 1)) + (at(3, r, 2) - at(3, r, -1))
+            put(1, r, at(1, r) + b * (near + RATIO * far))
+        for i, r in enumerate(tiles):
+            vx, vz = at(0, r), at(1, r)
+            exx = (turn(vx, -1) - vx) + RATIO * (turn(vx, -2) - turn(vx, 1))
+            ezz = (vz - at(1, r, -1)) + RATIO * (at(1, r, 1) - at(1, r, -2))
+            near = (at(0, r, 1) - vx) + (vz - turn(vz, 1))
+            far = (at(0, r, 2) - at(0, r, -1)) + (turn(vz, -1) - turn(vz, 2))
+            shear = near + RATIO * far
+            fxx, fzz, fxz = (
+                strains[j // 8, STRIP * (j % 8) + r : STRIP * (j % 8) + r + 8, :]
+                for j in range(3 * moment, 3 * moment + 3)
+            )
+            sums[0][i] += (fxx + fzz) * (exx + ezz)
+            sums[1][i] += 2.0 * (fxx * exx + fzz * ezz) + fxz * shear
+            if moment > 0:
+                whole, lam, mu = (media[k, r : r + 8, :] for k in (1, 2, 3))
+                put(2, r, at(2, r) + (whole * exx + lam * ezz))
+                put(3, r, at(3, r) + (lam * exx + whole * ezz))
+                put(4, r, at(4, r) + mu * shear)
+    return sums[0] + sums[1]
+
+
+def finish_kernel(
+    tracks, columns, notes, beside, obs, cells, base, strains, end,
+    lambda_out, mu_out, residual_out, end_out, state, media, low, high, sems,
+):
+    copy = pltpu.make_async_copy(end, end_out, sems.at[0])
+    copy.start()
     depth = lax.axis_index("depth")
     low[...] = jnp.where(depth == 0, notes[...], beside[...])
     high[...] = jnp.where(depth == 0, beside[...], notes[...])
-    start = lax.axis_index("track") * columns - EDGE
+    track = lax.axis_index("track")
+    start = track * columns - EDGE
     along, row = cells[0], cells[1]
     channels = along.shape[1]
     wanted = jnp.concatenate([along, start + lax.broadcasted_iota(jnp.int32, (1, LANES), 1)], axis=1)
@@ -463,64 +514,64 @@
         depth == 0, jnp.concatenate(traces[:2], axis=0), jnp.concatenate(traces[2:], axis=0)
     )
     near = jnp.concatenate([rate[8 * t : 8 * t + 4, channels:] for t in range(MOMENTS)], axis=0)
-    sources = jnp.where(depth == 0, count * near - seen, 0.0)
-    turned = jnp.concatenate([sources, jnp.zeros((LANES - IMAGE, LANES), F32)], axis=0).T
-    inject_out[...] = turned[: inject_out.shape[0]]
-
-
-def run_adjoint(states, medias, saveds, sums, inject=None):
-    rows = sums[0].shape[1]
-    for total in sums:
-        total[...] = jnp.zeros(total.shape, F32)
+    found = jnp.where(depth == 0, count * near - seen, 0.0)
+    nothing = jnp.zeros((8 - FIBRE_ROWS, LANES), F32)
+    sources = [
+        jnp.concatenate([found[FIBRE_ROWS * t : FIBRE_ROWS * (t + 1)], nothing], axis=0) for t in range(MOMENTS)
+    ]
+    own = [
+        NEAR * strip_window(f, low, high, track - 1, columns - EDGE, tracks, columns) for f in (5, 6, 7)
+    ]
+    media[0, 0] = own[0]
+    media[1, 0] = own[1] + 2.0 * own[2]
+    media[2, 0] = own[1]
+    media[3, 0] = own[2]
+    added = response(state.at[:, 0], media.at[:, 0], sources, strains)
+    rows = base.shape[1]
+    added = jnp.concatenate(added + [jnp.zeros((LANES - 32, LANES), F32)], axis=0).T[EDGE : EDGE + rows]
+    lane = lane_ids(rows)
+    for k, out in enumerate((lambda_out, mu_out)):
+        more = jnp.where(lane < STRIP, turn(added, -STRIP * k), 0.0)
+        out[:, :LANES] = (NEAR * NEAR) * (base[k, :, :LANES] + more)
+        out[:, LANES:] = (NEAR * NEAR) * base[k, :, LANES:]
+    copy.wait()
+
+
+def adjoint_kernel(
+    held, got_even, got_odd, got_depth, corner, media, saved, inner_media, inner_saved,
+    base_out, strains_out, state, sums,
+):
+    states, totals = each(state, 3, 1), each(sums, 3, 1)
+    rows = held.shape[1]
+    load_state(states, FORWARD, (0, 1, 2), held, got_even, got_odd, got_depth, corner)
+    medias = each(media, 2, 1) + each(inner_media, 1, 1)
+    saveds = each(saved, 2, 2) + each(inner_saved, 1, 2)
+    sums[...] = jnp.zeros(sums.shape, F32)
     for step in range(MOMENTS):
         fast, slow = spans(step, rows)
         moment = MOMENTS - 1 - step
-        if inject is not None:
-            inject(moment)
         velocities(states, medias, fast)
 
         def gather(i, r, exx, ezz, shear):
             if 0 <= r < rows:
                 fxx, fzz, fxz = (saveds[i][moment, k, r : r + 8, :] for k in range(3))
-                sums[i][0, r : r + 8, :] += (fxx + fzz) * (exx + ezz)
-                sums[i][1, r : r + 8, :] += 2.0 * (fxx * exx + fzz * ezz) + fxz * shear
+                totals[i][0, r : r + 8, :] += (fxx + fzz) * (exx + ezz)
+                totals[i][1, r : r + 8, :] += 2.0 * (fxx * exx + fzz * ezz) + fxz * shear
 
         stresses(states, medias, slow, step < MOMENTS - 1, gather)
-
-
-def adjoint_rest_kernel(
-    held, got_even, got_odd, got_depth, corner, media, saved, inner_media, inner_saved, sums, state
-):
-    states = each(state, 2, 1)
-    load_state(states, FORWARD, (1, 2), held, got_even, got_odd, got_depth, corner)
-    medias = [media.at[:, 1], inner_media.at[:, 0]]
-    saveds = [saved.at[:, :, 1], inner_saved.at[:, :, 0]]
-    run_adjoint(states, medias, saveds, each(sums, 2, 1))
-
-
-def adjoint_top_kernel(
-    held, got_even, got_odd, media, saved, rest, inject, end, residual,
-    lambda_out, mu_out, end_out, residual_out, state, sums, sems,
-):
-    copies = fetch((end, residual), (end_out, residual_out), sems)
-    rows = held.shape[1]
-    extent = rows + 2 * EDGE
-    states = each(state, 1, 1)
-    load_state(states, FORWARD, (0,), held, got_even, got_odd)
-    lane = lane_ids(extent)
-    here = (lane >= EDGE) & (lane < EDGE + FIBRE_ROWS)
-
-    def add(moment):
-        added = jnp.where(here, turn(inject[...], EDGE - FIBRE_ROWS * moment), 0.0)
-        states[0][2, PAD : PAD + extent, :] += added
-
-    run_adjoint(states, [media.at[:, 0]], [saved.at[:, :, 0]], each(sums, 1, 1), add)
-    for k, out in enumerate((lambda_out, mu_out)):
-        first, last = joined(sums[k, 0], rest[k, 0], rest[k, 1])
-        out[:, :LANES] = (NEAR * NEAR) * first
-        out[:, LANES:] = (NEAR * NEAR) * last
-    for copy in copies:
-        copy.wait()
+    for k in range(2):
+        first, last = joined(*(total[k] for total in totals))
+        base_out[k, :, :LANES] = first
+        base_out[k, :, LANES:] = last
+    lane = lane_ids(rows)
+    for group in range(2):
+        packed = jnp.zeros((rows, LANES), F32)
+        for j in range(8 * group, min(8 * group + 8, 3 * MOMENTS)):
+            spot = STRIP * (j % 8)
+            here = (lane >= spot) & (lane < spot + STRIP)
+            packed = jnp.where(here, turn(saveds[0][j // 3, j % 3], spot - EDGE), packed)
+        turned = packed.T
+        strains_out[group] = turn(jnp.concatenate([turned, jnp.zeros_like(turned)], axis=1), EDGE)
 
 
 def per_device(
@@ -629,15 +680,18 @@
         name="forward_inner",
     )(held, got_even, got_odd, got_depth, got_corner, end)
 
-    rest = pl.pallas_call(
-        adjoint_rest_kernel,
-        out_shape=jax.ShapeDtypeStruct((2, 2, rows, LANES), F32),
+    base, strains = pl.pallas_call(
+        adjoint_kernel,
+        out_shape=(
+            jax.ShapeDtypeStruct((2, rows, depth_cells), F32),
+            jax.ShapeDtypeStruct((2, LANES, LANES), F32),
+        ),
         in_specs=[inside] * 9,
-        out_specs=inside,
-        scratch_shapes=[state_of(2)],
+        out_specs=(inside,) * 2,
+        scratch_shapes=[state_of(3), VMEM((2, 3, rows, LANES), F32)],
         compiler_params=params(),
         cost_estimate=cost(20),
-        name="adjoint_rest",
+        name="adjoint",
     )(held_adj, got_even, got_odd, got_depth, got_corner, media, saved, inner_media, inner_saved)
 
     mine = pl.pallas_call(
@@ -648,43 +702,30 @@
         compiler_params=params(),
         cost_estimate=cost(1),
         name="relay",
-    )(notes, rest)
+    )(notes, base)
     beside = lax.ppermute(mine, "depth", depth_swap)
 
-    inject, residual = pl.pallas_call(
-        lambda *refs: surface_kernel(tracks, rows, *refs),
+    gradient_lambda, gradient_mu, residual, velocity_end = pl.pallas_call(
+        lambda *refs: finish_kernel(tracks, rows, *refs),
         out_shape=(
-            jax.ShapeDtypeStruct((extent, LANES), F32),
+            block,
+            block,
             jax.ShapeDtypeStruct((moments // 2, channels), F32),
+            jax.ShapeDtypeStruct(velocity.shape, F32),
         ),
-        in_specs=[inside] * 4,
-        out_specs=(inside,) * 2,
+        in_specs=[inside] * 7,
+        out_specs=(inside, inside, inside, outside),
         scratch_shapes=[
             VMEM((5, BATCH, 2 * PAD + STRIP, LANES), F32),
             VMEM((4, BATCH, STRIP, LANES), F32),
             VMEM(note.shape, F32),
             VMEM(note.shape, F32),
+            pltpu.SemaphoreType.DMA((1,)),
         ],
         compiler_params=params(),
         cost_estimate=cost(2),
-        name="surface",
-    )(mine, beside, traces, cells)
-
-    gradient_lambda, gradient_mu, velocity_end, residual = pl.pallas_call(
-        adjoint_top_kernel,
-        out_shape=(
-            block,
-            block,
-            jax.ShapeDtypeStruct(velocity.shape, F32),
-            jax.ShapeDtypeStruct((moments // 2, channels), F32),
-        ),
-        in_specs=[inside] * 9,
-        out_specs=(inside, inside, outside, outside),
-        scratch_shapes=[state_of(1), VMEM((2, 1, rows, LANES), F32), pltpu.SemaphoreType.DMA((2,))],
-        compiler_params=params(),
-        cost_estimate=cost(2),
-        name="adjoint_top",
-    )(held_adj, got_even, got_odd, media, saved, rest, inject, end, residual)
+        name="finish",
+    )(mine, beside, traces, cells, base, strains, end)
     return gradient_lambda, gradient_mu, velocity_end, residual
 
 

time: 26.5 us -> 26.3 us (level)
  waiting for transfers between devices: 4.73 us -> 3.73 us
  Pallas kernels: 9.34 us -> 10.1 us
    all_to_all x1, waiting for transfers between devices: 3.34 us -> 2.34 us  [per_device(): lax.all_to_all(note, 'track', split_axis=0, concat_axis=0, tiled=True)]
    pallas_call x3 -> x2, Pallas kernels: 4.21 us -> 4.96 us  [the longest x1 2.57 us: per_device(): pl.pallas_call(lambda *refs: finish_kernel(tracks, rows, *refs), out_shap...]
  transfers between devices with their start and end apart: 6 -> 6, of which waited for: 2 -> 2; matrix products, arithmetic and copies ran while one was open for 0% -> 0% of each run, Pallas kernels for 18% -> 22%
where the time goes in v15:
time: 26.3 us; the launch traced here: 26 us
  starting transfers between devices  11.5 us (44%)
  Pallas kernels  10.1 us (38%)
  waiting for transfers between devices  3.73 us (14%)
  between operations  0.72 us (3%)
    all_to_all x1, starting transfers between devices, per_device(): lax.all_to_all(note, 'track', split_axis=0, concat_axis=0, tiled=True)  7.58 us
    pallas_call x1, Pallas kernels, per_device(): pl.pallas_call(lambda *refs: finish_kernel(tracks, rows, *refs), out_shap...  2.57 us
    ppermute x1, starting transfers between devices, per_device(): got_even = lax.ppermute(to_even, 'track', swap(0))  2.56 us
    pallas_call x1, Pallas kernels, per_device(): pl.pallas_call(adjoint_kernel, out_shape=(jax.ShapeDtypeStruct((2, rows,...  2.39 us
    all_to_all x1, waiting for transfers between devices, per_device(): lax.all_to_all(note, 'track', split_axis=0, concat_axis=0, tiled=True)  2.34 us
    pallas_call x1, Pallas kernels, per_device(): pl.pallas_call(pack_kernel, out_shape=(jax.ShapeDtypeStruct((FORWARD, row...  1.73 us
    pallas_call x1, Pallas kernels, per_device(): pl.pallas_call(forward_kernel, out_shape=(media_of(2), saved_of(2), jax.S...  1.54 us
    ppermute x1, waiting for transfers between devices, per_device(): beside = lax.ppermute(mine, 'depth', depth_swap)  1.38 us
  transfers between devices with their start and end apart: 6, of which 2 were waited for; matrix products, arithmetic and copies ran while one was open for 0% of the time, Pallas kernels for 22%

profile of v15, /device:TPU:0, one launch (start us, length us, event | category | flops | bytes accessed | tf_op | source)
XLA Modules:
  0.0 26.0 jit_solution(12990774958891268777)
XLA Ops:
  0.6 1.7 %pack.1 = (f32[8,64,256]{2,1,0:T(8,128)S(1)}, f32[5,64,256]{2,1,0:T(8,128)S(1)}, f32[80,256]{1,0:T(8,128)S(1)}, f32[168,256]{1,0:T(8,128)S(1)}, f32[168,256]{1,0...) custom-call(f32[2,64,256]{2,1,0:T(8,128)} %refs_0_.1, ...), custom_call_target="tpu_custom_call" | custom-call | flops 5000000000 | bytes 1048576 | tf_op jit(solution)/shard_map/pack/pallas_call | solution.py:605
  2.4 0.5 %collective-permute-start = (f32[80,256]{1,0:T(8,128)S(1)}, f32[80,256]{1,0:T(8,128)S(1)}, u32[]{:S(2)}, u32[]{:S(2)}) collective-permute-start(f32[80,256]{1,0:T(8,128)S(1)} %get-tuple-element.25), channel_id=1, source_target_pairs={{0,1},{1,0},{2,3},{3,2},{4,5},{5,4},{6,7},{7,6},{8,9},{9,8},{10,11... | collective-permute-start | bytes 245768 | tf_op jit(solution)/shard_map/ppermute | solution.py:625
  2.9 2.6 %collective-permute-start.1 = (f32[168,256]{1,0:T(8,128)S(1)}, f32[168,256]{1,0:T(8,128)S(1)}, u32[]{:S(2)}, u32[]{:S(2)}) collective-permute-start(f32[168,256]{1,0:T(8,128)S(1)} %get-tuple-element.29), channel_id=1, source_target_pairs={{0,2},{2,0},{4,6},{6,4},{8,10},{10,8},{12,14},{14,12},{1,3},{3,1},... | collective-permute-start | bytes 516104 | tf_op jit(solution)/shard_map/ppermute | solution.py:628
  5.5 0.7 %collective-permute-start.2 = (f32[168,256]{1,0:T(8,128)S(1)}, f32[168,256]{1,0:T(8,128)S(1)}, u32[]{:S(2)}, u32[]{:S(2)}) collective-permute-start(f32[168,256]{1,0:T(8,128)S(1)} %get-tuple-element.30), channel_id=1, source_target_pairs={{2,4},{4,2},{6,8},{8,6},{10,12},{12,10},{3,5},{5,3},{7,9},{9,7},{1... | collective-permute-start | bytes 516104 | tf_op jit(solution)/shard_map/ppermute | solution.py:627
  6.1 0.0 collective-permute-done.got_depth
  6.1 0.7 %note.1 = f32[8,40,128]{2,1,0:T(8,128)} custom-call(f32[32,128]{1,0:T(8,128)S(1)} %get-tuple-element.24.strip, f32[80,256]{1,0:T(8,128)S(1)} %collective-permute-done.got_depth, f32[4,256]{1,0:T(4,128)S(1)} %get-tuple-element.26.traces.refs_2_, s32[2,1,256]{2,1,0:T(1,128)S(1)} %get-tuple-element.27.cells.refs_3_), custom_call_target="tpu_custom_call" | custom-call | flops 1000000000 | bytes 1048576 | tf_op jit(solution)/shard_map/note/pallas_call | solution.py:633
  6.8 7.6 %all-to-all-start = ((f32[8,40,128]{2,1,0:T(8,128)}), f32[8,40,128]{2,1,0:T(8,128)S(1)}, u32[]{:S(2)}, u32[]{:S(2)}) async-start(f32[8,40,128]{2,1,0:T(8,128)} %note.1), calls=%async_computation | async-start | bytes 327680 | tf_op jit(solution)/shard_map/all_to_all | solution.py:642
  14.4 0.0 collective-permute-done.1.got_even
  14.4 0.0 collective-permute-done.2.got_odd
  14.4 0.1 corners.1
  14.6 0.1 collective-permute-start.3
  14.6 1.5 %forward.1 = (f32[4,2,96,128]{3,2,1,0:T(8,128)S(1)}, f32[4,3,2,64,128]{4,3,2,1,0:T(8,128)S(1)}, f32[2,2,64,128]{3,2,1,0:T(8,128)S(1)}) custom-call(f32[8,64,256]{2,1,0:T(8,128)S(1)} %get-tuple-element.31.held, f32[168,256]{1,0:T(8,128)S(1)} %collective-permute-done.1.got_even, f32[168,256]{1,0:T(8,128)S(1)} %collective-permute-done.2.got_odd), custom_call_target="tpu_custom_call" | custom-call | flops 20000000000 | bytes 1048576 | tf_op jit(solution)/shard_map/forward/pallas_call | solution.py:661
  16.2 0.0 collective-permute-done.3.corner
  16.2 1.0 %forward_inner.1 = (f32[4,1,96,128]{3,2,1,0:T(8,128)S(1)}, f32[4,3,1,64,128]{4,3,2,1,0:T(8,128)S(1)}, f32[2,64,256]{2,1,0:T(8,128)S(1)}) custom-call(f32[8,64,256]{2,1,0:T(8,128)S(1)} %get-tuple-element.31.held, f32[168,256]{1,0:T(8,128)S(1)} %collective-permute-done.1.got_even, f32[168,256]{1,0:T(8,128)S(1)} %collective-permute-done.2.got_odd, ...), custom_call_target="tpu_custom_call" | custom-call | flops 20000000000 | bytes 1048576 | tf_op jit(solution)/shard_map/forward_inner/pallas_call | solution.py:672
  17.2 2.4 %adjoint.1 = (f32[2,64,256]{2,1,0:T(8,128)S(1)}, f32[2,128,128]{2,1,0:T(8,128)S(1)}) custom-call(f32[5,64,256]{2,1,0:T(8,128)S(1)} %get-tuple-element.28.held, f32[168,256]{1,0:T(8,128)S(1)} %collective-permute-done.1.got_even, f32[168,256]{1,0:T(8,128)S(1)} %collective-permute-done.2.got_odd, f32[80,256]{1,0:T(8,128)S(1)} %collective-permute-done.got_depth, ...), custom_call_target="tpu_custom_call" | custom-call | flops 20000000000 | bytes 1048576 | tf_op jit(solution)/shard_map/adjoint/pallas_call | solution.py:683
  19.6 2.3 %all-to-all-done.notes = f32[8,40,128]{2,1,0:T(8,128)S(1)} async-done(((f32[8,40,128]{2,1,0:T(8,128)}), f32[8,40,128]{2,1,0:T(8,128)S(1)}, u32[]{:S(2)}, u32[]{:S(2)}) %all-to-all-start) | async-done | bytes 163872 | tf_op jit(solution)/shard_map/all_to_all | solution.py:642
  22.0 0.1 collective-permute-start.4
  22.1 1.4 %collective-permute-done.4.refs_1_ = f32[8,40,128]{2,1,0:T(8,128)S(1)} collective-permute-done((f32[8,40,128]{2,1,0:T(8,128)S(1)}, f32[8,40,128]{2,1,0:T(8,128)S(1)}, u32[]{:S(2)}, u32[]{:S(2)}) %collective-permute-start.4) | collective-permute-done | bytes 163872 | tf_op jit(solution)/shard_map/ppermute | solution.py:706
  23.4 2.6 %finish.1 = (f32[64,256]{1,0:T(8,128)}, f32[64,256]{1,0:T(8,128)}, f32[2,256]{1,0:T(2,128)}, f32[2,64,256]{2,1,0:T(8,128)}) custom-call(f32[8,40,128]{2,1,0:T(8,128)S(1)} %relay.1.refs_0_, f32[8,40,128]{2,1,0:T(8,128)S(1)} %collective-permute-done.4.refs_1_, f32[4,256]{1,0:T(4,128)S(1)} %get-tuple-element.26.traces.refs_2_, ...), custom_call_target="tpu_custom_call" | custom-call | flops 2000000000 | bytes 1048576 | tf_op jit(solution)/shard_map/finish/pallas_call | solution.py:708
  (1 shorter events, 0.0 us)
Async XLA Ops:
  2.4 3.8 %collective-permute-start = (f32[80,256]{1,0:T(8,128)S(1)}, f32[80,256]{1,0:T(8,128)S(1)}, u32[]{:S(2)}, u32[]{:S(2)}) collective-permute-start(f32[80,256]{1,0:T(8,128)S(1)} %get-tuple-element.25), channel_id=1, source_target_pairs={{0,1},{1,0},{2,3},{3,2},{4,5},{5,4},{6,7},{7,6},{8,9},{9,8},{10,11... | collective-permute-start | bytes 245768 | tf_op jit(solution)/shard_map/ppermute | solution.py:625
  2.9 11.5 %collective-permute-start.1 = (f32[168,256]{1,0:T(8,128)S(1)}, f32[168,256]{1,0:T(8,128)S(1)}, u32[]{:S(2)}, u32[]{:S(2)}) collective-permute-start(f32[168,256]{1,0:T(8,128)S(1)} %get-tuple-element.29), channel_id=1, source_target_pairs={{0,2},{2,0},{4,6},{6,4},{8,10},{10,8},{12,14},{14,12},{1,3},{3,1},... | collective-permute-start | bytes 516104 | tf_op jit(solution)/shard_map/ppermute | solution.py:628
  5.5 8.9 %collective-permute-start.2 = (f32[168,256]{1,0:T(8,128)S(1)}, f32[168,256]{1,0:T(8,128)S(1)}, u32[]{:S(2)}, u32[]{:S(2)}) collective-permute-start(f32[168,256]{1,0:T(8,128)S(1)} %get-tuple-element.30), channel_id=1, source_target_pairs={{2,4},{4,2},{6,8},{8,6},{10,12},{12,10},{3,5},{5,3},{7,9},{9,7},{1... | collective-permute-start | bytes 516104 | tf_op jit(solution)/shard_map/ppermute | solution.py:627
  6.8 15.1 %all-to-all-start = ((f32[8,40,128]{2,1,0:T(8,128)}), f32[8,40,128]{2,1,0:T(8,128)S(1)}, u32[]{:S(2)}, u32[]{:S(2)}) async-start(f32[8,40,128]{2,1,0:T(8,128)} %note.1), calls=%async_computation | async-start | bytes 327680 | tf_op jit(solution)/shard_map/all_to_all | solution.py:642
  14.6 1.6 %collective-permute-start.3 = (f32[32,256]{1,0:T(8,128)S(1)}, f32[32,256]{1,0:T(8,128)S(1)}, u32[]{:S(2)}, u32[]{:S(2)}) collective-permute-start(f32[32,256]{1,0:T(8,128)S(1)} %corners.1), channel_id=1, source_target_pairs={{0,1},{1,0},{2,3},{3,2},{4,5},{5,4},{6,7},{7,6},{8,9},{9,8},{10,11... | collective-permute-start | bytes 98312 | tf_op jit(solution)/shard_map/ppermute | solution.py:653
  22.0 1.5 %collective-permute-start.4 = (f32[8,40,128]{2,1,0:T(8,128)S(1)}, f32[8,40,128]{2,1,0:T(8,128)S(1)}, u32[]{:S(2)}, u32[]{:S(2)}) collective-permute-start(f32[8,40,128]{2,1,0:T(8,128)S(1)} %relay.1.refs_0_), channel_id=1, source_target_pairs={{0,1},{1,0},{2,3},{3,2},{4,5},{5,4},{6,7},{7,6},{8,9},{9,8},{10,11... | collective-permute-start | bytes 491528 | tf_op jit(solution)/shard_map/ppermute | solution.py:706

commit v16 on v15

--- a/solution.py
+++ b/solution.py
@@ -44,8 +44,8 @@
     return pltpu.roll(value, by % LANES, 1)
 
 
-def is_even():
-    return lax.rem(lax.axis_index("track"), 2) == 0
+def is_lower():
+    return lax.rem(lax.axis_index("track"), 2) == 1
 
 
 def fetch(sources, targets, sems):
@@ -74,7 +74,7 @@
     copies = fetch((*sources[:2], *sources[4:], *sources[2:4], *channel_arrays), targets, sems)
     arriving = {0: copies[0], 2: copies[1], 5: copies[2], 6: copies[3], 7: copies[4], 8: copies[5], 10: copies[6]}
     depth = lax.axis_index("depth")
-    even = is_even()
+    lower = is_lower()
     rows = held.shape[1]
     lane = lane_ids(rows)
     tail = BASE + HALO * FIELDS
@@ -98,8 +98,8 @@
             strip = jnp.where(here, turn(first, spot), strip)
         low, high = ref[:HALO, :], ref[rows - HALO :, :]
         at = BASE + HALO * f
-        edge_outs[0][at : at + HALO, :] = jnp.where(even, high, low)
-        edge_outs[1][at : at + HALO, :] = jnp.where(even, low, high)
+        edge_outs[0][at : at + HALO, :] = jnp.where(lower, high, low)
+        edge_outs[1][at : at + HALO, :] = jnp.where(lower, low, high)
     depth_out[:rows, :LANES] = packed[0]
     depth_out[:rows, LANES:] = packed[1]
     turned = strip.T
@@ -115,14 +115,14 @@
     cells_out[1] = numbers[1] & 3
 
 
-def edge_rows(f, side, got_even, got_odd):
+def edge_rows(f, side, got_first, got_second):
     at = BASE + HALO * f
     span = slice(at - BASE, at + HALO) if side == 0 else slice(at, at + EDGE)
-    use_odd = is_even() if side == 0 else ~is_even()
-    return jnp.where(use_odd, got_odd[span, :], got_even[span, :])
-
-
-def corner_kernel(got_even, got_odd, corner_out):
+    use_second = is_lower() if side == 0 else ~is_lower()
+    return jnp.where(use_second, got_second[span, :], got_first[span, :])
+
+
+def corner_kernel(got_first, got_second, corner_out):
     depth = lax.axis_index("depth")
     lane = lane_ids(EDGE)
     for side in range(2):
@@ -130,7 +130,7 @@
         for f in range(FIELDS):
             group, place = divmod(f, FORWARD)
             spot = EDGE * place
-            value = edge_rows(f, side, got_even, got_odd)
+            value = edge_rows(f, side, got_first, got_second)
             edge = jnp.where(depth == 0, value[:, LANES:], value[:, :LANES])
             shift = lax.rem(spot + EDGE * (1 - depth), LANES)
             here = (lane >= spot) & (lane < spot + EDGE)
@@ -156,13 +156,13 @@
     return jnp.where(low < LANES - EDGE, own, pltpu.roll(halo, beside, 1))
 
 
-def field_windows(f, planes, held, got_even, got_odd, got_depth=None, corner=None):
+def field_windows(f, planes, held, got_first, got_second, got_depth=None, corner=None):
     rows = held.shape[1]
     col = LANES * (f // FORWARD)
     blocks = (
-        (0, edge_rows(f, 0, got_even, got_odd), corner, 0),
+        (0, edge_rows(f, 0, got_first, got_second), corner, 0),
         (EDGE, held[f % FORWARD], got_depth, 0),
-        (EDGE + rows, edge_rows(f, 1, got_even, got_odd), corner, EDGE),
+        (EDGE + rows, edge_rows(f, 1, got_first, got_second), corner, EDGE),
     )
     found = [[] for _ in planes]
     for at, value, halo, start in blocks:
@@ -267,19 +267,19 @@
     return [ref.at[(slice(None),) * axis + (i,)] for i in range(count)]
 
 
-def forward_kernel(held, got_even, got_odd, media, saved, end_out, state):
+def forward_kernel(held, got_first, got_second, media, saved, end_out, state):
     states = each(state, 2, 1)
-    run_forward(states, each(media, 2, 1), each(saved, 2, 2), (0, 1), held, got_even, got_odd)
+    run_forward(states, each(media, 2, 1), each(saved, 2, 2), (0, 1), held, got_first, got_second)
     top, rows = PAD + EDGE, held.shape[1]
     for f in range(2):
         for i in range(2):
             end_out[f, i] = states[i][f, top : top + rows, :]
 
 
-def forward_inner_kernel(held, got_even, got_odd, got_depth, corner, end, media, saved, end_out, state):
+def forward_inner_kernel(held, got_first, got_second, got_depth, corner, end, media, saved, end_out, state):
     states = each(state, 1, 1)
     run_forward(
-        states, each(media, 1, 1), each(saved, 1, 2), (2,), held, got_even, got_odd, got_depth, corner
+        states, each(media, 1, 1), each(saved, 1, 2), (2,), held, got_first, got_second, got_depth, corner
     )
     top, rows = PAD + EDGE, held.shape[1]
     for f in range(2):
@@ -538,12 +538,12 @@
 
 
 def adjoint_kernel(
-    held, got_even, got_odd, got_depth, corner, media, saved, inner_media, inner_saved,
+    held, got_first, got_second, got_depth, corner, media, saved, inner_media, inner_saved,
     base_out, strains_out, state, sums,
 ):
     states, totals = each(state, 3, 1), each(sums, 3, 1)
     rows = held.shape[1]
-    load_state(states, FORWARD, (0, 1, 2), held, got_even, got_odd, got_depth, corner)
+    load_state(states, FORWARD, (0, 1, 2), held, got_first, got_second, got_depth, corner)
     medias = each(media, 2, 1) + each(inner_media, 1, 1)
     saveds = each(saved, 2, 2) + each(inner_saved, 1, 2)
     sums[...] = jnp.zeros(sums.shape, F32)
@@ -602,7 +602,7 @@
     inside = pl.BlockSpec(memory_space=VMEM)
     outside = pl.BlockSpec(memory_space=pltpu.HBM)
     anywhere = pl.BlockSpec(memory_space=pl.ANY)
-    held, held_adj, to_depth, to_even, to_odd, strip, traces, cells = pl.pallas_call(
+    held, held_adj, to_depth, to_first, to_second, strip, traces, cells = pl.pallas_call(
         pack_kernel,
         out_shape=(
             jax.ShapeDtypeStruct((FORWARD, rows, depth_cells), F32),
@@ -624,8 +624,8 @@
     depth_swap = [(0, 1), (1, 0)]
     got_depth = lax.ppermute(to_depth, "depth", depth_swap)
     swap = lambda k: [pair for i in range(k, tracks - 1, 2) for pair in ((i, i + 1), (i + 1, i))]
-    got_odd = lax.ppermute(to_odd, "track", swap(1))
-    got_even = lax.ppermute(to_even, "track", swap(0))
+    got_first = lax.ppermute(to_first, "track", swap(1))
+    got_second = lax.ppermute(to_second, "track", swap(0))
 
     def state_of(planes):
         return VMEM((5, planes, extent + 2 * PAD, LANES), F32)
@@ -649,7 +649,7 @@
         compiler_params=params(),
         cost_estimate=cost(1),
         name="corners",
-    )(got_even, got_odd)
+    )(got_first, got_second)
     got_corner = lax.ppermute(corner, "depth", depth_swap)
 
     def media_of(planes):
@@ -667,7 +667,7 @@
         compiler_params=params(),
         cost_estimate=cost(20),
         name="forward",
-    )(held, got_even, got_odd)
+    )(held, got_first, got_second)
 
     inner_media, inner_saved, end = pl.pallas_call(
         forward_inner_kernel,
@@ -678,7 +678,7 @@
         compiler_params=params(),
         cost_estimate=cost(20),
         name="forward_inner",
-    )(held, got_even, got_odd, got_depth, got_corner, end)
+    )(held, got_first, got_second, got_depth, got_corner, end)
 
     base, strains = pl.pallas_call(
         adjoint_kernel,
@@ -692,7 +692,7 @@
         compiler_params=params(),
         cost_estimate=cost(20),
         name="adjoint",
-    )(held_adj, got_even, got_odd, got_depth, got_corner, media, saved, inner_media, inner_saved)
+    )(held_adj, got_first, got_second, got_depth, got_corner, media, saved, inner_media, inner_saved)
 
     mine = pl.pallas_call(
         relay_kernel,

time: 26.3 us -> 27.2 us (1.034)
  the two profiles are of different devices: /device:TPU:0 before, /device:TPU:23 now
where the time goes in v16:
time: 27.2 us; the launch traced here: 27 us
  starting transfers between devices  10.3 us (38%)
  Pallas kernels  10.1 us (37%)
  waiting for transfers between devices  5.94 us (22%)
  between operations  0.7 us (3%)
    all_to_all x1, starting transfers between devices, per_device(): lax.all_to_all(note, 'track', split_axis=0, concat_axis=0, tiled=True)  5.55 us
    ppermute x1, waiting for transfers between devices, per_device(): got_second = lax.ppermute(to_second, 'track', swap(0))  4.55 us
    ppermute x1, starting transfers between devices, per_device(): got_first = lax.ppermute(to_first, 'track', swap(1))  3.16 us
    pallas_call x1, Pallas kernels, per_device(): pl.pallas_call(lambda *refs: finish_kernel(tracks, rows, *refs), out_shap...  2.57 us
    pallas_call x1, Pallas kernels, per_device(): pl.pallas_call(adjoint_kernel, out_shape=(jax.ShapeDtypeStruct((2, rows,...  2.39 us
    pallas_call x1, Pallas kernels, per_device(): pl.pallas_call(pack_kernel, out_shape=(jax.ShapeDtypeStruct((FORWARD, row...  1.73 us
    pallas_call x1, Pallas kernels, per_device(): pl.pallas_call(forward_kernel, out_shape=(media_of(2), saved_of(2), jax.S...  1.54 us
    ppermute x1, waiting for transfers between devices, per_device(): beside = lax.ppermute(mine, 'depth', depth_swap)  1.38 us
  transfers between devices with their start and end apart: 6, of which 2 were waited for; matrix products, arithmetic and copies ran while one was open for 0% of the time, Pallas kernels for 21%

profile of v16, /device:TPU:23, one launch (start us, length us, event | category | flops | bytes accessed | tf_op | source)
XLA Modules:
  0.0 27.0 jit_solution(3266419958668201968)
XLA Ops:
  0.6 1.7 %pack.1 = (f32[8,64,256]{2,1,0:T(8,128)S(1)}, f32[5,64,256]{2,1,0:T(8,128)S(1)}, f32[80,256]{1,0:T(8,128)S(1)}, f32[168,256]{1,0:T(8,128)S(1)}, f32[168,256]{1,0...) custom-call(f32[2,64,256]{2,1,0:T(8,128)} %refs_0_.1, ...), custom_call_target="tpu_custom_call" | custom-call | flops 5000000000 | bytes 1048576 | tf_op jit(solution)/shard_map/pack/pallas_call | solution.py:605
  2.4 0.7 %collective-permute-start = (f32[80,256]{1,0:T(8,128)S(1)}, f32[80,256]{1,0:T(8,128)S(1)}, u32[]{:S(2)}, u32[]{:S(2)}) collective-permute-start(f32[80,256]{1,0:T(8,128)S(1)} %get-tuple-element.25), channel_id=1, source_target_pairs={{0,1},{1,0},{2,3},{3,2},{4,5},{5,4},{6,7},{7,6},{8,9},{9,8},{10,11... | collective-permute-start | bytes 245768 | tf_op jit(solution)/shard_map/ppermute | solution.py:625
  3.1 3.2 %collective-permute-start.1 = (f32[168,256]{1,0:T(8,128)S(1)}, f32[168,256]{1,0:T(8,128)S(1)}, u32[]{:S(2)}, u32[]{:S(2)}) collective-permute-start(f32[168,256]{1,0:T(8,128)S(1)} %get-tuple-element.29), channel_id=1, source_target_pairs={{2,4},{4,2},{6,8},{8,6},{10,12},{12,10},{3,5},{5,3},{7,9},{9,7},{1... | collective-permute-start | bytes 516104 | tf_op jit(solution)/shard_map/ppermute | solution.py:627
  6.3 0.1 collective-permute-start.2
  6.4 0.0 collective-permute-done.got_depth
  6.4 0.7 %note.1 = f32[8,40,128]{2,1,0:T(8,128)} custom-call(f32[32,128]{1,0:T(8,128)S(1)} %get-tuple-element.24.strip, f32[80,256]{1,0:T(8,128)S(1)} %collective-permute-done.got_depth, f32[4,256]{1,0:T(4,128)S(1)} %get-tuple-element.26.traces.refs_2_, s32[2,1,256]{2,1,0:T(1,128)S(1)} %get-tuple-element.27.cells.refs_3_), custom_call_target="tpu_custom_call" | custom-call | flops 1000000000 | bytes 1048576 | tf_op jit(solution)/shard_map/note/pallas_call | solution.py:633
  7.1 5.5 %all-to-all-start = ((f32[8,40,128]{2,1,0:T(8,128)}), f32[8,40,128]{2,1,0:T(8,128)S(1)}, u32[]{:S(2)}, u32[]{:S(2)}) async-start(f32[8,40,128]{2,1,0:T(8,128)} %note.1), calls=%async_computation | async-start | bytes 327680 | tf_op jit(solution)/shard_map/all_to_all | solution.py:642
  12.7 0.0 collective-permute-done.1.got_first
  12.7 4.5 %collective-permute-done.2.got_second = f32[168,256]{1,0:T(8,128)S(1)} collective-permute-done((f32[168,256]{1,0:T(8,128)S(1)}, f32[168,256]{1,0:T(8,128)S(1)}, u32[]{:S(2)}, u32[]{:S(2)}) %collective-permute-start.2) | collective-permute-done | bytes 172064 | tf_op jit(solution)/shard_map/ppermute | solution.py:628
  17.2 0.1 corners.1
  17.4 0.6 %collective-permute-start.3 = (f32[32,256]{1,0:T(8,128)S(1)}, f32[32,256]{1,0:T(8,128)S(1)}, u32[]{:S(2)}, u32[]{:S(2)}) collective-permute-start(f32[32,256]{1,0:T(8,128)S(1)} %corners.1), channel_id=1, source_target_pairs={{0,1},{1,0},{2,3},{3,2},{4,5},{5,4},{6,7},{7,6},{8,9},{9,8},{10,11... | collective-permute-start | bytes 98312 | tf_op jit(solution)/shard_map/ppermute | solution.py:653
  18.0 1.5 %forward.1 = (f32[4,2,96,128]{3,2,1,0:T(8,128)S(1)}, f32[4,3,2,64,128]{4,3,2,1,0:T(8,128)S(1)}, f32[2,2,64,128]{3,2,1,0:T(8,128)S(1)}) custom-call(f32[8,64,256]{2,1,0:T(8,128)S(1)} %get-tuple-element.31.held, f32[168,256]{1,0:T(8,128)S(1)} %collective-permute-done.1.got_first, f32[168,256]{1,0:T(8,128)S(1)} %collective-permute-done.2.got_second), custom_call_target="tpu_custom_call" | custom-call | flops 20000000000 | bytes 1048576 | tf_op jit(solution)/shard_map/forward/pallas_call | solution.py:661
  19.5 0.0 collective-permute-done.3.corner
  19.5 1.0 %forward_inner.1 = (f32[4,1,96,128]{3,2,1,0:T(8,128)S(1)}, f32[4,3,1,64,128]{4,3,2,1,0:T(8,128)S(1)}, f32[2,64,256]{2,1,0:T(8,128)S(1)}) custom-call(f32[8,64,256]{2,1,0:T(8,128)S(1)} %get-tuple-element.31.held, f32[168,256]{1,0:T(8,128)S(1)} %collective-permute-done.1.got_first, f32[168,256]{1,0:T(8,128)S(1)} %collective-permute-done.2.got_second, ...), custom_call_target="tpu_custom_call" | custom-call | flops 20000000000 | bytes 1048576 | tf_op jit(solution)/shard_map/forward_inner/pallas_call | solution.py:672
  20.6 2.4 %adjoint.1 = (f32[2,64,256]{2,1,0:T(8,128)S(1)}, f32[2,128,128]{2,1,0:T(8,128)S(1)}) custom-call(f32[5,64,256]{2,1,0:T(8,128)S(1)} %get-tuple-element.28.held, f32[168,256]{1,0:T(8,128)S(1)} %collective-permute-done.1.got_first, f32[168,256]{1,0:T(8,128)S(1)} %collective-permute-done.2.got_second, f32[80,256]{1,0:T(8,128)S(1)} %collective-permute-done.got_depth, ...), custom_call_target="tpu_custom_call" | custom-call | flops 20000000000 | bytes 1048576 | tf_op jit(solution)/shard_map/adjoint/pallas_call | solution.py:683
  22.9 0.0 all-to-all-done.notes
  23.0 0.1 collective-permute-start.4
  23.1 1.4 %collective-permute-done.4.refs_1_ = f32[8,40,128]{2,1,0:T(8,128)S(1)} collective-permute-done((f32[8,40,128]{2,1,0:T(8,128)S(1)}, f32[8,40,128]{2,1,0:T(8,128)S(1)}, u32[]{:S(2)}, u32[]{:S(2)}) %collective-permute-start.4) | collective-permute-done | bytes 163872 | tf_op jit(solution)/shard_map/ppermute | solution.py:706
  24.4 2.6 %finish.1 = (f32[64,256]{1,0:T(8,128)}, f32[64,256]{1,0:T(8,128)}, f32[2,256]{1,0:T(2,128)}, f32[2,64,256]{2,1,0:T(8,128)}) custom-call(f32[8,40,128]{2,1,0:T(8,128)S(1)} %relay.1.refs_0_, f32[8,40,128]{2,1,0:T(8,128)S(1)} %collective-permute-done.4.refs_1_, f32[4,256]{1,0:T(4,128)S(1)} %get-tuple-element.26.traces.refs_2_, ...), custom_call_target="tpu_custom_call" | custom-call | flops 2000000000 | bytes 1048576 | tf_op jit(solution)/shard_map/finish/pallas_call | solution.py:708
  (1 shorter events, 0.0 us)
Async XLA Ops:
  2.4 4.1 %collective-permute-start = (f32[80,256]{1,0:T(8,128)S(1)}, f32[80,256]{1,0:T(8,128)S(1)}, u32[]{:S(2)}, u32[]{:S(2)}) collective-permute-start(f32[80,256]{1,0:T(8,128)S(1)} %get-tuple-element.25), channel_id=1, source_target_pairs={{0,1},{1,0},{2,3},{3,2},{4,5},{5,4},{6,7},{7,6},{8,9},{9,8},{10,11... | collective-permute-start | bytes 245768 | tf_op jit(solution)/shard_map/ppermute | solution.py:625
  3.1 9.6 %collective-permute-start.1 = (f32[168,256]{1,0:T(8,128)S(1)}, f32[168,256]{1,0:T(8,128)S(1)}, u32[]{:S(2)}, u32[]{:S(2)}) collective-permute-start(f32[168,256]{1,0:T(8,128)S(1)} %get-tuple-element.29), channel_id=1, source_target_pairs={{2,4},{4,2},{6,8},{8,6},{10,12},{12,10},{3,5},{5,3},{7,9},{9,7},{1... | collective-permute-start | bytes 516104 | tf_op jit(solution)/shard_map/ppermute | solution.py:627
  6.3 10.9 %collective-permute-start.2 = (f32[168,256]{1,0:T(8,128)S(1)}, f32[168,256]{1,0:T(8,128)S(1)}, u32[]{:S(2)}, u32[]{:S(2)}) collective-permute-start(f32[168,256]{1,0:T(8,128)S(1)} %get-tuple-element.30), channel_id=1, source_target_pairs={{0,2},{2,0},{4,6},{6,4},{8,10},{10,8},{12,14},{14,12},{1,3},{3,1},... | collective-permute-start | bytes 516104 | tf_op jit(solution)/shard_map/ppermute | solution.py:628
  7.1 15.8 %all-to-all-start = ((f32[8,40,128]{2,1,0:T(8,128)}), f32[8,40,128]{2,1,0:T(8,128)S(1)}, u32[]{:S(2)}, u32[]{:S(2)}) async-start(f32[8,40,128]{2,1,0:T(8,128)} %note.1), calls=%async_computation | async-start | bytes 327680 | tf_op jit(solution)/shard_map/all_to_all | solution.py:642
  17.4 2.1 %collective-permute-start.3 = (f32[32,256]{1,0:T(8,128)S(1)}, f32[32,256]{1,0:T(8,128)S(1)}, u32[]{:S(2)}, u32[]{:S(2)}) collective-permute-start(f32[32,256]{1,0:T(8,128)S(1)} %corners.1), channel_id=1, source_target_pairs={{0,1},{1,0},{2,3},{3,2},{4,5},{5,4},{6,7},{7,6},{8,9},{9,8},{10,11... | collective-permute-start | bytes 98312 | tf_op jit(solution)/shard_map/ppermute | solution.py:653
  23.0 1.5 %collective-permute-start.4 = (f32[8,40,128]{2,1,0:T(8,128)S(1)}, f32[8,40,128]{2,1,0:T(8,128)S(1)}, u32[]{:S(2)}, u32[]{:S(2)}) collective-permute-start(f32[8,40,128]{2,1,0:T(8,128)S(1)} %relay.1.refs_0_), channel_id=1, source_target_pairs={{0,1},{1,0},{2,3},{3,2},{4,5},{5,4},{6,7},{7,6},{8,9},{9,8},{10,11... | collective-permute-start | bytes 491528 | tf_op jit(solution)/shard_map/ppermute | solution.py:706

commit v17 on v15

--- a/solution.py
+++ b/solution.py
@@ -16,6 +16,7 @@
 ADJOINT = 5
 FIELDS = FORWARD + ADJOINT
 STRIP = 16
+CELL_ROWS = (14, 15, 30, 31)
 BASE = EDGE - HALO
 MOMENTS = 4
 IMAGE = MOMENTS * FIBRE_ROWS
@@ -72,7 +73,6 @@
         numbers.at[1],
     )
     copies = fetch((*sources[:2], *sources[4:], *sources[2:4], *channel_arrays), targets, sems)
-    arriving = {0: copies[0], 2: copies[1], 5: copies[2], 6: copies[3], 7: copies[4], 8: copies[5], 10: copies[6]}
     depth = lax.axis_index("depth")
     even = is_even()
     rows = held.shape[1]
@@ -81,11 +81,11 @@
     for out in edge_outs:
         out[:BASE, :] = jnp.zeros((BASE, 2 * LANES), F32)
         out[tail:, :] = jnp.zeros((out.shape[0] - tail, 2 * LANES), F32)
+    for copy in copies:
+        copy.wait()
     packed = [jnp.zeros((rows, LANES), F32) for _ in range(2)]
     strip = jnp.zeros((rows, LANES), F32)
     for f in range(FIELDS):
-        if f in arriving:
-            arriving[f].wait()
         ref = held.at[f] if f < FORWARD else held_adj.at[f - FORWARD]
         first, last = ref[:, :LANES], ref[:, LANES:]
         group, place = divmod(f, FORWARD)
@@ -109,8 +109,6 @@
     depth_out[rows:, rows : 2 * rows] = turned[6 * STRIP : 7 * STRIP]
     depth_out[rows:, 2 * rows : 3 * rows] = turned[5 * STRIP : 6 * STRIP]
     depth_out[rows:, 3 * rows :] = turned[7 * STRIP :]
-    for copy in copies[7:]:
-        copy.wait()
     cells_out[0] = numbers[0] * rows + lax.shift_right_logical(numbers[1], 2)
     cells_out[1] = numbers[1] & 3
 
@@ -293,11 +291,12 @@
     beside = got_depth[got_depth.shape[0] - STRIP :, :]
     beside = jnp.concatenate([beside[:, :LANES], beside[:, LANES:]], axis=0)
     seen = jnp.concatenate([traces[:, :LANES], traces[:, LANES:]], axis=0)
-    along, row = cells[0], cells[1]
-    places = jnp.concatenate([along[:, :LANES], along[:, LANES:], row[:, :LANES], row[:, LANES:]] * 2, axis=0)
-    block = jnp.concatenate(
-        [jnp.where(first, strip[...], beside), jnp.where(first, seen, places.astype(F32))], axis=0
-    )
+    value = jnp.where(first, strip[...], beside)
+    row = row_ids(2 * STRIP, LANES)
+    for i, place in enumerate(CELL_ROWS):
+        cell = cells[i // 2][:, LANES * (i % 2) : LANES * (i % 2 + 1)].astype(F32)
+        value = jnp.where((row == place) & first, cell, value)
+    block = jnp.concatenate([value, seen], axis=0)
     for k in range(note_out.shape[0]):
         note_out[k] = block
 
@@ -411,7 +410,8 @@
     return add_up(rate, 8 * MOMENTS)
 
 
-def window_sums(low, high, start, tracks):
+def sums_kernel(tracks, columns, notes, sums_out):
+    start = lax.axis_index("track") * columns - EDGE
     group = min(8, tracks)
     row16 = row_ids(IMAGE, LANES)
 
@@ -419,10 +419,10 @@
         weights, hots = [], []
         for k in range(group):
             who = number * group + k
-            traces = low[who, 2 * STRIP :, :]
-            places = high[who, 2 * STRIP :, :]
+            traces = notes[who, 2 * STRIP :, :]
+            places = [notes[who, place : place + 1, :] for place in CELL_ROWS]
             for h in range(2):
-                mask = (row16 & 3).astype(F32) == places[2 + h : 3 + h]
+                mask = (row16 & 3).astype(F32) == places[2 + h]
                 seen = [traces[4 * h + t : 4 * h + t + 1] for t in range(MOMENTS)]
                 value = jnp.where(
                     row16 < 8,
@@ -432,7 +432,7 @@
                 pieces = three(jnp.where(mask, value, 0.0)) + [mask.astype(F32).astype(BF16)]
                 weights.append(jnp.concatenate(pieces, axis=0))
                 spot = (start + row_ids(LANES, LANES)).astype(F32)
-                hots.append((spot == places[h : h + 1]).astype(F32).astype(BF16))
+                hots.append((spot == places[h]).astype(F32).astype(BF16))
         return image + lax.dot_general(
             jnp.concatenate(weights, axis=1),
             jnp.concatenate(hots, axis=1),
@@ -442,7 +442,8 @@
 
     image = jnp.zeros((4 * IMAGE, LANES), F32)
     image = body(0, image) if tracks == group else lax.fori_loop(0, tracks // group, body, image)
-    return add_up(image, IMAGE), image[3 * IMAGE :]
+    sums_out[:IMAGE, :] = add_up(image, IMAGE)
+    sums_out[IMAGE:, :] = image[3 * IMAGE :]
 
 
 def response(state, media, sources, strains):
@@ -489,7 +490,7 @@
 
 
 def finish_kernel(
-    tracks, columns, notes, beside, obs, cells, base, strains, end,
+    tracks, columns, notes, beside, sums, obs, cells, base, strains, end,
     lambda_out, mu_out, residual_out, end_out, state, media, low, high, sems,
 ):
     copy = pltpu.make_async_copy(end, end_out, sems.at[0])
@@ -502,7 +503,7 @@
     along, row = cells[0], cells[1]
     channels = along.shape[1]
     wanted = jnp.concatenate([along, start + lax.broadcasted_iota(jnp.int32, (1, LANES), 1)], axis=1)
-    seen, count = window_sums(low, high, start, tracks)
+    seen, count = sums[:IMAGE, :], sums[IMAGE:, :]
     rate = recorded_rates(state, media, low, high, wanted, tracks, columns)
     mask = row_ids(8, channels) == row
     traces = [
@@ -705,6 +706,16 @@
     )(notes, base)
     beside = lax.ppermute(mine, "depth", depth_swap)
 
+    sums = pl.pallas_call(
+        lambda *refs: sums_kernel(tracks, rows, *refs),
+        out_shape=jax.ShapeDtypeStruct((2 * IMAGE, LANES), F32),
+        in_specs=[inside],
+        out_specs=inside,
+        compiler_params=params(),
+        cost_estimate=cost(20),
+        name="sums",
+    )(mine)
+
     gradient_lambda, gradient_mu, residual, velocity_end = pl.pallas_call(
         lambda *refs: finish_kernel(tracks, rows, *refs),
         out_shape=(
@@ -713,7 +724,7 @@
             jax.ShapeDtypeStruct((moments // 2, channels), F32),
             jax.ShapeDtypeStruct(velocity.shape, F32),
         ),
-        in_specs=[inside] * 7,
+        in_specs=[inside] * 8,
         out_specs=(inside, inside, inside, outside),
         scratch_shapes=[
             VMEM((5, BATCH, 2 * PAD + STRIP, LANES), F32),
@@ -725,7 +736,7 @@
         compiler_params=params(),
         cost_estimate=cost(2),
         name="finish",
-    )(mine, beside, traces, cells, base, strains, end)
+    )(mine, beside, sums, traces, cells, base, strains, end)
     return gradient_lambda, gradient_mu, velocity_end, residual
 
 

time: 26.3 us -> 26.1 us (level)
  waiting for transfers between devices: 3.73 us -> 3.45 us
    ppermute x1, waiting for transfers between devices: 1.38 us -> 1.1 us  [per_device(): beside = lax.ppermute(mine, 'depth', depth_swap)]
    pallas_call x0 -> x1, Pallas kernels: none -> 0.28 us  [per_device(): pl.pallas_call(lambda *refs: sums_kernel(tracks, rows, *refs), out_shape=...]
  transfers between devices with their start and end apart: 6 -> 6, of which waited for: 2 -> 2; matrix products, arithmetic and copies ran while one was open for 0% -> 0% of each run, Pallas kernels for 22% -> 23%
where the time goes in v17:
time: 26.1 us; the launch traced here: 25.9 us
  starting transfers between devices  11.5 us (44%)
  Pallas kernels  10.2 us (39%)
  waiting for transfers between devices  3.45 us (13%)
  between operations  0.72 us (3%)
    all_to_all x1, starting transfers between devices, per_device(): lax.all_to_all(note, 'track', split_axis=0, concat_axis=0, tiled=True)  7.58 us
    ppermute x1, starting transfers between devices, per_device(): got_even = lax.ppermute(to_even, 'track', swap(0))  2.56 us
    pallas_call x1, Pallas kernels, per_device(): pl.pallas_call(lambda *refs: finish_kernel(tracks, rows, *refs), out_shap...  2.5 us
    pallas_call x1, Pallas kernels, per_device(): pl.pallas_call(adjoint_kernel, out_shape=(jax.ShapeDtypeStruct((2, rows,...  2.39 us
    all_to_all x1, waiting for transfers between devices, per_device(): lax.all_to_all(note, 'track', split_axis=0, concat_axis=0, tiled=True)  2.34 us
    pallas_call x1, Pallas kernels, per_device(): pl.pallas_call(pack_kernel, out_shape=(jax.ShapeDtypeStruct((FORWARD, row...  1.66 us
    pallas_call x1, Pallas kernels, per_device(): pl.pallas_call(forward_kernel, out_shape=(media_of(2), saved_of(2), jax.S...  1.54 us
    ppermute x1, waiting for transfers between devices, per_device(): beside = lax.ppermute(mine, 'depth', depth_swap)  1.1 us
  transfers between devices with their start and end apart: 6, of which 2 were waited for; matrix products, arithmetic and copies ran while one was open for 0% of the time, Pallas kernels for 23%

profile of v17, /device:TPU:0, one launch (start us, length us, event | category | flops | bytes accessed | tf_op | source)
XLA Modules:
  0.0 25.9 jit_solution(14224080382844607631)
XLA Ops:
  0.6 1.7 %pack.1 = (f32[8,64,256]{2,1,0:T(8,128)S(1)}, f32[5,64,256]{2,1,0:T(8,128)S(1)}, f32[80,256]{1,0:T(8,128)S(1)}, f32[168,256]{1,0:T(8,128)S(1)}, f32[168,256]{1,0...) custom-call(f32[2,64,256]{2,1,0:T(8,128)} %refs_0_.1, ...), custom_call_target="tpu_custom_call" | custom-call | flops 5000000000 | bytes 1048576 | tf_op jit(solution)/shard_map/pack/pallas_call | solution.py:606
  2.3 0.5 %collective-permute-start = (f32[80,256]{1,0:T(8,128)S(1)}, f32[80,256]{1,0:T(8,128)S(1)}, u32[]{:S(2)}, u32[]{:S(2)}) collective-permute-start(f32[80,256]{1,0:T(8,128)S(1)} %get-tuple-element.25), channel_id=1, source_target_pairs={{0,1},{1,0},{2,3},{3,2},{4,5},{5,4},{6,7},{7,6},{8,9},{9,8},{10,11... | collective-permute-start | bytes 245768 | tf_op jit(solution)/shard_map/ppermute | solution.py:626
  2.8 2.6 %collective-permute-start.1 = (f32[168,256]{1,0:T(8,128)S(1)}, f32[168,256]{1,0:T(8,128)S(1)}, u32[]{:S(2)}, u32[]{:S(2)}) collective-permute-start(f32[168,256]{1,0:T(8,128)S(1)} %get-tuple-element.29), channel_id=1, source_target_pairs={{0,2},{2,0},{4,6},{6,4},{8,10},{10,8},{12,14},{14,12},{1,3},{3,1},... | collective-permute-start | bytes 516104 | tf_op jit(solution)/shard_map/ppermute | solution.py:629
  5.4 0.7 %collective-permute-start.2 = (f32[168,256]{1,0:T(8,128)S(1)}, f32[168,256]{1,0:T(8,128)S(1)}, u32[]{:S(2)}, u32[]{:S(2)}) collective-permute-start(f32[168,256]{1,0:T(8,128)S(1)} %get-tuple-element.30), channel_id=1, source_target_pairs={{2,4},{4,2},{6,8},{8,6},{10,12},{12,10},{3,5},{5,3},{7,9},{9,7},{1... | collective-permute-start | bytes 516104 | tf_op jit(solution)/shard_map/ppermute | solution.py:628
  6.1 0.0 collective-permute-done.got_depth
  6.1 0.7 %note.1 = f32[8,40,128]{2,1,0:T(8,128)} custom-call(f32[32,128]{1,0:T(8,128)S(1)} %get-tuple-element.24.strip, f32[80,256]{1,0:T(8,128)S(1)} %collective-permute-done.got_depth, f32[4,256]{1,0:T(4,128)S(1)} %get-tuple-element.26.traces.refs_3_, s32[2,1,256]{2,1,0:T(1,128)S(1)} %get-tuple-element.27.cells.refs_4_), custom_call_target="tpu_custom_call" | custom-call | flops 1000000000 | bytes 1048576 | tf_op jit(solution)/shard_map/note/pallas_call | solution.py:634
  6.7 7.6 %all-to-all-start = ((f32[8,40,128]{2,1,0:T(8,128)}), f32[8,40,128]{2,1,0:T(8,128)S(1)}, u32[]{:S(2)}, u32[]{:S(2)}) async-start(f32[8,40,128]{2,1,0:T(8,128)} %note.1), calls=%async_computation | async-start | bytes 327680 | tf_op jit(solution)/shard_map/all_to_all | solution.py:643
  14.3 0.0 collective-permute-done.1.got_even
  14.3 0.0 collective-permute-done.2.got_odd
  14.3 0.1 corners.1
  14.5 0.1 collective-permute-start.3
  14.6 1.5 %forward.1 = (f32[4,2,96,128]{3,2,1,0:T(8,128)S(1)}, f32[4,3,2,64,128]{4,3,2,1,0:T(8,128)S(1)}, f32[2,2,64,128]{3,2,1,0:T(8,128)S(1)}) custom-call(f32[8,64,256]{2,1,0:T(8,128)S(1)} %get-tuple-element.31.held, f32[168,256]{1,0:T(8,128)S(1)} %collective-permute-done.1.got_even, f32[168,256]{1,0:T(8,128)S(1)} %collective-permute-done.2.got_odd), custom_call_target="tpu_custom_call" | custom-call | flops 20000000000 | bytes 1048576 | tf_op jit(solution)/shard_map/forward/pallas_call | solution.py:662
  16.1 0.0 collective-permute-done.3.corner
  16.1 1.0 %forward_inner.1 = (f32[4,1,96,128]{3,2,1,0:T(8,128)S(1)}, f32[4,3,1,64,128]{4,3,2,1,0:T(8,128)S(1)}, f32[2,64,256]{2,1,0:T(8,128)S(1)}) custom-call(f32[8,64,256]{2,1,0:T(8,128)S(1)} %get-tuple-element.31.held, f32[168,256]{1,0:T(8,128)S(1)} %collective-permute-done.1.got_even, f32[168,256]{1,0:T(8,128)S(1)} %collective-permute-done.2.got_odd, ...), custom_call_target="tpu_custom_call" | custom-call | flops 20000000000 | bytes 1048576 | tf_op jit(solution)/shard_map/forward_inner/pallas_call | solution.py:673
  17.2 2.4 %adjoint.1 = (f32[2,64,256]{2,1,0:T(8,128)S(1)}, f32[2,128,128]{2,1,0:T(8,128)S(1)}) custom-call(f32[5,64,256]{2,1,0:T(8,128)S(1)} %get-tuple-element.28.held, f32[168,256]{1,0:T(8,128)S(1)} %collective-permute-done.1.got_even, f32[168,256]{1,0:T(8,128)S(1)} %collective-permute-done.2.got_odd, f32[80,256]{1,0:T(8,128)S(1)} %collective-permute-done.got_depth, ...), custom_call_target="tpu_custom_call" | custom-call | flops 20000000000 | bytes 1048576 | tf_op jit(solution)/shard_map/adjoint/pallas_call | solution.py:684
  19.5 2.3 %all-to-all-done.notes = f32[8,40,128]{2,1,0:T(8,128)S(1)} async-done(((f32[8,40,128]{2,1,0:T(8,128)}), f32[8,40,128]{2,1,0:T(8,128)S(1)}, u32[]{:S(2)}, u32[]{:S(2)}) %all-to-all-start) | async-done | bytes 163872 | tf_op jit(solution)/shard_map/all_to_all | solution.py:643
  21.9 0.1 collective-permute-start.4
  22.0 0.3 %sums.1.refs_2_ = f32[32,128]{1,0:T(8,128)S(1)} custom-call(f32[8,40,128]{2,1,0:T(8,128)S(1)} %relay.1.refs_0_), custom_call_target="tpu_custom_call" | custom-call | flops 20000000000 | bytes 1048576 | tf_op jit(solution)/shard_map/sums/pallas_call | solution.py:709
  22.3 1.1 %collective-permute-done.4.refs_1_ = f32[8,40,128]{2,1,0:T(8,128)S(1)} collective-permute-done((f32[8,40,128]{2,1,0:T(8,128)S(1)}, f32[8,40,128]{2,1,0:T(8,128)S(1)}, u32[]{:S(2)}, u32[]{:S(2)}) %collective-permute-start.4) | collective-permute-done | bytes 163872 | tf_op jit(solution)/shard_map/ppermute | solution.py:707
  23.4 2.5 %finish.1 = (f32[64,256]{1,0:T(8,128)}, f32[64,256]{1,0:T(8,128)}, f32[2,256]{1,0:T(2,128)}, f32[2,64,256]{2,1,0:T(8,128)}) custom-call(f32[8,40,128]{2,1,0:T(8,128)S(1)} %relay.1.refs_0_, f32[8,40,128]{2,1,0:T(8,128)S(1)} %collective-permute-done.4.refs_1_, f32[32,128]{1,0:T(8,128)S(1)} %sums.1.refs_2_, f32[4,256]{1,0:T(4,128)S(1)} %get-tuple-element.26.traces.refs_3_, ...), custom_call_target="tpu_custom_call" | custom-call | flops 2000000000 | bytes 1048576 | tf_op jit(solution)/shard_map/finish/pallas_call | solution.py:719
  (1 shorter events, 0.0 us)
Async XLA Ops:
  2.3 3.8 %collective-permute-start = (f32[80,256]{1,0:T(8,128)S(1)}, f32[80,256]{1,0:T(8,128)S(1)}, u32[]{:S(2)}, u32[]{:S(2)}) collective-permute-start(f32[80,256]{1,0:T(8,128)S(1)} %get-tuple-element.25), channel_id=1, source_target_pairs={{0,1},{1,0},{2,3},{3,2},{4,5},{5,4},{6,7},{7,6},{8,9},{9,8},{10,11... | collective-permute-start | bytes 245768 | tf_op jit(solution)/shard_map/ppermute | solution.py:626
  2.8 11.5 %collective-permute-start.1 = (f32[168,256]{1,0:T(8,128)S(1)}, f32[168,256]{1,0:T(8,128)S(1)}, u32[]{:S(2)}, u32[]{:S(2)}) collective-permute-start(f32[168,256]{1,0:T(8,128)S(1)} %get-tuple-element.29), channel_id=1, source_target_pairs={{0,2},{2,0},{4,6},{6,4},{8,10},{10,8},{12,14},{14,12},{1,3},{3,1},... | collective-permute-start | bytes 516104 | tf_op jit(solution)/shard_map/ppermute | solution.py:629
  5.4 8.9 %collective-permute-start.2 = (f32[168,256]{1,0:T(8,128)S(1)}, f32[168,256]{1,0:T(8,128)S(1)}, u32[]{:S(2)}, u32[]{:S(2)}) collective-permute-start(f32[168,256]{1,0:T(8,128)S(1)} %get-tuple-element.30), channel_id=1, source_target_pairs={{2,4},{4,2},{6,8},{8,6},{10,12},{12,10},{3,5},{5,3},{7,9},{9,7},{1... | collective-permute-start | bytes 516104 | tf_op jit(solution)/shard_map/ppermute | solution.py:628
  6.7 15.1 %all-to-all-start = ((f32[8,40,128]{2,1,0:T(8,128)}), f32[8,40,128]{2,1,0:T(8,128)S(1)}, u32[]{:S(2)}, u32[]{:S(2)}) async-start(f32[8,40,128]{2,1,0:T(8,128)} %note.1), calls=%async_computation | async-start | bytes 327680 | tf_op jit(solution)/shard_map/all_to_all | solution.py:643
  14.5 1.6 %collective-permute-start.3 = (f32[32,256]{1,0:T(8,128)S(1)}, f32[32,256]{1,0:T(8,128)S(1)}, u32[]{:S(2)}, u32[]{:S(2)}) collective-permute-start(f32[32,256]{1,0:T(8,128)S(1)} %corners.1), channel_id=1, source_target_pairs={{0,1},{1,0},{2,3},{3,2},{4,5},{5,4},{6,7},{7,6},{8,9},{9,8},{10,11... | collective-permute-start | bytes 98312 | tf_op jit(solution)/shard_map/ppermute | solution.py:654
  21.9 1.5 %collective-permute-start.4 = (f32[8,40,128]{2,1,0:T(8,128)S(1)}, f32[8,40,128]{2,1,0:T(8,128)S(1)}, u32[]{:S(2)}, u32[]{:S(2)}) collective-permute-start(f32[8,40,128]{2,1,0:T(8,128)S(1)} %relay.1.refs_0_), channel_id=1, source_target_pairs={{0,1},{1,0},{2,3},{3,2},{4,5},{5,4},{6,7},{7,6},{8,9},{9,8},{10,11... | collective-permute-start | bytes 491528 | tf_op jit(solution)/shard_map/ppermute | solution.py:707

commit v18 on v17

--- a/solution.py
+++ b/solution.py
@@ -17,6 +17,7 @@
 FIELDS = FORWARD + ADJOINT
 STRIP = 16
 CELL_ROWS = (14, 15, 30, 31)
+EXTRA = 168
 BASE = EDGE - HALO
 MOMENTS = 4
 IMAGE = MOMENTS * FIBRE_ROWS
@@ -59,7 +60,7 @@
 def pack_kernel(*refs):
     sources, channel_arrays = refs[:7], refs[7:10]
     held, held_adj, depth_out, edge_outs, strip_out, traces_out, cells_out = *refs[10:13], refs[13:15], *refs[15:18]
-    numbers, sems = refs[18:]
+    rows_out, numbers, sems = refs[18:]
     targets = (
         held.at[pl.ds(0, 2)],
         held.at[pl.ds(2, 3)],
@@ -102,6 +103,10 @@
         edge_outs[1][at : at + HALO, :] = jnp.where(even, low, high)
     depth_out[:rows, :LANES] = packed[0]
     depth_out[:rows, LANES:] = packed[1]
+    rows_out[...] = strip
+    low, high = strip[HALO : 2 * HALO], strip[rows - 2 * HALO : rows - HALO]
+    edge_outs[0][EXTRA : EXTRA + HALO, :LANES] = jnp.where(even, high, low)
+    edge_outs[1][EXTRA : EXTRA + HALO, :LANES] = jnp.where(even, low, high)
     turned = strip.T
     strip_out[:, :rows] = turned[: 2 * STRIP]
     strip_out[:, rows:] = turned[2 * STRIP : 4 * STRIP]
@@ -301,8 +306,8 @@
         note_out[k] = block
 
 
-def relay_kernel(notes, rest, notes_out):
-    del rest
+def relay_kernel(notes, base, rates, notes_out):
+    del base, rates
     notes_out[...] = notes[...]
 
 
@@ -356,11 +361,12 @@
     def at(f, w, r, by=0):
         return state[f, w, PAD + r + by : PAD + r + by + 8, :]
 
-    strains = [[] for _ in range(BATCH)]
+    count = state.shape[1]
+    strains = [[] for _ in range(count)]
     for moment in range(MOMENTS):
         last = moment == MOMENTS - 1
         for r in (0, 8) if moment < 2 else (0,):
-            for w in range(BATCH):
+            for w in range(count):
                 here = slice(PAD + r, PAD + r + 8)
                 xx, xz, zz = at(2, w, r), at(4, w, r), at(3, w, r)
                 b = media[0, w, r : r + 8, :]
@@ -372,7 +378,7 @@
                     far = (turn(xz, -2) - turn(xz, 1)) + (at(3, w, r, 2) - at(3, w, r, -1))
                     state[1, w, here, :] = at(1, w, r) + b * (near + RATIO * far)
         for r in (0, 8) if moment < 1 else (0,):
-            for w in range(BATCH):
+            for w in range(count):
                 here = slice(PAD + r, PAD + r + 8)
                 vx, vz = at(0, w, r), at(1, w, r)
                 exx = (turn(vx, -1) - vx) + RATIO * (turn(vx, -2) - turn(vx, 1))
@@ -489,46 +495,53 @@
     return sums[0] + sums[1]
 
 
-def finish_kernel(
-    tracks, columns, notes, beside, sums, obs, cells, base, strains, end,
-    lambda_out, mu_out, residual_out, end_out, state, media, low, high, sems,
-):
+def fibre_kernel(strip, got_even, got_odd, rates_out, media_out, state, media, rows_in):
+    rows = strip.shape[0]
+    rows_in[...] = jnp.zeros(rows_in.shape, F32)
+    rows_in[EDGE : EDGE + rows, :] = strip[...]
+    lane = lane_ids(HALO)
+    for side in range(2):
+        use_odd = is_even() if side == 0 else ~is_even()
+        near = jnp.zeros((HALO, LANES), F32)
+        for f in range(FORWARD):
+            span = slice(BASE + HALO * f, BASE + HALO * (f + 1))
+            value = jnp.where(use_odd, got_odd[span, :LANES], got_even[span, :LANES])
+            here = (lane >= STRIP * f) & (lane < STRIP * (f + 1))
+            near = jnp.where(here, turn(value, STRIP * f), near)
+        span = slice(EXTRA, EXTRA + HALO)
+        far = jnp.where(use_odd, got_odd[span, :LANES], got_even[span, :LANES])
+        if side == 0:
+            rows_in[BASE:EDGE, :] = near
+            rows_in[:BASE, :] = far[HALO - BASE :]
+            rows_in[LANES - (HALO - BASE) :, :] = far[: HALO - BASE]
+        else:
+            rows_in[EDGE + rows : EDGE + rows + HALO, :] = near
+            rows_in[EDGE + rows + HALO : EDGE + rows + 2 * HALO, :] = far
+    turned = rows_in[...].T
+    values = [turned[STRIP * f : STRIP * (f + 1)] for f in range(FORWARD)]
+    state[...] = jnp.zeros(state.shape, F32)
+    for f in range(5):
+        state[f, 0, PAD : PAD + STRIP, :] = values[f]
+    buoyancy, lame, shear = (NEAR * value for value in values[5:])
+    for k, value in enumerate((buoyancy, lame + 2.0 * shear, lame, shear)):
+        media[k, 0] = value
+        media_out[k] = value
+    rates_out[...] = strip_steps(state, media)[0]
+
+
+def gradient_kernel(sums, rates, media, base, strains, end, lambda_out, mu_out, end_out, state, sems):
     copy = pltpu.make_async_copy(end, end_out, sems.at[0])
     copy.start()
-    depth = lax.axis_index("depth")
-    low[...] = jnp.where(depth == 0, notes[...], beside[...])
-    high[...] = jnp.where(depth == 0, beside[...], notes[...])
-    track = lax.axis_index("track")
-    start = track * columns - EDGE
-    along, row = cells[0], cells[1]
-    channels = along.shape[1]
-    wanted = jnp.concatenate([along, start + lax.broadcasted_iota(jnp.int32, (1, LANES), 1)], axis=1)
-    seen, count = sums[:IMAGE, :], sums[IMAGE:, :]
-    rate = recorded_rates(state, media, low, high, wanted, tracks, columns)
-    mask = row_ids(8, channels) == row
-    traces = [
-        jnp.sum(jnp.where(mask, rate[8 * t : 8 * t + 8, :channels], 0.0), axis=0, keepdims=True)
-        - obs[t : t + 1, :]
-        for t in range(MOMENTS)
-    ]
-    residual_out[...] = jnp.where(
-        depth == 0, jnp.concatenate(traces[:2], axis=0), jnp.concatenate(traces[2:], axis=0)
-    )
-    near = jnp.concatenate([rate[8 * t : 8 * t + 4, channels:] for t in range(MOMENTS)], axis=0)
-    found = jnp.where(depth == 0, count * near - seen, 0.0)
+    rows = base.shape[1]
+    near = jnp.concatenate([rates[8 * t : 8 * t + 4, :] for t in range(MOMENTS)], axis=0)
+    lane = lane_ids(IMAGE)
+    reached = (lane >= BASE) & (lane < EDGE + rows + HALO) & (lax.axis_index("depth") == 0)
+    found = jnp.where(reached, sums[IMAGE:, :] * near - sums[:IMAGE, :], 0.0)
     nothing = jnp.zeros((8 - FIBRE_ROWS, LANES), F32)
     sources = [
         jnp.concatenate([found[FIBRE_ROWS * t : FIBRE_ROWS * (t + 1)], nothing], axis=0) for t in range(MOMENTS)
     ]
-    own = [
-        NEAR * strip_window(f, low, high, track - 1, columns - EDGE, tracks, columns) for f in (5, 6, 7)
-    ]
-    media[0, 0] = own[0]
-    media[1, 0] = own[1] + 2.0 * own[2]
-    media[2, 0] = own[1]
-    media[3, 0] = own[2]
-    added = response(state.at[:, 0], media.at[:, 0], sources, strains)
-    rows = base.shape[1]
+    added = response(state, media, sources, strains)
     added = jnp.concatenate(added + [jnp.zeros((LANES - 32, LANES), F32)], axis=0).T[EDGE : EDGE + rows]
     lane = lane_ids(rows)
     for k, out in enumerate((lambda_out, mu_out)):
@@ -536,6 +549,23 @@
         out[:, :LANES] = (NEAR * NEAR) * (base[k, :, :LANES] + more)
         out[:, LANES:] = (NEAR * NEAR) * base[k, :, LANES:]
     copy.wait()
+
+
+def residual_kernel(tracks, columns, notes, beside, obs, cells, residual_out, state, media, low, high):
+    depth = lax.axis_index("depth")
+    low[...] = jnp.where(depth == 0, notes[...], beside[...])
+    high[...] = jnp.where(depth == 0, beside[...], notes[...])
+    along, row = cells[0], cells[1]
+    channels = along.shape[1]
+    rate = recorded_rates(state, media, low, high, along, tracks, columns)
+    mask = row_ids(8, channels) == row
+    traces = [
+        jnp.sum(jnp.where(mask, rate[8 * t : 8 * t + 8], 0.0), axis=0, keepdims=True) - obs[t : t + 1, :]
+        for t in range(MOMENTS)
+    ]
+    residual_out[...] = jnp.where(
+        depth == 0, jnp.concatenate(traces[:2], axis=0), jnp.concatenate(traces[2:], axis=0)
+    )
 
 
 def adjoint_kernel(
@@ -598,12 +628,11 @@
     channel_arrays = (pinned(observed), pinned(owner), pinned(cell))
     extent = rows + 2 * EDGE
     block = jax.ShapeDtypeStruct((rows, depth_cells), F32)
-    length = BASE + HALO * FIELDS + BASE
-    edges = jax.ShapeDtypeStruct((length + (-length) % 8, depth_cells), F32)
+    edges = jax.ShapeDtypeStruct((EXTRA + EDGE, depth_cells), F32)
     inside = pl.BlockSpec(memory_space=VMEM)
     outside = pl.BlockSpec(memory_space=pltpu.HBM)
     anywhere = pl.BlockSpec(memory_space=pl.ANY)
-    held, held_adj, to_depth, to_even, to_odd, strip, traces, cells = pl.pallas_call(
+    held, held_adj, to_depth, to_even, to_odd, strip, traces, cells, strip_rows = pl.pallas_call(
         pack_kernel,
         out_shape=(
             jax.ShapeDtypeStruct((FORWARD, rows, depth_cells), F32),
@@ -614,9 +643,10 @@
             jax.ShapeDtypeStruct((2 * STRIP, LANES), F32),
             jax.ShapeDtypeStruct((moments, channels), F32),
             jax.ShapeDtypeStruct((2, 1, channels), jnp.int32),
+            jax.ShapeDtypeStruct((rows, LANES), F32),
         ),
         in_specs=[outside] * 10,
-        out_specs=(inside,) * 8,
+        out_specs=(inside,) * 9,
         scratch_shapes=[VMEM((2, 1, channels), jnp.int32), pltpu.SemaphoreType.DMA((10,))],
         compiler_params=params(),
         cost_estimate=cost(5),
@@ -695,15 +725,33 @@
         name="adjoint",
     )(held_adj, got_even, got_odd, got_depth, got_corner, media, saved, inner_media, inner_saved)
 
+    rates, own_media = pl.pallas_call(
+        fibre_kernel,
+        out_shape=(
+            jax.ShapeDtypeStruct((8 * MOMENTS, LANES), F32),
+            jax.ShapeDtypeStruct((4, STRIP, LANES), F32),
+        ),
+        in_specs=[inside] * 3,
+        out_specs=(inside,) * 2,
+        scratch_shapes=[
+            VMEM((5, 1, 2 * PAD + STRIP, LANES), F32),
+            VMEM((4, 1, STRIP, LANES), F32),
+            VMEM((LANES, LANES), F32),
+        ],
+        compiler_params=params(),
+        cost_estimate=cost(5),
+        name="fibre",
+    )(strip_rows, got_even, got_odd)
+
     mine = pl.pallas_call(
         relay_kernel,
         out_shape=jax.ShapeDtypeStruct(note.shape, F32),
-        in_specs=[inside, anywhere],
+        in_specs=[inside, anywhere, anywhere],
         out_specs=inside,
         compiler_params=params(),
         cost_estimate=cost(1),
         name="relay",
-    )(notes, base)
+    )(notes, base, rates)
     beside = lax.ppermute(mine, "depth", depth_swap)
 
     sums = pl.pallas_call(
@@ -716,27 +764,32 @@
         name="sums",
     )(mine)
 
-    gradient_lambda, gradient_mu, residual, velocity_end = pl.pallas_call(
-        lambda *refs: finish_kernel(tracks, rows, *refs),
-        out_shape=(
-            block,
-            block,
-            jax.ShapeDtypeStruct((moments // 2, channels), F32),
-            jax.ShapeDtypeStruct(velocity.shape, F32),
-        ),
-        in_specs=[inside] * 8,
-        out_specs=(inside, inside, inside, outside),
+    gradient_lambda, gradient_mu, velocity_end = pl.pallas_call(
+        gradient_kernel,
+        out_shape=(block, block, jax.ShapeDtypeStruct(velocity.shape, F32)),
+        in_specs=[inside] * 6,
+        out_specs=(inside, inside, outside),
+        scratch_shapes=[VMEM((5, 2 * PAD + STRIP, LANES), F32), pltpu.SemaphoreType.DMA((1,))],
+        compiler_params=params(),
+        cost_estimate=cost(20),
+        name="gradient",
+    )(sums, rates, own_media, base, strains, end)
+
+    residual = pl.pallas_call(
+        lambda *refs: residual_kernel(tracks, rows, *refs),
+        out_shape=jax.ShapeDtypeStruct((moments // 2, channels), F32),
+        in_specs=[inside] * 4,
+        out_specs=inside,
         scratch_shapes=[
             VMEM((5, BATCH, 2 * PAD + STRIP, LANES), F32),
             VMEM((4, BATCH, STRIP, LANES), F32),
             VMEM(note.shape, F32),
             VMEM(note.shape, F32),
-            pltpu.SemaphoreType.DMA((1,)),
         ],
         compiler_params=params(),
         cost_estimate=cost(2),
-        name="finish",
-    )(mine, beside, sums, traces, cells, base, strains, end)
+        name="residual",
+    )(mine, beside, traces, cells)
     return gradient_lambda, gradient_mu, velocity_end, residual
 
 

time: 26.1 us -> 27.2 us (1.042)
  Pallas kernels: 10.2 us -> 11.6 us
  waiting for transfers between devices: 3.45 us -> 3.05 us
    pallas_call x1 -> x3, Pallas kernels: 2.5 us -> 3.88 us  [the longest x1 1.6 us: per_device(): pl.pallas_call(lambda *refs: residual_kernel(tracks, rows, *refs), out_sh...]
    ppermute x1, waiting for transfers between devices: 0.01 us -> 1.26 us  [per_device(): got_depth = lax.ppermute(to_depth, 'depth', depth_swap)]
    ppermute x1, waiting for transfers between devices: 1.1 us -> 0.01 us  [per_device(): beside = lax.ppermute(mine, 'depth', depth_swap)]
    all_to_all x1, waiting for transfers between devices: 2.34 us -> 1.77 us  [per_device(): lax.all_to_all(note, 'track', split_axis=0, concat_axis=0, tiled=True)]
    ppermute x1, starting transfers between devices: 0.52 us -> 0.07 us  [per_device(): got_depth = lax.ppermute(to_depth, 'depth', depth_swap)]
    ppermute x1, starting transfers between devices: 2.56 us -> 3 us  [per_device(): got_even = lax.ppermute(to_even, 'track', swap(0))]
  transfers between devices with their start and end apart: 6 -> 6, of which waited for: 2 -> 2; matrix products, arithmetic and copies ran while one was open for 0% -> 0% of each run, Pallas kernels for 23% -> 31%
where the time goes in v18:
time: 27.2 us; the launch traced here: 26.9 us
  Pallas kernels  11.6 us (43%)
  starting transfers between devices  11.5 us (42%)
  waiting for transfers between devices  3.05 us (11%)
  between operations  0.73 us (3%)
    all_to_all x1, starting transfers between devices, per_device(): lax.all_to_all(note, 'track', split_axis=0, concat_axis=0, tiled=True)  7.58 us
    ppermute x1, starting transfers between devices, per_device(): got_even = lax.ppermute(to_even, 'track', swap(0))  3 us
    pallas_call x1, Pallas kernels, per_device(): pl.pallas_call(adjoint_kernel, out_shape=(jax.ShapeDtypeStruct((2, rows,...  2.39 us
    all_to_all x1, waiting for transfers between devices, per_device(): lax.all_to_all(note, 'track', split_axis=0, concat_axis=0, tiled=True)  1.77 us
    pallas_call x1, Pallas kernels, per_device(): pl.pallas_call(pack_kernel, out_shape=(jax.ShapeDtypeStruct((FORWARD, row...  1.66 us
    pallas_call x1, Pallas kernels, per_device(): pl.pallas_call(lambda *refs: residual_kernel(tracks, rows, *refs), out_sh...  1.6 us
    pallas_call x1, Pallas kernels, per_device(): pl.pallas_call(forward_kernel, out_shape=(media_of(2), saved_of(2), jax.S...  1.54 us
    pallas_call x1, Pallas kernels, per_device(): pl.pallas_call(gradient_kernel, out_shape=(block, block, jax.ShapeDtypeSt...  1.5 us
  transfers between devices with their start and end apart: 6, of which 2 were waited for; matrix products, arithmetic and copies ran while one was open for 0% of the time, Pallas kernels for 31%

profile of v18, /device:TPU:0, one launch (start us, length us, event | category | flops | bytes accessed | tf_op | source)
XLA Modules:
  0.0 26.9 jit_solution(3701799565543920463)
XLA Ops:
  0.6 1.7 %pack.1 = (f32[8,64,256]{2,1,0:T(8,128)S(1)}, f32[5,64,256]{2,1,0:T(8,128)S(1)}, f32[80,256]{1,0:T(8,128)S(1)}, f32[184,256]{1,0:T(8,128)S(1)}, f32[184,256]{1,0...) custom-call(f32[2,64,256]{2,1,0:T(8,128)} %refs_0_.1, ...), custom_call_target="tpu_custom_call" | custom-call | flops 5000000000 | bytes 1048576 | tf_op jit(solution)/shard_map/pack/pallas_call | solution.py:635
  2.3 3.0 %collective-permute-start.1 = (f32[184,256]{1,0:T(8,128)S(1)}, f32[184,256]{1,0:T(8,128)S(1)}, u32[]{:S(2)}, u32[]{:S(2)}) collective-permute-start(f32[184,256]{1,0:T(8,128)S(1)} %get-tuple-element.31), channel_id=1, source_target_pairs={{0,2},{2,0},{4,6},{6,4},{8,10},{10,8},{12,14},{14,12},{1,3},{3,1},... | collective-permute-start | bytes 565256 | tf_op jit(solution)/shard_map/ppermute | solution.py:659
  5.3 0.7 %collective-permute-start.2 = (f32[184,256]{1,0:T(8,128)S(1)}, f32[184,256]{1,0:T(8,128)S(1)}, u32[]{:S(2)}, u32[]{:S(2)}) collective-permute-start(f32[184,256]{1,0:T(8,128)S(1)} %get-tuple-element.32), channel_id=1, source_target_pairs={{2,4},{4,2},{6,8},{8,6},{10,12},{12,10},{3,5},{5,3},{7,9},{9,7},{1... | collective-permute-start | bytes 565256 | tf_op jit(solution)/shard_map/ppermute | solution.py:658
  6.0 0.1 collective-permute-start
  6.1 1.3 %collective-permute-done.got_depth = f32[80,256]{1,0:T(8,128)S(1)} collective-permute-done((f32[80,256]{1,0:T(8,128)S(1)}, f32[80,256]{1,0:T(8,128)S(1)}, u32[]{:S(2)}, u32[]{:S(2)}) %collective-permute-start) | collective-permute-done | bytes 81952 | tf_op jit(solution)/shard_map/ppermute | solution.py:656
  7.3 0.7 %note.1 = f32[8,40,128]{2,1,0:T(8,128)} custom-call(f32[32,128]{1,0:T(8,128)S(1)} %get-tuple-element.26.strip, f32[80,256]{1,0:T(8,128)S(1)} %collective-permute-done.got_depth, f32[4,256]{1,0:T(4,128)S(1)} %get-tuple-element.28.traces.refs_2_, s32[2,1,256]{2,1,0:T(1,128)S(1)} %get-tuple-element.29.cells.refs_3_), custom_call_target="tpu_custom_call" | custom-call | flops 1000000000 | bytes 1048576 | tf_op jit(solution)/shard_map/note/pallas_call | solution.py:664
  8.0 7.6 %all-to-all-start = ((f32[8,40,128]{2,1,0:T(8,128)}), f32[8,40,128]{2,1,0:T(8,128)S(1)}, u32[]{:S(2)}, u32[]{:S(2)}) async-start(f32[8,40,128]{2,1,0:T(8,128)} %note.1), calls=%async_computation | async-start | bytes 327680 | tf_op jit(solution)/shard_map/all_to_all | solution.py:673
  15.6 0.0 collective-permute-done.1.got_even
  15.6 0.0 collective-permute-done.2.got_odd
  15.6 0.1 corners.1
  15.7 0.1 collective-permute-start.3
  15.8 1.5 %forward.1 = (f32[4,2,96,128]{3,2,1,0:T(8,128)S(1)}, f32[4,3,2,64,128]{4,3,2,1,0:T(8,128)S(1)}, f32[2,2,64,128]{3,2,1,0:T(8,128)S(1)}) custom-call(f32[8,64,256]{2,1,0:T(8,128)S(1)} %get-tuple-element.33.held, f32[184,256]{1,0:T(8,128)S(1)} %collective-permute-done.1.got_even, f32[184,256]{1,0:T(8,128)S(1)} %collective-permute-done.2.got_odd), custom_call_target="tpu_custom_call" | custom-call | flops 20000000000 | bytes 1048576 | tf_op jit(solution)/shard_map/forward/pallas_call | solution.py:692
  17.4 0.8 %fibre.1 = (f32[32,128]{1,0:T(8,128)S(1)}, f32[4,16,128]{2,1,0:T(8,128)S(1)}) custom-call(f32[64,128]{1,0:T(8,128)S(1)} %get-tuple-element.40.strip, f32[184,256]{1,0:T(8,128)S(1)} %collective-permute-done.1.got_even, f32[184,256]{1,0:T(8,128)S(1)} %collective-permute-done.2.got_odd), custom_call_target="tpu_custom_call" | custom-call | flops 5000000000 | bytes 1048576 | tf_op jit(solution)/shard_map/fibre/pallas_call | solution.py:728
  18.2 0.0 collective-permute-done.3.corner
  18.2 1.0 %forward_inner.1 = (f32[4,1,96,128]{3,2,1,0:T(8,128)S(1)}, f32[4,3,1,64,128]{4,3,2,1,0:T(8,128)S(1)}, f32[2,64,256]{2,1,0:T(8,128)S(1)}) custom-call(f32[8,64,256]{2,1,0:T(8,128)S(1)} %get-tuple-element.33.held, f32[184,256]{1,0:T(8,128)S(1)} %collective-permute-done.1.got_even, f32[184,256]{1,0:T(8,128)S(1)} %collective-permute-done.2.got_odd, ...), custom_call_target="tpu_custom_call" | custom-call | flops 20000000000 | bytes 1048576 | tf_op jit(solution)/shard_map/forward_inner/pallas_call | solution.py:703
  19.2 2.4 %adjoint.1 = (f32[2,64,256]{2,1,0:T(8,128)S(1)}, f32[2,128,128]{2,1,0:T(8,128)S(1)}) custom-call(f32[5,64,256]{2,1,0:T(8,128)S(1)} %get-tuple-element.30.held, f32[184,256]{1,0:T(8,128)S(1)} %collective-permute-done.1.got_even, f32[184,256]{1,0:T(8,128)S(1)} %collective-permute-done.2.got_odd, f32[80,256]{1,0:T(8,128)S(1)} %collective-permute-done.got_depth, ...), custom_call_target="tpu_custom_call" | custom-call | flops 20000000000 | bytes 1048576 | tf_op jit(solution)/shard_map/adjoint/pallas_call | solution.py:714
  21.6 1.8 %all-to-all-done.notes = f32[8,40,128]{2,1,0:T(8,128)S(1)} async-done(((f32[8,40,128]{2,1,0:T(8,128)}), f32[8,40,128]{2,1,0:T(8,128)S(1)}, u32[]{:S(2)}, u32[]{:S(2)}) %all-to-all-start) | async-done | bytes 163872 | tf_op jit(solution)/shard_map/all_to_all | solution.py:673
  23.4 0.1 collective-permute-start.4
  23.5 0.3 %sums.1 = f32[32,128]{1,0:T(8,128)S(1)} custom-call(f32[8,40,128]{2,1,0:T(8,128)S(1)} %relay.1.refs_0_), custom_call_target="tpu_custom_call" | custom-call | flops 20000000000 | bytes 1048576 | tf_op jit(solution)/shard_map/sums/pallas_call | solution.py:757
  23.8 1.5 %gradient.1 = (f32[64,256]{1,0:T(8,128)}, f32[64,256]{1,0:T(8,128)}, f32[2,64,256]{2,1,0:T(8,128)}) custom-call(f32[32,128]{1,0:T(8,128)S(1)} %sums.1, f32[32,128]{1,0:T(8,128)S(1)} %get-tuple-element.41.rates, f32[4,16,128]{2,1,0:T(8,128)S(1)} %get-tuple-element.42.media, f32[2,64,256]{2,1,0:T(8,128)S(1)} %get-tuple-element.39.base, ...), custom_call_target="tpu_custom_call" | custom-call | flops 20000000000 | bytes 1048576 | tf_op jit(solution)/shard_map/gradient/pallas_call | solution.py:767
  25.3 0.0 collective-permute-done.4.refs_1_
  25.3 1.6 %residual.1 = f32[2,256]{1,0:T(2,128)} custom-call(f32[8,40,128]{2,1,0:T(8,128)S(1)} %relay.1.refs_0_, f32[8,40,128]{2,1,0:T(8,128)S(1)} %collective-permute-done.4.refs_1_, f32[4,256]{1,0:T(4,128)S(1)} %get-tuple-element.28.traces.refs_2_, s32[2,1,256]{2,1,0:T(1,128)S(1)} %get-tuple-element.29.cells.refs_3_), custom_call_target="tpu_custom_call" | custom-call | flops 2000000000 | bytes 1048576 | tf_op jit(solution)/shard_map/residual/pallas_call | solution.py:778
  (1 shorter events, 0.0 us)
Async XLA Ops:
  2.3 13.3 %collective-permute-start.1 = (f32[184,256]{1,0:T(8,128)S(1)}, f32[184,256]{1,0:T(8,128)S(1)}, u32[]{:S(2)}, u32[]{:S(2)}) collective-permute-start(f32[184,256]{1,0:T(8,128)S(1)} %get-tuple-element.31), channel_id=1, source_target_pairs={{0,2},{2,0},{4,6},{6,4},{8,10},{10,8},{12,14},{14,12},{1,3},{3,1},... | collective-permute-start | bytes 565256 | tf_op jit(solution)/shard_map/ppermute | solution.py:659
  5.3 10.3 %collective-permute-start.2 = (f32[184,256]{1,0:T(8,128)S(1)}, f32[184,256]{1,0:T(8,128)S(1)}, u32[]{:S(2)}, u32[]{:S(2)}) collective-permute-start(f32[184,256]{1,0:T(8,128)S(1)} %get-tuple-element.32), channel_id=1, source_target_pairs={{2,4},{4,2},{6,8},{8,6},{10,12},{12,10},{3,5},{5,3},{7,9},{9,7},{1... | collective-permute-start | bytes 565256 | tf_op jit(solution)/shard_map/ppermute | solution.py:658
  6.0 1.3 %collective-permute-start = (f32[80,256]{1,0:T(8,128)S(1)}, f32[80,256]{1,0:T(8,128)S(1)}, u32[]{:S(2)}, u32[]{:S(2)}) collective-permute-start(f32[80,256]{1,0:T(8,128)S(1)} %get-tuple-element.27), channel_id=1, source_target_pairs={{0,1},{1,0},{2,3},{3,2},{4,5},{5,4},{6,7},{7,6},{8,9},{9,8},{10,11... | collective-permute-start | bytes 245768 | tf_op jit(solution)/shard_map/ppermute | solution.py:656
  8.0 15.4 %all-to-all-start = ((f32[8,40,128]{2,1,0:T(8,128)}), f32[8,40,128]{2,1,0:T(8,128)S(1)}, u32[]{:S(2)}, u32[]{:S(2)}) async-start(f32[8,40,128]{2,1,0:T(8,128)} %note.1), calls=%async_computation | async-start | bytes 327680 | tf_op jit(solution)/shard_map/all_to_all | solution.py:673
  15.7 2.4 %collective-permute-start.3 = (f32[32,256]{1,0:T(8,128)S(1)}, f32[32,256]{1,0:T(8,128)S(1)}, u32[]{:S(2)}, u32[]{:S(2)}) collective-permute-start(f32[32,256]{1,0:T(8,128)S(1)} %corners.1), channel_id=1, source_target_pairs={{0,1},{1,0},{2,3},{3,2},{4,5},{5,4},{6,7},{7,6},{8,9},{9,8},{10,11... | collective-permute-start | bytes 98312 | tf_op jit(solution)/shard_map/ppermute | solution.py:684
  23.4 1.9 %collective-permute-start.4 = (f32[8,40,128]{2,1,0:T(8,128)S(1)}, f32[8,40,128]{2,1,0:T(8,128)S(1)}, u32[]{:S(2)}, u32[]{:S(2)}) collective-permute-start(f32[8,40,128]{2,1,0:T(8,128)S(1)} %relay.1.refs_0_), channel_id=1, source_target_pairs={{0,1},{1,0},{2,3},{3,2},{4,5},{5,4},{6,7},{7,6},{8,9},{9,8},{10,11... | collective-permute-start | bytes 491528 | tf_op jit(solution)/shard_map/ppermute | solution.py:755

commit v19 on v18

--- a/solution.py
+++ b/solution.py
@@ -529,9 +529,7 @@
     rates_out[...] = strip_steps(state, media)[0]
 
 
-def gradient_kernel(sums, rates, media, base, strains, end, lambda_out, mu_out, end_out, state, sems):
-    copy = pltpu.make_async_copy(end, end_out, sems.at[0])
-    copy.start()
+def gradient_kernel(sums, rates, media, base, strains, gradients_out, state):
     rows = base.shape[1]
     near = jnp.concatenate([rates[8 * t : 8 * t + 4, :] for t in range(MOMENTS)], axis=0)
     lane = lane_ids(IMAGE)
@@ -544,14 +542,17 @@
     added = response(state, media, sources, strains)
     added = jnp.concatenate(added + [jnp.zeros((LANES - 32, LANES), F32)], axis=0).T[EDGE : EDGE + rows]
     lane = lane_ids(rows)
-    for k, out in enumerate((lambda_out, mu_out)):
+    for k in range(2):
         more = jnp.where(lane < STRIP, turn(added, -STRIP * k), 0.0)
-        out[:, :LANES] = (NEAR * NEAR) * (base[k, :, :LANES] + more)
-        out[:, LANES:] = (NEAR * NEAR) * base[k, :, LANES:]
-    copy.wait()
-
-
-def residual_kernel(tracks, columns, notes, beside, obs, cells, residual_out, state, media, low, high):
+        gradients_out[k, :, :LANES] = (NEAR * NEAR) * (base[k, :, :LANES] + more)
+        gradients_out[k, :, LANES:] = (NEAR * NEAR) * base[k, :, LANES:]
+
+
+def residual_kernel(
+    tracks, columns, notes, beside, obs, cells, gradients, end,
+    residual_out, lambda_out, mu_out, end_out, state, media, low, high, sems,
+):
+    copies = fetch((gradients.at[0], gradients.at[1], end), (lambda_out, mu_out, end_out), sems)
     depth = lax.axis_index("depth")
     low[...] = jnp.where(depth == 0, notes[...], beside[...])
     high[...] = jnp.where(depth == 0, beside[...], notes[...])
@@ -566,6 +567,8 @@
     residual_out[...] = jnp.where(
         depth == 0, jnp.concatenate(traces[:2], axis=0), jnp.concatenate(traces[2:], axis=0)
     )
+    for copy in copies:
+        copy.wait()
 
 
 def adjoint_kernel(
@@ -667,7 +670,7 @@
         in_specs=[inside] * 4,
         out_specs=inside,
         compiler_params=params(),
-        cost_estimate=cost(1),
+        cost_estimate=cost(20),
         name="note",
     )(strip, got_depth, traces, cells)
     notes = lax.all_to_all(note, "track", split_axis=0, concat_axis=0, tiled=True)
@@ -764,32 +767,38 @@
         name="sums",
     )(mine)
 
-    gradient_lambda, gradient_mu, velocity_end = pl.pallas_call(
+    gradients = pl.pallas_call(
         gradient_kernel,
-        out_shape=(block, block, jax.ShapeDtypeStruct(velocity.shape, F32)),
-        in_specs=[inside] * 6,
-        out_specs=(inside, inside, outside),
-        scratch_shapes=[VMEM((5, 2 * PAD + STRIP, LANES), F32), pltpu.SemaphoreType.DMA((1,))],
+        out_shape=jax.ShapeDtypeStruct((2, rows, depth_cells), F32),
+        in_specs=[inside] * 5,
+        out_specs=inside,
+        scratch_shapes=[VMEM((5, 2 * PAD + STRIP, LANES), F32)],
         compiler_params=params(),
         cost_estimate=cost(20),
         name="gradient",
-    )(sums, rates, own_media, base, strains, end)
-
-    residual = pl.pallas_call(
+    )(sums, rates, own_media, base, strains)
+
+    residual, gradient_lambda, gradient_mu, velocity_end = pl.pallas_call(
         lambda *refs: residual_kernel(tracks, rows, *refs),
-        out_shape=jax.ShapeDtypeStruct((moments // 2, channels), F32),
-        in_specs=[inside] * 4,
-        out_specs=inside,
+        out_shape=(
+            jax.ShapeDtypeStruct((moments // 2, channels), F32),
+            block,
+            block,
+            jax.ShapeDtypeStruct(velocity.shape, F32),
+        ),
+        in_specs=[inside] * 6,
+        out_specs=(inside, outside, outside, outside),
         scratch_shapes=[
             VMEM((5, BATCH, 2 * PAD + STRIP, LANES), F32),
             VMEM((4, BATCH, STRIP, LANES), F32),
             VMEM(note.shape, F32),
             VMEM(note.shape, F32),
+            pltpu.SemaphoreType.DMA((3,)),
         ],
         compiler_params=params(),
         cost_estimate=cost(2),
         name="residual",
-    )(mine, beside, traces, cells)
+    )(mine, beside, traces, cells, gradients, end)
     return gradient_lambda, gradient_mu, velocity_end, residual
 
 

time: 27.2 us -> 25.9 us (0.952)
  waiting for transfers between devices: 3.05 us -> 2.14 us
    ppermute x1, waiting for transfers between devices: 1.26 us -> 0.01 us  [per_device(): got_depth = lax.ppermute(to_depth, 'depth', depth_swap)]
    pallas_call x1, Pallas kernels: 1.5 us -> 0.82 us  [per_device(): pl.pallas_call(gradient_kernel, out_shape=jax.ShapeDtypeStruct((2, rows,...]
    ppermute x1, waiting for transfers between devices: 0.01 us -> 0.57 us  [per_device(): beside = lax.ppermute(mine, 'depth', depth_swap)]
    pallas_call x1, Pallas kernels: 1.6 us -> 2.08 us  [per_device(): pl.pallas_call(lambda *refs: residual_kernel(tracks, rows, *refs), out_sh...]
    ppermute x1, starting transfers between devices: 0.07 us -> 0.52 us  [per_device(): got_depth = lax.ppermute(to_depth, 'depth', depth_swap)]
    ppermute x1, starting transfers between devices: 3 us -> 2.56 us  [per_device(): got_even = lax.ppermute(to_even, 'track', swap(0))]
  transfers between devices with their start and end apart: 6 -> 6, of which waited for: 2 -> 2; matrix products, arithmetic and copies ran while one was open for 0% -> 0% of each run, Pallas kernels for 31% -> 29%
where the time goes in v19:
time: 25.9 us; the launch traced here: 25.7 us
  Pallas kernels  11.4 us (44%)
  starting transfers between devices  11.4 us (44%)
  waiting for transfers between devices  2.14 us (8%)
  between operations  0.73 us (3%)
    all_to_all x1, starting transfers between devices, per_device(): lax.all_to_all(note, 'track', split_axis=0, concat_axis=0, tiled=True)  7.58 us
    ppermute x1, starting transfers between devices, per_device(): got_even = lax.ppermute(to_even, 'track', swap(0))  2.56 us
    pallas_call x1, Pallas kernels, per_device(): pl.pallas_call(adjoint_kernel, out_shape=(jax.ShapeDtypeStruct((2, rows,...  2.39 us
    pallas_call x1, Pallas kernels, per_device(): pl.pallas_call(lambda *refs: residual_kernel(tracks, rows, *refs), out_sh...  2.08 us
    pallas_call x1, Pallas kernels, per_device(): pl.pallas_call(pack_kernel, out_shape=(jax.ShapeDtypeStruct((FORWARD, row...  1.66 us
    all_to_all x1, waiting for transfers between devices, per_device(): lax.all_to_all(note, 'track', split_axis=0, concat_axis=0, tiled=True)  1.55 us
    pallas_call x1, Pallas kernels, per_device(): pl.pallas_call(forward_kernel, out_shape=(media_of(2), saved_of(2), jax.S...  1.54 us
    pallas_call x1, Pallas kernels, per_device(): pl.pallas_call(forward_inner_kernel, out_shape=(media_of(1), saved_of(1),...  1.04 us
  transfers between devices with their start and end apart: 6, of which 2 were waited for; matrix products, arithmetic and copies ran while one was open for 0% of the time, Pallas kernels for 29%

profile of v19, /device:TPU:0, one launch (start us, length us, event | category | flops | bytes accessed | tf_op | source)
XLA Modules:
  0.0 25.7 jit_solution(7825738851799933814)
XLA Ops:
  0.6 1.7 %pack.1 = (f32[8,64,256]{2,1,0:T(8,128)S(1)}, f32[5,64,256]{2,1,0:T(8,128)S(1)}, f32[80,256]{1,0:T(8,128)S(1)}, f32[184,256]{1,0:T(8,128)S(1)}, f32[184,256]{1,0...) custom-call(f32[2,64,256]{2,1,0:T(8,128)} %refs_0_.1, ...), custom_call_target="tpu_custom_call" | custom-call | flops 5000000000 | bytes 1048576 | tf_op jit(solution)/shard_map/pack/pallas_call | solution.py:638
  2.3 0.5 %collective-permute-start = (f32[80,256]{1,0:T(8,128)S(1)}, f32[80,256]{1,0:T(8,128)S(1)}, u32[]{:S(2)}, u32[]{:S(2)}) collective-permute-start(f32[80,256]{1,0:T(8,128)S(1)} %get-tuple-element.28), channel_id=1, source_target_pairs={{0,1},{1,0},{2,3},{3,2},{4,5},{5,4},{6,7},{7,6},{8,9},{9,8},{10,11... | collective-permute-start | bytes 245768 | tf_op jit(solution)/shard_map/ppermute | solution.py:659
  2.8 2.6 %collective-permute-start.1 = (f32[184,256]{1,0:T(8,128)S(1)}, f32[184,256]{1,0:T(8,128)S(1)}, u32[]{:S(2)}, u32[]{:S(2)}) collective-permute-start(f32[184,256]{1,0:T(8,128)S(1)} %get-tuple-element.32), channel_id=1, source_target_pairs={{0,2},{2,0},{4,6},{6,4},{8,10},{10,8},{12,14},{14,12},{1,3},{3,1},... | collective-permute-start | bytes 565256 | tf_op jit(solution)/shard_map/ppermute | solution.py:662
  5.4 0.7 %collective-permute-start.2 = (f32[184,256]{1,0:T(8,128)S(1)}, f32[184,256]{1,0:T(8,128)S(1)}, u32[]{:S(2)}, u32[]{:S(2)}) collective-permute-start(f32[184,256]{1,0:T(8,128)S(1)} %get-tuple-element.33), channel_id=1, source_target_pairs={{2,4},{4,2},{6,8},{8,6},{10,12},{12,10},{3,5},{5,3},{7,9},{9,7},{1... | collective-permute-start | bytes 565256 | tf_op jit(solution)/shard_map/ppermute | solution.py:661
  6.1 0.0 collective-permute-done.got_depth
  6.1 0.7 %note.1 = f32[8,40,128]{2,1,0:T(8,128)} custom-call(f32[32,128]{1,0:T(8,128)S(1)} %get-tuple-element.27.strip, f32[80,256]{1,0:T(8,128)S(1)} %collective-permute-done.got_depth, f32[4,256]{1,0:T(4,128)S(1)} %get-tuple-element.29.traces.refs_2_, s32[2,1,256]{2,1,0:T(1,128)S(1)} %get-tuple-element.30.cells.refs_3_), custom_call_target="tpu_custom_call" | custom-call | flops 20000000000 | bytes 1048576 | tf_op jit(solution)/shard_map/note/pallas_call | solution.py:667
  6.8 7.6 %all-to-all-start = ((f32[8,40,128]{2,1,0:T(8,128)}), f32[8,40,128]{2,1,0:T(8,128)S(1)}, u32[]{:S(2)}, u32[]{:S(2)}) async-start(f32[8,40,128]{2,1,0:T(8,128)} %note.1), calls=%async_computation | async-start | bytes 327680 | tf_op jit(solution)/shard_map/all_to_all | solution.py:676
  14.3 0.0 collective-permute-done.1.got_even
  14.3 0.0 collective-permute-done.2.got_odd
  14.3 0.1 corners.1
  14.5 0.1 collective-permute-start.3
  14.6 1.5 %forward.1 = (f32[4,2,96,128]{3,2,1,0:T(8,128)S(1)}, f32[4,3,2,64,128]{4,3,2,1,0:T(8,128)S(1)}, f32[2,2,64,128]{3,2,1,0:T(8,128)S(1)}) custom-call(f32[8,64,256]{2,1,0:T(8,128)S(1)} %get-tuple-element.34.held, f32[184,256]{1,0:T(8,128)S(1)} %collective-permute-done.1.got_even, f32[184,256]{1,0:T(8,128)S(1)} %collective-permute-done.2.got_odd), custom_call_target="tpu_custom_call" | custom-call | flops 20000000000 | bytes 1048576 | tf_op jit(solution)/shard_map/forward/pallas_call | solution.py:695
  16.1 0.8 %fibre.1 = (f32[32,128]{1,0:T(8,128)S(1)}, f32[4,16,128]{2,1,0:T(8,128)S(1)}) custom-call(f32[64,128]{1,0:T(8,128)S(1)} %get-tuple-element.41.strip, f32[184,256]{1,0:T(8,128)S(1)} %collective-permute-done.1.got_even, f32[184,256]{1,0:T(8,128)S(1)} %collective-permute-done.2.got_odd), custom_call_target="tpu_custom_call" | custom-call | flops 5000000000 | bytes 1048576 | tf_op jit(solution)/shard_map/fibre/pallas_call | solution.py:731
  16.9 0.0 collective-permute-done.3.corner
  16.9 1.0 %forward_inner.1 = (f32[4,1,96,128]{3,2,1,0:T(8,128)S(1)}, f32[4,3,1,64,128]{4,3,2,1,0:T(8,128)S(1)}, f32[2,64,256]{2,1,0:T(8,128)S(1)}) custom-call(f32[8,64,256]{2,1,0:T(8,128)S(1)} %get-tuple-element.34.held, f32[184,256]{1,0:T(8,128)S(1)} %collective-permute-done.1.got_even, f32[184,256]{1,0:T(8,128)S(1)} %collective-permute-done.2.got_odd, ...), custom_call_target="tpu_custom_call" | custom-call | flops 20000000000 | bytes 1048576 | tf_op jit(solution)/shard_map/forward_inner/pallas_call | solution.py:706
  18.0 2.4 %adjoint.1 = (f32[2,64,256]{2,1,0:T(8,128)S(1)}, f32[2,128,128]{2,1,0:T(8,128)S(1)}) custom-call(f32[5,64,256]{2,1,0:T(8,128)S(1)} %get-tuple-element.31.held, f32[184,256]{1,0:T(8,128)S(1)} %collective-permute-done.1.got_even, f32[184,256]{1,0:T(8,128)S(1)} %collective-permute-done.2.got_odd, f32[80,256]{1,0:T(8,128)S(1)} %collective-permute-done.got_depth, ...), custom_call_target="tpu_custom_call" | custom-call | flops 20000000000 | bytes 1048576 | tf_op jit(solution)/shard_map/adjoint/pallas_call | solution.py:717
  20.3 1.6 %all-to-all-done.notes = f32[8,40,128]{2,1,0:T(8,128)S(1)} async-done(((f32[8,40,128]{2,1,0:T(8,128)}), f32[8,40,128]{2,1,0:T(8,128)S(1)}, u32[]{:S(2)}, u32[]{:S(2)}) %all-to-all-start) | async-done | bytes 163872 | tf_op jit(solution)/shard_map/all_to_all | solution.py:676
  21.9 0.3 %sums.1 = f32[32,128]{1,0:T(8,128)S(1)} custom-call(f32[8,40,128]{2,1,0:T(8,128)S(1)} %relay.1.refs_0_), custom_call_target="tpu_custom_call" | custom-call | flops 20000000000 | bytes 1048576 | tf_op jit(solution)/shard_map/sums/pallas_call | solution.py:760
  22.2 0.0 collective-permute-start.4
  22.2 0.8 %gradient.1.refs_4_ = f32[2,64,256]{2,1,0:T(8,128)S(1)} custom-call(f32[32,128]{1,0:T(8,128)S(1)} %sums.1, f32[32,128]{1,0:T(8,128)S(1)} %get-tuple-element.42.rates, f32[4,16,128]{2,1,0:T(8,128)S(1)} %get-tuple-element.43.media, f32[2,64,256]{2,1,0:T(8,128)S(1)} %get-tuple-element.40.base, f32[2,128,128]{2,1,0:T(8,128)S(1)} %get-tuple-element.44.strains), custom_call_target="tpu_custom_call" | custom-call | flops 20000000000 | bytes 1048576 | tf_op jit(solution)/shard_map/gradient/pallas_call | solution.py:770
  23.0 0.6 %collective-permute-done.4.refs_1_ = f32[8,40,128]{2,1,0:T(8,128)S(1)} collective-permute-done((f32[8,40,128]{2,1,0:T(8,128)S(1)}, f32[8,40,128]{2,1,0:T(8,128)S(1)}, u32[]{:S(2)}, u32[]{:S(2)}) %collective-permute-start.4) | collective-permute-done | bytes 163872 | tf_op jit(solution)/shard_map/ppermute | solution.py:758
  23.6 2.1 %residual.1 = (f32[2,256]{1,0:T(2,128)}, f32[64,256]{1,0:T(8,128)}, f32[64,256]{1,0:T(8,128)}, f32[2,64,256]{2,1,0:T(8,128)}) custom-call(f32[8,40,128]{2,1,0:T(8,128)S(1)} %relay.1.refs_0_, f32[8,40,128]{2,1,0:T(8,128)S(1)} %collective-permute-done.4.refs_1_, f32[4,256]{1,0:T(4,128)S(1)} %get-tuple-element.29.traces.refs_2_, ...), custom_call_target="tpu_custom_call" | custom-call | flops 2000000000 | bytes 1048576 | tf_op jit(solution)/shard_map/residual/pallas_call | solution.py:781
  (1 shorter events, 0.0 us)
Async XLA Ops:
  2.3 3.8 %collective-permute-start = (f32[80,256]{1,0:T(8,128)S(1)}, f32[80,256]{1,0:T(8,128)S(1)}, u32[]{:S(2)}, u32[]{:S(2)}) collective-permute-start(f32[80,256]{1,0:T(8,128)S(1)} %get-tuple-element.28), channel_id=1, source_target_pairs={{0,1},{1,0},{2,3},{3,2},{4,5},{5,4},{6,7},{7,6},{8,9},{9,8},{10,11... | collective-permute-start | bytes 245768 | tf_op jit(solution)/shard_map/ppermute | solution.py:659
  2.8 11.5 %collective-permute-start.1 = (f32[184,256]{1,0:T(8,128)S(1)}, f32[184,256]{1,0:T(8,128)S(1)}, u32[]{:S(2)}, u32[]{:S(2)}) collective-permute-start(f32[184,256]{1,0:T(8,128)S(1)} %get-tuple-element.32), channel_id=1, source_target_pairs={{0,2},{2,0},{4,6},{6,4},{8,10},{10,8},{12,14},{14,12},{1,3},{3,1},... | collective-permute-start | bytes 565256 | tf_op jit(solution)/shard_map/ppermute | solution.py:662
  5.4 9.0 %collective-permute-start.2 = (f32[184,256]{1,0:T(8,128)S(1)}, f32[184,256]{1,0:T(8,128)S(1)}, u32[]{:S(2)}, u32[]{:S(2)}) collective-permute-start(f32[184,256]{1,0:T(8,128)S(1)} %get-tuple-element.33), channel_id=1, source_target_pairs={{2,4},{4,2},{6,8},{8,6},{10,12},{12,10},{3,5},{5,3},{7,9},{9,7},{1... | collective-permute-start | bytes 565256 | tf_op jit(solution)/shard_map/ppermute | solution.py:661
  6.8 15.1 %all-to-all-start = ((f32[8,40,128]{2,1,0:T(8,128)}), f32[8,40,128]{2,1,0:T(8,128)S(1)}, u32[]{:S(2)}, u32[]{:S(2)}) async-start(f32[8,40,128]{2,1,0:T(8,128)} %note.1), calls=%async_computation | async-start | bytes 327680 | tf_op jit(solution)/shard_map/all_to_all | solution.py:676
  14.5 2.4 %collective-permute-start.3 = (f32[32,256]{1,0:T(8,128)S(1)}, f32[32,256]{1,0:T(8,128)S(1)}, u32[]{:S(2)}, u32[]{:S(2)}) collective-permute-start(f32[32,256]{1,0:T(8,128)S(1)} %corners.1), channel_id=1, source_target_pairs={{0,1},{1,0},{2,3},{3,2},{4,5},{5,4},{6,7},{7,6},{8,9},{9,8},{10,11... | collective-permute-start | bytes 98312 | tf_op jit(solution)/shard_map/ppermute | solution.py:687
  22.2 1.4 %collective-permute-start.4 = (f32[8,40,128]{2,1,0:T(8,128)S(1)}, f32[8,40,128]{2,1,0:T(8,128)S(1)}, u32[]{:S(2)}, u32[]{:S(2)}) collective-permute-start(f32[8,40,128]{2,1,0:T(8,128)S(1)} %relay.1.refs_0_), channel_id=1, source_target_pairs={{0,1},{1,0},{2,3},{3,2},{4,5},{5,4},{6,7},{7,6},{8,9},{9,8},{10,11... | collective-permute-start | bytes 491528 | tf_op jit(solution)/shard_map/ppermute | solution.py:758

commit v20 on v19

--- a/solution.py
+++ b/solution.py
@@ -549,10 +549,10 @@
 
 
 def residual_kernel(
-    tracks, columns, notes, beside, obs, cells, gradients, end,
-    residual_out, lambda_out, mu_out, end_out, state, media, low, high, sems,
+    tracks, columns, notes, beside, obs, cells, gradients,
+    residual_out, lambda_out, mu_out, state, media, low, high, sems,
 ):
-    copies = fetch((gradients.at[0], gradients.at[1], end), (lambda_out, mu_out, end_out), sems)
+    copies = fetch((gradients.at[0], gradients.at[1]), (lambda_out, mu_out), sems)
     depth = lax.axis_index("depth")
     low[...] = jnp.where(depth == 0, notes[...], beside[...])
     high[...] = jnp.where(depth == 0, beside[...], notes[...])
@@ -572,9 +572,10 @@
 
 
 def adjoint_kernel(
-    held, got_even, got_odd, got_depth, corner, media, saved, inner_media, inner_saved,
-    base_out, strains_out, state, sums,
+    held, got_even, got_odd, got_depth, corner, media, saved, inner_media, inner_saved, end,
+    base_out, strains_out, end_out, state, sums, sems,
 ):
+    (copy,) = fetch((end,), (end_out,), sems)
     states, totals = each(state, 3, 1), each(sums, 3, 1)
     rows = held.shape[1]
     load_state(states, FORWARD, (0, 1, 2), held, got_even, got_odd, got_depth, corner)
@@ -606,6 +607,7 @@
             packed = jnp.where(here, turn(saveds[0][j // 3, j % 3], spot - EDGE), packed)
         turned = packed.T
         strains_out[group] = turn(jnp.concatenate([turned, jnp.zeros_like(turned)], axis=1), EDGE)
+    copy.wait()
 
 
 def per_device(
@@ -714,19 +716,20 @@
         name="forward_inner",
     )(held, got_even, got_odd, got_depth, got_corner, end)
 
-    base, strains = pl.pallas_call(
+    base, strains, velocity_end = pl.pallas_call(
         adjoint_kernel,
         out_shape=(
             jax.ShapeDtypeStruct((2, rows, depth_cells), F32),
             jax.ShapeDtypeStruct((2, LANES, LANES), F32),
+            jax.ShapeDtypeStruct(velocity.shape, F32),
         ),
-        in_specs=[inside] * 9,
-        out_specs=(inside,) * 2,
-        scratch_shapes=[state_of(3), VMEM((2, 3, rows, LANES), F32)],
+        in_specs=[inside] * 10,
+        out_specs=(inside, inside, outside),
+        scratch_shapes=[state_of(3), VMEM((2, 3, rows, LANES), F32), pltpu.SemaphoreType.DMA((1,))],
         compiler_params=params(),
         cost_estimate=cost(20),
         name="adjoint",
-    )(held_adj, got_even, got_odd, got_depth, got_corner, media, saved, inner_media, inner_saved)
+    )(held_adj, got_even, got_odd, got_depth, got_corner, media, saved, inner_media, inner_saved, end)
 
     rates, own_media = pl.pallas_call(
         fibre_kernel,
@@ -763,7 +766,7 @@
         in_specs=[inside],
         out_specs=inside,
         compiler_params=params(),
-        cost_estimate=cost(20),
+        cost_estimate=cost(2),
         name="sums",
     )(mine)
 
@@ -774,31 +777,30 @@
         out_specs=inside,
         scratch_shapes=[VMEM((5, 2 * PAD + STRIP, LANES), F32)],
         compiler_params=params(),
-        cost_estimate=cost(20),
+        cost_estimate=cost(2),
         name="gradient",
     )(sums, rates, own_media, base, strains)
 
-    residual, gradient_lambda, gradient_mu, velocity_end = pl.pallas_call(
+    residual, gradient_lambda, gradient_mu = pl.pallas_call(
         lambda *refs: residual_kernel(tracks, rows, *refs),
         out_shape=(
             jax.ShapeDtypeStruct((moments // 2, channels), F32),
             block,
             block,
-            jax.ShapeDtypeStruct(velocity.shape, F32),
         ),
-        in_specs=[inside] * 6,
-        out_specs=(inside, outside, outside, outside),
+        in_specs=[inside] * 5,
+        out_specs=(inside, outside, outside),
         scratch_shapes=[
             VMEM((5, BATCH, 2 * PAD + STRIP, LANES), F32),
             VMEM((4, BATCH, STRIP, LANES), F32),
             VMEM(note.shape, F32),
             VMEM(note.shape, F32),
-            pltpu.SemaphoreType.DMA((3,)),
+            pltpu.SemaphoreType.DMA((2,)),
         ],
         compiler_params=params(),
         cost_estimate=cost(2),
         name="residual",
-    )(mine, beside, traces, cells, gradients, end)
+    )(mine, beside, traces, cells, gradients)
     return gradient_lambda, gradient_mu, velocity_end, residual
 
 

time: 25.9 us -> 25.9 us (level)
  waiting for transfers between devices: 2.14 us -> 1.82 us
  Pallas kernels: 11.4 us -> 11.7 us
    all_to_all x1, waiting for transfers between devices: 1.55 us -> 1.23 us  [per_device(): lax.all_to_all(note, 'track', split_axis=0, concat_axis=0, tiled=True)]
    pallas_call x1, Pallas kernels: 2.39 us -> 2.7 us  [per_device(): pl.pallas_call(adjoint_kernel, out_shape=(jax.ShapeDtypeStruct((2, rows,...]
  transfers between devices with their start and end apart: 6 -> 6, of which waited for: 2 -> 2; matrix products, arithmetic and copies ran while one was open for 0% -> 0% of each run, Pallas kernels for 29% -> 30%
where the time goes in v20:
time: 25.9 us; the launch traced here: 25.6 us
  Pallas kernels  11.7 us (45%)
  starting transfers between devices  11.4 us (44%)
  waiting for transfers between devices  1.82 us (7%)
  between operations  0.73 us (3%)
    all_to_all x1, starting transfers between devices, per_device(): lax.all_to_all(note, 'track', split_axis=0, concat_axis=0, tiled=True)  7.58 us
    pallas_call x1, Pallas kernels, per_device(): pl.pallas_call(adjoint_kernel, out_shape=(jax.ShapeDtypeStruct((2, rows,...  2.7 us
    ppermute x1, starting transfers between devices, per_device(): got_even = lax.ppermute(to_even, 'track', swap(0))  2.56 us
    pallas_call x1, Pallas kernels, per_device(): pl.pallas_call(lambda *refs: residual_kernel(tracks, rows, *refs), out_sh...  2.02 us
    pallas_call x1, Pallas kernels, per_device(): pl.pallas_call(pack_kernel, out_shape=(jax.ShapeDtypeStruct((FORWARD, row...  1.66 us
    pallas_call x1, Pallas kernels, per_device(): pl.pallas_call(forward_kernel, out_shape=(media_of(2), saved_of(2), jax.S...  1.54 us
    all_to_all x1, waiting for transfers between devices, per_device(): lax.all_to_all(note, 'track', split_axis=0, concat_axis=0, tiled=True)  1.23 us
    pallas_call x1, Pallas kernels, per_device(): pl.pallas_call(forward_inner_kernel, out_shape=(media_of(1), saved_of(1),...  1.04 us
  transfers between devices with their start and end apart: 6, of which 2 were waited for; matrix products, arithmetic and copies ran while one was open for 0% of the time, Pallas kernels for 30%

profile of v20, /device:TPU:0, one launch (start us, length us, event | category | flops | bytes accessed | tf_op | source)
XLA Modules:
  0.0 25.6 jit_solution(16229832762940297327)
XLA Ops:
  0.6 1.7 %pack.1 = (f32[8,64,256]{2,1,0:T(8,128)S(1)}, f32[5,64,256]{2,1,0:T(8,128)S(1)}, f32[80,256]{1,0:T(8,128)S(1)}, f32[184,256]{1,0:T(8,128)S(1)}, f32[184,256]{1,0...) custom-call(f32[2,64,256]{2,1,0:T(8,128)} %refs_0_.1, ...), custom_call_target="tpu_custom_call" | custom-call | flops 5000000000 | bytes 1048576 | tf_op jit(solution)/shard_map/pack/pallas_call | solution.py:640
  2.3 0.5 %collective-permute-start = (f32[80,256]{1,0:T(8,128)S(1)}, f32[80,256]{1,0:T(8,128)S(1)}, u32[]{:S(2)}, u32[]{:S(2)}) collective-permute-start(f32[80,256]{1,0:T(8,128)S(1)} %get-tuple-element.28), channel_id=1, source_target_pairs={{0,1},{1,0},{2,3},{3,2},{4,5},{5,4},{6,7},{7,6},{8,9},{9,8},{10,11... | collective-permute-start | bytes 245768 | tf_op jit(solution)/shard_map/ppermute | solution.py:661
  2.8 2.6 %collective-permute-start.1 = (f32[184,256]{1,0:T(8,128)S(1)}, f32[184,256]{1,0:T(8,128)S(1)}, u32[]{:S(2)}, u32[]{:S(2)}) collective-permute-start(f32[184,256]{1,0:T(8,128)S(1)} %get-tuple-element.32), channel_id=1, source_target_pairs={{0,2},{2,0},{4,6},{6,4},{8,10},{10,8},{12,14},{14,12},{1,3},{3,1},... | collective-permute-start | bytes 565256 | tf_op jit(solution)/shard_map/ppermute | solution.py:664
  5.4 0.7 %collective-permute-start.2 = (f32[184,256]{1,0:T(8,128)S(1)}, f32[184,256]{1,0:T(8,128)S(1)}, u32[]{:S(2)}, u32[]{:S(2)}) collective-permute-start(f32[184,256]{1,0:T(8,128)S(1)} %get-tuple-element.33), channel_id=1, source_target_pairs={{2,4},{4,2},{6,8},{8,6},{10,12},{12,10},{3,5},{5,3},{7,9},{9,7},{1... | collective-permute-start | bytes 565256 | tf_op jit(solution)/shard_map/ppermute | solution.py:663
  6.1 0.0 collective-permute-done.got_depth
  6.1 0.7 %note.1 = f32[8,40,128]{2,1,0:T(8,128)} custom-call(f32[32,128]{1,0:T(8,128)S(1)} %get-tuple-element.27.strip, f32[80,256]{1,0:T(8,128)S(1)} %collective-permute-done.got_depth, f32[4,256]{1,0:T(4,128)S(1)} %get-tuple-element.29.traces.refs_2_, s32[2,1,256]{2,1,0:T(1,128)S(1)} %get-tuple-element.30.cells.refs_3_), custom_call_target="tpu_custom_call" | custom-call | flops 20000000000 | bytes 1048576 | tf_op jit(solution)/shard_map/note/pallas_call | solution.py:669
  6.8 7.6 %all-to-all-start = ((f32[8,40,128]{2,1,0:T(8,128)}), f32[8,40,128]{2,1,0:T(8,128)S(1)}, u32[]{:S(2)}, u32[]{:S(2)}) async-start(f32[8,40,128]{2,1,0:T(8,128)} %note.1), calls=%async_computation | async-start | bytes 327680 | tf_op jit(solution)/shard_map/all_to_all | solution.py:678
  14.3 0.0 collective-permute-done.1.got_even
  14.3 0.0 collective-permute-done.2.got_odd
  14.3 0.1 corners.1
  14.5 0.1 collective-permute-start.3
  14.6 1.5 %forward.1 = (f32[4,2,96,128]{3,2,1,0:T(8,128)S(1)}, f32[4,3,2,64,128]{4,3,2,1,0:T(8,128)S(1)}, f32[2,2,64,128]{3,2,1,0:T(8,128)S(1)}) custom-call(f32[8,64,256]{2,1,0:T(8,128)S(1)} %get-tuple-element.34.held, f32[184,256]{1,0:T(8,128)S(1)} %collective-permute-done.1.got_even, f32[184,256]{1,0:T(8,128)S(1)} %collective-permute-done.2.got_odd), custom_call_target="tpu_custom_call" | custom-call | flops 20000000000 | bytes 1048576 | tf_op jit(solution)/shard_map/forward/pallas_call | solution.py:697
  16.1 0.8 %fibre.1 = (f32[32,128]{1,0:T(8,128)S(1)}, f32[4,16,128]{2,1,0:T(8,128)S(1)}) custom-call(f32[64,128]{1,0:T(8,128)S(1)} %get-tuple-element.42.strip, f32[184,256]{1,0:T(8,128)S(1)} %collective-permute-done.1.got_even, f32[184,256]{1,0:T(8,128)S(1)} %collective-permute-done.2.got_odd), custom_call_target="tpu_custom_call" | custom-call | flops 5000000000 | bytes 1048576 | tf_op jit(solution)/shard_map/fibre/pallas_call | solution.py:734
  16.9 0.0 collective-permute-done.3.corner
  16.9 1.0 %forward_inner.1 = (f32[4,1,96,128]{3,2,1,0:T(8,128)S(1)}, f32[4,3,1,64,128]{4,3,2,1,0:T(8,128)S(1)}, f32[2,64,256]{2,1,0:T(8,128)S(1)}) custom-call(f32[8,64,256]{2,1,0:T(8,128)S(1)} %get-tuple-element.34.held, f32[184,256]{1,0:T(8,128)S(1)} %collective-permute-done.1.got_even, f32[184,256]{1,0:T(8,128)S(1)} %collective-permute-done.2.got_odd, ...), custom_call_target="tpu_custom_call" | custom-call | flops 20000000000 | bytes 1048576 | tf_op jit(solution)/shard_map/forward_inner/pallas_call | solution.py:708
  18.0 2.7 %adjoint.1 = (f32[2,64,256]{2,1,0:T(8,128)S(1)}, f32[2,128,128]{2,1,0:T(8,128)S(1)}, f32[2,64,256]{2,1,0:T(8,128)}) custom-call(f32[5,64,256]{2,1,0:T(8,128)S(1)} %get-tuple-element.31.held, f32[184,256]{1,0:T(8,128)S(1)} %collective-permute-done.1.got_even, f32[184,256]{1,0:T(8,128)S(1)} %collective-permute-done.2.got_odd, ...), custom_call_target="tpu_custom_call" | custom-call | flops 20000000000 | bytes 1048576 | tf_op jit(solution)/shard_map/adjoint/pallas_call | solution.py:719
  20.7 1.2 %all-to-all-done.notes = f32[8,40,128]{2,1,0:T(8,128)S(1)} async-done(((f32[8,40,128]{2,1,0:T(8,128)}), f32[8,40,128]{2,1,0:T(8,128)S(1)}, u32[]{:S(2)}, u32[]{:S(2)}) %all-to-all-start) | async-done | bytes 163872 | tf_op jit(solution)/shard_map/all_to_all | solution.py:678
  21.9 0.3 %sums.1 = f32[32,128]{1,0:T(8,128)S(1)} custom-call(f32[8,40,128]{2,1,0:T(8,128)S(1)} %relay.1.refs_0_), custom_call_target="tpu_custom_call" | custom-call | flops 2000000000 | bytes 1048576 | tf_op jit(solution)/shard_map/sums/pallas_call | solution.py:763
  22.2 0.0 collective-permute-start.4
  22.2 0.8 %gradient.1.refs_4_ = f32[2,64,256]{2,1,0:T(8,128)S(1)} custom-call(f32[32,128]{1,0:T(8,128)S(1)} %sums.1, f32[32,128]{1,0:T(8,128)S(1)} %get-tuple-element.43.rates, f32[4,16,128]{2,1,0:T(8,128)S(1)} %get-tuple-element.44.media, f32[2,64,256]{2,1,0:T(8,128)S(1)} %get-tuple-element.41.base, f32[2,128,128]{2,1,0:T(8,128)S(1)} %get-tuple-element.45.strains), custom_call_target="tpu_custom_call" | custom-call | flops 2000000000 | bytes 1048576 | tf_op jit(solution)/shard_map/gradient/pallas_call | solution.py:773
  23.0 0.6 %collective-permute-done.4.refs_1_ = f32[8,40,128]{2,1,0:T(8,128)S(1)} collective-permute-done((f32[8,40,128]{2,1,0:T(8,128)S(1)}, f32[8,40,128]{2,1,0:T(8,128)S(1)}, u32[]{:S(2)}, u32[]{:S(2)}) %collective-permute-start.4) | collective-permute-done | bytes 163872 | tf_op jit(solution)/shard_map/ppermute | solution.py:761
  23.6 2.0 %residual.1 = (f32[2,256]{1,0:T(2,128)}, f32[64,256]{1,0:T(8,128)}, f32[64,256]{1,0:T(8,128)}) custom-call(f32[8,40,128]{2,1,0:T(8,128)S(1)} %relay.1.refs_0_, f32[8,40,128]{2,1,0:T(8,128)S(1)} %collective-permute-done.4.refs_1_, f32[4,256]{1,0:T(4,128)S(1)} %get-tuple-element.29.traces.refs_2_, s32[2,1,256]{2,1,0:T(1,128)S(1)} %get-tuple-element.30.cells.refs_3_, ...), custom_call_target="tpu_custom_call" | custom-call | flops 2000000000 | bytes 1048576 | tf_op jit(solution)/shard_map/residual/pallas_call | solution.py:784
  (1 shorter events, 0.0 us)
Async XLA Ops:
  2.3 3.8 %collective-permute-start = (f32[80,256]{1,0:T(8,128)S(1)}, f32[80,256]{1,0:T(8,128)S(1)}, u32[]{:S(2)}, u32[]{:S(2)}) collective-permute-start(f32[80,256]{1,0:T(8,128)S(1)} %get-tuple-element.28), channel_id=1, source_target_pairs={{0,1},{1,0},{2,3},{3,2},{4,5},{5,4},{6,7},{7,6},{8,9},{9,8},{10,11... | collective-permute-start | bytes 245768 | tf_op jit(solution)/shard_map/ppermute | solution.py:661
  2.8 11.5 %collective-permute-start.1 = (f32[184,256]{1,0:T(8,128)S(1)}, f32[184,256]{1,0:T(8,128)S(1)}, u32[]{:S(2)}, u32[]{:S(2)}) collective-permute-start(f32[184,256]{1,0:T(8,128)S(1)} %get-tuple-element.32), channel_id=1, source_target_pairs={{0,2},{2,0},{4,6},{6,4},{8,10},{10,8},{12,14},{14,12},{1,3},{3,1},... | collective-permute-start | bytes 565256 | tf_op jit(solution)/shard_map/ppermute | solution.py:664
  5.4 9.0 %collective-permute-start.2 = (f32[184,256]{1,0:T(8,128)S(1)}, f32[184,256]{1,0:T(8,128)S(1)}, u32[]{:S(2)}, u32[]{:S(2)}) collective-permute-start(f32[184,256]{1,0:T(8,128)S(1)} %get-tuple-element.33), channel_id=1, source_target_pairs={{2,4},{4,2},{6,8},{8,6},{10,12},{12,10},{3,5},{5,3},{7,9},{9,7},{1... | collective-permute-start | bytes 565256 | tf_op jit(solution)/shard_map/ppermute | solution.py:663
  6.8 15.1 %all-to-all-start = ((f32[8,40,128]{2,1,0:T(8,128)}), f32[8,40,128]{2,1,0:T(8,128)S(1)}, u32[]{:S(2)}, u32[]{:S(2)}) async-start(f32[8,40,128]{2,1,0:T(8,128)} %note.1), calls=%async_computation | async-start | bytes 327680 | tf_op jit(solution)/shard_map/all_to_all | solution.py:678
  14.5 2.4 %collective-permute-start.3 = (f32[32,256]{1,0:T(8,128)S(1)}, f32[32,256]{1,0:T(8,128)S(1)}, u32[]{:S(2)}, u32[]{:S(2)}) collective-permute-start(f32[32,256]{1,0:T(8,128)S(1)} %corners.1), channel_id=1, source_target_pairs={{0,1},{1,0},{2,3},{3,2},{4,5},{5,4},{6,7},{7,6},{8,9},{9,8},{10,11... | collective-permute-start | bytes 98312 | tf_op jit(solution)/shard_map/ppermute | solution.py:689
  22.2 1.4 %collective-permute-start.4 = (f32[8,40,128]{2,1,0:T(8,128)S(1)}, f32[8,40,128]{2,1,0:T(8,128)S(1)}, u32[]{:S(2)}, u32[]{:S(2)}) collective-permute-start(f32[8,40,128]{2,1,0:T(8,128)S(1)} %relay.1.refs_0_), channel_id=1, source_target_pairs={{0,1},{1,0},{2,3},{3,2},{4,5},{5,4},{6,7},{7,6},{8,9},{9,8},{10,11... | collective-permute-start | bytes 491528 | tf_op jit(solution)/shard_map/ppermute | solution.py:761

commit v21 on v19

--- a/solution.py
+++ b/solution.py
@@ -416,7 +416,7 @@
     return add_up(rate, 8 * MOMENTS)
 
 
-def sums_kernel(tracks, columns, notes, sums_out):
+def window_sums(tracks, columns, notes, sums_out):
     start = lax.axis_index("track") * columns - EDGE
     group = min(8, tracks)
     row16 = row_ids(IMAGE, LANES)
@@ -529,7 +529,8 @@
     rates_out[...] = strip_steps(state, media)[0]
 
 
-def gradient_kernel(sums, rates, media, base, strains, gradients_out, state):
+def gradient_kernel(tracks, columns, notes, rates, media, base, strains, gradients_out, state, sums):
+    window_sums(tracks, columns, notes, sums)
     rows = base.shape[1]
     near = jnp.concatenate([rates[8 * t : 8 * t + 4, :] for t in range(MOMENTS)], axis=0)
     lane = lane_ids(IMAGE)
@@ -757,26 +758,16 @@
     )(notes, base, rates)
     beside = lax.ppermute(mine, "depth", depth_swap)
 
-    sums = pl.pallas_call(
-        lambda *refs: sums_kernel(tracks, rows, *refs),
-        out_shape=jax.ShapeDtypeStruct((2 * IMAGE, LANES), F32),
-        in_specs=[inside],
-        out_specs=inside,
-        compiler_params=params(),
-        cost_estimate=cost(20),
-        name="sums",
-    )(mine)
-
     gradients = pl.pallas_call(
-        gradient_kernel,
+        lambda *refs: gradient_kernel(tracks, rows, *refs),
         out_shape=jax.ShapeDtypeStruct((2, rows, depth_cells), F32),
         in_specs=[inside] * 5,
         out_specs=inside,
-        scratch_shapes=[VMEM((5, 2 * PAD + STRIP, LANES), F32)],
+        scratch_shapes=[VMEM((5, 2 * PAD + STRIP, LANES), F32), VMEM((2 * IMAGE, LANES), F32)],
         compiler_params=params(),
         cost_estimate=cost(20),
         name="gradient",
-    )(sums, rates, own_media, base, strains)
+    )(mine, rates, own_media, base, strains)
 
     residual, gradient_lambda, gradient_mu, velocity_end = pl.pallas_call(
         lambda *refs: residual_kernel(tracks, rows, *refs),

time: 25.9 us -> 25.7 us (level)
  waiting for transfers between devices: 2.14 us -> 1.83 us
    ppermute x1, waiting for transfers between devices: 0.57 us -> 0.26 us  [per_device(): beside = lax.ppermute(mine, 'depth', depth_swap)]
    pallas_call x2 -> x1, Pallas kernels: 1.1 us -> 1.11 us  [per_device(): pl.pallas_call(lambda *refs: gradient_kernel(tracks, rows, *refs), out_sh...]
  transfers between devices with their start and end apart: 6 -> 6, of which waited for: 2 -> 2; matrix products, arithmetic and copies ran while one was open for 0% -> 0% of each run, Pallas kernels for 29% -> 30%
where the time goes in v21:
time: 25.7 us; the launch traced here: 25.5 us
  starting transfers between devices  11.5 us (45%)
  Pallas kernels  11.4 us (44%)
  waiting for transfers between devices  1.83 us (7%)
  between operations  0.72 us (3%)
    all_to_all x1, starting transfers between devices, per_device(): lax.all_to_all(note, 'track', split_axis=0, concat_axis=0, tiled=True)  7.58 us
    ppermute x1, starting transfers between devices, per_device(): got_even = lax.ppermute(to_even, 'track', swap(0))  2.56 us
    pallas_call x1, Pallas kernels, per_device(): pl.pallas_call(adjoint_kernel, out_shape=(jax.ShapeDtypeStruct((2, rows,...  2.39 us
    pallas_call x1, Pallas kernels, per_device(): pl.pallas_call(lambda *refs: residual_kernel(tracks, rows, *refs), out_sh...  2.08 us
    pallas_call x1, Pallas kernels, per_device(): pl.pallas_call(pack_kernel, out_shape=(jax.ShapeDtypeStruct((FORWARD, row...  1.66 us
    all_to_all x1, waiting for transfers between devices, per_device(): lax.all_to_all(note, 'track', split_axis=0, concat_axis=0, tiled=True)  1.55 us
    pallas_call x1, Pallas kernels, per_device(): pl.pallas_call(forward_kernel, out_shape=(media_of(2), saved_of(2), jax.S...  1.54 us
    pallas_call x1, Pallas kernels, per_device(): pl.pallas_call(lambda *refs: gradient_kernel(tracks, rows, *refs), out_sh...  1.11 us
  transfers between devices with their start and end apart: 6, of which 2 were waited for; matrix products, arithmetic and copies ran while one was open for 0% of the time, Pallas kernels for 30%

profile of v21, /device:TPU:0, one launch (start us, length us, event | category | flops | bytes accessed | tf_op | source)
XLA Modules:
  0.0 25.5 jit_solution(12449728556428015911)
XLA Ops:
  0.6 1.7 %pack.1 = (f32[8,64,256]{2,1,0:T(8,128)S(1)}, f32[5,64,256]{2,1,0:T(8,128)S(1)}, f32[80,256]{1,0:T(8,128)S(1)}, f32[184,256]{1,0:T(8,128)S(1)}, f32[184,256]{1,0...) custom-call(f32[2,64,256]{2,1,0:T(8,128)} %refs_0_.1, ...), custom_call_target="tpu_custom_call" | custom-call | flops 5000000000 | bytes 1048576 | tf_op jit(solution)/shard_map/pack/pallas_call | solution.py:639
  2.3 0.5 %collective-permute-start = (f32[80,256]{1,0:T(8,128)S(1)}, f32[80,256]{1,0:T(8,128)S(1)}, u32[]{:S(2)}, u32[]{:S(2)}) collective-permute-start(f32[80,256]{1,0:T(8,128)S(1)} %get-tuple-element.28), channel_id=1, source_target_pairs={{0,1},{1,0},{2,3},{3,2},{4,5},{5,4},{6,7},{7,6},{8,9},{9,8},{10,11... | collective-permute-start | bytes 245768 | tf_op jit(solution)/shard_map/ppermute | solution.py:660
  2.8 2.6 %collective-permute-start.1 = (f32[184,256]{1,0:T(8,128)S(1)}, f32[184,256]{1,0:T(8,128)S(1)}, u32[]{:S(2)}, u32[]{:S(2)}) collective-permute-start(f32[184,256]{1,0:T(8,128)S(1)} %get-tuple-element.32), channel_id=1, source_target_pairs={{0,2},{2,0},{4,6},{6,4},{8,10},{10,8},{12,14},{14,12},{1,3},{3,1},... | collective-permute-start | bytes 565256 | tf_op jit(solution)/shard_map/ppermute | solution.py:663
  5.4 0.7 %collective-permute-start.2 = (f32[184,256]{1,0:T(8,128)S(1)}, f32[184,256]{1,0:T(8,128)S(1)}, u32[]{:S(2)}, u32[]{:S(2)}) collective-permute-start(f32[184,256]{1,0:T(8,128)S(1)} %get-tuple-element.33), channel_id=1, source_target_pairs={{2,4},{4,2},{6,8},{8,6},{10,12},{12,10},{3,5},{5,3},{7,9},{9,7},{1... | collective-permute-start | bytes 565256 | tf_op jit(solution)/shard_map/ppermute | solution.py:662
  6.1 0.0 collective-permute-done.got_depth
  6.1 0.7 %note.1 = f32[8,40,128]{2,1,0:T(8,128)} custom-call(f32[32,128]{1,0:T(8,128)S(1)} %get-tuple-element.27.strip, f32[80,256]{1,0:T(8,128)S(1)} %collective-permute-done.got_depth, f32[4,256]{1,0:T(4,128)S(1)} %get-tuple-element.29.traces.refs_2_, s32[2,1,256]{2,1,0:T(1,128)S(1)} %get-tuple-element.30.cells.refs_3_), custom_call_target="tpu_custom_call" | custom-call | flops 20000000000 | bytes 1048576 | tf_op jit(solution)/shard_map/note/pallas_call | solution.py:668
  6.8 7.6 %all-to-all-start = ((f32[8,40,128]{2,1,0:T(8,128)}), f32[8,40,128]{2,1,0:T(8,128)S(1)}, u32[]{:S(2)}, u32[]{:S(2)}) async-start(f32[8,40,128]{2,1,0:T(8,128)} %note.1), calls=%async_computation | async-start | bytes 327680 | tf_op jit(solution)/shard_map/all_to_all | solution.py:677
  14.3 0.0 collective-permute-done.1.got_even
  14.3 0.0 collective-permute-done.2.got_odd
  14.3 0.1 corners.1
  14.5 0.1 collective-permute-start.3
  14.6 1.5 %forward.1 = (f32[4,2,96,128]{3,2,1,0:T(8,128)S(1)}, f32[4,3,2,64,128]{4,3,2,1,0:T(8,128)S(1)}, f32[2,2,64,128]{3,2,1,0:T(8,128)S(1)}) custom-call(f32[8,64,256]{2,1,0:T(8,128)S(1)} %get-tuple-element.34.held, f32[184,256]{1,0:T(8,128)S(1)} %collective-permute-done.1.got_even, f32[184,256]{1,0:T(8,128)S(1)} %collective-permute-done.2.got_odd), custom_call_target="tpu_custom_call" | custom-call | flops 20000000000 | bytes 1048576 | tf_op jit(solution)/shard_map/forward/pallas_call | solution.py:696
  16.1 0.8 %fibre.1 = (f32[32,128]{1,0:T(8,128)S(1)}, f32[4,16,128]{2,1,0:T(8,128)S(1)}) custom-call(f32[64,128]{1,0:T(8,128)S(1)} %get-tuple-element.41.strip, f32[184,256]{1,0:T(8,128)S(1)} %collective-permute-done.1.got_even, f32[184,256]{1,0:T(8,128)S(1)} %collective-permute-done.2.got_odd), custom_call_target="tpu_custom_call" | custom-call | flops 5000000000 | bytes 1048576 | tf_op jit(solution)/shard_map/fibre/pallas_call | solution.py:732
  16.9 0.0 collective-permute-done.3.corner
  16.9 1.0 %forward_inner.1 = (f32[4,1,96,128]{3,2,1,0:T(8,128)S(1)}, f32[4,3,1,64,128]{4,3,2,1,0:T(8,128)S(1)}, f32[2,64,256]{2,1,0:T(8,128)S(1)}) custom-call(f32[8,64,256]{2,1,0:T(8,128)S(1)} %get-tuple-element.34.held, f32[184,256]{1,0:T(8,128)S(1)} %collective-permute-done.1.got_even, f32[184,256]{1,0:T(8,128)S(1)} %collective-permute-done.2.got_odd, ...), custom_call_target="tpu_custom_call" | custom-call | flops 20000000000 | bytes 1048576 | tf_op jit(solution)/shard_map/forward_inner/pallas_call | solution.py:707
  18.0 2.4 %adjoint.1 = (f32[2,64,256]{2,1,0:T(8,128)S(1)}, f32[2,128,128]{2,1,0:T(8,128)S(1)}) custom-call(f32[5,64,256]{2,1,0:T(8,128)S(1)} %get-tuple-element.31.held, f32[184,256]{1,0:T(8,128)S(1)} %collective-permute-done.1.got_even, f32[184,256]{1,0:T(8,128)S(1)} %collective-permute-done.2.got_odd, f32[80,256]{1,0:T(8,128)S(1)} %collective-permute-done.got_depth, ...), custom_call_target="tpu_custom_call" | custom-call | flops 20000000000 | bytes 1048576 | tf_op jit(solution)/shard_map/adjoint/pallas_call | solution.py:718
  20.3 1.6 %all-to-all-done.notes = f32[8,40,128]{2,1,0:T(8,128)S(1)} async-done(((f32[8,40,128]{2,1,0:T(8,128)}), f32[8,40,128]{2,1,0:T(8,128)S(1)}, u32[]{:S(2)}, u32[]{:S(2)}) %all-to-all-start) | async-done | bytes 163872 | tf_op jit(solution)/shard_map/all_to_all | solution.py:677
  21.9 0.1 collective-permute-start.4
  22.0 1.1 %gradient.1.refs_4_ = f32[2,64,256]{2,1,0:T(8,128)S(1)} custom-call(f32[8,40,128]{2,1,0:T(8,128)S(1)} %relay.1.refs_0_, f32[32,128]{1,0:T(8,128)S(1)} %get-tuple-element.42.rates.refs_1_, f32[4,16,128]{2,1,0:T(8,128)S(1)} %get-tuple-element.43.refs_2_, f32[2,64,256]{2,1,0:T(8,128)S(1)} %get-tuple-element.40.base.refs_3_, ...), custom_call_target="tpu_custom_call" | custom-call | flops 20000000000 | bytes 1048576 | tf_op jit(solution)/shard_map/gradient/pallas_call | solution.py:761
  23.1 0.3 %collective-permute-done.4.refs_1_ = f32[8,40,128]{2,1,0:T(8,128)S(1)} collective-permute-done((f32[8,40,128]{2,1,0:T(8,128)S(1)}, f32[8,40,128]{2,1,0:T(8,128)S(1)}, u32[]{:S(2)}, u32[]{:S(2)}) %collective-permute-start.4) | collective-permute-done | bytes 163872 | tf_op jit(solution)/shard_map/ppermute | solution.py:759
  23.4 2.1 %residual.1 = (f32[2,256]{1,0:T(2,128)}, f32[64,256]{1,0:T(8,128)}, f32[64,256]{1,0:T(8,128)}, f32[2,64,256]{2,1,0:T(8,128)}) custom-call(f32[8,40,128]{2,1,0:T(8,128)S(1)} %relay.1.refs_0_, f32[8,40,128]{2,1,0:T(8,128)S(1)} %collective-permute-done.4.refs_1_, f32[4,256]{1,0:T(4,128)S(1)} %get-tuple-element.29.traces.refs_2_, ...), custom_call_target="tpu_custom_call" | custom-call | flops 2000000000 | bytes 1048576 | tf_op jit(solution)/shard_map/residual/pallas_call | solution.py:772
  (1 shorter events, 0.0 us)
Async XLA Ops:
  2.3 3.8 %collective-permute-start = (f32[80,256]{1,0:T(8,128)S(1)}, f32[80,256]{1,0:T(8,128)S(1)}, u32[]{:S(2)}, u32[]{:S(2)}) collective-permute-start(f32[80,256]{1,0:T(8,128)S(1)} %get-tuple-element.28), channel_id=1, source_target_pairs={{0,1},{1,0},{2,3},{3,2},{4,5},{5,4},{6,7},{7,6},{8,9},{9,8},{10,11... | collective-permute-start | bytes 245768 | tf_op jit(solution)/shard_map/ppermute | solution.py:660
  2.8 11.5 %collective-permute-start.1 = (f32[184,256]{1,0:T(8,128)S(1)}, f32[184,256]{1,0:T(8,128)S(1)}, u32[]{:S(2)}, u32[]{:S(2)}) collective-permute-start(f32[184,256]{1,0:T(8,128)S(1)} %get-tuple-element.32), channel_id=1, source_target_pairs={{0,2},{2,0},{4,6},{6,4},{8,10},{10,8},{12,14},{14,12},{1,3},{3,1},... | collective-permute-start | bytes 565256 | tf_op jit(solution)/shard_map/ppermute | solution.py:663
  5.4 9.0 %collective-permute-start.2 = (f32[184,256]{1,0:T(8,128)S(1)}, f32[184,256]{1,0:T(8,128)S(1)}, u32[]{:S(2)}, u32[]{:S(2)}) collective-permute-start(f32[184,256]{1,0:T(8,128)S(1)} %get-tuple-element.33), channel_id=1, source_target_pairs={{2,4},{4,2},{6,8},{8,6},{10,12},{12,10},{3,5},{5,3},{7,9},{9,7},{1... | collective-permute-start | bytes 565256 | tf_op jit(solution)/shard_map/ppermute | solution.py:662
  6.8 15.1 %all-to-all-start = ((f32[8,40,128]{2,1,0:T(8,128)}), f32[8,40,128]{2,1,0:T(8,128)S(1)}, u32[]{:S(2)}, u32[]{:S(2)}) async-start(f32[8,40,128]{2,1,0:T(8,128)} %note.1), calls=%async_computation | async-start | bytes 327680 | tf_op jit(solution)/shard_map/all_to_all | solution.py:677
  14.5 2.4 %collective-permute-start.3 = (f32[32,256]{1,0:T(8,128)S(1)}, f32[32,256]{1,0:T(8,128)S(1)}, u32[]{:S(2)}, u32[]{:S(2)}) collective-permute-start(f32[32,256]{1,0:T(8,128)S(1)} %corners.1), channel_id=1, source_target_pairs={{0,1},{1,0},{2,3},{3,2},{4,5},{5,4},{6,7},{7,6},{8,9},{9,8},{10,11... | collective-permute-start | bytes 98312 | tf_op jit(solution)/shard_map/ppermute | solution.py:688
  21.9 1.5 %collective-permute-start.4 = (f32[8,40,128]{2,1,0:T(8,128)S(1)}, f32[8,40,128]{2,1,0:T(8,128)S(1)}, u32[]{:S(2)}, u32[]{:S(2)}) collective-permute-start(f32[8,40,128]{2,1,0:T(8,128)S(1)} %relay.1.refs_0_), channel_id=1, source_target_pairs={{0,1},{1,0},{2,3},{3,2},{4,5},{5,4},{6,7},{7,6},{8,9},{9,8},{10,11... | collective-permute-start | bytes 491528 | tf_op jit(solution)/shard_map/ppermute | solution.py:759
